TPU v7x, 32 devices: a whole 2x2x4 slice. The times are simulated.
32 devices in a mesh: leaf: 8 (over z, x), rows: 2 (over y), rhs: 2 (over core).
Axes of the slice: x: 2, y: 2, z: 4, core: 2. Of those that a mesh axis runs over, the one named last changes fastest.
Arguments:
- right_side: float32 [16, 128, 2048], P('leaf', 'rhs', 'rows'), may hold values from -6 to 6
- inverse_diag: bfloat16 [16, 2048, 2048], P('leaf', None, ('rows', 'rhs')), may hold values from -0.1 to 1.5, as said below
- lower_blocks: bfloat16 [16, 16, 128, 2048], P('leaf', None, None, 'rows'), may hold values from -0.0625 to 0.0625
- block_rows: int32 [16, 16], P('leaf'), may hold values from 0 to 47, as said below
Outputs:
- solved: float32 [16, 128, 2048], P('leaf', 'rhs', 'rows')
Inputs may be any that keep to these rules, and one draw needn't show every extreme that they name: `inverse_diag`: in every row of an inverse block, the diagonal entry is positive and larger than every other entry of that row. `block_rows`: row i lists 16 distinct block numbers below 2048 / 128 times the depth of slot i; the first is 0, the first block of the root's rows, and the second is the last block of its parent's rows; the rows of the root and of slot 15 are not read.
All inputs are finite; a program needn't handle non-finite values.
Results may differ from a plain program's by a relative error of at most 0.004.
Values may be sent and summed in bfloat16 or wider, within the bound.
No kernel may reach another device: no remote copies, remote signals or barrier semaphores. Data moves between devices by JAX's collectives and lax.ppermute only.
A program may use at most 64 MiB of HBM per device.

v0:
```python
import jax
import jax.numpy as jnp
from jax import lax
from jax.sharding import PartitionSpec as P


def swapped(value, axis, stride):
    mask = 2**stride
    pairs = [(source, source ^ mask) for source in range(lax.axis_size(axis))]
    return lax.ppermute(value, axis, pairs)


def count_divides(number, highest):
    running = jnp.zeros((), jnp.int32)
    for power_index in range(1, highest + 1):
        running = running + (number % 2**power_index == 0).astype(jnp.int32)
    return running


def fold_solve(reduced, inverse_slot, active):
    empty_sum = jnp.zeros((reduced.shape[0], inverse_slot.shape[1]), jnp.float32)
    shard_piece = lax.all_gather(reduced, "rows", axis=1, tiled=True)

    def apply_rows():
        return jnp.dot(shard_piece, inverse_slot, preferred_element_type=jnp.float32)

    return lax.cond(active, apply_rows, lambda: empty_sum)


def local(right_side, inverse_diag, lower_blocks, block_rows):
    leaf_count = lax.axis_size("leaf")
    top_depth = leaf_count.bit_length() - 1
    leaf_index = lax.axis_index("leaf")
    inverse_local = lax.all_gather(inverse_diag, "rhs", axis=2, tiled=True)
    inverse_upper = inverse_local[1]
    depth_upper = top_depth - 1 - count_divides(leaf_index + 1, top_depth)
    block_width = lower_blocks.shape[2]
    rhs_count = right_side.shape[1]
    piece_width = right_side.shape[2]
    ancestors = []
    empty_piece = jnp.zeros((rhs_count, piece_width), jnp.float32)
    solved_upper = jnp.zeros((rhs_count, inverse_upper.shape[1]), jnp.float32)
    solved_lower = empty_piece
    for depth_now in range(top_depth + 1):
        slot_now = 1 if depth_now < top_depth else 0
        if slot_now == 1:
            active = depth_upper == depth_now
        else:
            active = jnp.ones((), jnp.bool_)
        if depth_now > 0:
            joined = jnp.concatenate(ancestors, axis=1)
            slot_rows = block_rows[slot_now]
            slot_weights = lower_blocks[slot_now]

            def apply_offset():
                tile_view = joined.reshape(rhs_count, -1, block_width)
                picked = jnp.take(tile_view, slot_rows, axis=1, mode="clip").reshape(rhs_count, -1)
                weights = slot_weights.reshape(-1, piece_width)
                return jnp.dot(picked, weights, preferred_element_type=jnp.float32)

            offset = lax.cond(active, apply_offset, lambda: empty_piece)
            reduced = (right_side[slot_now] - offset).astype(jnp.bfloat16)
        else:
            reduced = right_side[slot_now].astype(jnp.bfloat16)
        if slot_now == 1:
            result = fold_solve(reduced, inverse_upper, active)
            solved_upper = jnp.where(active, result, solved_upper)
        else:
            solved_lower = fold_solve(reduced, inverse_local[0], active)
        if depth_now < top_depth:
            height = top_depth - depth_now
            sending = solved_upper.astype(jnp.bfloat16)
            arrived = sending
            for bit_number in range(height - 1, -1, -1):
                partner_value = swapped(arrived, "leaf", bit_number)
                if bit_number == height - 1:
                    holder = leaf_index % 2**height == 2 ** (height - 1) - 1
                else:
                    holder = leaf_index % 2 ** (bit_number + 1) == 2 ** (bit_number + 1) - 1
                arrived = jnp.where(holder, arrived, partner_value)
            ancestors.append(lax.all_gather(arrived, "rows", axis=1, tiled=True))
    return jnp.stack([solved_lower, solved_upper])


def solution(mesh):
    return jax.shard_map(
        local,
        mesh=mesh,
        in_specs=(
            P("leaf", "rhs", "rows"),
            P("leaf", None, ("rows", "rhs")),
            P("leaf", None, None, "rows"),
            P("leaf", None),
        ),
        out_specs=P("leaf", "rhs", "rows"),
        check_vma=False,
    )
```

profile of v0, /device:TPU:0, one launch (start us, length us, event | category | flops | bytes accessed | tf_op | source)
XLA Modules:
  0.0 135.9 jit_solution(17161056951711523542)
XLA Ops:
  6.5 0.0 copy-start
  6.5 0.0 all-gather.2.cloned.1.call-start
  6.5 0.7 all-gather.2.cloned.1.call-update
  7.3 0.3 copy-done
  7.6 7.1 %all_gather.24 = bf16[64,2048]{1,0:T(8,128)(2,1)S(1)} all-gather(bf16[64,1024]{1,0:T(8,128)(2,1)S(1)} %bitcast_convert_fusion), channel_id=1, replica_groups=mesh['leaf'=8,'rows'=2,'rhs'=2] {'rows'}, dimensions={1}, use_global_device_ids=true | all-gather | bytes 393216 | tf_op jit(solution)/shard_map/all_gather | solution.py:22
  14.7 16.8 %all-gather.2.cloned.1.call-done = bf16[2,2048,1024]{2,1,0:T(8,128)(2,1)} async-done(((bf16[2,2048,512]{2,1,0:T(8,128)(2,1)}), bf16[2,2048,1024]{2,1,0:T(8,128)(2,1)}) %all-gather.2.cloned.1.call-update) | async-done | bytes 8388624 | tf_op jit(solution)/shard_map/all_gather | solution.py:34
  31.5 4.6 %slice_bitcast_fusion.2 = bf16[2048,1024]{1,0:T(8,128)(2,1)} fusion(bf16[2,2048,1024]{2,1,0:T(8,128)(2,1)} %all-gather.2.cloned.1.call-done), kind=kLoop, calls=%fused_computation.15 | loop fusion | bytes 8388608 | tf_op jit(solution)/shard_map/squeeze | solution.py:35
  36.2 2.7 %collective-permute-start = (bf16[64,1024]{1,0:T(8,128)(2,1)S(1)}, bf16[64,1024]{1,0:T(8,128)(2,1)S(1)}, u32[]{:S(2)}, u32[]{:S(2)}) collective-permute-start(bf16[64,1024]{1,0:T(8,128)(2,1)S(1)} %select_convert_fusion), channel_id=1, source_target_pairs={{0,16},{4,20},{8,24},{12,28},{16,0},{20,4},{24,8},{28,12},{1,17},{... | collective-permute-start | bytes 393224 | tf_op jit(solution)/shard_map/ppermute | solution.py:10
  38.9 6.8 %collective-permute-done = bf16[64,1024]{1,0:T(8,128)(2,1)S(1)} collective-permute-done((bf16[64,1024]{1,0:T(8,128)(2,1)S(1)}, bf16[64,1024]{1,0:T(8,128)(2,1)S(1)}, u32[]{:S(2)}, u32[]{:S(2)}) %collective-permute-start) | collective-permute-done | bytes 131104 | tf_op jit(solution)/shard_map/ppermute | solution.py:10
  45.7 0.0 copy-start.1
  45.7 0.8 collective-permute-start.1
  46.5 6.1 %fusion.16 = (bf16[1,16,128,1024]{3,2,1,0:T(8,128)(2,1)}, bf16[1,16,128,1024]{3,2,1,0:T(8,128)(2,1)}) fusion(bf16[2,16,128,1024]{3,2,1,0:T(8,128)(2,1)} %param.16), kind=kLoop, calls=%fused_computation.45 | loop fusion | bytes 16777216 | tf_op jit(solution)/shard_map/slice | solution.py:53
  52.6 0.0 collective-permute-done.1
  52.6 2.7 %collective-permute-start.2 = (bf16[64,1024]{1,0:T(8,128)(2,1)S(1)}, bf16[64,1024]{1,0:T(8,128)(2,1)S(1)}, u32[]{:S(2)}, u32[]{:S(2)}) collective-permute-start(bf16[64,1024]{1,0:T(8,128)(2,1)S(1)} %broadcast_select_fusion.4), channel_id=1, source_target_pairs={{0,4},{4,0},{8,12},{12,8},{16,20},{20,16},{24,28},{28,24},{1,5},{5... | collective-permute-start | bytes 393224 | tf_op jit(solution)/shard_map/ppermute | solution.py:10
  55.3 0.0 copy-done.1
  55.3 2.9 %collective-permute-done.2 = bf16[64,1024]{1,0:T(8,128)(2,1)S(1)} collective-permute-done((bf16[64,1024]{1,0:T(8,128)(2,1)S(1)}, bf16[64,1024]{1,0:T(8,128)(2,1)S(1)}, u32[]{:S(2)}, u32[]{:S(2)}) %collective-permute-start.2) | collective-permute-done | bytes 131104 | tf_op jit(solution)/shard_map/ppermute | solution.py:10
  58.3 5.6 %all_gather.26 = bf16[64,2048]{1,0:T(8,128)(2,1)S(1)} all-gather(bf16[64,1024]{1,0:T(8,128)(2,1)S(1)} %broadcast_select_fusion.6), channel_id=1, replica_groups=mesh['leaf'=8,'rows'=2,'rhs'=2] {'rows'}, dimensions={1}, use_global_device_ids=true | all-gather | bytes 393216 | tf_op jit(solution)/shard_map/all_gather | solution.py:81
  64.0 5.6 %all_gather.27 = bf16[64,2048]{1,0:T(8,128)(2,1)S(1)} all-gather(bf16[64,1024]{1,0:T(8,128)(2,1)S(1)} %fusion.11), channel_id=1, replica_groups=mesh['leaf'=8,'rows'=2,'rhs'=2] {'rows'}, dimensions={1}, use_global_device_ids=true | all-gather | bytes 393216 | tf_op jit(solution)/shard_map/all_gather | solution.py:22
  69.7 0.7 collective-permute-start.3
  70.5 4.3 %collective-permute-done.3 = bf16[64,1024]{1,0:T(8,128)(2,1)S(1)} collective-permute-done((bf16[64,1024]{1,0:T(8,128)(2,1)S(1)}, bf16[64,1024]{1,0:T(8,128)(2,1)S(1)}, u32[]{:S(2)}, u32[]{:S(2)}) %collective-permute-start.3) | collective-permute-done | bytes 131104 | tf_op jit(solution)/shard_map/ppermute | solution.py:10
  74.8 8.8 %collective-permute-start.4 = (bf16[64,1024]{1,0:T(8,128)(2,1)S(1)}, bf16[64,1024]{1,0:T(8,128)(2,1)S(1)}, u32[]{:S(2)}, u32[]{:S(2)}) collective-permute-start(bf16[64,1024]{1,0:T(8,128)(2,1)S(1)} %broadcast_select_fusion.2), channel_id=1, source_target_pairs={{0,4},{4,0},{8,12},{12,8},{16,20},{20,16},{24,28},{28,24},{1,5},{5... | collective-permute-start | bytes 393224 | tf_op jit(solution)/shard_map/ppermute | solution.py:10
  83.6 2.9 %collective-permute-done.4 = bf16[64,1024]{1,0:T(8,128)(2,1)S(1)} collective-permute-done((bf16[64,1024]{1,0:T(8,128)(2,1)S(1)}, bf16[64,1024]{1,0:T(8,128)(2,1)S(1)}, u32[]{:S(2)}, u32[]{:S(2)}) %collective-permute-start.4) | collective-permute-done | bytes 131104 | tf_op jit(solution)/shard_map/ppermute | solution.py:10
  86.5 5.9 %all_gather.28 = bf16[64,2048]{1,0:T(8,128)(2,1)S(1)} all-gather(bf16[64,1024]{1,0:T(8,128)(2,1)S(1)} %broadcast_select_fusion.5), channel_id=1, replica_groups=mesh['leaf'=8,'rows'=2,'rhs'=2] {'rows'}, dimensions={1}, use_global_device_ids=true | all-gather | bytes 393216 | tf_op jit(solution)/shard_map/all_gather | solution.py:81
  92.4 3.8 %conditional.8 = (f32[64,1024]{1,0:T(8,128)S(1)}) conditional(s32[]{:T(128)} %convert_element_type.50, () %tuple.42, (bf16[64,4096]{1,0:T(8,128)(2,1)S(1)}, s32[16]{0:T(128)S(1)}, bf16[1,16,128,1024]{3,2,1,0:T(8,128)(2,1)}) %tuple.43), branch_computations={%region_6.7_spmd, %region_7.8_spmd} | conditional | flops 268436480 | bytes 6295688 | solution.py:61
  92.4 0.1 copy_bitcast_fusion.1
  92.6 0.6 gather_fusion.1
  93.2 3.0 %fusion.3 = f32[64,1024]{1,0:T(8,128)S(1)} fusion(bf16[2048,1024]{1,0:T(8,128)(2,1)} %bitcast.78, bf16[16,64,128]{2,1,0:T(8,128)(2,1)S(1)} %gather_fusion.1), kind=kOutput, calls=%fused_computation.9 | convolution fusion | flops 268435456 | bytes 4718592 | tf_op jit(solution)/shard_map/cond/branch_1_fun/dot_general | solution.py:59
  96.3 5.6 %all_gather.29 = bf16[64,2048]{1,0:T(8,128)(2,1)S(1)} all-gather(bf16[64,1024]{1,0:T(8,128)(2,1)S(1)} %fusion.12), channel_id=1, replica_groups=mesh['leaf'=8,'rows'=2,'rhs'=2] {'rows'}, dimensions={1}, use_global_device_ids=true | all-gather | bytes 393216 | tf_op jit(solution)/shard_map/all_gather | solution.py:22
  101.9 3.0 %conditional.9 = (f32[64,1024]{1,0:T(8,128)S(1)}) conditional(s32[]{:T(128)} %convert_element_type.50, () %tuple.41, (bf16[64,2048]{1,0:T(8,128)(2,1)S(1)}, bf16[2048,1024]{1,0:T(8,128)(2,1)}) %tuple.44), branch_computations={%region_8.9_spmd, %region_9.10_spmd} | conditional | flops 268435456 | bytes 4718600 | solution.py:27
  101.9 3.0 %fusion.19 = f32[64,1024]{1,0:T(8,128)S(1)} fusion(bf16[64,2048]{1,0:T(8,128)(2,1)S(1)} %get-tuple-element.54, bf16[2048,1024]{1,0:T(8,128)(2,1)} %get-tuple-element.55), kind=kOutput, calls=%fused_computation.48 | convolution fusion | flops 268435456 | bytes 4718592 | tf_op jit(solution)/shard_map/cond/branch_1_fun/dot_general | solution.py:25
  105.0 0.1 collective-permute-start.5
  105.1 4.9 %collective-permute-done.5 = bf16[64,1024]{1,0:T(8,128)(2,1)S(1)} collective-permute-done((bf16[64,1024]{1,0:T(8,128)(2,1)S(1)}, bf16[64,1024]{1,0:T(8,128)(2,1)S(1)}, u32[]{:S(2)}, u32[]{:S(2)}) %collective-permute-start.5) | collective-permute-done | bytes 131104 | tf_op jit(solution)/shard_map/ppermute | solution.py:10
  110.0 5.6 %all_gather.30 = bf16[64,2048]{1,0:T(8,128)(2,1)S(1)} all-gather(bf16[64,1024]{1,0:T(8,128)(2,1)S(1)} %broadcast_select_fusion.1), channel_id=1, replica_groups=mesh['leaf'=8,'rows'=2,'rhs'=2] {'rows'}, dimensions={1}, use_global_device_ids=true | all-gather | bytes 393216 | tf_op jit(solution)/shard_map/all_gather | solution.py:81
  115.7 0.2 copy_bitcast_fusion.2
  115.9 0.6 gather_fusion.2
  116.5 3.0 %fusion.8 = bf16[64,1024]{1,0:T(8,128)(2,1)S(1)} fusion(bf16[2048,1024]{1,0:T(8,128)(2,1)} %bitcast.79, f32[2,64,1024]{2,1,0:T(8,128)S(1)} %copy-done, bf16[16,64,128]{2,1,0:T(8,128)(2,1)S(1)} %gather_fusion.2), kind=kOutput, calls=%fused_computation.18 | convolution fusion | flops 268566528 | bytes 4849664 | tf_op jit(solution)/shard_map/cond/branch_1_fun/dot_general | solution.py:59
  119.6 5.6 %all_gather.31 = bf16[64,2048]{1,0:T(8,128)(2,1)S(1)} all-gather(bf16[64,1024]{1,0:T(8,128)(2,1)S(1)} %fusion.8), channel_id=1, replica_groups=mesh['leaf'=8,'rows'=2,'rhs'=2] {'rows'}, dimensions={1}, use_global_device_ids=true | all-gather | bytes 393216 | tf_op jit(solution)/shard_map/all_gather | solution.py:22
  125.2 3.0 %fusion.7 = f32[1,64,1024]{2,1,0:T(8,128)S(1)} fusion(bf16[64,2048]{1,0:T(8,128)(2,1)S(1)} %all_gather.31, bf16[2,2048,1024]{2,1,0:T(8,128)(2,1)} %all-gather.2.cloned.1.call-done), kind=kOutput, calls=%fused_computation.17 | convolution fusion | flops 268435456 | bytes 4718592 | tf_op jit(solution)/shard_map/cond/branch_1_fun/dot_general | solution.py:25
  128.2 0.8 pad_maximum_fusion.1
  (23 shorter events, 0.5 us)
Async XLA Ops:
  6.5 1.0 copy-start
  6.5 25.0 %all-gather.2.cloned.1.call-start = ((), (), s32[]{:S(2)}) async-start(), calls=%async_computation | async-start | bytes 12582912 | tf_op jit(solution)/shard_map/all_gather | solution.py:34
  36.2 9.5 %collective-permute-start = (bf16[64,1024]{1,0:T(8,128)(2,1)S(1)}, bf16[64,1024]{1,0:T(8,128)(2,1)S(1)}, u32[]{:S(2)}, u32[]{:S(2)}) collective-permute-start(bf16[64,1024]{1,0:T(8,128)(2,1)S(1)} %select_convert_fusion), channel_id=1, source_target_pairs={{0,16},{4,20},{8,24},{12,28},{16,0},{20,4},{24,8},{28,12},{1,17},{... | collective-permute-start | bytes 393224 | tf_op jit(solution)/shard_map/ppermute | solution.py:10
  45.7 9.6 %copy-start.1 = (s32[2,16]{1,0:T(2,128)S(1)}, s32[2,16]{1,0:T(2,128)}, u32[]{:S(2)}) copy-start(s32[2,16]{1,0:T(2,128)} %param.17) | copy-start | bytes 388
  45.7 6.9 %collective-permute-start.1 = (bf16[64,1024]{1,0:T(8,128)(2,1)S(1)}, bf16[64,1024]{1,0:T(8,128)(2,1)S(1)}, u32[]{:S(2)}, u32[]{:S(2)}) collective-permute-start(bf16[64,1024]{1,0:T(8,128)(2,1)S(1)} %broadcast_select_fusion.3), channel_id=1, source_target_pairs={{0,8},{4,12},{8,0},{12,4},{16,24},{20,28},{24,16},{28,20},{1,9},{5... | collective-permute-start | bytes 393224 | tf_op jit(solution)/shard_map/ppermute | solution.py:10
  52.6 5.7 %collective-permute-start.2 = (bf16[64,1024]{1,0:T(8,128)(2,1)S(1)}, bf16[64,1024]{1,0:T(8,128)(2,1)S(1)}, u32[]{:S(2)}, u32[]{:S(2)}) collective-permute-start(bf16[64,1024]{1,0:T(8,128)(2,1)S(1)} %broadcast_select_fusion.4), channel_id=1, source_target_pairs={{0,4},{4,0},{8,12},{12,8},{16,20},{20,16},{24,28},{28,24},{1,5},{5... | collective-permute-start | bytes 393224 | tf_op jit(solution)/shard_map/ppermute | solution.py:10
  69.7 5.0 %collective-permute-start.3 = (bf16[64,1024]{1,0:T(8,128)(2,1)S(1)}, bf16[64,1024]{1,0:T(8,128)(2,1)S(1)}, u32[]{:S(2)}, u32[]{:S(2)}) collective-permute-start(bf16[64,1024]{1,0:T(8,128)(2,1)S(1)} %get-tuple-element.56), channel_id=1, source_target_pairs={{0,8},{4,12},{8,0},{12,4},{16,24},{20,28},{24,16},{28,20},{1,9},{5... | collective-permute-start | bytes 393224 | tf_op jit(solution)/shard_map/ppermute | solution.py:10
  74.8 11.7 %collective-permute-start.4 = (bf16[64,1024]{1,0:T(8,128)(2,1)S(1)}, bf16[64,1024]{1,0:T(8,128)(2,1)S(1)}, u32[]{:S(2)}, u32[]{:S(2)}) collective-permute-start(bf16[64,1024]{1,0:T(8,128)(2,1)S(1)} %broadcast_select_fusion.2), channel_id=1, source_target_pairs={{0,4},{4,0},{8,12},{12,8},{16,20},{20,16},{24,28},{28,24},{1,5},{5... | collective-permute-start | bytes 393224 | tf_op jit(solution)/shard_map/ppermute | solution.py:10
  105.0 5.0 %collective-permute-start.5 = (bf16[64,1024]{1,0:T(8,128)(2,1)S(1)}, bf16[64,1024]{1,0:T(8,128)(2,1)S(1)}, u32[]{:S(2)}, u32[]{:S(2)}) collective-permute-start(bf16[64,1024]{1,0:T(8,128)(2,1)S(1)} %fusion.14), channel_id=1, source_target_pairs={{0,4},{4,0},{8,12},{12,8},{16,20},{20,16},{24,28},{28,24},{1,5},{5... | collective-permute-start | bytes 393224 | tf_op jit(solution)/shard_map/ppermute | solution.py:10
Sparse Core Ops, SparseCore 0:
  8.9 22.5 all-gather.1
where the time goes:
time: 136 us
  blocking collectives  41.2 us (30%)
  waiting for transfers between devices  39.4 us (29%)
  starting transfers between devices  15.8 us (12%)
  between operations  13.6 us (10%)
  local copies, waits for them, and re-layouts  12.4 us (9%)
  matrix products  12.1 us (9%)
  other arithmetic  1.4 us (1%)
    all_gather x4, blocking collectives, fold_solve(): shard_piece = lax.all_gather(reduced, 'rows', axis=1, tiled=True)  24.1 us
    ppermute x6, waiting for transfers between devices, swapped(): return lax.ppermute(value, axis, pairs)  21.9 us
    all_gather x3, blocking collectives, local(): ancestors.append(lax.all_gather(arrived, 'rows', axis=1, tiled=True))  17.1 us
    all_gather x1, waiting for transfers between devices, local(): inverse_local = lax.all_gather(inverse_diag, 'rhs', axis=2, tiled=True)  16.8 us
    ppermute x6, starting transfers between devices, swapped(): return lax.ppermute(value, axis, pairs)  15.8 us
    slice x1, local copies, waits for them, and re-layouts, local(): slot_weights = lower_blocks[slot_now]  6.08 us
    dot_general x2, matrix products, apply_rows(): jnp.dot(shard_piece, inverse_slot, preferred_element_type=jnp.float32)  6.06 us
    dot_general x2, matrix products, apply_offset(): return jnp.dot(picked, weights, preferred_element_type=jnp.float32)  6.06 us
  transfers between devices with their start and end apart: 7, of which 6 were waited for; matrix products, arithmetic and copies ran while one was open for 5% of the time, Pallas kernels for 0%

commit v1 on v0

v1 whole, which is shorter than its diff:
```python
import functools
import jax
import jax.numpy as jnp
from jax import lax
from jax.experimental import pallas as pl
from jax.experimental.pallas import tpu as pltpu
from jax.sharding import PartitionSpec as P

F32 = jnp.float32
BF16 = jnp.bfloat16
VMEM = pltpu.VMEM


def cast_kernel(right_ref, out_ref):
    out_ref[...] = right_ref[1].astype(BF16)


def offset_kernel(level, slot, rows, fulls, position_ref, block_rows_ref, right_ref, lower_ref, *refs):
    full_refs = refs[:fulls]
    piece_refs = refs[fulls:fulls + rows]
    reduced_ref, newest_ref, picked = refs[fulls + rows:]
    width = piece_refs[0].shape[1]
    block_width = lower_ref.shape[2]
    blocks = lower_ref.shape[1]
    own = position_ref[0]
    for shift, piece_ref in enumerate(piece_refs):
        source = lax.rem(own - shift + rows, rows)
        newest_ref[:, pl.ds(pl.multiple_of(source * width, width), width)] = piece_ref[...]
    blocks_each = rows * width // block_width
    known = [*full_refs, newest_ref]
    for index in range(blocks):
        number = jnp.clip(block_rows_ref[slot, index], 0, level * blocks_each - 1)
        ancestor = number // blocks_each
        column = pl.multiple_of((number - ancestor * blocks_each) * block_width, block_width)
        target = pl.ds(index * block_width, block_width)
        for which, known_ref in enumerate(known):
            @pl.when(ancestor == which)
            def _():
                picked[:, target] = known_ref[:, pl.ds(column, block_width)]
    weights = lower_ref[slot].reshape(blocks * block_width, width)
    offset = jnp.dot(picked[...], weights, preferred_element_type=F32)
    reduced_ref[...] = (right_ref[slot] - offset).astype(BF16)


def apply_inverse(slot, rows, cores, position_ref, piece_refs, inverse_refs, store):
    width = piece_refs[0].shape[1]
    quarter = inverse_refs[0].shape[-1]
    own = position_ref[0]
    own_core = position_ref[1]
    for turn, inverse_ref in enumerate(inverse_refs):
        total = None
        for shift, piece_ref in enumerate(piece_refs):
            source = lax.rem(own - shift + rows, rows)
            depth = pl.ds(pl.multiple_of(source * width, width), width)
            part = inverse_ref[slot, depth, :]
            term = jnp.dot(piece_ref[...], part, preferred_element_type=F32)
            total = term if total is None else total + term
        core = lax.rem(own_core - turn + cores, cores)
        store(pl.ds(pl.multiple_of(core * quarter, quarter), quarter), total)


def solve_kernel(rows, cores, depth_now, position_ref, *refs):
    piece_refs = refs[:rows]
    inverse_refs = refs[rows:rows + cores]
    rest = refs[rows + cores:]
    if depth_now == 0:
        before_ref, (rounded_ref, solved_ref) = None, rest
    else:
        before_ref, rounded_ref, solved_ref = rest
    active = position_ref[2] == depth_now

    def store(columns, total):
        rounded_ref[:, columns] = total.astype(BF16)
        before = jnp.zeros_like(total) if before_ref is None else before_ref[:, columns]
        solved_ref[:, columns] = jnp.where(active, total, before)

    apply_inverse(1, rows, cores, position_ref, piece_refs, inverse_refs, store)


def last_kernel(rows, cores, position_ref, *refs):
    piece_refs = refs[:rows]
    inverse_refs = refs[rows:rows + cores]
    before_ref, out_ref = refs[rows + cores:]
    out_ref[1] = before_ref[...]

    def store(columns, total):
        out_ref[0, :, columns] = total

    apply_inverse(0, rows, cores, position_ref, piece_refs, inverse_refs, store)


SCALARS = pl.BlockSpec(memory_space=pltpu.SMEM)
WHOLE = pl.BlockSpec(memory_space=pltpu.VMEM)


def call(kernel, scalars, arrays, outs, scratch=(), flops=0):
    several = len(outs) > 1
    size = sum(a.size * a.dtype.itemsize for a in arrays)
    return pl.pallas_call(
        kernel,
        in_specs=[SCALARS] * len(scalars) + [WHOLE] * len(arrays),
        out_specs=[WHOLE] * len(outs) if several else WHOLE,
        out_shape=list(outs) if several else outs[0],
        scratch_shapes=list(scratch),
        cost_estimate=pl.CostEstimate(flops=flops, bytes_accessed=size, transcendentals=0),
        compiler_params=pltpu.CompilerParams(vmem_limit_bytes=24 * 2**20),
    )(*scalars, *arrays)


def local(right_side, inverse_diag, lower_blocks, block_rows):
    leafs, rows, cores = (lax.axis_size(name) for name in ("leaf", "rows", "rhs"))
    top = leafs.bit_length() - 1
    leaf = lax.axis_index("leaf")
    depth_upper = top - 1 - sum(((leaf + 1) % 2**power == 0).astype(jnp.int32) for power in range(1, top + 1))
    position = jnp.stack([lax.axis_index("rows"), lax.axis_index("rhs"), depth_upper]).astype(jnp.int32)
    count, width = right_side.shape[1:]
    quarter = inverse_diag.shape[2]
    full_width = rows * width
    places = ("leaf", "rows")

    def send(value, hops, shift):
        pairs = [(a * rows + r, b * rows + (r + shift) % rows) for a, b in hops for r in range(rows)]
        return lax.ppermute(value, places, pairs)

    def spread(value, hops):
        return [send(value, hops, shift) for shift in range(rows)]

    def rows_of(value, holders):
        return [value] + [send(value, [(h, h) for h in holders], shift) for shift in range(1, rows)]

    inverses = [inverse_diag]
    for turn in range(1, cores):
        inverses.append(lax.ppermute(inverse_diag, "rhs", [(c, (c + turn) % cores) for c in range(cores)]))

    half = jax.ShapeDtypeStruct((count, width), BF16)
    half_f32 = jax.ShapeDtypeStruct((count, width), F32)
    full = jax.ShapeDtypeStruct((count, full_width), BF16)
    work = 2 * count * full_width * width

    def holders(depth):
        return [(2 * p + 1) * 2 ** (top - depth - 1) - 1 for p in range(2**depth)]

    reduced = call(cast_kernel, [], [right_side], [half])
    known = []
    solved = None
    for depth in range(top + 1):
        last = depth == top
        slot = 0 if last else 1
        if depth > 0:
            kernel = functools.partial(offset_kernel, depth, slot, rows, len(known))
            reduced, newest = call(
                kernel, [position, block_rows], [right_side, lower_blocks, *known, *pieces], [half, full],
                [pltpu.VMEM((count, full_width), BF16)], work)
            known.append(newest)
        if last:
            everyone = range(leafs)
            gathered = rows_of(reduced, everyone)
            kernel = functools.partial(last_kernel, rows, cores)
            return call(kernel, [position], [*gathered, *inverses, solved],
                        [jax.ShapeDtypeStruct(right_side.shape, F32)], (), work)
        here = holders(depth)
        gathered = rows_of(reduced, here)
        kernel = functools.partial(solve_kernel, rows, cores, depth)
        arrays = [*gathered, *inverses] + ([] if depth == 0 else [solved])
        rounded, solved = call(kernel, [position], arrays, [half, half_f32], (), work)
        if depth + 1 < top:
            reach = 2 ** (top - depth - 2)
            left = [(h, h - reach) for h in here]
            right = [(h, h + reach) for h in here]
            moved = []
            lefts, rights = spread(rounded, left), spread(rounded, right)
            is_left = ((leaf + 1) // reach) % 4 == 1
            pieces = [jnp.where(is_left, a, b) for a, b in zip(lefts, rights)]
            known = [jnp.where(is_left, send(k, left, 0), send(k, right, 0)) for k in known]
        else:
            over = [(h, h + 1) for h in here]
            is_here = leaf % 2 == 0
            own = rows_of(rounded, here)
            others = spread(rounded, over)
            pieces = [jnp.where(is_here, a, b) for a, b in zip(own, others)]
            known = [jnp.where(is_here, k, send(k, over, 0)) for k in known]


def solution(mesh):
    return jax.shard_map(
        local,
        mesh=mesh,
        in_specs=(
            P("leaf", "rhs", "rows"),
            P("leaf", None, ("rows", "rhs")),
            P("leaf", None, None, "rows"),
            P("leaf", None),
        ),
        out_specs=P("leaf", "rhs", "rows"),
        check_vma=False,
    )
```

time: 136 us -> 96.5 us (0.71); the launches traced: 136 us -> 94.6 us
  blocking collectives: 41.2 us -> 0 us
  starting transfers between devices: 15.8 us -> 35.8 us
  Pallas kernels: 0 us -> 19 us
  waiting for transfers between devices: 39.4 us -> 21.3 us
  between operations: 13.6 us -> 0.47 us
  matrix products: 12.1 us -> 0 us
  local copies, waits for them, and re-layouts: 12.4 us -> 17.7 us
    all_gather x7 -> x0, blocking collectives: 41.2 us -> none  [the longest x4 24.1 us: fold_solve(): shard_piece = lax.all_gather(reduced, 'rows', axis=1, tiled=True)]
    ppermute x6 -> x20, starting transfers between devices: 15.8 us -> 35.8 us  [the longest x19 35.4 us: send(): return lax.ppermute(value, places, pairs)]
    pallas_call x0 -> x8, Pallas kernels: none -> 19 us  [call(): pl.pallas_call(kernel, in_specs=[SCALARS] * len(scalars) + [WHOLE] * len(...]
    unnamed x4 -> x20, local copies, waits for them, and re-layouts: 0.29 us -> 17.7 us
    all_gather x1 -> x0, waiting for transfers between devices: 16.8 us -> none  [local(): inverse_local = lax.all_gather(inverse_diag, 'rhs', axis=2, tiled=True)]
    dot_general x4 -> x0, matrix products: 12.1 us -> none  [the longest x2 6.06 us: apply_rows(): jnp.dot(shard_piece, inverse_slot, preferred_element_type=jnp.float32)]
    slice x1 -> x0, local copies, waits for them, and re-layouts: 6.08 us -> none  [local(): slot_weights = lower_blocks[slot_now]]
    squeeze x1 -> x0, local copies, waits for them, and re-layouts: 4.6 us -> none  [local(): inverse_upper = inverse_local[1]]
  transfers between devices with their start and end apart: 7 -> 20, of which waited for: 6 -> 6; matrix products, arithmetic and copies ran while one was open for 5% -> 0% of each run, Pallas kernels for 0% -> 8%
where the time goes in v1:
time: 96.5 us; the launch traced here: 94.6 us
  starting transfers between devices  35.8 us (37%)
  waiting for transfers between devices  21.3 us (22%)
  Pallas kernels  19 us (20%)
  local copies, waits for them, and re-layouts  17.7 us (18%)
    ppermute x19, starting transfers between devices, send(): return lax.ppermute(value, places, pairs)  35.4 us
    pallas_call x8, Pallas kernels, call(): pl.pallas_call(kernel, in_specs=[SCALARS] * len(scalars) + [WHOLE] * len(...  19 us
    unnamed x20, local copies, waits for them, and re-layouts  17.7 us
    ppermute x19, waiting for transfers between devices, send(): return lax.ppermute(value, places, pairs)  16 us
    ppermute x1, waiting for transfers between devices, local(): lax.ppermute(inverse_diag, 'rhs', [(c, (c + turn) % cores) for c in range...  5.26 us
  transfers between devices with their start and end apart: 20, of which 6 were waited for; matrix products, arithmetic and copies ran while one was open for 0% of the time, Pallas kernels for 8%

profile of v1, /device:TPU:0, one launch (start us, length us, event | category | flops | bytes accessed | tf_op | source)
XLA Modules:
  0.0 94.6 jit_solution(4622567514786278385)
XLA Ops:
  0.0 0.5 collective-permute-start.1
  0.5 1.0 %copy-done.7 = f32[2,64,1024]{2,1,0:T(8,128)S(1)} copy-done((f32[2,64,1024]{2,1,0:T(8,128)S(1)}, f32[2,64,1024]{2,1,0:T(8,128)}, u32[]{:S(2)}) %copy-start.7) | copy-done | bytes 524312
  1.5 0.7 collective-permute-start
  2.2 0.0 copy-start.9
  2.2 0.1 pad_add_fusion.position_ref
  2.3 0.0 collective-permute-done.refs_1_
  2.3 5.3 %collective-permute-done.1.refs_3_ = bf16[2,2048,512]{2,1,0:T(8,128)(2,1)} collective-permute-done((bf16[2,2048,512]{2,1,0:T(8,128)(2,1)}, bf16[2,2048,512]{2,1,0:T(8,128)(2,1)}, u32[]{:S(2)}, u32[]{:S(2)}) %collective-permute-start.1) | collective-permute-done | bytes 4194336 | tf_op jit(solution)/shard_map/ppermute | solution.py:133
  7.6 2.2 %copy-done.3 = bf16[2,2048,512]{2,1,0:T(8,128)(2,1)S(1)} copy-done((bf16[2,2048,512]{2,1,0:T(8,128)(2,1)S(1)}, bf16[2,2048,512]{2,1,0:T(8,128)(2,1)}, u32[]{:S(2)}) %copy-start.3) | copy-done | bytes 4194328
  9.8 3.1 %shard_map.47 = (bf16[64,1024]{1,0:T(8,128)(2,1)S(1)}, f32[64,1024]{1,0:T(8,128)S(1)}) custom-call(s32[3]{0:T(128)S(1)} %pad_add_fusion.position_ref, bf16[64,1024]{1,0:T(8,128)(2,1)S(1)} %shard_map.46.refs_0_, bf16[64,1024]{1,0:T(8,128)(2,1)S(1)} %collective-permute-done.refs_1_, bf16[2,2048,512]{2,1,0:T(8,128)(2,1)S(1)} %copy-done.3, ...), custom_call_target="tpu_custom_call" | custom-call | flops 268435456 | bytes 8650752 | tf_op jit(solution)/shard_map/pallas_call | solution.py:99
  12.9 0.7 collective-permute-start.2
  13.6 0.7 collective-permute-start.3
  14.3 0.7 collective-permute-start.4
  14.9 0.7 collective-permute-start.5
  15.6 0.0 collective-permute-done.2
  15.6 0.0 collective-permute-done.3
  15.7 0.0 copy-start
  15.7 3.4 %copy-done = bf16[2,16,128,1024]{3,2,1,0:T(8,128)(2,1)S(1)} copy-done((bf16[2,16,128,1024]{3,2,1,0:T(8,128)(2,1)S(1)}, bf16[2,16,128,1024]{3,2,1,0:T(8,128)(2,1)}, u32[]{:S(2)}) %copy-start) | copy-done | bytes 8388632
  19.1 1.7 %shard_map.48 = (bf16[64,1024]{1,0:T(8,128)(2,1)S(1)}, bf16[64,2048]{1,0:T(8,128)(2,1)S(1)}) custom-call(s32[3]{0:T(128)S(1)} %pad_add_fusion.position_ref, s32[2,16]{1,0:T(2,128)S(1)} %copy-done.9, f32[2,64,1024]{2,1,0:T(8,128)S(1)} %copy-done.8, bf16[2,16,128,1024]{3,2,1,0:T(8,128)(2,1)S(1)} %copy-done, ...), custom_call_target="tpu_custom_call" | custom-call | flops 268435456 | bytes 9175040 | tf_op jit(solution)/shard_map/pallas_call | solution.py:99
  20.8 1.3 %collective-permute-start.6 = (bf16[64,2048]{1,0:T(8,128)(2,1)S(1)}, bf16[64,2048]{1,0:T(8,128)(2,1)S(1)}, u32[]{:S(2)}, u32[]{:S(2)}) collective-permute-start(bf16[64,2048]{1,0:T(8,128)(2,1)S(1)} %get-tuple-element.17), channel_id=1, source_target_pairs={{4,0},{6,2},{20,16},{22,18},{5,1},{7,3},{21,17},{23,19}} | collective-permute-start | bytes 786440 | tf_op jit(solution)/shard_map/ppermute | solution.py:123
  22.1 0.7 collective-permute-start.7
  22.8 0.7 collective-permute-start.9
  23.5 0.0 copy-start.4
  23.5 2.2 %copy-done.4 = bf16[2,2048,512]{2,1,0:T(8,128)(2,1)S(1)} copy-done((bf16[2,2048,512]{2,1,0:T(8,128)(2,1)S(1)}, bf16[2,2048,512]{2,1,0:T(8,128)(2,1)}, u32[]{:S(2)}) %copy-start.4) | copy-done | bytes 4194328
  25.7 3.0 %shard_map.49 = (bf16[64,1024]{1,0:T(8,128)(2,1)S(1)}, f32[64,1024]{1,0:T(8,128)S(1)}) custom-call(s32[3]{0:T(128)S(1)} %pad_add_fusion.position_ref, bf16[64,1024]{1,0:T(8,128)(2,1)S(1)} %get-tuple-element.18.refs_0_, bf16[64,1024]{1,0:T(8,128)(2,1)S(1)} %collective-permute-done.9.refs_1_, bf16[2,2048,512]{2,1,0:T(8,128)(2,1)S(1)} %copy-done.4, ...), custom_call_target="tpu_custom_call" | custom-call | flops 268435456 | bytes 8912896 | tf_op jit(solution)/shard_map/pallas_call | solution.py:99
  28.8 1.3 %collective-permute-start.10 = (bf16[64,1024]{1,0:T(8,128)(2,1)S(1)}, bf16[64,1024]{1,0:T(8,128)(2,1)S(1)}, u32[]{:S(2)}, u32[]{:S(2)}) collective-permute-start(bf16[64,1024]{1,0:T(8,128)(2,1)S(1)} %get-tuple-element.20), channel_id=1, source_target_pairs={{4,0},{6,2},{20,16},{22,18},{5,1},{7,3},{21,17},{23,19}} | collective-permute-start | bytes 393224 | tf_op jit(solution)/shard_map/ppermute | solution.py:123
  30.1 0.7 collective-permute-start.11
  30.7 1.3 %collective-permute-start.12 = (bf16[64,1024]{1,0:T(8,128)(2,1)S(1)}, bf16[64,1024]{1,0:T(8,128)(2,1)S(1)}, u32[]{:S(2)}, u32[]{:S(2)}) collective-permute-start(bf16[64,1024]{1,0:T(8,128)(2,1)S(1)} %get-tuple-element.20), channel_id=1, source_target_pairs={{4,2},{6,0},{20,18},{22,16},{5,3},{7,1},{21,19},{23,17}} | collective-permute-start | bytes 393224 | tf_op jit(solution)/shard_map/ppermute | solution.py:123
  32.0 7.4 %collective-permute-done.6 = bf16[64,2048]{1,0:T(8,128)(2,1)S(1)} collective-permute-done((bf16[64,2048]{1,0:T(8,128)(2,1)S(1)}, bf16[64,2048]{1,0:T(8,128)(2,1)S(1)}, u32[]{:S(2)}, u32[]{:S(2)}) %collective-permute-start.6) | collective-permute-done | bytes 262176 | tf_op jit(solution)/shard_map/ppermute | solution.py:123
  39.5 0.7 collective-permute-start.13
  40.2 14.2 %collective-permute-start.8 = (bf16[64,2048]{1,0:T(8,128)(2,1)S(1)}, bf16[64,2048]{1,0:T(8,128)(2,1)S(1)}, u32[]{:S(2)}, u32[]{:S(2)}) collective-permute-start(bf16[64,2048]{1,0:T(8,128)(2,1)S(1)} %broadcast_select_fusion.refs_0_), channel_id=1, source_target_pairs={{0,4},{2,6},{8,12},{10,14},{16,20},{18,22},{24,28},{26,30},{1,5},{... | collective-permute-start | bytes 786440 | tf_op jit(solution)/shard_map/ppermute | solution.py:123
  54.5 0.0 copy-start.1
  54.5 3.4 %copy-done.1 = bf16[2,16,128,1024]{3,2,1,0:T(8,128)(2,1)S(1)} copy-done((bf16[2,16,128,1024]{3,2,1,0:T(8,128)(2,1)S(1)}, bf16[2,16,128,1024]{3,2,1,0:T(8,128)(2,1)}, u32[]{:S(2)}) %copy-start.1) | copy-done | bytes 8388632
  57.8 1.8 %shard_map.50 = (bf16[64,1024]{1,0:T(8,128)(2,1)S(1)}, bf16[64,2048]{1,0:T(8,128)(2,1)S(1)}) custom-call(s32[3]{0:T(128)S(1)} %pad_add_fusion.position_ref, s32[2,16]{1,0:T(2,128)S(1)} %copy-done.9, f32[2,64,1024]{2,1,0:T(8,128)S(1)} %copy-done.8, bf16[2,16,128,1024]{3,2,1,0:T(8,128)(2,1)S(1)} %copy-done.1, ...), custom_call_target="tpu_custom_call" | custom-call | flops 268435456 | bytes 9437184 | tf_op jit(solution)/shard_map/pallas_call | solution.py:99
  59.6 3.1 %collective-permute-start.15 = (bf16[64,1024]{1,0:T(8,128)(2,1)S(1)}, bf16[64,1024]{1,0:T(8,128)(2,1)S(1)}, u32[]{:S(2)}, u32[]{:S(2)}) collective-permute-start(bf16[64,1024]{1,0:T(8,128)(2,1)S(1)} %get-tuple-element.22.refs_0_), channel_id=1, source_target_pairs={{0,2},{2,0},{8,10},{10,8},{16,18},{18,16},{24,26},{26,24},{1,3},{3... | collective-permute-start | bytes 393224 | tf_op jit(solution)/shard_map/ppermute | solution.py:123
  62.8 1.3 %collective-permute-start.14 = (bf16[64,2048]{1,0:T(8,128)(2,1)S(1)}, bf16[64,2048]{1,0:T(8,128)(2,1)S(1)}, u32[]{:S(2)}, u32[]{:S(2)}) collective-permute-start(bf16[64,2048]{1,0:T(8,128)(2,1)S(1)} %get-tuple-element.21), channel_id=1, source_target_pairs={{0,4},{2,6},{8,12},{10,14},{16,20},{18,22},{24,28},{26,30},{1,5},{... | collective-permute-start | bytes 786440 | tf_op jit(solution)/shard_map/ppermute | solution.py:123
  64.1 2.4 %collective-permute-done.15.refs_1_ = bf16[64,1024]{1,0:T(8,128)(2,1)S(1)} collective-permute-done((bf16[64,1024]{1,0:T(8,128)(2,1)S(1)}, bf16[64,1024]{1,0:T(8,128)(2,1)S(1)}, u32[]{:S(2)}, u32[]{:S(2)}) %collective-permute-start.15) | collective-permute-done | bytes 131104 | tf_op jit(solution)/shard_map/ppermute | solution.py:123
  66.5 2.2 %copy-done.5 = bf16[2,2048,512]{2,1,0:T(8,128)(2,1)S(1)} copy-done((bf16[2,2048,512]{2,1,0:T(8,128)(2,1)S(1)}, bf16[2,2048,512]{2,1,0:T(8,128)(2,1)}, u32[]{:S(2)}) %copy-start.5) | copy-done | bytes 4194328
  68.7 3.0 %shard_map.51 = (bf16[64,1024]{1,0:T(8,128)(2,1)S(1)}, f32[64,1024]{1,0:T(8,128)S(1)}) custom-call(s32[3]{0:T(128)S(1)} %pad_add_fusion.position_ref, bf16[64,1024]{1,0:T(8,128)(2,1)S(1)} %get-tuple-element.22.refs_0_, bf16[64,1024]{1,0:T(8,128)(2,1)S(1)} %collective-permute-done.15.refs_1_, bf16[2,2048,512]{2,1,0:T(8,128)(2,1)S(1)} %copy-done.5, ...), custom_call_target="tpu_custom_call" | custom-call | flops 268435456 | bytes 8912896 | tf_op jit(solution)/shard_map/pallas_call | solution.py:99
  71.7 1.3 %collective-permute-start.16 = (bf16[64,1024]{1,0:T(8,128)(2,1)S(1)}, bf16[64,1024]{1,0:T(8,128)(2,1)S(1)}, u32[]{:S(2)}, u32[]{:S(2)}) collective-permute-start(bf16[64,1024]{1,0:T(8,128)(2,1)S(1)} %get-tuple-element.24), channel_id=1, source_target_pairs={{0,4},{2,6},{8,12},{10,14},{16,20},{18,22},{24,28},{26,30},{1,5},{... | collective-permute-start | bytes 393224 | tf_op jit(solution)/shard_map/ppermute | solution.py:123
  73.0 3.1 %collective-permute-start.17 = (bf16[64,1024]{1,0:T(8,128)(2,1)S(1)}, bf16[64,1024]{1,0:T(8,128)(2,1)S(1)}, u32[]{:S(2)}, u32[]{:S(2)}) collective-permute-start(bf16[64,1024]{1,0:T(8,128)(2,1)S(1)} %get-tuple-element.24), channel_id=1, source_target_pairs={{0,2},{2,0},{8,10},{10,8},{16,18},{18,16},{24,26},{26,24},{1,3},{3... | collective-permute-start | bytes 393224 | tf_op jit(solution)/shard_map/ppermute | solution.py:123
  76.2 1.3 %collective-permute-start.18 = (bf16[64,1024]{1,0:T(8,128)(2,1)S(1)}, bf16[64,1024]{1,0:T(8,128)(2,1)S(1)}, u32[]{:S(2)}, u32[]{:S(2)}) collective-permute-start(bf16[64,1024]{1,0:T(8,128)(2,1)S(1)} %get-tuple-element.24), channel_id=1, source_target_pairs={{0,6},{2,4},{8,14},{10,12},{16,22},{18,20},{24,30},{26,28},{1,7},{... | collective-permute-start | bytes 393224 | tf_op jit(solution)/shard_map/ppermute | solution.py:123
  77.6 2.3 %collective-permute-done.17 = bf16[64,1024]{1,0:T(8,128)(2,1)S(1)} collective-permute-done((bf16[64,1024]{1,0:T(8,128)(2,1)S(1)}, bf16[64,1024]{1,0:T(8,128)(2,1)S(1)}, u32[]{:S(2)}, u32[]{:S(2)}) %collective-permute-start.17) | collective-permute-done | bytes 131104 | tf_op jit(solution)/shard_map/ppermute | solution.py:123
  79.9 0.1 collective-permute-done.18
  80.0 3.4 %copy-done.2 = bf16[2,16,128,1024]{3,2,1,0:T(8,128)(2,1)S(1)} copy-done((bf16[2,16,128,1024]{3,2,1,0:T(8,128)(2,1)S(1)}, bf16[2,16,128,1024]{3,2,1,0:T(8,128)(2,1)}, u32[]{:S(2)}) %copy-start.2) | copy-done | bytes 8388632
  83.4 2.4 %shard_map.52 = (bf16[64,1024]{1,0:T(8,128)(2,1)S(1)}, bf16[64,2048]{1,0:T(8,128)(2,1)}) custom-call(s32[3]{0:T(128)S(1)} %pad_add_fusion.position_ref, s32[2,16]{1,0:T(2,128)S(1)} %copy-done.9, f32[2,64,1024]{2,1,0:T(8,128)S(1)} %copy-done.8, bf16[2,16,128,1024]{3,2,1,0:T(8,128)(2,1)S(1)} %copy-done.2, bf16[64,2048]{1,0:T(8,128)(2,1)S(1)} %broadcast_select_fusion.2.refs_0_, ...), custom_call_target="tpu_custom_call" | custom-call | flops 268435456 | bytes 9699328 | tf_op jit(solution)/shard_map/pallas_call | solution.py:99
  85.8 1.1 %collective-permute-start.19 = (bf16[64,1024]{1,0:T(8,128)(2,1)S(1)}, bf16[64,1024]{1,0:T(8,128)(2,1)S(1)}, u32[]{:S(2)}, u32[]{:S(2)}) collective-permute-start(bf16[64,1024]{1,0:T(8,128)(2,1)S(1)} %get-tuple-element.25.refs_0_), channel_id=1, source_target_pairs={{0,2},{2,0},{4,6},{6,4},{8,10},{10,8},{12,14},{14,12},{16,18},{18,... | collective-permute-start | bytes 393224 | tf_op jit(solution)/shard_map/ppermute | solution.py:123
  87.0 3.8 %collective-permute-done.19.refs_1_ = bf16[64,1024]{1,0:T(8,128)(2,1)S(1)} collective-permute-done((bf16[64,1024]{1,0:T(8,128)(2,1)S(1)}, bf16[64,1024]{1,0:T(8,128)(2,1)S(1)}, u32[]{:S(2)}, u32[]{:S(2)}) %collective-permute-start.19) | collective-permute-done | bytes 131104 | tf_op jit(solution)/shard_map/ppermute | solution.py:123
  90.8 3.8 %shard_map.53 = f32[2,64,1024]{2,1,0:T(8,128)} custom-call(s32[3]{0:T(128)S(1)} %pad_add_fusion.position_ref, bf16[64,1024]{1,0:T(8,128)(2,1)S(1)} %get-tuple-element.25.refs_0_, bf16[64,1024]{1,0:T(8,128)(2,1)S(1)} %collective-permute-done.19.refs_1_, bf16[2,2048,512]{2,1,0:T(8,128)(2,1)S(1)} %copy-done.6, ...), custom_call_target="tpu_custom_call" | custom-call | flops 268435456 | bytes 8912896 | tf_op jit(solution)/shard_map/pallas_call | solution.py:99
  (30 shorter events, 0.3 us)
Async XLA Ops:
  0.0 7.6 %collective-permute-start.1 = (bf16[2,2048,512]{2,1,0:T(8,128)(2,1)}, bf16[2,2048,512]{2,1,0:T(8,128)(2,1)}, u32[]{:S(2)}, u32[]{:S(2)}) collective-permute-start(bf16[2,2048,512]{2,1,0:T(8,128)(2,1)} %refs_2_.7), channel_id=1, source_target_pairs={{0,1},{1,0},{2,3},{3,2},{4,5},{5,4},{6,7},{7,6},{8,9},{9,8},{10,11... | collective-permute-start | bytes 12582920 | tf_op jit(solution)/shard_map/ppermute | solution.py:133
  0.5 1.0 %copy-start.7 = (f32[2,64,1024]{2,1,0:T(8,128)S(1)}, f32[2,64,1024]{2,1,0:T(8,128)}, u32[]{:S(2)}) copy-start(f32[2,64,1024]{2,1,0:T(8,128)} %right_ref.7) | copy-start | bytes 1572868
  1.5 0.8 collective-permute-start
  2.2 13.5 %copy-start.9 = (s32[2,16]{1,0:T(2,128)S(1)}, s32[2,16]{1,0:T(2,128)}, u32[]{:S(2)}) copy-start(s32[2,16]{1,0:T(2,128)} %block_rows_ref.5) | copy-start | bytes 388
  7.6 2.2 %copy-start.3 = (bf16[2,2048,512]{2,1,0:T(8,128)(2,1)S(1)}, bf16[2,2048,512]{2,1,0:T(8,128)(2,1)}, u32[]{:S(2)}) copy-start(bf16[2,2048,512]{2,1,0:T(8,128)(2,1)} %refs_2_.7) | copy-start | bytes 12582916
  9.8 6.0 %copy-start.8 = (f32[2,64,1024]{2,1,0:T(8,128)S(1)}, f32[2,64,1024]{2,1,0:T(8,128)}, u32[]{:S(2)}) copy-start(f32[2,64,1024]{2,1,0:T(8,128)} %right_ref.7) | copy-start | bytes 1572868
  12.9 2.7 %collective-permute-start.2 = (bf16[64,1024]{1,0:T(8,128)(2,1)S(1)}, bf16[64,1024]{1,0:T(8,128)(2,1)S(1)}, u32[]{:S(2)}, u32[]{:S(2)}) collective-permute-start(bf16[64,1024]{1,0:T(8,128)(2,1)S(1)} %get-tuple-element.16), channel_id=1, source_target_pairs={{12,4},{14,6},{13,5},{15,7}} | collective-permute-start | bytes 393224 | tf_op jit(solution)/shard_map/ppermute | solution.py:123
  13.6 2.1 %collective-permute-start.3 = (bf16[64,1024]{1,0:T(8,128)(2,1)S(1)}, bf16[64,1024]{1,0:T(8,128)(2,1)S(1)}, u32[]{:S(2)}, u32[]{:S(2)}) collective-permute-start(bf16[64,1024]{1,0:T(8,128)(2,1)S(1)} %get-tuple-element.16), channel_id=1, source_target_pairs={{12,20},{14,22},{13,21},{15,23}} | collective-permute-start | bytes 393224 | tf_op jit(solution)/shard_map/ppermute | solution.py:123
  14.3 1.4 %collective-permute-start.4 = (bf16[64,1024]{1,0:T(8,128)(2,1)S(1)}, bf16[64,1024]{1,0:T(8,128)(2,1)S(1)}, u32[]{:S(2)}, u32[]{:S(2)}) collective-permute-start(bf16[64,1024]{1,0:T(8,128)(2,1)S(1)} %get-tuple-element.16), channel_id=1, source_target_pairs={{12,6},{14,4},{13,7},{15,5}} | collective-permute-start | bytes 393224 | tf_op jit(solution)/shard_map/ppermute | solution.py:123
  14.9 0.7 collective-permute-start.5
  15.7 3.4 %copy-start = (bf16[2,16,128,1024]{3,2,1,0:T(8,128)(2,1)S(1)}, bf16[2,16,128,1024]{3,2,1,0:T(8,128)(2,1)}, u32[]{:S(2)}) copy-start(bf16[2,16,128,1024]{3,2,1,0:T(8,128)(2,1)} %lower_ref.5) | copy-start | bytes 25165828
  20.8 18.6 %collective-permute-start.6 = (bf16[64,2048]{1,0:T(8,128)(2,1)S(1)}, bf16[64,2048]{1,0:T(8,128)(2,1)S(1)}, u32[]{:S(2)}, u32[]{:S(2)}) collective-permute-start(bf16[64,2048]{1,0:T(8,128)(2,1)S(1)} %get-tuple-element.17), channel_id=1, source_target_pairs={{4,0},{6,2},{20,16},{22,18},{5,1},{7,3},{21,17},{23,19}} | collective-permute-start | bytes 786440 | tf_op jit(solution)/shard_map/ppermute | solution.py:123
  22.1 18.0 %collective-permute-start.7 = (bf16[64,2048]{1,0:T(8,128)(2,1)S(1)}, bf16[64,2048]{1,0:T(8,128)(2,1)S(1)}, u32[]{:S(2)}, u32[]{:S(2)}) collective-permute-start(bf16[64,2048]{1,0:T(8,128)(2,1)S(1)} %get-tuple-element.17), channel_id=1, source_target_pairs={{4,8},{6,10},{20,24},{22,26},{5,9},{7,11},{21,25},{23,27}} | collective-permute-start | bytes 786440 | tf_op jit(solution)/shard_map/ppermute | solution.py:123
  22.8 0.7 collective-permute-start.9
  23.5 2.2 %copy-start.4 = (bf16[2,2048,512]{2,1,0:T(8,128)(2,1)S(1)}, bf16[2,2048,512]{2,1,0:T(8,128)(2,1)}, u32[]{:S(2)}) copy-start(bf16[2,2048,512]{2,1,0:T(8,128)(2,1)} %refs_2_.7) | copy-start | bytes 12582916
  28.8 25.6 %collective-permute-start.10 = (bf16[64,1024]{1,0:T(8,128)(2,1)S(1)}, bf16[64,1024]{1,0:T(8,128)(2,1)S(1)}, u32[]{:S(2)}, u32[]{:S(2)}) collective-permute-start(bf16[64,1024]{1,0:T(8,128)(2,1)S(1)} %get-tuple-element.20), channel_id=1, source_target_pairs={{4,0},{6,2},{20,16},{22,18},{5,1},{7,3},{21,17},{23,19}} | collective-permute-start | bytes 393224 | tf_op jit(solution)/shard_map/ppermute | solution.py:123
  30.1 24.3 %collective-permute-start.11 = (bf16[64,1024]{1,0:T(8,128)(2,1)S(1)}, bf16[64,1024]{1,0:T(8,128)(2,1)S(1)}, u32[]{:S(2)}, u32[]{:S(2)}) collective-permute-start(bf16[64,1024]{1,0:T(8,128)(2,1)S(1)} %get-tuple-element.20), channel_id=1, source_target_pairs={{4,8},{6,10},{20,24},{22,26},{5,9},{7,11},{21,25},{23,27}} | collective-permute-start | bytes 393224 | tf_op jit(solution)/shard_map/ppermute | solution.py:123
  30.7 23.7 %collective-permute-start.12 = (bf16[64,1024]{1,0:T(8,128)(2,1)S(1)}, bf16[64,1024]{1,0:T(8,128)(2,1)S(1)}, u32[]{:S(2)}, u32[]{:S(2)}) collective-permute-start(bf16[64,1024]{1,0:T(8,128)(2,1)S(1)} %get-tuple-element.20), channel_id=1, source_target_pairs={{4,2},{6,0},{20,18},{22,16},{5,3},{7,1},{21,19},{23,17}} | collective-permute-start | bytes 393224 | tf_op jit(solution)/shard_map/ppermute | solution.py:123
  39.5 15.0 %collective-permute-start.13 = (bf16[64,1024]{1,0:T(8,128)(2,1)S(1)}, bf16[64,1024]{1,0:T(8,128)(2,1)S(1)}, u32[]{:S(2)}, u32[]{:S(2)}) collective-permute-start(bf16[64,1024]{1,0:T(8,128)(2,1)S(1)} %get-tuple-element.20), channel_id=1, source_target_pairs={{4,10},{6,8},{20,26},{22,24},{5,11},{7,9},{21,27},{23,25}} | collective-permute-start | bytes 393224 | tf_op jit(solution)/shard_map/ppermute | solution.py:123
  40.2 37.3 %collective-permute-start.8 = (bf16[64,2048]{1,0:T(8,128)(2,1)S(1)}, bf16[64,2048]{1,0:T(8,128)(2,1)S(1)}, u32[]{:S(2)}, u32[]{:S(2)}) collective-permute-start(bf16[64,2048]{1,0:T(8,128)(2,1)S(1)} %broadcast_select_fusion.refs_0_), channel_id=1, source_target_pairs={{0,4},{2,6},{8,12},{10,14},{16,20},{18,22},{24,28},{26,30},{1,5},{... | collective-permute-start | bytes 786440 | tf_op jit(solution)/shard_map/ppermute | solution.py:123
  54.5 3.4 %copy-start.1 = (bf16[2,16,128,1024]{3,2,1,0:T(8,128)(2,1)S(1)}, bf16[2,16,128,1024]{3,2,1,0:T(8,128)(2,1)}, u32[]{:S(2)}) copy-start(bf16[2,16,128,1024]{3,2,1,0:T(8,128)(2,1)} %lower_ref.5) | copy-start | bytes 25165828
  59.6 6.9 %collective-permute-start.15 = (bf16[64,1024]{1,0:T(8,128)(2,1)S(1)}, bf16[64,1024]{1,0:T(8,128)(2,1)S(1)}, u32[]{:S(2)}, u32[]{:S(2)}) collective-permute-start(bf16[64,1024]{1,0:T(8,128)(2,1)S(1)} %get-tuple-element.22.refs_0_), channel_id=1, source_target_pairs={{0,2},{2,0},{8,10},{10,8},{16,18},{18,16},{24,26},{26,24},{1,3},{3... | collective-permute-start | bytes 393224 | tf_op jit(solution)/shard_map/ppermute | solution.py:123
  62.8 14.8 %collective-permute-start.14 = (bf16[64,2048]{1,0:T(8,128)(2,1)S(1)}, bf16[64,2048]{1,0:T(8,128)(2,1)S(1)}, u32[]{:S(2)}, u32[]{:S(2)}) collective-permute-start(bf16[64,2048]{1,0:T(8,128)(2,1)S(1)} %get-tuple-element.21), channel_id=1, source_target_pairs={{0,4},{2,6},{8,12},{10,14},{16,20},{18,22},{24,28},{26,30},{1,5},{... | collective-permute-start | bytes 786440 | tf_op jit(solution)/shard_map/ppermute | solution.py:123
  66.5 2.2 %copy-start.5 = (bf16[2,2048,512]{2,1,0:T(8,128)(2,1)S(1)}, bf16[2,2048,512]{2,1,0:T(8,128)(2,1)}, u32[]{:S(2)}) copy-start(bf16[2,2048,512]{2,1,0:T(8,128)(2,1)} %refs_2_.7) | copy-start | bytes 12582916
  71.7 5.8 %collective-permute-start.16 = (bf16[64,1024]{1,0:T(8,128)(2,1)S(1)}, bf16[64,1024]{1,0:T(8,128)(2,1)S(1)}, u32[]{:S(2)}, u32[]{:S(2)}) collective-permute-start(bf16[64,1024]{1,0:T(8,128)(2,1)S(1)} %get-tuple-element.24), channel_id=1, source_target_pairs={{0,4},{2,6},{8,12},{10,14},{16,20},{18,22},{24,28},{26,30},{1,5},{... | collective-permute-start | bytes 393224 | tf_op jit(solution)/shard_map/ppermute | solution.py:123
  73.0 6.9 %collective-permute-start.17 = (bf16[64,1024]{1,0:T(8,128)(2,1)S(1)}, bf16[64,1024]{1,0:T(8,128)(2,1)S(1)}, u32[]{:S(2)}, u32[]{:S(2)}) collective-permute-start(bf16[64,1024]{1,0:T(8,128)(2,1)S(1)} %get-tuple-element.24), channel_id=1, source_target_pairs={{0,2},{2,0},{8,10},{10,8},{16,18},{18,16},{24,26},{26,24},{1,3},{3... | collective-permute-start | bytes 393224 | tf_op jit(solution)/shard_map/ppermute | solution.py:123
  76.2 3.8 %collective-permute-start.18 = (bf16[64,1024]{1,0:T(8,128)(2,1)S(1)}, bf16[64,1024]{1,0:T(8,128)(2,1)S(1)}, u32[]{:S(2)}, u32[]{:S(2)}) collective-permute-start(bf16[64,1024]{1,0:T(8,128)(2,1)S(1)} %get-tuple-element.24), channel_id=1, source_target_pairs={{0,6},{2,4},{8,14},{10,12},{16,22},{18,20},{24,30},{26,28},{1,7},{... | collective-permute-start | bytes 393224 | tf_op jit(solution)/shard_map/ppermute | solution.py:123
  80.0 3.4 %copy-start.2 = (bf16[2,16,128,1024]{3,2,1,0:T(8,128)(2,1)S(1)}, bf16[2,16,128,1024]{3,2,1,0:T(8,128)(2,1)}, u32[]{:S(2)}) copy-start(bf16[2,16,128,1024]{3,2,1,0:T(8,128)(2,1)} %lower_ref.5) | copy-start | bytes 25165828
  83.4 7.4 %copy-start.6 = (bf16[2,2048,512]{2,1,0:T(8,128)(2,1)S(1)}, bf16[2,2048,512]{2,1,0:T(8,128)(2,1)}, u32[]{:S(2)}) copy-start(bf16[2,2048,512]{2,1,0:T(8,128)(2,1)} %refs_2_.7) | copy-start | bytes 12582916
  85.8 5.0 %collective-permute-start.19 = (bf16[64,1024]{1,0:T(8,128)(2,1)S(1)}, bf16[64,1024]{1,0:T(8,128)(2,1)S(1)}, u32[]{:S(2)}, u32[]{:S(2)}) collective-permute-start(bf16[64,1024]{1,0:T(8,128)(2,1)S(1)} %get-tuple-element.25.refs_0_), channel_id=1, source_target_pairs={{0,2},{2,0},{4,6},{6,4},{8,10},{10,8},{12,14},{14,12},{16,18},{18,... | collective-permute-start | bytes 393224 | tf_op jit(solution)/shard_map/ppermute | solution.py:123

commit v2 on v1

v2 whole, which is shorter than its diff:
```python
import functools
import jax
import jax.numpy as jnp
from jax import lax
from jax.experimental import pallas as pl
from jax.experimental.pallas import tpu as pltpu
from jax.sharding import PartitionSpec as P

F32 = jnp.float32
BF16 = jnp.bfloat16
VMEM = pltpu.VMEM


def first_kernel(right_ref, inverse_ref, cast_ref, inverse_out, staged, semaphores):
    weights = pltpu.make_async_copy(inverse_ref.at[1], inverse_out, semaphores.at[0])
    values = pltpu.make_async_copy(right_ref.at[1], staged, semaphores.at[1])
    values.start()
    weights.start()
    values.wait()
    cast_ref[...] = staged[...].astype(BF16)
    weights.wait()


def load_kernel(after_ref, right_ref, inverse_ref, lower_ref, right_out, inverse_out, upper_out, lower_out, semaphores):
    copies = [
        pltpu.make_async_copy(lower_ref.at[1], upper_out, semaphores.at[0]),
        pltpu.make_async_copy(inverse_ref.at[0], inverse_out, semaphores.at[1]),
        pltpu.make_async_copy(right_ref, right_out, semaphores.at[2]),
        pltpu.make_async_copy(lower_ref.at[0], lower_out, semaphores.at[3]),
    ]
    for copy in copies:
        copy.start()
    for copy in copies:
        copy.wait()


def place_pieces(position_ref, piece_refs, target_ref, base):
    rows = len(piece_refs)
    width = piece_refs[0].shape[1]
    for shift, piece_ref in enumerate(piece_refs):
        source = lax.rem(position_ref[0] - shift + rows, rows)
        target_ref[:, pl.ds(pl.multiple_of(base + source * width, width), width)] = piece_ref[...]


def whole_kernel(rows, position_ref, after_ref, *refs):
    place_pieces(position_ref, refs[:rows], refs[rows], 0)


def offset_kernel(level, slot, rows, position_ref, block_rows_ref, right_ref, lower_ref, *refs):
    full_refs = refs[:level - 1]
    piece_refs = refs[level - 1:level - 1 + rows]
    reduced_ref, joined, picked = refs[level - 1 + rows:]
    width = piece_refs[0].shape[1]
    blocks, block_width = lower_ref.shape[:2]
    for index, full_ref in enumerate(full_refs):
        joined[:, index * rows * width:(index + 1) * rows * width] = full_ref[...]
    place_pieces(position_ref, piece_refs, joined, (level - 1) * rows * width)
    highest = joined.shape[1] // block_width - 1
    for index in range(blocks):
        number = jnp.clip(block_rows_ref[slot, index], 0, highest)
        column = pl.multiple_of(number * block_width, block_width)
        picked[:, index * block_width:(index + 1) * block_width] = joined[:, pl.ds(column, block_width)]
    weights = lower_ref[...].reshape(blocks * block_width, width)
    offset = jnp.dot(picked[...], weights, preferred_element_type=F32)
    reduced_ref[...] = (right_ref[slot] - offset).astype(BF16)


def apply_inverse(rows, cores, position_ref, piece_refs, inverse_refs, store):
    width = piece_refs[0].shape[1]
    quarter = inverse_refs[0].shape[-1]
    for turn, inverse_ref in enumerate(inverse_refs):
        total = None
        for shift, piece_ref in enumerate(piece_refs):
            source = lax.rem(position_ref[0] - shift + rows, rows)
            part = inverse_ref[pl.ds(pl.multiple_of(source * width, width), width), :]
            term = jnp.dot(piece_ref[...], part, preferred_element_type=F32)
            total = term if total is None else total + term
        core = lax.rem(position_ref[1] - turn + cores, cores)
        store(pl.ds(pl.multiple_of(core * quarter, quarter), quarter), total)


def solve_kernel(rows, cores, depth_now, position_ref, *refs):
    piece_refs = refs[:rows]
    inverse_refs = refs[rows:rows + cores]
    rest = refs[rows + cores:]
    if depth_now == 0:
        before_ref, (rounded_ref, solved_ref) = None, rest
    else:
        before_ref, rounded_ref, solved_ref = rest
    active = position_ref[2] == depth_now

    def store(columns, total):
        rounded_ref[:, columns] = total.astype(BF16)
        before = jnp.zeros_like(total) if before_ref is None else before_ref[:, columns]
        solved_ref[:, columns] = jnp.where(active, total, before)

    apply_inverse(rows, cores, position_ref, piece_refs, inverse_refs, store)


def last_kernel(rows, cores, position_ref, *refs):
    piece_refs = refs[:rows]
    inverse_refs = refs[rows:rows + cores]
    before_ref, out_ref = refs[rows + cores:]
    out_ref[1] = before_ref[...]

    def store(columns, total):
        out_ref[0, :, columns] = total

    apply_inverse(rows, cores, position_ref, piece_refs, inverse_refs, store)


SCALARS = pl.BlockSpec(memory_space=pltpu.SMEM)
WHOLE = pl.BlockSpec(memory_space=pltpu.VMEM)
FAR = pl.BlockSpec(memory_space=pltpu.HBM)


def call(kernel, scalars, arrays, outs, scratch=(), flops=0, far=0):
    several = len(outs) > 1
    size = sum(a.size * a.dtype.itemsize for a in arrays)
    here = len(arrays) - far
    arrays = [pltpu.with_memory_space_constraint(a, pltpu.VMEM) for a in arrays[:here]] + list(arrays[here:])
    return pl.pallas_call(
        kernel,
        in_specs=[SCALARS] * len(scalars) + [WHOLE] * here + [FAR] * far,
        out_specs=[WHOLE] * len(outs) if several else WHOLE,
        out_shape=list(outs) if several else outs[0],
        scratch_shapes=list(scratch),
        cost_estimate=pl.CostEstimate(flops=flops, bytes_accessed=size, transcendentals=0),
        compiler_params=pltpu.CompilerParams(vmem_limit_bytes=8 * 2**20),
    )(*scalars, *arrays)


def local(right_side, inverse_diag, lower_blocks, block_rows):
    leafs, rows, cores = (lax.axis_size(name) for name in ("leaf", "rows", "rhs"))
    top = leafs.bit_length() - 1
    leaf = lax.axis_index("leaf")
    depth_upper = top - 1 - sum(((leaf + 1) % 2**power == 0).astype(jnp.int32) for power in range(1, top + 1))
    position = jnp.stack([lax.axis_index("rows"), lax.axis_index("rhs"), depth_upper]).astype(jnp.int32)
    count, width = right_side.shape[1:]
    full_width = rows * width
    places = ("leaf", "rows")

    def send(value, hops, shift):
        pairs = [(a * rows + r, b * rows + (r + shift) % rows) for a, b in hops for r in range(rows)]
        return lax.ppermute(value, places, pairs)

    def spread(value, hops):
        return [send(value, hops, shift) for shift in range(rows)]

    def rows_of(value, holders):
        return [value] + [send(value, [(h, h) for h in holders], shift) for shift in range(1, rows)]

    def core_columns(own):
        turns = range(1, cores)
        return [own] + [lax.ppermute(own, "rhs", [(c, (c + t) % cores) for c in range(cores)]) for t in turns]

    def near(shape, dtype):
        return pltpu.VMEM(shape, dtype)

    half = near((count, width), BF16)
    half_f32 = near((count, width), F32)
    full = near((count, full_width), BF16)
    work = 2 * count * full_width * width
    square = near(inverse_diag.shape[1:], BF16)
    lower = near(lower_blocks.shape[1:], BF16)

    def depth_of(h):
        return top - 1 - sum((h + 1) % 2**power == 0 for power in range(1, top + 1))

    def holders(depth):
        return [(2 * p + 1) * 2 ** (top - depth - 1) - 1 for p in range(2**depth)]

    reduced, inverse_upper = call(
        first_kernel, [], [right_side, inverse_diag], [half, square],
        [pltpu.VMEM((count, width), F32), pltpu.SemaphoreType.DMA((2,))], far=2)
    gathered = rows_of(reduced, holders(0))
    inverse_upper = core_columns(inverse_upper)
    right, inverse_lower, lower_upper, lower_lower = call(
        load_kernel, [], [reduced, right_side, inverse_diag, lower_blocks],
        [near(right_side.shape, F32), square, lower, lower], [pltpu.SemaphoreType.DMA((4,))], far=3)
    inverse_lower = core_columns(inverse_lower)
    known = []
    solved = None
    for depth in range(top + 1):
        last = depth == top
        if depth > 0:
            slot = 0 if last else 1
            kernel = functools.partial(offset_kernel, depth, slot, rows)
            reduced = call(
                kernel, [position, block_rows],
                [right, lower_lower if last else lower_upper, *known, *pieces], [half],
                [pltpu.VMEM((count, depth * full_width), BF16), pltpu.VMEM((count, full_width), BF16)], work)
            gathered = rows_of(reduced, range(leafs) if last else holders(depth))
        if last:
            kernel = functools.partial(last_kernel, rows, cores)
            return call(kernel, [position], [*gathered, *inverse_lower, solved],
                        [jax.ShapeDtypeStruct(right_side.shape, F32)], (), work)
        here = holders(depth)
        if depth > 0:
            newest = call(functools.partial(whole_kernel, rows), [position], [reduced, *pieces], [full])
            known = [*known, newest]
        if depth + 1 < top:
            reach = 2 ** (top - depth - 2)
            left = [(h, h - reach) for h in here]
            right_hops = [(h, h + reach) for h in here]
            is_left = (depth_upper == depth + 1) & (((leaf + 1) // reach) % 4 == 1)
            is_right = (depth_upper == depth + 1) & (((leaf + 1) // reach) % 4 == 3)
            known = [jnp.where(is_left, send(k, left, 0), jnp.where(is_right, send(k, right_hops, 0), k)) for k in known]
        elif depth > 0:
            passed = []
            for index, k in enumerate(known):
                hops = [(h, h + 1) for h in here if depth_of(h + 1) <= index]
                goes = (leaf % 2 == 1) & (depth_upper <= index)
                passed.append(jnp.where(goes, send(k, hops, 0), k))
            known = passed
        kernel = functools.partial(solve_kernel, rows, cores, depth)
        arrays = [*gathered, *inverse_upper] + ([] if depth == 0 else [solved])
        rounded, solved = call(kernel, [position], arrays, [half, half_f32], (), work)
        if depth + 1 < top:
            lefts, rights = spread(rounded, left), spread(rounded, right_hops)
            pieces = [jnp.where(is_left, a, b) for a, b in zip(lefts, rights)]
        else:
            own = rows_of(rounded, here)
            others = spread(rounded, [(h, h + 1) for h in here])
            pieces = [jnp.where(leaf % 2 == 0, a, b) for a, b in zip(own, others)]


def solution(mesh):
    return jax.shard_map(
        local,
        mesh=mesh,
        in_specs=(
            P("leaf", "rhs", "rows"),
            P("leaf", None, ("rows", "rhs")),
            P("leaf", None, None, "rows"),
            P("leaf", None),
        ),
        out_specs=P("leaf", "rhs", "rows"),
        check_vma=False,
    )
```

time: 96.5 us -> 97.9 us (1.015); the launches traced: 94.6 us -> 97.3 us
  waiting for transfers between devices: 21.3 us -> 32.9 us
  starting transfers between devices: 35.8 us -> 26.2 us
  local copies, waits for them, and re-layouts: 17.7 us -> 15.7 us
  other arithmetic: 0.3 us -> 2.18 us
    ppermute x19, waiting for transfers between devices: 16 us -> 29.7 us  [send(): return lax.ppermute(value, places, pairs)]
    ppermute x19, starting transfers between devices: 35.4 us -> 25.3 us  [send(): return lax.ppermute(value, places, pairs)]
    ppermute x1 -> x2, waiting for transfers between devices: 5.26 us -> 3.14 us  [core_columns(): lax.ppermute(own, 'rhs', [(c, (c + t) % cores) for c in range(cores)])]
    unnamed x20 -> x26, local copies, waits for them, and re-layouts: 17.7 us -> 15.7 us
    pallas_call x8 -> x11, Pallas kernels: 19 us -> 19.9 us  [call(): pl.pallas_call(kernel, in_specs=[SCALARS] * len(scalars) + [WHOLE] * here...]
  transfers between devices with their start and end apart: 20 -> 21, of which waited for: 6 -> 7; matrix products, arithmetic and copies ran while one was open for 0% -> 2% of each run, Pallas kernels for 8% -> 11%
where the time goes in v2:
time: 97.9 us; the launch traced here: 97.3 us
  waiting for transfers between devices  32.9 us (34%)
  starting transfers between devices  26.2 us (27%)
  Pallas kernels  19.9 us (20%)
  local copies, waits for them, and re-layouts  15.7 us (16%)
  other arithmetic  2.18 us (2%)
    ppermute x19, waiting for transfers between devices, send(): return lax.ppermute(value, places, pairs)  29.7 us
    ppermute x19, starting transfers between devices, send(): return lax.ppermute(value, places, pairs)  25.3 us
    pallas_call x11, Pallas kernels, call(): pl.pallas_call(kernel, in_specs=[SCALARS] * len(scalars) + [WHOLE] * here...  19.9 us
    unnamed x26, local copies, waits for them, and re-layouts  15.7 us
    ppermute x2, waiting for transfers between devices, core_columns(): lax.ppermute(own, 'rhs', [(c, (c + t) % cores) for c in range(cores)])  3.14 us
  transfers between devices with their start and end apart: 21, of which 7 were waited for; matrix products, arithmetic and copies ran while one was open for 2% of the time, Pallas kernels for 11%

profile of v2, /device:TPU:0, one launch (start us, length us, event | category | flops | bytes accessed | tf_op | source)
XLA Modules:
  0.0 97.3 jit_solution(839866848516820474)
XLA Ops:
  0.0 2.2 %copy-done = bf16[2,2048,512]{2,1,0:T(8,128)(2,1)S(1)} copy-done((bf16[2,2048,512]{2,1,0:T(8,128)(2,1)S(1)}, bf16[2,2048,512]{2,1,0:T(8,128)(2,1)}, u32[]{:S(2)}) %copy-start) | copy-done | bytes 4194328
  2.2 1.0 %copy-done.8 = f32[2,64,1024]{2,1,0:T(8,128)S(1)} copy-done((f32[2,64,1024]{2,1,0:T(8,128)S(1)}, f32[2,64,1024]{2,1,0:T(8,128)}, u32[]{:S(2)}) %copy-start.8) | copy-done | bytes 524312
  3.4 0.5 collective-permute-start.1
  4.0 0.7 collective-permute-start
  4.7 3.1 %collective-permute-done.1.refs_3_ = bf16[2048,512]{1,0:T(8,128)(2,1)} collective-permute-done((bf16[2048,512]{1,0:T(8,128)(2,1)S(1)}, bf16[2048,512]{1,0:T(8,128)(2,1)}, u32[]{:S(2)}, u32[]{:S(2)}) %collective-permute-start.1) | collective-permute-done | bytes 2097184 | tf_op jit(solution)/shard_map/ppermute | solution.py:155
  7.9 3.1 %shard_map.48 = (bf16[64,1024]{1,0:T(8,128)(2,1)}, f32[64,1024]{1,0:T(8,128)S(1)}) custom-call(s32[3]{0:T(128)S(1)} %pad_add_fusion.position_ref, bf16[64,1024]{1,0:T(8,128)(2,1)S(1)} %get-tuple-element.17.after_ref.refs_0_, bf16[64,1024]{1,0:T(8,128)(2,1)S(1)} %collective-permute-done.refs_1_, bf16[2048,512]{1,0:T(8,128)(2,1)S(1)} %get-tuple-element.21.refs_2_, ...), custom_call_target="tpu_custom_call" | custom-call | flops 268435456 | bytes 4456448 | tf_op jit(solution)/shard_map/pallas_call | solution.py:122
  11.0 1.3 %collective-permute-start.5 = (bf16[64,1024]{1,0:T(8,128)(2,1)}, bf16[64,1024]{1,0:T(8,128)(2,1)}, u32[]{:S(2)}, u32[]{:S(2)}) collective-permute-start(bf16[64,1024]{1,0:T(8,128)(2,1)} %get-tuple-element.22), channel_id=1, source_target_pairs={{12,22},{14,20},{13,23},{15,21}} | collective-permute-start | bytes 393224 | tf_op jit(solution)/shard_map/ppermute | solution.py:145
  12.3 1.3 %collective-permute-start.4 = (bf16[64,1024]{1,0:T(8,128)(2,1)}, bf16[64,1024]{1,0:T(8,128)(2,1)}, u32[]{:S(2)}, u32[]{:S(2)}) collective-permute-start(bf16[64,1024]{1,0:T(8,128)(2,1)} %get-tuple-element.22), channel_id=1, source_target_pairs={{12,6},{14,4},{13,7},{15,5}} | collective-permute-start | bytes 393224 | tf_op jit(solution)/shard_map/ppermute | solution.py:145
  13.6 2.2 %copy-done.1 = bf16[2,2048,512]{2,1,0:T(8,128)(2,1)S(1)} copy-done((bf16[2,2048,512]{2,1,0:T(8,128)(2,1)S(1)}, bf16[2,2048,512]{2,1,0:T(8,128)(2,1)}, u32[]{:S(2)}) %copy-start.1) | copy-done | bytes 4194328
  15.8 3.4 %copy-done.5 = bf16[2,16,128,1024]{3,2,1,0:T(8,128)(2,1)S(1)} copy-done((bf16[2,16,128,1024]{3,2,1,0:T(8,128)(2,1)S(1)}, bf16[2,16,128,1024]{3,2,1,0:T(8,128)(2,1)}, u32[]{:S(2)}) %copy-start.5) | copy-done | bytes 8388632
  19.2 2.1 %shard_map.47 = (f32[2,64,1024]{2,1,0:T(8,128)S(1)}, bf16[2048,512]{1,0:T(8,128)(2,1)}, bf16[16,128,1024]{2,1,0:T(8,128)(2,1)S(1)}, bf16[16,128,1024]{2,1,0:T(8,128)(2,1)S(1)}) custom-call(bf16[64,1024]{1,0:T(8,128)(2,1)S(1)} %get-tuple-element.17.after_ref.refs_0_, f32[2,64,1024]{2,1,0:T(8,128)S(1)} %copy-done.9, bf16[2,2048,512]{2,1,0:T(8,128)(2,1)S(1)} %copy-done.1, ...), custom_call_target="tpu_custom_call" | custom-call | bytes 13238272 | tf_op jit(solution)/shard_map/pallas_call | solution.py:122
  21.3 2.0 %copy-done.2 = bf16[16,128,1024]{2,1,0:T(8,128)(2,1)} copy-done((bf16[16,128,1024]{2,1,0:T(8,128)(2,1)}, bf16[16,128,1024]{2,1,0:T(8,128)(2,1)S(1)}, u32[]{:S(2)}) %copy-start.2) | copy-done | bytes 4194328
  23.3 2.0 %copy-done.6 = bf16[16,128,1024]{2,1,0:T(8,128)(2,1)} copy-done((bf16[16,128,1024]{2,1,0:T(8,128)(2,1)}, bf16[16,128,1024]{2,1,0:T(8,128)(2,1)S(1)}, u32[]{:S(2)}) %copy-start.6) | copy-done | bytes 4194328
  25.3 0.7 collective-permute-start.3
  26.0 0.7 collective-permute-start.2
  26.7 0.9 broadcast_select_fusion.6.refs_1_
  27.7 2.2 %copy-done.3 = bf16[16,128,1024]{2,1,0:T(8,128)(2,1)S(1)} copy-done((bf16[16,128,1024]{2,1,0:T(8,128)(2,1)S(1)}, bf16[16,128,1024]{2,1,0:T(8,128)(2,1)}, u32[]{:S(2)}) %copy-start.3) | copy-done | bytes 4194328
  29.9 1.4 %shard_map.49.after_ref.refs_0_ = bf16[64,1024]{1,0:T(8,128)(2,1)S(1)} custom-call(s32[3]{0:T(128)S(1)} %pad_add_fusion.position_ref, s32[2,16]{1,0:T(2,128)S(1)} %copy-done.12, f32[2,64,1024]{2,1,0:T(8,128)S(1)} %get-tuple-element.18.right_ref, bf16[16,128,1024]{2,1,0:T(8,128)(2,1)S(1)} %copy-done.3, bf16[64,1024]{1,0:T(8,128)(2,1)S(1)} %broadcast_select_fusion.7.refs_0_, ...), custom_call_target="tpu_custom_call" | custom-call | flops 268435456 | bytes 4980736 | tf_op jit(solution)/shard_map/pallas_call | solution.py:122
  31.3 0.6 shard_map.50
  31.9 1.4 %collective-permute-start.7 = (bf16[64,2048]{1,0:T(8,128)(2,1)S(1)}, bf16[64,2048]{1,0:T(8,128)(2,1)}, u32[]{:S(2)}, u32[]{:S(2)}) collective-permute-start(bf16[64,2048]{1,0:T(8,128)(2,1)S(1)} %shard_map.50), channel_id=1, source_target_pairs={{4,8},{6,10},{20,24},{22,26},{5,9},{7,11},{21,25},{23,27}} | collective-permute-start | bytes 786440 | tf_op jit(solution)/shard_map/ppermute | solution.py:145
  33.2 1.3 %collective-permute-start.6 = (bf16[64,2048]{1,0:T(8,128)(2,1)S(1)}, bf16[64,2048]{1,0:T(8,128)(2,1)}, u32[]{:S(2)}, u32[]{:S(2)}) collective-permute-start(bf16[64,2048]{1,0:T(8,128)(2,1)S(1)} %shard_map.50), channel_id=1, source_target_pairs={{4,0},{6,2},{20,16},{22,18},{5,1},{7,3},{21,17},{23,19}} | collective-permute-start | bytes 786440 | tf_op jit(solution)/shard_map/ppermute | solution.py:145
  34.5 0.7 collective-permute-start.9
  35.2 0.4 collective-permute-start.20
  35.6 2.6 %shard_map.51 = (bf16[64,1024]{1,0:T(8,128)(2,1)S(1)}, f32[64,1024]{1,0:T(8,128)S(1)}) custom-call(s32[3]{0:T(128)S(1)} %pad_add_fusion.position_ref, bf16[64,1024]{1,0:T(8,128)(2,1)S(1)} %shard_map.49.after_ref.refs_0_, bf16[64,1024]{1,0:T(8,128)(2,1)S(1)} %collective-permute-done.9.refs_1_, bf16[2048,512]{1,0:T(8,128)(2,1)S(1)} %get-tuple-element.21.refs_2_, ...), custom_call_target="tpu_custom_call" | custom-call | flops 268435456 | bytes 4718592 | tf_op jit(solution)/shard_map/pallas_call | solution.py:122
  38.3 0.7 copy-done.10
  39.0 0.8 collective-permute-start.13
  39.7 1.3 %collective-permute-start.12 = (bf16[64,1024]{1,0:T(8,128)(2,1)S(1)}, bf16[64,1024]{1,0:T(8,128)(2,1)S(1)}, u32[]{:S(2)}, u32[]{:S(2)}) collective-permute-start(bf16[64,1024]{1,0:T(8,128)(2,1)S(1)} %get-tuple-element.24), channel_id=1, source_target_pairs={{4,2},{6,0},{20,18},{22,16},{5,3},{7,1},{21,19},{23,17}} | collective-permute-start | bytes 393224 | tf_op jit(solution)/shard_map/ppermute | solution.py:145
  41.1 0.7 collective-permute-start.11
  41.7 12.1 %collective-permute-done.6 = bf16[64,2048]{1,0:T(8,128)(2,1)} collective-permute-done((bf16[64,2048]{1,0:T(8,128)(2,1)S(1)}, bf16[64,2048]{1,0:T(8,128)(2,1)}, u32[]{:S(2)}, u32[]{:S(2)}) %collective-permute-start.6) | collective-permute-done | bytes 262176 | tf_op jit(solution)/shard_map/ppermute | solution.py:145
  53.9 1.3 %collective-permute-start.10 = (bf16[64,1024]{1,0:T(8,128)(2,1)S(1)}, bf16[64,1024]{1,0:T(8,128)(2,1)S(1)}, u32[]{:S(2)}, u32[]{:S(2)}) collective-permute-start(bf16[64,1024]{1,0:T(8,128)(2,1)S(1)} %get-tuple-element.24), channel_id=1, source_target_pairs={{4,0},{6,2},{20,16},{22,18},{5,1},{7,3},{21,17},{23,19}} | collective-permute-start | bytes 393224 | tf_op jit(solution)/shard_map/ppermute | solution.py:145
  55.1 1.0 %select_select_fusion.refs_0_ = bf16[64,2048]{1,0:T(8,128)(2,1)S(1)} fusion(bf16[64,2048]{1,0:T(8,128)(2,1)} %collective-permute-done.6, bf16[64,2048]{1,0:T(8,128)(2,1)} %collective-permute-done.7, bf16[64,2048]{1,0:T(8,128)(2,1)S(1)} %shard_map.50, pred[]{:T(512)S(6)} %and.62, pred[]{:T(512)S(6)} %and.58), kind=kLoop, calls=%fused_computation | loop fusion | flops 262144 | bytes 1048578 | tf_op jit(solution)/shard_map/jit(_where)/select_n | solution.py:208
  56.2 1.4 %collective-permute-start.8 = (bf16[64,2048]{1,0:T(8,128)(2,1)S(1)}, bf16[64,2048]{1,0:T(8,128)(2,1)}, u32[]{:S(2)}, u32[]{:S(2)}) collective-permute-start(bf16[64,2048]{1,0:T(8,128)(2,1)S(1)} %select_select_fusion.refs_0_), channel_id=1, source_target_pairs={{8,12},{10,14},{24,28},{26,30},{9,13},{11,15},{25,29},{27,31}} | collective-permute-start | bytes 786440 | tf_op jit(solution)/shard_map/ppermute | solution.py:145
  57.5 9.3 %collective-permute-done.12 = bf16[64,1024]{1,0:T(8,128)(2,1)S(1)} collective-permute-done((bf16[64,1024]{1,0:T(8,128)(2,1)S(1)}, bf16[64,1024]{1,0:T(8,128)(2,1)S(1)}, u32[]{:S(2)}, u32[]{:S(2)}) %collective-permute-start.12) | collective-permute-done | bytes 131104 | tf_op jit(solution)/shard_map/ppermute | solution.py:145
  66.8 0.5 collective-permute-done.10
  67.4 1.5 %shard_map.52.after_ref.refs_0_ = bf16[64,1024]{1,0:T(8,128)(2,1)S(1)} custom-call(s32[3]{0:T(128)S(1)} %pad_add_fusion.position_ref, s32[2,16]{1,0:T(2,128)S(1)} %copy-done.12, f32[2,64,1024]{2,1,0:T(8,128)S(1)} %get-tuple-element.18.right_ref, bf16[16,128,1024]{2,1,0:T(8,128)(2,1)S(1)} %copy-done.4, bf16[64,2048]{1,0:T(8,128)(2,1)S(1)} %select_select_fusion.refs_0_, ...), custom_call_target="tpu_custom_call" | custom-call | flops 268435456 | bytes 5242880 | tf_op jit(solution)/shard_map/pallas_call | solution.py:122
  68.8 3.4 %collective-permute-start.15 = (bf16[64,1024]{1,0:T(8,128)(2,1)S(1)}, bf16[64,1024]{1,0:T(8,128)(2,1)}, u32[]{:S(2)}, u32[]{:S(2)}) collective-permute-start(bf16[64,1024]{1,0:T(8,128)(2,1)S(1)} %shard_map.52.after_ref.refs_0_), channel_id=1, source_target_pairs={{0,2},{2,0},{8,10},{10,8},{16,18},{18,16},{24,26},{26,24},{1,3},{3... | collective-permute-start | bytes 393224 | tf_op jit(solution)/shard_map/ppermute | solution.py:145
  72.2 0.6 shard_map.53
  72.8 1.4 %collective-permute-start.14 = (bf16[64,2048]{1,0:T(8,128)(2,1)S(1)}, bf16[64,2048]{1,0:T(8,128)(2,1)S(1)}, u32[]{:S(2)}, u32[]{:S(2)}) collective-permute-start(bf16[64,2048]{1,0:T(8,128)(2,1)S(1)} %shard_map.53), channel_id=1, source_target_pairs={{0,4},{2,6},{8,12},{10,14},{16,20},{18,22},{24,28},{26,30},{1,5},{... | collective-permute-start | bytes 786440 | tf_op jit(solution)/shard_map/ppermute | solution.py:145
  74.2 1.5 %collective-permute-done.15.refs_1_ = bf16[64,1024]{1,0:T(8,128)(2,1)} collective-permute-done((bf16[64,1024]{1,0:T(8,128)(2,1)S(1)}, bf16[64,1024]{1,0:T(8,128)(2,1)}, u32[]{:S(2)}, u32[]{:S(2)}) %collective-permute-start.15) | collective-permute-done | bytes 131104 | tf_op jit(solution)/shard_map/ppermute | solution.py:145
  75.8 2.5 %shard_map.54 = (bf16[64,1024]{1,0:T(8,128)(2,1)S(1)}, f32[64,1024]{1,0:T(8,128)S(1)}) custom-call(s32[3]{0:T(128)S(1)} %pad_add_fusion.position_ref, bf16[64,1024]{1,0:T(8,128)(2,1)S(1)} %shard_map.52.after_ref.refs_0_, bf16[64,1024]{1,0:T(8,128)(2,1)} %collective-permute-done.15.refs_1_, bf16[2048,512]{1,0:T(8,128)(2,1)S(1)} %get-tuple-element.21.refs_2_, ...), custom_call_target="tpu_custom_call" | custom-call | flops 268435456 | bytes 4718592 | tf_op jit(solution)/shard_map/pallas_call | solution.py:122
  78.3 1.3 %collective-permute-start.18 = (bf16[64,1024]{1,0:T(8,128)(2,1)S(1)}, bf16[64,1024]{1,0:T(8,128)(2,1)S(1)}, u32[]{:S(2)}, u32[]{:S(2)}) collective-permute-start(bf16[64,1024]{1,0:T(8,128)(2,1)S(1)} %get-tuple-element.26), channel_id=1, source_target_pairs={{0,6},{2,4},{8,14},{10,12},{16,22},{18,20},{24,30},{26,28},{1,7},{... | collective-permute-start | bytes 393224 | tf_op jit(solution)/shard_map/ppermute | solution.py:145
  79.6 3.4 %collective-permute-start.17 = (bf16[64,1024]{1,0:T(8,128)(2,1)S(1)}, bf16[64,1024]{1,0:T(8,128)(2,1)S(1)}, u32[]{:S(2)}, u32[]{:S(2)}) collective-permute-start(bf16[64,1024]{1,0:T(8,128)(2,1)S(1)} %get-tuple-element.26), channel_id=1, source_target_pairs={{0,2},{2,0},{8,10},{10,8},{16,18},{18,16},{24,26},{26,24},{1,3},{3... | collective-permute-start | bytes 393224 | tf_op jit(solution)/shard_map/ppermute | solution.py:145
  83.0 1.3 %collective-permute-start.16 = (bf16[64,1024]{1,0:T(8,128)(2,1)S(1)}, bf16[64,1024]{1,0:T(8,128)(2,1)S(1)}, u32[]{:S(2)}, u32[]{:S(2)}) collective-permute-start(bf16[64,1024]{1,0:T(8,128)(2,1)S(1)} %get-tuple-element.26), channel_id=1, source_target_pairs={{0,4},{2,6},{8,12},{10,14},{16,20},{18,22},{24,28},{26,30},{1,5},{... | collective-permute-start | bytes 393224 | tf_op jit(solution)/shard_map/ppermute | solution.py:145
  84.4 2.4 %collective-permute-done.16 = bf16[64,1024]{1,0:T(8,128)(2,1)S(1)} collective-permute-done((bf16[64,1024]{1,0:T(8,128)(2,1)S(1)}, bf16[64,1024]{1,0:T(8,128)(2,1)S(1)}, u32[]{:S(2)}, u32[]{:S(2)}) %collective-permute-start.16) | collective-permute-done | bytes 131104 | tf_op jit(solution)/shard_map/ppermute | solution.py:145
  86.9 1.5 %shard_map.55.refs_0_ = bf16[64,1024]{1,0:T(8,128)(2,1)S(1)} custom-call(s32[3]{0:T(128)S(1)} %pad_add_fusion.position_ref, s32[2,16]{1,0:T(2,128)S(1)} %copy-done.12, f32[2,64,1024]{2,1,0:T(8,128)S(1)} %get-tuple-element.18.right_ref, bf16[16,128,1024]{2,1,0:T(8,128)(2,1)S(1)} %copy-done.7, bf16[64,2048]{1,0:T(8,128)(2,1)S(1)} %broadcast_select_fusion.1.refs_0_, ...), custom_call_target="tpu_custom_call" | custom-call | flops 268435456 | bytes 5505024 | tf_op jit(solution)/shard_map/pallas_call | solution.py:122
  88.3 1.2 %collective-permute-start.19 = (bf16[64,1024]{1,0:T(8,128)(2,1)S(1)}, bf16[64,1024]{1,0:T(8,128)(2,1)S(1)}, u32[]{:S(2)}, u32[]{:S(2)}) collective-permute-start(bf16[64,1024]{1,0:T(8,128)(2,1)S(1)} %shard_map.55.refs_0_), channel_id=1, source_target_pairs={{0,2},{2,0},{4,6},{6,4},{8,10},{10,8},{12,14},{14,12},{16,18},{18,... | collective-permute-start | bytes 393224 | tf_op jit(solution)/shard_map/ppermute | solution.py:145
  89.5 3.9 %collective-permute-done.19.refs_1_ = bf16[64,1024]{1,0:T(8,128)(2,1)S(1)} collective-permute-done((bf16[64,1024]{1,0:T(8,128)(2,1)S(1)}, bf16[64,1024]{1,0:T(8,128)(2,1)S(1)}, u32[]{:S(2)}, u32[]{:S(2)}) %collective-permute-start.19) | collective-permute-done | bytes 131104 | tf_op jit(solution)/shard_map/ppermute | solution.py:145
  93.4 3.9 %shard_map.56 = f32[2,64,1024]{2,1,0:T(8,128)} custom-call(s32[3]{0:T(128)S(1)} %pad_add_fusion.position_ref, bf16[64,1024]{1,0:T(8,128)(2,1)S(1)} %shard_map.55.refs_0_, bf16[64,1024]{1,0:T(8,128)(2,1)S(1)} %collective-permute-done.19.refs_1_, bf16[2048,512]{1,0:T(8,128)(2,1)} %get-tuple-element.27.refs_2_, ...), custom_call_target="tpu_custom_call" | custom-call | flops 268435456 | bytes 4718592 | tf_op jit(solution)/shard_map/pallas_call | solution.py:122
  (41 shorter events, 0.5 us)
Async XLA Ops:
  0.0 2.2 %copy-start = (bf16[2,2048,512]{2,1,0:T(8,128)(2,1)S(1)}, bf16[2,2048,512]{2,1,0:T(8,128)(2,1)}, u32[]{:S(2)}) copy-start(bf16[2,2048,512]{2,1,0:T(8,128)(2,1)} %inverse_ref.3) | copy-start | bytes 12582916
  2.2 1.0 %copy-start.8 = (f32[2,64,1024]{2,1,0:T(8,128)S(1)}, f32[2,64,1024]{2,1,0:T(8,128)}, u32[]{:S(2)}) copy-start(f32[2,64,1024]{2,1,0:T(8,128)} %right_ref.3) | copy-start | bytes 1572868
  3.2 10.4 %copy-start.9 = (f32[2,64,1024]{2,1,0:T(8,128)S(1)}, f32[2,64,1024]{2,1,0:T(8,128)}, u32[]{:S(2)}) copy-start(f32[2,64,1024]{2,1,0:T(8,128)} %right_ref.3) | copy-start | bytes 1572868
  3.4 4.4 %collective-permute-start.1 = (bf16[2048,512]{1,0:T(8,128)(2,1)S(1)}, bf16[2048,512]{1,0:T(8,128)(2,1)}, u32[]{:S(2)}, u32[]{:S(2)}) collective-permute-start(bf16[2048,512]{1,0:T(8,128)(2,1)S(1)} %get-tuple-element.21.refs_2_), channel_id=1, source_target_pairs={{0,1},{1,0},{2,3},{3,2},{4,5},{5,4},{6,7},{7,6},{8,9},{9,8},{10,11... | collective-permute-start | bytes 6291464 | tf_op jit(solution)/shard_map/ppermute | solution.py:155
  4.0 0.8 collective-permute-start
  11.0 15.7 %collective-permute-start.5 = (bf16[64,1024]{1,0:T(8,128)(2,1)}, bf16[64,1024]{1,0:T(8,128)(2,1)}, u32[]{:S(2)}, u32[]{:S(2)}) collective-permute-start(bf16[64,1024]{1,0:T(8,128)(2,1)} %get-tuple-element.22), channel_id=1, source_target_pairs={{12,22},{14,20},{13,23},{15,21}} | collective-permute-start | bytes 393224 | tf_op jit(solution)/shard_map/ppermute | solution.py:145
  12.3 14.4 %collective-permute-start.4 = (bf16[64,1024]{1,0:T(8,128)(2,1)}, bf16[64,1024]{1,0:T(8,128)(2,1)}, u32[]{:S(2)}, u32[]{:S(2)}) collective-permute-start(bf16[64,1024]{1,0:T(8,128)(2,1)} %get-tuple-element.22), channel_id=1, source_target_pairs={{12,6},{14,4},{13,7},{15,5}} | collective-permute-start | bytes 393224 | tf_op jit(solution)/shard_map/ppermute | solution.py:145
  13.6 2.2 %copy-start.1 = (bf16[2,2048,512]{2,1,0:T(8,128)(2,1)S(1)}, bf16[2,2048,512]{2,1,0:T(8,128)(2,1)}, u32[]{:S(2)}) copy-start(bf16[2,2048,512]{2,1,0:T(8,128)(2,1)} %inverse_ref.3) | copy-start | bytes 12582916
  15.8 3.4 %copy-start.5 = (bf16[2,16,128,1024]{3,2,1,0:T(8,128)(2,1)S(1)}, bf16[2,16,128,1024]{3,2,1,0:T(8,128)(2,1)}, u32[]{:S(2)}) copy-start(bf16[2,16,128,1024]{3,2,1,0:T(8,128)(2,1)} %lower_ref.1) | copy-start | bytes 25165828
  19.2 8.5 %copy-start.12 = (s32[2,16]{1,0:T(2,128)S(1)}, s32[2,16]{1,0:T(2,128)}, u32[]{:S(2)}) copy-start(s32[2,16]{1,0:T(2,128)} %block_rows_ref.5) | copy-start | bytes 388
  21.3 2.0 %copy-start.2 = (bf16[16,128,1024]{2,1,0:T(8,128)(2,1)}, bf16[16,128,1024]{2,1,0:T(8,128)(2,1)S(1)}, u32[]{:S(2)}) copy-start(bf16[16,128,1024]{2,1,0:T(8,128)(2,1)S(1)} %get-tuple-element.20.lower_ref) | copy-start | bytes 12582916
  23.3 2.0 %copy-start.6 = (bf16[16,128,1024]{2,1,0:T(8,128)(2,1)}, bf16[16,128,1024]{2,1,0:T(8,128)(2,1)S(1)}, u32[]{:S(2)}) copy-start(bf16[16,128,1024]{2,1,0:T(8,128)(2,1)S(1)} %get-tuple-element.19.lower_ref) | copy-start | bytes 12582916
  25.3 2.3 %collective-permute-start.3 = (bf16[64,1024]{1,0:T(8,128)(2,1)}, bf16[64,1024]{1,0:T(8,128)(2,1)S(1)}, u32[]{:S(2)}, u32[]{:S(2)}) collective-permute-start(bf16[64,1024]{1,0:T(8,128)(2,1)} %get-tuple-element.22), channel_id=1, source_target_pairs={{12,20},{14,22},{13,21},{15,23}} | collective-permute-start | bytes 393224 | tf_op jit(solution)/shard_map/ppermute | solution.py:145
  26.0 1.6 %collective-permute-start.2 = (bf16[64,1024]{1,0:T(8,128)(2,1)}, bf16[64,1024]{1,0:T(8,128)(2,1)S(1)}, u32[]{:S(2)}, u32[]{:S(2)}) collective-permute-start(bf16[64,1024]{1,0:T(8,128)(2,1)} %get-tuple-element.22), channel_id=1, source_target_pairs={{12,4},{14,6},{13,5},{15,7}} | collective-permute-start | bytes 393224 | tf_op jit(solution)/shard_map/ppermute | solution.py:145
  27.7 2.2 %copy-start.3 = (bf16[16,128,1024]{2,1,0:T(8,128)(2,1)S(1)}, bf16[16,128,1024]{2,1,0:T(8,128)(2,1)}, u32[]{:S(2)}) copy-start(bf16[16,128,1024]{2,1,0:T(8,128)(2,1)} %copy-done.2) | copy-start | bytes 12582916
  31.9 9.2 %collective-permute-start.7 = (bf16[64,2048]{1,0:T(8,128)(2,1)S(1)}, bf16[64,2048]{1,0:T(8,128)(2,1)}, u32[]{:S(2)}, u32[]{:S(2)}) collective-permute-start(bf16[64,2048]{1,0:T(8,128)(2,1)S(1)} %shard_map.50), channel_id=1, source_target_pairs={{4,8},{6,10},{20,24},{22,26},{5,9},{7,11},{21,25},{23,27}} | collective-permute-start | bytes 786440 | tf_op jit(solution)/shard_map/ppermute | solution.py:145
  33.2 20.6 %collective-permute-start.6 = (bf16[64,2048]{1,0:T(8,128)(2,1)S(1)}, bf16[64,2048]{1,0:T(8,128)(2,1)}, u32[]{:S(2)}, u32[]{:S(2)}) collective-permute-start(bf16[64,2048]{1,0:T(8,128)(2,1)S(1)} %shard_map.50), channel_id=1, source_target_pairs={{4,0},{6,2},{20,16},{22,18},{5,1},{7,3},{21,17},{23,19}} | collective-permute-start | bytes 786440 | tf_op jit(solution)/shard_map/ppermute | solution.py:145
  34.5 1.1 %collective-permute-start.9 = (bf16[64,1024]{1,0:T(8,128)(2,1)S(1)}, bf16[64,1024]{1,0:T(8,128)(2,1)S(1)}, u32[]{:S(2)}, u32[]{:S(2)}) collective-permute-start(bf16[64,1024]{1,0:T(8,128)(2,1)S(1)} %shard_map.49.after_ref.refs_0_), channel_id=1, source_target_pairs={{4,6},{6,4},{20,22},{22,20},{5,7},{7,5},{21,23},{23,21}} | collective-permute-start | bytes 393224 | tf_op jit(solution)/shard_map/ppermute | solution.py:145
  35.2 54.3 %collective-permute-start.20 = (bf16[2048,512]{1,0:T(8,128)(2,1)}, bf16[2048,512]{1,0:T(8,128)(2,1)}, u32[]{:S(2)}, u32[]{:S(2)}) collective-permute-start(bf16[2048,512]{1,0:T(8,128)(2,1)} %get-tuple-element.27.refs_2_), channel_id=1, source_target_pairs={{0,1},{1,0},{2,3},{3,2},{4,5},{5,4},{6,7},{7,6},{8,9},{9,8},{10,11... | collective-permute-start | bytes 6291464 | tf_op jit(solution)/shard_map/ppermute | solution.py:155
  35.6 31.7 %copy-start.4 = (bf16[16,128,1024]{2,1,0:T(8,128)(2,1)S(1)}, bf16[16,128,1024]{2,1,0:T(8,128)(2,1)}, u32[]{:S(2)}) copy-start(bf16[16,128,1024]{2,1,0:T(8,128)(2,1)} %copy-done.2) | copy-start | bytes 12582916
  38.2 0.7 copy-start.10
  39.0 36.8 %copy-start.11 = (f32[64,1024]{1,0:T(8,128)S(1)}, f32[64,1024]{1,0:T(8,128)}, u32[]{:S(2)}) copy-start(f32[64,1024]{1,0:T(8,128)} %copy-done.10) | copy-start | bytes 786436
  39.0 17.2 %collective-permute-start.13 = (bf16[64,1024]{1,0:T(8,128)(2,1)S(1)}, bf16[64,1024]{1,0:T(8,128)(2,1)S(1)}, u32[]{:S(2)}, u32[]{:S(2)}) collective-permute-start(bf16[64,1024]{1,0:T(8,128)(2,1)S(1)} %get-tuple-element.24), channel_id=1, source_target_pairs={{4,10},{6,8},{20,26},{22,24},{5,11},{7,9},{21,27},{23,25}} | collective-permute-start | bytes 393224 | tf_op jit(solution)/shard_map/ppermute | solution.py:145
  39.7 27.1 %collective-permute-start.12 = (bf16[64,1024]{1,0:T(8,128)(2,1)S(1)}, bf16[64,1024]{1,0:T(8,128)(2,1)S(1)}, u32[]{:S(2)}, u32[]{:S(2)}) collective-permute-start(bf16[64,1024]{1,0:T(8,128)(2,1)S(1)} %get-tuple-element.24), channel_id=1, source_target_pairs={{4,2},{6,0},{20,18},{22,16},{5,3},{7,1},{21,19},{23,17}} | collective-permute-start | bytes 393224 | tf_op jit(solution)/shard_map/ppermute | solution.py:145
  41.1 25.8 %collective-permute-start.11 = (bf16[64,1024]{1,0:T(8,128)(2,1)S(1)}, bf16[64,1024]{1,0:T(8,128)(2,1)S(1)}, u32[]{:S(2)}, u32[]{:S(2)}) collective-permute-start(bf16[64,1024]{1,0:T(8,128)(2,1)S(1)} %get-tuple-element.24), channel_id=1, source_target_pairs={{4,8},{6,10},{20,24},{22,26},{5,9},{7,11},{21,25},{23,27}} | collective-permute-start | bytes 393224 | tf_op jit(solution)/shard_map/ppermute | solution.py:145
  53.9 13.5 %collective-permute-start.10 = (bf16[64,1024]{1,0:T(8,128)(2,1)S(1)}, bf16[64,1024]{1,0:T(8,128)(2,1)S(1)}, u32[]{:S(2)}, u32[]{:S(2)}) collective-permute-start(bf16[64,1024]{1,0:T(8,128)(2,1)S(1)} %get-tuple-element.24), channel_id=1, source_target_pairs={{4,0},{6,2},{20,16},{22,18},{5,1},{7,3},{21,17},{23,19}} | collective-permute-start | bytes 393224 | tf_op jit(solution)/shard_map/ppermute | solution.py:145
  56.2 26.8 %collective-permute-start.8 = (bf16[64,2048]{1,0:T(8,128)(2,1)S(1)}, bf16[64,2048]{1,0:T(8,128)(2,1)}, u32[]{:S(2)}, u32[]{:S(2)}) collective-permute-start(bf16[64,2048]{1,0:T(8,128)(2,1)S(1)} %select_select_fusion.refs_0_), channel_id=1, source_target_pairs={{8,12},{10,14},{24,28},{26,30},{9,13},{11,15},{25,29},{27,31}} | collective-permute-start | bytes 786440 | tf_op jit(solution)/shard_map/ppermute | solution.py:145
  68.8 7.0 %collective-permute-start.15 = (bf16[64,1024]{1,0:T(8,128)(2,1)S(1)}, bf16[64,1024]{1,0:T(8,128)(2,1)}, u32[]{:S(2)}, u32[]{:S(2)}) collective-permute-start(bf16[64,1024]{1,0:T(8,128)(2,1)S(1)} %shard_map.52.after_ref.refs_0_), channel_id=1, source_target_pairs={{0,2},{2,0},{8,10},{10,8},{16,18},{18,16},{24,26},{26,24},{1,3},{3... | collective-permute-start | bytes 393224 | tf_op jit(solution)/shard_map/ppermute | solution.py:145
  72.2 14.7 %copy-start.7 = (bf16[16,128,1024]{2,1,0:T(8,128)(2,1)S(1)}, bf16[16,128,1024]{2,1,0:T(8,128)(2,1)}, u32[]{:S(2)}) copy-start(bf16[16,128,1024]{2,1,0:T(8,128)(2,1)} %copy-done.6) | copy-start | bytes 12582916
  72.8 11.6 %collective-permute-start.14 = (bf16[64,2048]{1,0:T(8,128)(2,1)S(1)}, bf16[64,2048]{1,0:T(8,128)(2,1)S(1)}, u32[]{:S(2)}, u32[]{:S(2)}) collective-permute-start(bf16[64,2048]{1,0:T(8,128)(2,1)S(1)} %shard_map.53), channel_id=1, source_target_pairs={{0,4},{2,6},{8,12},{10,14},{16,20},{18,22},{24,28},{26,30},{1,5},{... | collective-permute-start | bytes 786440 | tf_op jit(solution)/shard_map/ppermute | solution.py:145
  78.3 8.5 %collective-permute-start.18 = (bf16[64,1024]{1,0:T(8,128)(2,1)S(1)}, bf16[64,1024]{1,0:T(8,128)(2,1)S(1)}, u32[]{:S(2)}, u32[]{:S(2)}) collective-permute-start(bf16[64,1024]{1,0:T(8,128)(2,1)S(1)} %get-tuple-element.26), channel_id=1, source_target_pairs={{0,6},{2,4},{8,14},{10,12},{16,22},{18,20},{24,30},{26,28},{1,7},{... | collective-permute-start | bytes 393224 | tf_op jit(solution)/shard_map/ppermute | solution.py:145
  79.6 7.2 %collective-permute-start.17 = (bf16[64,1024]{1,0:T(8,128)(2,1)S(1)}, bf16[64,1024]{1,0:T(8,128)(2,1)S(1)}, u32[]{:S(2)}, u32[]{:S(2)}) collective-permute-start(bf16[64,1024]{1,0:T(8,128)(2,1)S(1)} %get-tuple-element.26), channel_id=1, source_target_pairs={{0,2},{2,0},{8,10},{10,8},{16,18},{18,16},{24,26},{26,24},{1,3},{3... | collective-permute-start | bytes 393224 | tf_op jit(solution)/shard_map/ppermute | solution.py:145
  83.0 3.8 %collective-permute-start.16 = (bf16[64,1024]{1,0:T(8,128)(2,1)S(1)}, bf16[64,1024]{1,0:T(8,128)(2,1)S(1)}, u32[]{:S(2)}, u32[]{:S(2)}) collective-permute-start(bf16[64,1024]{1,0:T(8,128)(2,1)S(1)} %get-tuple-element.26), channel_id=1, source_target_pairs={{0,4},{2,6},{8,12},{10,14},{16,20},{18,22},{24,28},{26,30},{1,5},{... | collective-permute-start | bytes 393224 | tf_op jit(solution)/shard_map/ppermute | solution.py:145
  88.3 5.0 %collective-permute-start.19 = (bf16[64,1024]{1,0:T(8,128)(2,1)S(1)}, bf16[64,1024]{1,0:T(8,128)(2,1)S(1)}, u32[]{:S(2)}, u32[]{:S(2)}) collective-permute-start(bf16[64,1024]{1,0:T(8,128)(2,1)S(1)} %shard_map.55.refs_0_), channel_id=1, source_target_pairs={{0,2},{2,0},{4,6},{6,4},{8,10},{10,8},{12,14},{14,12},{16,18},{18,... | collective-permute-start | bytes 393224 | tf_op jit(solution)/shard_map/ppermute | solution.py:145

commit v3 on v2

--- a/solution.py
+++ b/solution.py
@@ -65,16 +65,11 @@
     reduced_ref[...] = (right_ref[slot] - offset).astype(BF16)
 
 
-def apply_inverse(rows, cores, position_ref, piece_refs, inverse_refs, store):
-    width = piece_refs[0].shape[1]
+def apply_inverse(cores, position_ref, piece_refs, inverse_refs, joined, store):
     quarter = inverse_refs[0].shape[-1]
+    place_pieces(position_ref, piece_refs, joined, 0)
     for turn, inverse_ref in enumerate(inverse_refs):
-        total = None
-        for shift, piece_ref in enumerate(piece_refs):
-            source = lax.rem(position_ref[0] - shift + rows, rows)
-            part = inverse_ref[pl.ds(pl.multiple_of(source * width, width), width), :]
-            term = jnp.dot(piece_ref[...], part, preferred_element_type=F32)
-            total = term if total is None else total + term
+        total = jnp.dot(joined[...], inverse_ref[...], preferred_element_type=F32)
         core = lax.rem(position_ref[1] - turn + cores, cores)
         store(pl.ds(pl.multiple_of(core * quarter, quarter), quarter), total)
 
@@ -84,9 +79,9 @@
     inverse_refs = refs[rows:rows + cores]
     rest = refs[rows + cores:]
     if depth_now == 0:
-        before_ref, (rounded_ref, solved_ref) = None, rest
+        before_ref, (rounded_ref, solved_ref, joined) = None, rest
     else:
-        before_ref, rounded_ref, solved_ref = rest
+        before_ref, rounded_ref, solved_ref, joined = rest
     active = position_ref[2] == depth_now
 
     def store(columns, total):
@@ -94,19 +89,19 @@
         before = jnp.zeros_like(total) if before_ref is None else before_ref[:, columns]
         solved_ref[:, columns] = jnp.where(active, total, before)
 
-    apply_inverse(rows, cores, position_ref, piece_refs, inverse_refs, store)
+    apply_inverse(cores, position_ref, piece_refs, inverse_refs, joined, store)
 
 
 def last_kernel(rows, cores, position_ref, *refs):
     piece_refs = refs[:rows]
     inverse_refs = refs[rows:rows + cores]
-    before_ref, out_ref = refs[rows + cores:]
+    before_ref, out_ref, joined = refs[rows + cores:]
     out_ref[1] = before_ref[...]
 
     def store(columns, total):
         out_ref[0, :, columns] = total
 
-    apply_inverse(rows, cores, position_ref, piece_refs, inverse_refs, store)
+    apply_inverse(cores, position_ref, piece_refs, inverse_refs, joined, store)
 
 
 SCALARS = pl.BlockSpec(memory_space=pltpu.SMEM)
@@ -118,7 +113,8 @@
     several = len(outs) > 1
     size = sum(a.size * a.dtype.itemsize for a in arrays)
     here = len(arrays) - far
-    arrays = [pltpu.with_memory_space_constraint(a, pltpu.VMEM) for a in arrays[:here]] + list(arrays[here:])
+    spaces = [pltpu.VMEM] * here + [pltpu.HBM] * far
+    arrays = [pltpu.with_memory_space_constraint(a, space) for a, space in zip(arrays, spaces)]
     return pl.pallas_call(
         kernel,
         in_specs=[SCALARS] * len(scalars) + [WHOLE] * here + [FAR] * far,
@@ -161,6 +157,7 @@
     half_f32 = near((count, width), F32)
     full = near((count, full_width), BF16)
     work = 2 * count * full_width * width
+    joined = pltpu.VMEM((count, full_width), BF16)
     square = near(inverse_diag.shape[1:], BF16)
     lower = near(lower_blocks.shape[1:], BF16)
 
@@ -189,20 +186,21 @@
             reduced = call(
                 kernel, [position, block_rows],
                 [right, lower_lower if last else lower_upper, *known, *pieces], [half],
-                [pltpu.VMEM((count, depth * full_width), BF16), pltpu.VMEM((count, full_width), BF16)], work)
+                [pltpu.VMEM((count, depth * full_width), BF16), joined], work)
             gathered = rows_of(reduced, range(leafs) if last else holders(depth))
         if last:
             kernel = functools.partial(last_kernel, rows, cores)
             return call(kernel, [position], [*gathered, *inverse_lower, solved],
-                        [jax.ShapeDtypeStruct(right_side.shape, F32)], (), work)
+                        [jax.ShapeDtypeStruct(right_side.shape, F32)], [joined], work)
         here = holders(depth)
         if depth > 0:
-            newest = call(functools.partial(whole_kernel, rows), [position], [reduced, *pieces], [full])
+            newest = call(functools.partial(whole_kernel, rows), [position], [reduced, *pieces], [full], (), 8 * work)
             known = [*known, newest]
         if depth + 1 < top:
             reach = 2 ** (top - depth - 2)
-            left = [(h, h - reach) for h in here]
-            right_hops = [(h, h + reach) for h in here]
+            idle = [(h + (2 if reach == 1 else 1), h) for h in here]
+            left = [(h, h - reach) for h in here] + idle
+            right_hops = [(h, h + reach) for h in here] + idle
             is_left = (depth_upper == depth + 1) & (((leaf + 1) // reach) % 4 == 1)
             is_right = (depth_upper == depth + 1) & (((leaf + 1) // reach) % 4 == 3)
             known = [jnp.where(is_left, send(k, left, 0), jnp.where(is_right, send(k, right_hops, 0), k)) for k in known]
@@ -215,7 +213,7 @@
             known = passed
         kernel = functools.partial(solve_kernel, rows, cores, depth)
         arrays = [*gathered, *inverse_upper] + ([] if depth == 0 else [solved])
-        rounded, solved = call(kernel, [position], arrays, [half, half_f32], (), work)
+        rounded, solved = call(kernel, [position], arrays, [half, half_f32], [joined], work)
         if depth + 1 < top:
             lefts, rights = spread(rounded, left), spread(rounded, right_hops)
             pieces = [jnp.where(is_left, a, b) for a, b in zip(lefts, rights)]

time: 97.9 us -> 97 us (level)
  local copies, waits for them, and re-layouts: 15.7 us -> 6.17 us
  waiting for transfers between devices: 32.9 us -> 37.4 us
  Pallas kernels: 19.9 us -> 24.1 us
    unnamed x26 -> x12, local copies, waits for them, and re-layouts: 15.7 us -> 6.17 us
    ppermute x19, waiting for transfers between devices: 29.7 us -> 34.3 us  [send(): return lax.ppermute(value, places, pairs)]
    pallas_call x11, Pallas kernels: 19.9 us -> 24.1 us  [call(): pl.pallas_call(kernel, in_specs=[SCALARS] * len(scalars) + [WHOLE] * here...]
  transfers between devices with their start and end apart: 21 -> 21, of which waited for: 7 -> 6; matrix products, arithmetic and copies ran while one was open for 2% -> 1% of each run, Pallas kernels for 11% -> 15%
where the time goes in v3:
time: 97 us; the launch traced here: 96.5 us
  waiting for transfers between devices  37.4 us (39%)
  starting transfers between devices  27.1 us (28%)
  Pallas kernels  24.1 us (25%)
  local copies, waits for them, and re-layouts  6.17 us (6%)
  other arithmetic  1.26 us (1%)
    ppermute x19, waiting for transfers between devices, send(): return lax.ppermute(value, places, pairs)  34.3 us
    ppermute x19, starting transfers between devices, send(): return lax.ppermute(value, places, pairs)  26.1 us
    pallas_call x11, Pallas kernels, call(): pl.pallas_call(kernel, in_specs=[SCALARS] * len(scalars) + [WHOLE] * here...  24.1 us
    unnamed x12, local copies, waits for them, and re-layouts  6.17 us
    ppermute x2, waiting for transfers between devices, core_columns(): lax.ppermute(own, 'rhs', [(c, (c + t) % cores) for c in range(cores)])  3.14 us
  transfers between devices with their start and end apart: 21, of which 6 were waited for; matrix products, arithmetic and copies ran while one was open for 1% of the time, Pallas kernels for 15%

profile of v3, /device:TPU:0, one launch (start us, length us, event | category | flops | bytes accessed | tf_op | source)
XLA Modules:
  0.0 96.5 jit_solution(6487923074445129401)
XLA Ops:
  0.0 1.7 %shard_map.46 = (bf16[64,1024]{1,0:T(8,128)(2,1)S(1)}, bf16[2048,512]{1,0:T(8,128)(2,1)S(1)}) custom-call(f32[2,64,1024]{2,1,0:T(8,128)} %right_ref.3, bf16[2,2048,512]{2,1,0:T(8,128)(2,1)} %inverse_ref.3), custom_call_target="tpu_custom_call" | custom-call | bytes 4718592 | tf_op jit(solution)/shard_map/pallas_call | solution.py:118
  1.7 0.5 collective-permute-start.1
  2.2 0.7 collective-permute-start
  2.9 0.1 pad_add_fusion.position_ref
  3.0 0.0 collective-permute-done.refs_1_
  3.0 3.1 %collective-permute-done.1.refs_3_ = bf16[2048,512]{1,0:T(8,128)(2,1)} collective-permute-done((bf16[2048,512]{1,0:T(8,128)(2,1)S(1)}, bf16[2048,512]{1,0:T(8,128)(2,1)}, u32[]{:S(2)}, u32[]{:S(2)}) %collective-permute-start.1) | collective-permute-done | bytes 2097184 | tf_op jit(solution)/shard_map/ppermute | solution.py:151
  6.2 2.4 %shard_map.48 = (bf16[64,1024]{1,0:T(8,128)(2,1)S(1)}, f32[64,1024]{1,0:T(8,128)S(1)}) custom-call(s32[3]{0:T(128)S(1)} %pad_add_fusion.position_ref, bf16[64,1024]{1,0:T(8,128)(2,1)S(1)} %get-tuple-element.17.after_ref.refs_0_, bf16[64,1024]{1,0:T(8,128)(2,1)S(1)} %collective-permute-done.refs_1_, bf16[2048,512]{1,0:T(8,128)(2,1)S(1)} %get-tuple-element.21.refs_2_, ...), custom_call_target="tpu_custom_call" | custom-call | flops 268435456 | bytes 4456448 | tf_op jit(solution)/shard_map/pallas_call | solution.py:118
  8.6 0.7 collective-permute-start.5
  9.3 0.7 collective-permute-start.4
  10.0 0.0 copy-start.5
  10.0 5.6 %shard_map.47 = (f32[2,64,1024]{2,1,0:T(8,128)S(1)}, bf16[2048,512]{1,0:T(8,128)(2,1)}, bf16[16,128,1024]{2,1,0:T(8,128)(2,1)S(1)}, bf16[16,128,1024]{2,1,0:T(8,128)(2,1)S(1)}) custom-call(bf16[64,1024]{1,0:T(8,128)(2,1)S(1)} %get-tuple-element.17.after_ref.refs_0_, f32[2,64,1024]{2,1,0:T(8,128)} %right_ref.3, bf16[2,2048,512]{2,1,0:T(8,128)(2,1)} %inverse_ref.3, ...), custom_call_target="tpu_custom_call" | custom-call | bytes 13238272 | tf_op jit(solution)/shard_map/pallas_call | solution.py:118
  15.6 2.0 %copy-done = bf16[16,128,1024]{2,1,0:T(8,128)(2,1)} copy-done((bf16[16,128,1024]{2,1,0:T(8,128)(2,1)}, bf16[16,128,1024]{2,1,0:T(8,128)(2,1)S(1)}, u32[]{:S(2)}) %copy-start) | copy-done | bytes 4194328
  17.6 2.0 %copy-done.3 = bf16[16,128,1024]{2,1,0:T(8,128)(2,1)} copy-done((bf16[16,128,1024]{2,1,0:T(8,128)(2,1)}, bf16[16,128,1024]{2,1,0:T(8,128)(2,1)S(1)}, u32[]{:S(2)}) %copy-start.3) | copy-done | bytes 4194328
  19.6 0.7 collective-permute-start.3
  20.3 0.7 collective-permute-start.2
  21.0 0.0 collective-permute-done.2
  21.0 2.2 %copy-done.1 = bf16[16,128,1024]{2,1,0:T(8,128)(2,1)S(1)} copy-done((bf16[16,128,1024]{2,1,0:T(8,128)(2,1)S(1)}, bf16[16,128,1024]{2,1,0:T(8,128)(2,1)}, u32[]{:S(2)}) %copy-start.1) | copy-done | bytes 4194328
  23.2 1.4 %shard_map.49.after_ref.refs_0_ = bf16[64,1024]{1,0:T(8,128)(2,1)S(1)} custom-call(s32[3]{0:T(128)S(1)} %pad_add_fusion.position_ref, s32[2,16]{1,0:T(2,128)S(1)} %copy-done.5, f32[2,64,1024]{2,1,0:T(8,128)S(1)} %get-tuple-element.18.right_ref, bf16[16,128,1024]{2,1,0:T(8,128)(2,1)S(1)} %copy-done.1, bf16[64,1024]{1,0:T(8,128)(2,1)S(1)} %broadcast_select_fusion.7.refs_0_, ...), custom_call_target="tpu_custom_call" | custom-call | flops 268435456 | bytes 4980736 | tf_op jit(solution)/shard_map/pallas_call | solution.py:118
  24.6 0.6 shard_map.50
  25.2 1.4 %collective-permute-start.7 = (bf16[64,2048]{1,0:T(8,128)(2,1)S(1)}, bf16[64,2048]{1,0:T(8,128)(2,1)}, u32[]{:S(2)}, u32[]{:S(2)}) collective-permute-start(bf16[64,2048]{1,0:T(8,128)(2,1)S(1)} %shard_map.50), channel_id=1, source_target_pairs={{4,8},{6,10},{20,24},{22,26},{12,4},{14,6},{28,20},{30,22},{5,9},{... | collective-permute-start | bytes 786440 | tf_op jit(solution)/shard_map/ppermute | solution.py:141
  26.6 1.3 %collective-permute-start.6 = (bf16[64,2048]{1,0:T(8,128)(2,1)S(1)}, bf16[64,2048]{1,0:T(8,128)(2,1)}, u32[]{:S(2)}, u32[]{:S(2)}) collective-permute-start(bf16[64,2048]{1,0:T(8,128)(2,1)S(1)} %shard_map.50), channel_id=1, source_target_pairs={{4,0},{6,2},{20,16},{22,18},{12,4},{14,6},{28,20},{30,22},{5,1},{7... | collective-permute-start | bytes 786440 | tf_op jit(solution)/shard_map/ppermute | solution.py:141
  27.9 0.7 collective-permute-start.9
  28.5 0.4 collective-permute-start.20
  29.0 2.6 %shard_map.51 = (bf16[64,1024]{1,0:T(8,128)(2,1)S(1)}, f32[64,1024]{1,0:T(8,128)S(1)}) custom-call(s32[3]{0:T(128)S(1)} %pad_add_fusion.position_ref, bf16[64,1024]{1,0:T(8,128)(2,1)S(1)} %shard_map.49.after_ref.refs_0_, bf16[64,1024]{1,0:T(8,128)(2,1)S(1)} %collective-permute-done.9.refs_1_, bf16[2048,512]{1,0:T(8,128)(2,1)S(1)} %get-tuple-element.21.refs_2_, ...), custom_call_target="tpu_custom_call" | custom-call | flops 268435456 | bytes 4718592 | tf_op jit(solution)/shard_map/pallas_call | solution.py:118
  31.6 0.7 collective-permute-start.13
  32.3 1.3 %collective-permute-start.12 = (bf16[64,1024]{1,0:T(8,128)(2,1)S(1)}, bf16[64,1024]{1,0:T(8,128)(2,1)S(1)}, u32[]{:S(2)}, u32[]{:S(2)}) collective-permute-start(bf16[64,1024]{1,0:T(8,128)(2,1)S(1)} %get-tuple-element.24), channel_id=1, source_target_pairs={{4,2},{6,0},{20,18},{22,16},{12,6},{14,4},{28,22},{30,20},{5,3},{7... | collective-permute-start | bytes 393224 | tf_op jit(solution)/shard_map/ppermute | solution.py:141
  33.6 0.7 collective-permute-start.11
  34.2 16.7 %collective-permute-done.6 = bf16[64,2048]{1,0:T(8,128)(2,1)} collective-permute-done((bf16[64,2048]{1,0:T(8,128)(2,1)S(1)}, bf16[64,2048]{1,0:T(8,128)(2,1)}, u32[]{:S(2)}, u32[]{:S(2)}) %collective-permute-start.6) | collective-permute-done | bytes 262176 | tf_op jit(solution)/shard_map/ppermute | solution.py:141
  51.0 1.3 %collective-permute-start.10 = (bf16[64,1024]{1,0:T(8,128)(2,1)S(1)}, bf16[64,1024]{1,0:T(8,128)(2,1)S(1)}, u32[]{:S(2)}, u32[]{:S(2)}) collective-permute-start(bf16[64,1024]{1,0:T(8,128)(2,1)S(1)} %get-tuple-element.24), channel_id=1, source_target_pairs={{4,0},{6,2},{20,16},{22,18},{12,4},{14,6},{28,20},{30,22},{5,1},{7... | collective-permute-start | bytes 393224 | tf_op jit(solution)/shard_map/ppermute | solution.py:141
  52.3 1.0 %select_select_fusion.refs_0_ = bf16[64,2048]{1,0:T(8,128)(2,1)S(1)} fusion(bf16[64,2048]{1,0:T(8,128)(2,1)} %collective-permute-done.6, bf16[64,2048]{1,0:T(8,128)(2,1)} %collective-permute-done.7, bf16[64,2048]{1,0:T(8,128)(2,1)S(1)} %shard_map.50, pred[]{:T(512)S(6)} %and.62, pred[]{:T(512)S(6)} %and.58), kind=kLoop, calls=%fused_computation | loop fusion | flops 262144 | bytes 1048578 | tf_op jit(solution)/shard_map/jit(_where)/select_n | solution.py:206
  53.3 0.7 collective-permute-start.8
  54.0 8.4 %collective-permute-done.12 = bf16[64,1024]{1,0:T(8,128)(2,1)S(1)} collective-permute-done((bf16[64,1024]{1,0:T(8,128)(2,1)S(1)}, bf16[64,1024]{1,0:T(8,128)(2,1)S(1)}, u32[]{:S(2)}, u32[]{:S(2)}) %collective-permute-start.12) | collective-permute-done | bytes 131104 | tf_op jit(solution)/shard_map/ppermute | solution.py:141
  62.4 0.0 collective-permute-done.11
  62.4 2.9 %collective-permute-done.10 = bf16[64,1024]{1,0:T(8,128)(2,1)S(1)} collective-permute-done((bf16[64,1024]{1,0:T(8,128)(2,1)S(1)}, bf16[64,1024]{1,0:T(8,128)(2,1)S(1)}, u32[]{:S(2)}, u32[]{:S(2)}) %collective-permute-start.10) | collective-permute-done | bytes 131104 | tf_op jit(solution)/shard_map/ppermute | solution.py:141
  65.3 1.5 %shard_map.52.after_ref.refs_0_ = bf16[64,1024]{1,0:T(8,128)(2,1)S(1)} custom-call(s32[3]{0:T(128)S(1)} %pad_add_fusion.position_ref, s32[2,16]{1,0:T(2,128)S(1)} %copy-done.5, f32[2,64,1024]{2,1,0:T(8,128)S(1)} %get-tuple-element.18.right_ref, bf16[16,128,1024]{2,1,0:T(8,128)(2,1)S(1)} %copy-done.2, bf16[64,2048]{1,0:T(8,128)(2,1)S(1)} %select_select_fusion.refs_0_, ...), custom_call_target="tpu_custom_call" | custom-call | flops 268435456 | bytes 5242880 | tf_op jit(solution)/shard_map/pallas_call | solution.py:118
  66.7 3.4 %collective-permute-start.15 = (bf16[64,1024]{1,0:T(8,128)(2,1)S(1)}, bf16[64,1024]{1,0:T(8,128)(2,1)S(1)}, u32[]{:S(2)}, u32[]{:S(2)}) collective-permute-start(bf16[64,1024]{1,0:T(8,128)(2,1)S(1)} %shard_map.52.after_ref.refs_0_), channel_id=1, source_target_pairs={{0,2},{2,0},{8,10},{10,8},{16,18},{18,16},{24,26},{26,24},{1,3},{3... | collective-permute-start | bytes 393224 | tf_op jit(solution)/shard_map/ppermute | solution.py:141
  70.2 0.6 shard_map.53
  70.8 4.4 %collective-permute-start.14 = (bf16[64,2048]{1,0:T(8,128)(2,1)S(1)}, bf16[64,2048]{1,0:T(8,128)(2,1)S(1)}, u32[]{:S(2)}, u32[]{:S(2)}) collective-permute-start(bf16[64,2048]{1,0:T(8,128)(2,1)S(1)} %shard_map.53), channel_id=1, source_target_pairs={{0,4},{2,6},{8,12},{10,14},{16,20},{18,22},{24,28},{26,30},{1,5},{... | collective-permute-start | bytes 786440 | tf_op jit(solution)/shard_map/ppermute | solution.py:141
  75.1 2.4 %shard_map.54 = (bf16[64,1024]{1,0:T(8,128)(2,1)S(1)}, f32[64,1024]{1,0:T(8,128)S(1)}) custom-call(s32[3]{0:T(128)S(1)} %pad_add_fusion.position_ref, bf16[64,1024]{1,0:T(8,128)(2,1)S(1)} %shard_map.52.after_ref.refs_0_, bf16[64,1024]{1,0:T(8,128)(2,1)S(1)} %collective-permute-done.15.refs_1_, bf16[2048,512]{1,0:T(8,128)(2,1)S(1)} %get-tuple-element.21.refs_2_, ...), custom_call_target="tpu_custom_call" | custom-call | flops 268435456 | bytes 4718592 | tf_op jit(solution)/shard_map/pallas_call | solution.py:118
  77.6 1.3 %collective-permute-start.18 = (bf16[64,1024]{1,0:T(8,128)(2,1)S(1)}, bf16[64,1024]{1,0:T(8,128)(2,1)S(1)}, u32[]{:S(2)}, u32[]{:S(2)}) collective-permute-start(bf16[64,1024]{1,0:T(8,128)(2,1)S(1)} %get-tuple-element.26), channel_id=1, source_target_pairs={{0,6},{2,4},{8,14},{10,12},{16,22},{18,20},{24,30},{26,28},{1,7},{... | collective-permute-start | bytes 393224 | tf_op jit(solution)/shard_map/ppermute | solution.py:141
  78.9 3.4 %collective-permute-start.17 = (bf16[64,1024]{1,0:T(8,128)(2,1)S(1)}, bf16[64,1024]{1,0:T(8,128)(2,1)S(1)}, u32[]{:S(2)}, u32[]{:S(2)}) collective-permute-start(bf16[64,1024]{1,0:T(8,128)(2,1)S(1)} %get-tuple-element.26), channel_id=1, source_target_pairs={{0,2},{2,0},{8,10},{10,8},{16,18},{18,16},{24,26},{26,24},{1,3},{3... | collective-permute-start | bytes 393224 | tf_op jit(solution)/shard_map/ppermute | solution.py:141
  82.3 1.3 %collective-permute-start.16 = (bf16[64,1024]{1,0:T(8,128)(2,1)S(1)}, bf16[64,1024]{1,0:T(8,128)(2,1)S(1)}, u32[]{:S(2)}, u32[]{:S(2)}) collective-permute-start(bf16[64,1024]{1,0:T(8,128)(2,1)S(1)} %get-tuple-element.26), channel_id=1, source_target_pairs={{0,4},{2,6},{8,12},{10,14},{16,20},{18,22},{24,28},{26,30},{1,5},{... | collective-permute-start | bytes 393224 | tf_op jit(solution)/shard_map/ppermute | solution.py:141
  83.6 0.0 collective-permute-done.14
  83.7 2.4 %collective-permute-done.16 = bf16[64,1024]{1,0:T(8,128)(2,1)S(1)} collective-permute-done((bf16[64,1024]{1,0:T(8,128)(2,1)S(1)}, bf16[64,1024]{1,0:T(8,128)(2,1)S(1)}, u32[]{:S(2)}, u32[]{:S(2)}) %collective-permute-start.16) | collective-permute-done | bytes 131104 | tf_op jit(solution)/shard_map/ppermute | solution.py:141
  86.1 1.5 %shard_map.55.refs_0_ = bf16[64,1024]{1,0:T(8,128)(2,1)S(1)} custom-call(s32[3]{0:T(128)S(1)} %pad_add_fusion.position_ref, s32[2,16]{1,0:T(2,128)S(1)} %copy-done.5, f32[2,64,1024]{2,1,0:T(8,128)S(1)} %get-tuple-element.18.right_ref, bf16[16,128,1024]{2,1,0:T(8,128)(2,1)S(1)} %copy-done.4, bf16[64,2048]{1,0:T(8,128)(2,1)S(1)} %broadcast_select_fusion.1.refs_0_, ...), custom_call_target="tpu_custom_call" | custom-call | flops 268435456 | bytes 5505024 | tf_op jit(solution)/shard_map/pallas_call | solution.py:118
  87.6 1.2 %collective-permute-start.19 = (bf16[64,1024]{1,0:T(8,128)(2,1)S(1)}, bf16[64,1024]{1,0:T(8,128)(2,1)S(1)}, u32[]{:S(2)}, u32[]{:S(2)}) collective-permute-start(bf16[64,1024]{1,0:T(8,128)(2,1)S(1)} %shard_map.55.refs_0_), channel_id=1, source_target_pairs={{0,2},{2,0},{4,6},{6,4},{8,10},{10,8},{12,14},{14,12},{16,18},{18,... | collective-permute-start | bytes 393224 | tf_op jit(solution)/shard_map/ppermute | solution.py:141
  88.8 3.9 %collective-permute-done.19.refs_1_ = bf16[64,1024]{1,0:T(8,128)(2,1)S(1)} collective-permute-done((bf16[64,1024]{1,0:T(8,128)(2,1)S(1)}, bf16[64,1024]{1,0:T(8,128)(2,1)S(1)}, u32[]{:S(2)}, u32[]{:S(2)}) %collective-permute-start.19) | collective-permute-done | bytes 131104 | tf_op jit(solution)/shard_map/ppermute | solution.py:141
  92.6 3.9 %shard_map.56 = f32[2,64,1024]{2,1,0:T(8,128)} custom-call(s32[3]{0:T(128)S(1)} %pad_add_fusion.position_ref, bf16[64,1024]{1,0:T(8,128)(2,1)S(1)} %shard_map.55.refs_0_, bf16[64,1024]{1,0:T(8,128)(2,1)S(1)} %collective-permute-done.19.refs_1_, bf16[2048,512]{1,0:T(8,128)(2,1)} %get-tuple-element.27.refs_2_, ...), custom_call_target="tpu_custom_call" | custom-call | flops 268435456 | bytes 4718592 | tf_op jit(solution)/shard_map/pallas_call | solution.py:118
  (27 shorter events, 0.2 us)
Async XLA Ops:
  1.7 4.4 %collective-permute-start.1 = (bf16[2048,512]{1,0:T(8,128)(2,1)S(1)}, bf16[2048,512]{1,0:T(8,128)(2,1)}, u32[]{:S(2)}, u32[]{:S(2)}) collective-permute-start(bf16[2048,512]{1,0:T(8,128)(2,1)S(1)} %get-tuple-element.21.refs_2_), channel_id=1, source_target_pairs={{0,1},{1,0},{2,3},{3,2},{4,5},{5,4},{6,7},{7,6},{8,9},{9,8},{10,11... | collective-permute-start | bytes 6291464 | tf_op jit(solution)/shard_map/ppermute | solution.py:151
  2.2 0.8 collective-permute-start
  8.6 12.3 %collective-permute-start.5 = (bf16[64,1024]{1,0:T(8,128)(2,1)S(1)}, bf16[64,1024]{1,0:T(8,128)(2,1)S(1)}, u32[]{:S(2)}, u32[]{:S(2)}) collective-permute-start(bf16[64,1024]{1,0:T(8,128)(2,1)S(1)} %get-tuple-element.22), channel_id=1, source_target_pairs={{12,22},{14,20},{16,14},{18,12},{13,23},{15,21},{17,15},{19,13}} | collective-permute-start | bytes 393224 | tf_op jit(solution)/shard_map/ppermute | solution.py:141
  9.3 11.7 %collective-permute-start.4 = (bf16[64,1024]{1,0:T(8,128)(2,1)S(1)}, bf16[64,1024]{1,0:T(8,128)(2,1)S(1)}, u32[]{:S(2)}, u32[]{:S(2)}) collective-permute-start(bf16[64,1024]{1,0:T(8,128)(2,1)S(1)} %get-tuple-element.22), channel_id=1, source_target_pairs={{12,6},{14,4},{16,14},{18,12},{13,7},{15,5},{17,15},{19,13}} | collective-permute-start | bytes 393224 | tf_op jit(solution)/shard_map/ppermute | solution.py:141
  10.0 11.1 %copy-start.5 = (s32[2,16]{1,0:T(2,128)S(1)}, s32[2,16]{1,0:T(2,128)}, u32[]{:S(2)}) copy-start(s32[2,16]{1,0:T(2,128)} %block_rows_ref.5) | copy-start | bytes 388
  15.6 2.0 %copy-start = (bf16[16,128,1024]{2,1,0:T(8,128)(2,1)}, bf16[16,128,1024]{2,1,0:T(8,128)(2,1)S(1)}, u32[]{:S(2)}) copy-start(bf16[16,128,1024]{2,1,0:T(8,128)(2,1)S(1)} %get-tuple-element.20.lower_ref) | copy-start | bytes 12582916
  17.6 2.0 %copy-start.3 = (bf16[16,128,1024]{2,1,0:T(8,128)(2,1)}, bf16[16,128,1024]{2,1,0:T(8,128)(2,1)S(1)}, u32[]{:S(2)}) copy-start(bf16[16,128,1024]{2,1,0:T(8,128)(2,1)S(1)} %get-tuple-element.19.lower_ref) | copy-start | bytes 12582916
  19.6 1.4 %collective-permute-start.3 = (bf16[64,1024]{1,0:T(8,128)(2,1)S(1)}, bf16[64,1024]{1,0:T(8,128)(2,1)S(1)}, u32[]{:S(2)}, u32[]{:S(2)}) collective-permute-start(bf16[64,1024]{1,0:T(8,128)(2,1)S(1)} %get-tuple-element.22), channel_id=1, source_target_pairs={{12,20},{14,22},{16,12},{18,14},{13,21},{15,23},{17,13},{19,15}} | collective-permute-start | bytes 393224 | tf_op jit(solution)/shard_map/ppermute | solution.py:141
  20.3 0.7 collective-permute-start.2
  21.0 2.2 %copy-start.1 = (bf16[16,128,1024]{2,1,0:T(8,128)(2,1)S(1)}, bf16[16,128,1024]{2,1,0:T(8,128)(2,1)}, u32[]{:S(2)}) copy-start(bf16[16,128,1024]{2,1,0:T(8,128)(2,1)} %copy-done) | copy-start | bytes 12582916
  25.2 8.3 %collective-permute-start.7 = (bf16[64,2048]{1,0:T(8,128)(2,1)S(1)}, bf16[64,2048]{1,0:T(8,128)(2,1)}, u32[]{:S(2)}, u32[]{:S(2)}) collective-permute-start(bf16[64,2048]{1,0:T(8,128)(2,1)S(1)} %shard_map.50), channel_id=1, source_target_pairs={{4,8},{6,10},{20,24},{22,26},{12,4},{14,6},{28,20},{30,22},{5,9},{... | collective-permute-start | bytes 786440 | tf_op jit(solution)/shard_map/ppermute | solution.py:141
  26.6 24.4 %collective-permute-start.6 = (bf16[64,2048]{1,0:T(8,128)(2,1)S(1)}, bf16[64,2048]{1,0:T(8,128)(2,1)}, u32[]{:S(2)}, u32[]{:S(2)}) collective-permute-start(bf16[64,2048]{1,0:T(8,128)(2,1)S(1)} %shard_map.50), channel_id=1, source_target_pairs={{4,0},{6,2},{20,16},{22,18},{12,4},{14,6},{28,20},{30,22},{5,1},{7... | collective-permute-start | bytes 786440 | tf_op jit(solution)/shard_map/ppermute | solution.py:141
  27.9 1.1 %collective-permute-start.9 = (bf16[64,1024]{1,0:T(8,128)(2,1)S(1)}, bf16[64,1024]{1,0:T(8,128)(2,1)S(1)}, u32[]{:S(2)}, u32[]{:S(2)}) collective-permute-start(bf16[64,1024]{1,0:T(8,128)(2,1)S(1)} %shard_map.49.after_ref.refs_0_), channel_id=1, source_target_pairs={{4,6},{6,4},{20,22},{22,20},{5,7},{7,5},{21,23},{23,21}} | collective-permute-start | bytes 393224 | tf_op jit(solution)/shard_map/ppermute | solution.py:141
  28.5 60.2 %collective-permute-start.20 = (bf16[2048,512]{1,0:T(8,128)(2,1)}, bf16[2048,512]{1,0:T(8,128)(2,1)}, u32[]{:S(2)}, u32[]{:S(2)}) collective-permute-start(bf16[2048,512]{1,0:T(8,128)(2,1)} %get-tuple-element.27.refs_2_), channel_id=1, source_target_pairs={{0,1},{1,0},{2,3},{3,2},{4,5},{5,4},{6,7},{7,6},{8,9},{9,8},{10,11... | collective-permute-start | bytes 6291464 | tf_op jit(solution)/shard_map/ppermute | solution.py:151
  29.0 36.3 %copy-start.2 = (bf16[16,128,1024]{2,1,0:T(8,128)(2,1)S(1)}, bf16[16,128,1024]{2,1,0:T(8,128)(2,1)}, u32[]{:S(2)}) copy-start(bf16[16,128,1024]{2,1,0:T(8,128)(2,1)} %copy-done) | copy-start | bytes 12582916
  31.6 21.7 %collective-permute-start.13 = (bf16[64,1024]{1,0:T(8,128)(2,1)S(1)}, bf16[64,1024]{1,0:T(8,128)(2,1)S(1)}, u32[]{:S(2)}, u32[]{:S(2)}) collective-permute-start(bf16[64,1024]{1,0:T(8,128)(2,1)S(1)} %get-tuple-element.24), channel_id=1, source_target_pairs={{4,10},{6,8},{20,26},{22,24},{12,6},{14,4},{28,22},{30,20},{5,11},... | collective-permute-start | bytes 393224 | tf_op jit(solution)/shard_map/ppermute | solution.py:141
  32.3 30.1 %collective-permute-start.12 = (bf16[64,1024]{1,0:T(8,128)(2,1)S(1)}, bf16[64,1024]{1,0:T(8,128)(2,1)S(1)}, u32[]{:S(2)}, u32[]{:S(2)}) collective-permute-start(bf16[64,1024]{1,0:T(8,128)(2,1)S(1)} %get-tuple-element.24), channel_id=1, source_target_pairs={{4,2},{6,0},{20,18},{22,16},{12,6},{14,4},{28,22},{30,20},{5,3},{7... | collective-permute-start | bytes 393224 | tf_op jit(solution)/shard_map/ppermute | solution.py:141
  33.6 28.8 %collective-permute-start.11 = (bf16[64,1024]{1,0:T(8,128)(2,1)S(1)}, bf16[64,1024]{1,0:T(8,128)(2,1)S(1)}, u32[]{:S(2)}, u32[]{:S(2)}) collective-permute-start(bf16[64,1024]{1,0:T(8,128)(2,1)S(1)} %get-tuple-element.24), channel_id=1, source_target_pairs={{4,8},{6,10},{20,24},{22,26},{12,4},{14,6},{28,20},{30,22},{5,9},{... | collective-permute-start | bytes 393224 | tf_op jit(solution)/shard_map/ppermute | solution.py:141
  51.0 14.3 %collective-permute-start.10 = (bf16[64,1024]{1,0:T(8,128)(2,1)S(1)}, bf16[64,1024]{1,0:T(8,128)(2,1)S(1)}, u32[]{:S(2)}, u32[]{:S(2)}) collective-permute-start(bf16[64,1024]{1,0:T(8,128)(2,1)S(1)} %get-tuple-element.24), channel_id=1, source_target_pairs={{4,0},{6,2},{20,16},{22,18},{12,4},{14,6},{28,20},{30,22},{5,1},{7... | collective-permute-start | bytes 393224 | tf_op jit(solution)/shard_map/ppermute | solution.py:141
  53.3 29.0 %collective-permute-start.8 = (bf16[64,2048]{1,0:T(8,128)(2,1)S(1)}, bf16[64,2048]{1,0:T(8,128)(2,1)S(1)}, u32[]{:S(2)}, u32[]{:S(2)}) collective-permute-start(bf16[64,2048]{1,0:T(8,128)(2,1)S(1)} %select_select_fusion.refs_0_), channel_id=1, source_target_pairs={{8,12},{10,14},{24,28},{26,30},{9,13},{11,15},{25,29},{27,31}} | collective-permute-start | bytes 786440 | tf_op jit(solution)/shard_map/ppermute | solution.py:141
  66.7 8.4 %collective-permute-start.15 = (bf16[64,1024]{1,0:T(8,128)(2,1)S(1)}, bf16[64,1024]{1,0:T(8,128)(2,1)S(1)}, u32[]{:S(2)}, u32[]{:S(2)}) collective-permute-start(bf16[64,1024]{1,0:T(8,128)(2,1)S(1)} %shard_map.52.after_ref.refs_0_), channel_id=1, source_target_pairs={{0,2},{2,0},{8,10},{10,8},{16,18},{18,16},{24,26},{26,24},{1,3},{3... | collective-permute-start | bytes 393224 | tf_op jit(solution)/shard_map/ppermute | solution.py:141
  70.7 15.4 %copy-start.4 = (bf16[16,128,1024]{2,1,0:T(8,128)(2,1)S(1)}, bf16[16,128,1024]{2,1,0:T(8,128)(2,1)}, u32[]{:S(2)}) copy-start(bf16[16,128,1024]{2,1,0:T(8,128)(2,1)} %copy-done.3) | copy-start | bytes 12582916
  70.8 12.9 %collective-permute-start.14 = (bf16[64,2048]{1,0:T(8,128)(2,1)S(1)}, bf16[64,2048]{1,0:T(8,128)(2,1)S(1)}, u32[]{:S(2)}, u32[]{:S(2)}) collective-permute-start(bf16[64,2048]{1,0:T(8,128)(2,1)S(1)} %shard_map.53), channel_id=1, source_target_pairs={{0,4},{2,6},{8,12},{10,14},{16,20},{18,22},{24,28},{26,30},{1,5},{... | collective-permute-start | bytes 786440 | tf_op jit(solution)/shard_map/ppermute | solution.py:141
  77.6 8.5 %collective-permute-start.18 = (bf16[64,1024]{1,0:T(8,128)(2,1)S(1)}, bf16[64,1024]{1,0:T(8,128)(2,1)S(1)}, u32[]{:S(2)}, u32[]{:S(2)}) collective-permute-start(bf16[64,1024]{1,0:T(8,128)(2,1)S(1)} %get-tuple-element.26), channel_id=1, source_target_pairs={{0,6},{2,4},{8,14},{10,12},{16,22},{18,20},{24,30},{26,28},{1,7},{... | collective-permute-start | bytes 393224 | tf_op jit(solution)/shard_map/ppermute | solution.py:141
  78.9 7.2 %collective-permute-start.17 = (bf16[64,1024]{1,0:T(8,128)(2,1)S(1)}, bf16[64,1024]{1,0:T(8,128)(2,1)S(1)}, u32[]{:S(2)}, u32[]{:S(2)}) collective-permute-start(bf16[64,1024]{1,0:T(8,128)(2,1)S(1)} %get-tuple-element.26), channel_id=1, source_target_pairs={{0,2},{2,0},{8,10},{10,8},{16,18},{18,16},{24,26},{26,24},{1,3},{3... | collective-permute-start | bytes 393224 | tf_op jit(solution)/shard_map/ppermute | solution.py:141
  82.3 3.8 %collective-permute-start.16 = (bf16[64,1024]{1,0:T(8,128)(2,1)S(1)}, bf16[64,1024]{1,0:T(8,128)(2,1)S(1)}, u32[]{:S(2)}, u32[]{:S(2)}) collective-permute-start(bf16[64,1024]{1,0:T(8,128)(2,1)S(1)} %get-tuple-element.26), channel_id=1, source_target_pairs={{0,4},{2,6},{8,12},{10,14},{16,20},{18,22},{24,28},{26,30},{1,5},{... | collective-permute-start | bytes 393224 | tf_op jit(solution)/shard_map/ppermute | solution.py:141
  87.6 5.0 %collective-permute-start.19 = (bf16[64,1024]{1,0:T(8,128)(2,1)S(1)}, bf16[64,1024]{1,0:T(8,128)(2,1)S(1)}, u32[]{:S(2)}, u32[]{:S(2)}) collective-permute-start(bf16[64,1024]{1,0:T(8,128)(2,1)S(1)} %shard_map.55.refs_0_), channel_id=1, source_target_pairs={{0,2},{2,0},{4,6},{6,4},{8,10},{10,8},{12,14},{14,12},{16,18},{18,... | collective-permute-start | bytes 393224 | tf_op jit(solution)/shard_map/ppermute | solution.py:141

commit v4 on v3

v4 whole, which is shorter than its diff:
```python
import functools
import jax
import jax.numpy as jnp
from jax import lax
from jax.experimental import pallas as pl
from jax.experimental.pallas import tpu as pltpu
from jax.sharding import PartitionSpec as P

F32 = jnp.float32
BF16 = jnp.bfloat16


def upper_depth(leaf, top):
    return top - 1 - sum(((leaf + 1) % 2**power == 0).astype(jnp.int32) for power in range(1, top + 1))


def first_kernel(right_ref, inverse_ref, cast_ref, inverse_out, staged, semaphores):
    weights = pltpu.make_async_copy(inverse_ref.at[1], inverse_out, semaphores.at[0])
    values = pltpu.make_async_copy(right_ref.at[1], staged, semaphores.at[1])
    values.start()
    weights.start()
    values.wait()
    cast_ref[...] = staged[...].astype(BF16)
    weights.wait()


def upper_kernel(after_ref, right_ref, inverse_ref, lower_ref, right_out, lower_out, inverse_out, semaphores):
    copies = [
        pltpu.make_async_copy(lower_ref.at[1], lower_out, semaphores.at[0]),
        pltpu.make_async_copy(inverse_ref.at[0], inverse_out, semaphores.at[1]),
        pltpu.make_async_copy(right_ref, right_out, semaphores.at[2]),
    ]
    for copy in copies:
        copy.start()
    for copy in copies:
        copy.wait()


def lower_kernel(cores, after_ref, lower_ref, *refs):
    sources = [lower_ref.at[0], *refs[:cores]]
    targets = refs[cores:2 * cores + 1]
    semaphores = refs[2 * cores + 1]
    copies = [pltpu.make_async_copy(a, b, semaphores.at[i]) for i, (a, b) in enumerate(zip(sources, targets))]
    for copy in copies:
        copy.start()
    for copy in copies:
        copy.wait()


def place_pieces(piece_refs, target_ref, parts):
    rows = len(piece_refs)
    width = piece_refs[0].shape[1] // parts
    own = lax.axis_index("rows")
    first = target_ref.shape[1] // (rows * width) - parts
    for shift, piece_ref in enumerate(piece_refs):
        source = lax.rem(own - shift + rows, rows)
        for part in range(parts):
            column = (first + part) * rows * width + source * width
            from_column = (parts - 1 - part) * width
            target_ref[:, pl.ds(pl.multiple_of(column, width), width)] = piece_ref[:, from_column:from_column + width]


def place_either(choose, first_refs, second_refs, target_ref, parts):
    @pl.when(choose)
    def _():
        place_pieces(first_refs, target_ref, parts)

    @pl.when(jnp.logical_not(choose))
    def _():
        place_pieces(second_refs, target_ref, parts)


def offset_kernel(top, level, rows, block_rows_ref, right_ref, lower_ref, *refs):
    leaf = lax.axis_index("leaf")
    slot = 0 if level == top else 1
    first_refs, second_refs = refs[:rows], refs[rows:2 * rows]
    rest = refs[2 * rows:]
    width = right_ref.shape[2]
    numbers, semaphore, picked = rest[-3:]
    fetch = pltpu.make_async_copy(block_rows_ref, numbers, semaphore)
    fetch.start()
    if level == top:
        mine_ref, passed_ref, reduced_ref, joined = rest[:4]
        even = leaf % 2 == 0
        older = mine_ref.shape[1]

        @pl.when(even)
        def _():
            joined[:, :older] = mine_ref[...]

        @pl.when(jnp.logical_not(even))
        def _():
            joined[:, :older] = passed_ref[...]

        place_either(even, first_refs, second_refs, joined, 1)
    else:
        reduced_ref, joined = rest[:2]
        reach = 2 ** (top - level - 1)
        place_either(((leaf + 1) // reach) % 4 == 1, first_refs, second_refs, joined, level)
    blocks, block_width = lower_ref.shape[:2]
    highest = joined.shape[1] // block_width - 1
    fetch.wait()
    for index in range(blocks):
        number = jnp.clip(numbers[slot, index], 0, highest)
        column = pl.multiple_of(number * block_width, block_width)
        picked[:, index * block_width:(index + 1) * block_width] = joined[:, pl.ds(column, block_width)]
    weights = lower_ref[...].reshape(blocks * block_width, width)
    offset = jnp.dot(picked[...], weights, preferred_element_type=F32)
    reduced_ref[...] = (right_ref[slot] - offset).astype(BF16)


def apply_inverse(cores, piece_refs, inverse_refs, joined, store):
    quarter = inverse_refs[0].shape[-1]
    place_pieces(piece_refs, joined, 1)
    own = lax.axis_index("rhs")
    for turn, inverse_ref in enumerate(inverse_refs):
        total = jnp.dot(joined[...], inverse_ref[...], preferred_element_type=F32)
        core = lax.rem(own - turn + cores, cores)
        store(pl.ds(pl.multiple_of(core * quarter, quarter), quarter), total)


def solve_kernel(top, depth, rows, cores, carried, *refs):
    piece_refs = refs[:rows]
    inverse_refs = refs[rows:rows + cores]
    rest = list(refs[rows + cores:])
    joined = rest.pop()
    before_ref = rest.pop(0) if depth > 0 else None
    first_refs = [rest.pop(0) for _ in range(2 if carried else 0)]
    rounded_ref, solved_ref = rest
    width = piece_refs[0].shape[1]
    leaf = lax.axis_index("leaf")
    active = upper_depth(leaf, top) == depth
    if carried:
        reach = 2 ** (top - depth - 1)
        is_left = ((leaf + 1) // reach) % 4 == 1
        for wanted, ref in zip((is_left, jnp.logical_not(is_left)), first_refs):
            @pl.when(wanted)
            def _():
                rounded_ref[:, width:] = ref[...]

    def store(columns, total):
        rounded_ref[:, columns] = total.astype(BF16)
        before = jnp.zeros_like(total) if before_ref is None else before_ref[:, columns]
        solved_ref[:, columns] = jnp.where(active, total, before)

    apply_inverse(cores, piece_refs, inverse_refs, joined, store)


def last_kernel(rows, cores, *refs):
    piece_refs = refs[:rows]
    inverse_refs = refs[rows:rows + cores]
    before_ref, out_ref, joined = refs[rows + cores:]
    out_ref[1] = before_ref[...]

    def store(columns, total):
        out_ref[0, :, columns] = total

    apply_inverse(cores, piece_refs, inverse_refs, joined, store)


WHOLE = pl.BlockSpec(memory_space=pltpu.VMEM)
FAR = pl.BlockSpec(memory_space=pltpu.HBM)


def call(kernel, near, far, outs, scratch=(), flops=0):
    several = len(outs) > 1
    size = sum(a.size * a.dtype.itemsize for a in [*near, *far])
    near = [pltpu.with_memory_space_constraint(a, pltpu.VMEM) for a in near]
    far = [pltpu.with_memory_space_constraint(a, pltpu.HBM) for a in far]
    specs = [FAR if getattr(o, "memory_space", None) == pltpu.HBM else WHOLE for o in outs]
    return pl.pallas_call(
        kernel,
        in_specs=[WHOLE] * len(near) + [FAR] * len(far),
        out_specs=specs if several else specs[0],
        out_shape=list(outs) if several else outs[0],
        scratch_shapes=list(scratch),
        cost_estimate=pl.CostEstimate(flops=flops, bytes_accessed=size, transcendentals=0),
        compiler_params=pltpu.CompilerParams(vmem_limit_bytes=8 * 2**20),
    )(*near, *far)


def local(right_side, inverse_diag, lower_blocks, block_rows):
    leafs, rows, cores = (lax.axis_size(name) for name in ("leaf", "rows", "rhs"))
    top = leafs.bit_length() - 1
    count, width = right_side.shape[1:]
    full_width = rows * width
    places = ("leaf", "rows")

    def send(value, hops, shift):
        pairs = [(a * rows + r, b * rows + (r + shift) % rows) for a, b in hops for r in range(rows)]
        return lax.ppermute(value, places, pairs)

    def spread(value, hops):
        return [send(value, hops, shift) for shift in range(rows)]

    def rows_of(value, holders):
        return [value] + [send(value, [(h, h) for h in holders], shift) for shift in range(1, rows)]

    def core_columns(own):
        turns = range(1, cores)
        return [own] + [lax.ppermute(own, "rhs", [(c, (c + t) % cores) for c in range(cores)]) for t in turns]

    def holders(depth):
        return [(2 * p + 1) * 2 ** (top - depth - 1) - 1 for p in range(2**depth)]

    near = pltpu.VMEM
    half = near((count, width), BF16)
    half_f32 = near((count, width), F32)
    square = near(inverse_diag.shape[1:], BF16)
    lower = near(lower_blocks.shape[1:], BF16)
    joined = near((count, full_width), BF16)
    work = 2 * count * full_width * width
    semaphores = lambda n: pltpu.SemaphoreType.DMA((n,))

    reduced, inverse_upper = call(
        first_kernel, [], [right_side, inverse_diag], [half, square], [near((count, width), F32), semaphores(2)])
    gathered = rows_of(reduced, holders(0))
    inverse_upper = core_columns(inverse_upper)
    right, lower_upper, inverse_own = call(
        upper_kernel, [reduced], [right_side, inverse_diag, lower_blocks],
        [near(right_side.shape, F32), lower, pltpu.HBM(square.shape, BF16)], [semaphores(3)])
    inverse_lower = core_columns(inverse_own)
    solved = None
    lower_now = lower_upper
    for depth in range(top + 1):
        if depth > 0:
            all_joined = near((count, depth * full_width), BF16)
            fetched = [pltpu.SMEM(block_rows.shape, jnp.int32), pltpu.SemaphoreType.DMA(()), joined]
            kernel = functools.partial(offset_kernel, top, depth, rows)
            if depth == top:
                reduced = call(kernel, [block_rows, right, lower_now, *lefts, *rights, mine, passed], [],
                               [half], [all_joined, *fetched], work)
            elif depth == top - 1:
                reduced, mine = call(kernel, [block_rows, right, lower_now, *lefts, *rights], [],
                                     [half, all_joined], fetched, work)
                passed = send(mine, [(h, h + 1) for h in holders(depth)], 0)
            else:
                reduced = call(kernel, [block_rows, right, lower_now, *lefts, *rights], [],
                               [half], [all_joined, *fetched], work)
            gathered = rows_of(reduced, range(leafs) if depth == top else holders(depth))
        if depth == top:
            return call(functools.partial(last_kernel, rows, cores), [*gathered, *inverse_lower, solved], [],
                        [jax.ShapeDtypeStruct(right_side.shape, F32)], [joined], work)
        here = holders(depth)
        carried = depth > 0 and depth + 1 < top
        parts = depth + 1 if carried else 1
        kernel = functools.partial(solve_kernel, top, depth, rows, cores, carried)
        arrays = [*gathered, *inverse_upper] + ([solved] if depth else []) + ([lefts[0], rights[0]] if carried else [])
        rounded, solved = call(kernel, arrays, [], [near((count, parts * width), BF16), half_f32], [joined], work)
        if depth + 1 < top:
            reach = 2 ** (top - depth - 2)
            lefts = spread(rounded, [(h, h - reach) for h in here])
            rights = spread(rounded, [(h, h + reach) for h in here])
        else:
            lefts = rows_of(rounded, here)
            rights = spread(rounded, [(h, h + 1) for h in here])
            lower_now, *inverse_lower = call(
                functools.partial(lower_kernel, cores), [rounded], [lower_blocks, *inverse_lower],
                [lower] + [square] * cores, [semaphores(cores + 1)])


def solution(mesh):
    return jax.shard_map(
        local,
        mesh=mesh,
        in_specs=(
            P("leaf", "rhs", "rows"),
            P("leaf", None, ("rows", "rhs")),
            P("leaf", None, None, "rows"),
            P("leaf", None),
        ),
        out_specs=P("leaf", "rhs", "rows"),
        check_vma=False,
    )
```

time: 97 us -> 139 us (1.43)
  Pallas kernels: 24.1 us -> 78.5 us
  starting transfers between devices: 27.1 us -> 19.9 us
  local copies, waits for them, and re-layouts: 6.17 us -> 1.3 us
  waiting for transfers between devices: 37.4 us -> 38.8 us
    pallas_call x11 -> x10, Pallas kernels: 24.1 us -> 78.5 us  [call(): pl.pallas_call(kernel, in_specs=[WHOLE] * len(near) + [FAR] * len(far), o...]
    ppermute x19 -> x16, starting transfers between devices: 26.1 us -> 19.3 us  [send(): return lax.ppermute(value, places, pairs)]
    unnamed x12 -> x4, local copies, waits for them, and re-layouts: 6.17 us -> 1.3 us
    ppermute x19 -> x16, waiting for transfers between devices: 34.3 us -> 38.8 us  [send(): return lax.ppermute(value, places, pairs)]
    ppermute x2, waiting for transfers between devices: 3.14 us -> 0.01 us  [core_columns(): lax.ppermute(own, 'rhs', [(c, (c + t) % cores) for c in range(cores)])]
  transfers between devices with their start and end apart: 21 -> 18, of which waited for: 6 -> 4; matrix products, arithmetic and copies ran while one was open for 1% -> 0% of each run, Pallas kernels for 15% -> 53%
where the time goes in v4:
time: 139 us
  Pallas kernels  78.5 us (56%)
  waiting for transfers between devices  38.8 us (28%)
  starting transfers between devices  19.9 us (14%)
    pallas_call x10, Pallas kernels, call(): pl.pallas_call(kernel, in_specs=[WHOLE] * len(near) + [FAR] * len(far), o...  78.5 us
    ppermute x16, waiting for transfers between devices, send(): return lax.ppermute(value, places, pairs)  38.8 us
    ppermute x16, starting transfers between devices, send(): return lax.ppermute(value, places, pairs)  19.3 us
  transfers between devices with their start and end apart: 18, of which 4 were waited for; matrix products, arithmetic and copies ran while one was open for 0% of the time, Pallas kernels for 53%

profile of v4, /device:TPU:0, one launch (start us, length us, event | category | flops | bytes accessed | tf_op | source)
XLA Modules:
  0.0 138.8 jit_solution(13174966562856924132)
XLA Ops:
  0.0 1.7 %shard_map.46 = (bf16[64,1024]{1,0:T(8,128)(2,1)S(1)}, bf16[2048,512]{1,0:T(8,128)(2,1)S(1)}) custom-call(f32[2,64,1024]{2,1,0:T(8,128)} %right_ref.3, bf16[2,2048,512]{2,1,0:T(8,128)(2,1)} %inverse_ref.3), custom_call_target="tpu_custom_call" | custom-call | bytes 4718592 | tf_op jit(solution)/shard_map/pallas_call | solution.py:171
  1.7 0.5 collective-permute-start.1
  2.2 64.7 %shard_map.47 = (f32[2,64,1024]{2,1,0:T(8,128)S(1)}, bf16[16,128,1024]{2,1,0:T(8,128)(2,1)S(1)}, bf16[2048,512]{1,0:T(8,128)(2,1)}) custom-call(bf16[64,1024]{1,0:T(8,128)(2,1)S(1)} %get-tuple-element.21.after_ref.refs_0_, f32[2,64,1024]{2,1,0:T(8,128)} %right_ref.3, bf16[2,2048,512]{2,1,0:T(8,128)(2,1)} %inverse_ref.3, bf16[2,16,128,1024]{3,2,1,0:T(8,128)(2,1)} %lower_ref.3), custom_call_target="tpu_custom_call" | custom-call | bytes 13238272 | tf_op jit(solution)/shard_map/pallas_call | solution.py:171
  66.9 0.0 copy-start
  66.9 0.1 collective-permute-start.12
  67.0 0.7 collective-permute-start
  67.7 0.0 collective-permute-done.refs_1_
  67.7 0.0 collective-permute-done.1.refs_3_
  67.7 0.9 shard_map.48
  68.6 0.7 collective-permute-start.2
  69.3 0.7 collective-permute-start.4
  69.9 0.7 collective-permute-start.3
  70.6 0.7 collective-permute-start.5
  71.3 0.0 collective-permute-done.2.refs_0_.refs_5_
  71.3 0.0 collective-permute-done.4.refs_2_.refs_6_
  71.3 0.0 collective-permute-done.3.refs_1_
  71.3 0.0 collective-permute-done.5.refs_3_
  71.4 1.4 %shard_map.49.refs_0_ = bf16[64,1024]{1,0:T(8,128)(2,1)S(1)} custom-call(s32[2,16]{1,0:T(2,128)S(1)} %copy-done, f32[2,64,1024]{2,1,0:T(8,128)S(1)} %get-tuple-element.22.right_ref, bf16[16,128,1024]{2,1,0:T(8,128)(2,1)S(1)} %get-tuple-element.23.lower_ref, bf16[64,1024]{1,0:T(8,128)(2,1)S(1)} %collective-permute-done.2.refs_0_.refs_5_, ...), custom_call_target="tpu_custom_call" | custom-call | flops 268435456 | bytes 5243008 | tf_op jit(solution)/shard_map/pallas_call | solution.py:171
  72.8 0.7 collective-permute-start.6
  73.5 0.0 collective-permute-done.6.refs_1_
  73.5 0.9 shard_map.50
  74.4 0.7 collective-permute-start.10
  75.1 1.3 collective-permute-start.7
  76.4 1.3 collective-permute-start.8
  77.7 0.7 collective-permute-start.9
  78.4 0.0 collective-permute-done.10.refs_3_
  78.4 28.1 %collective-permute-done.7.refs_0_ = bf16[64,2048]{1,0:T(8,128)(2,1)S(1)} collective-permute-done((bf16[64,2048]{1,0:T(8,128)(2,1)S(1)}, bf16[64,2048]{1,0:T(8,128)(2,1)S(1)}, u32[]{:S(2)}, u32[]{:S(2)}) %collective-permute-start.7) | collective-permute-done | bytes 262176 | tf_op jit(solution)/shard_map/ppermute | solution.py:191
  106.5 2.7 %collective-permute-done.8.refs_1_ = bf16[64,2048]{1,0:T(8,128)(2,1)S(1)} collective-permute-done((bf16[64,2048]{1,0:T(8,128)(2,1)S(1)}, bf16[64,2048]{1,0:T(8,128)(2,1)S(1)}, u32[]{:S(2)}, u32[]{:S(2)}) %collective-permute-start.8) | collective-permute-done | bytes 262176 | tf_op jit(solution)/shard_map/ppermute | solution.py:191
  109.2 0.0 collective-permute-done.9.refs_2_
  109.2 1.4 %shard_map.51 = (bf16[64,1024]{1,0:T(8,128)(2,1)S(1)}, bf16[64,4096]{1,0:T(8,128)(2,1)S(1)}) custom-call(s32[2,16]{1,0:T(2,128)S(1)} %copy-done, f32[2,64,1024]{2,1,0:T(8,128)S(1)} %get-tuple-element.22.right_ref, bf16[16,128,1024]{2,1,0:T(8,128)(2,1)S(1)} %get-tuple-element.23.lower_ref, bf16[64,2048]{1,0:T(8,128)(2,1)S(1)} %collective-permute-done.7.refs_0_, ...), custom_call_target="tpu_custom_call" | custom-call | flops 268435456 | bytes 5767296 | tf_op jit(solution)/shard_map/pallas_call | solution.py:171
  110.7 1.5 %collective-permute-start.16 = (bf16[64,4096]{1,0:T(8,128)(2,1)S(1)}, bf16[64,4096]{1,0:T(8,128)(2,1)S(1)}, u32[]{:S(2)}, u32[]{:S(2)}) collective-permute-start(bf16[64,4096]{1,0:T(8,128)(2,1)S(1)} %get-tuple-element.33.refs_4_), channel_id=1, source_target_pairs={{0,4},{2,6},{8,12},{10,14},{16,20},{18,22},{24,28},{26,30},{1,5},{... | collective-permute-start | bytes 1572872 | tf_op jit(solution)/shard_map/ppermute | solution.py:191
  112.2 3.2 %collective-permute-start.11 = (bf16[64,1024]{1,0:T(8,128)(2,1)S(1)}, bf16[64,1024]{1,0:T(8,128)(2,1)S(1)}, u32[]{:S(2)}, u32[]{:S(2)}) collective-permute-start(bf16[64,1024]{1,0:T(8,128)(2,1)S(1)} %get-tuple-element.28.refs_0_), channel_id=1, source_target_pairs={{0,2},{2,0},{8,10},{10,8},{16,18},{18,16},{24,26},{26,24},{1,3},{3... | collective-permute-start | bytes 393224 | tf_op jit(solution)/shard_map/ppermute | solution.py:191
  115.4 3.6 %collective-permute-done.11.refs_1_ = bf16[64,1024]{1,0:T(8,128)(2,1)S(1)} collective-permute-done((bf16[64,1024]{1,0:T(8,128)(2,1)S(1)}, bf16[64,1024]{1,0:T(8,128)(2,1)S(1)}, u32[]{:S(2)}, u32[]{:S(2)}) %collective-permute-start.11) | collective-permute-done | bytes 131104 | tf_op jit(solution)/shard_map/ppermute | solution.py:191
  119.1 0.9 shard_map.52
  119.9 3.2 %collective-permute-start.13 = (bf16[64,1024]{1,0:T(8,128)(2,1)S(1)}, bf16[64,1024]{1,0:T(8,128)(2,1)S(1)}, u32[]{:S(2)}, u32[]{:S(2)}) collective-permute-start(bf16[64,1024]{1,0:T(8,128)(2,1)S(1)} %get-tuple-element.30.after_ref.refs_0_), channel_id=1, source_target_pairs={{0,2},{2,0},{8,10},{10,8},{16,18},{18,16},{24,26},{26,24},{1,3},{3... | collective-permute-start | bytes 393224 | tf_op jit(solution)/shard_map/ppermute | solution.py:191
  123.2 1.3 collective-permute-start.14
  124.5 1.3 collective-permute-start.15
  125.8 0.0 collective-permute-done.12.refs_1_
  125.8 1.3 copy-done.1
  127.1 3.5 %shard_map.53 = (bf16[16,128,1024]{2,1,0:T(8,128)(2,1)S(1)}, bf16[2048,512]{1,0:T(8,128)(2,1)S(1)}, bf16[2048,512]{1,0:T(8,128)(2,1)S(1)}) custom-call(bf16[64,1024]{1,0:T(8,128)(2,1)S(1)} %get-tuple-element.30.after_ref.refs_0_, bf16[2,16,128,1024]{3,2,1,0:T(8,128)(2,1)} %lower_ref.3, bf16[2048,512]{1,0:T(8,128)(2,1)} %get-tuple-element.31.refs_0_, ...), custom_call_target="tpu_custom_call" | custom-call | bytes 12713984 | tf_op jit(solution)/shard_map/pallas_call | solution.py:171
  130.6 0.0 collective-permute-done.13.refs_1_
  130.6 0.0 collective-permute-done.14.refs_2_
  130.6 0.0 collective-permute-done.15.refs_3_
  130.6 0.0 collective-permute-done.16.refs_5_
  130.6 1.4 %shard_map.54.refs_0_ = bf16[64,1024]{1,0:T(8,128)(2,1)S(1)} custom-call(s32[2,16]{1,0:T(2,128)S(1)} %copy-done, f32[2,64,1024]{2,1,0:T(8,128)S(1)} %get-tuple-element.22.right_ref, bf16[16,128,1024]{2,1,0:T(8,128)(2,1)S(1)} %get-tuple-element.32.lower_ref, bf16[64,1024]{1,0:T(8,128)(2,1)S(1)} %get-tuple-element.30.after_ref.refs_0_, ...), custom_call_target="tpu_custom_call" | custom-call | flops 268435456 | bytes 6291584 | tf_op jit(solution)/shard_map/pallas_call | solution.py:171
  132.1 0.8 collective-permute-start.17
  132.8 4.2 %collective-permute-done.17.refs_1_ = bf16[64,1024]{1,0:T(8,128)(2,1)S(1)} collective-permute-done((bf16[64,1024]{1,0:T(8,128)(2,1)S(1)}, bf16[64,1024]{1,0:T(8,128)(2,1)S(1)}, u32[]{:S(2)}, u32[]{:S(2)}) %collective-permute-start.17) | collective-permute-done | bytes 131104 | tf_op jit(solution)/shard_map/ppermute | solution.py:191
  137.1 1.7 %shard_map.55 = f32[2,64,1024]{2,1,0:T(8,128)} custom-call(bf16[64,1024]{1,0:T(8,128)(2,1)S(1)} %shard_map.54.refs_0_, bf16[64,1024]{1,0:T(8,128)(2,1)S(1)} %collective-permute-done.17.refs_1_, bf16[2048,512]{1,0:T(8,128)(2,1)S(1)} %get-tuple-element.34.refs_2_, bf16[2048,512]{1,0:T(8,128)(2,1)S(1)} %get-tuple-element.35.refs_3_, ...), custom_call_target="tpu_custom_call" | custom-call | flops 268435456 | bytes 4718592 | tf_op jit(solution)/shard_map/pallas_call | solution.py:171
  (2 shorter events, 0.0 us)
Async XLA Ops:
  1.7 66.0 %collective-permute-start.1 = (bf16[2048,512]{1,0:T(8,128)(2,1)S(1)}, bf16[2048,512]{1,0:T(8,128)(2,1)S(1)}, u32[]{:S(2)}, u32[]{:S(2)}) collective-permute-start(bf16[2048,512]{1,0:T(8,128)(2,1)S(1)} %get-tuple-element.24.refs_2_), channel_id=1, source_target_pairs={{0,1},{1,0},{2,3},{3,2},{4,5},{5,4},{6,7},{7,6},{8,9},{9,8},{10,11... | collective-permute-start | bytes 6291464 | tf_op jit(solution)/shard_map/ppermute | solution.py:201
  66.9 4.4 %copy-start = (s32[2,16]{1,0:T(2,128)S(1)}, s32[2,16]{1,0:T(2,128)}, u32[]{:S(2)}) copy-start(s32[2,16]{1,0:T(2,128)} %block_rows_ref.5) | copy-start | bytes 388
  66.9 58.9 %collective-permute-start.12 = (bf16[2048,512]{1,0:T(8,128)(2,1)}, bf16[2048,512]{1,0:T(8,128)(2,1)S(1)}, u32[]{:S(2)}, u32[]{:S(2)}) collective-permute-start(bf16[2048,512]{1,0:T(8,128)(2,1)} %get-tuple-element.31.refs_0_), channel_id=1, source_target_pairs={{0,1},{1,0},{2,3},{3,2},{4,5},{5,4},{6,7},{7,6},{8,9},{9,8},{10,11... | collective-permute-start | bytes 6291464 | tf_op jit(solution)/shard_map/ppermute | solution.py:201
  67.0 0.7 collective-permute-start
  68.6 2.7 %collective-permute-start.2 = (bf16[64,1024]{1,0:T(8,128)(2,1)S(1)}, bf16[64,1024]{1,0:T(8,128)(2,1)S(1)}, u32[]{:S(2)}, u32[]{:S(2)}) collective-permute-start(bf16[64,1024]{1,0:T(8,128)(2,1)S(1)} %get-tuple-element.25), channel_id=1, source_target_pairs={{12,4},{14,6},{13,5},{15,7}} | collective-permute-start | bytes 393224 | tf_op jit(solution)/shard_map/ppermute | solution.py:191
  69.3 2.0 %collective-permute-start.4 = (bf16[64,1024]{1,0:T(8,128)(2,1)S(1)}, bf16[64,1024]{1,0:T(8,128)(2,1)S(1)}, u32[]{:S(2)}, u32[]{:S(2)}) collective-permute-start(bf16[64,1024]{1,0:T(8,128)(2,1)S(1)} %get-tuple-element.25), channel_id=1, source_target_pairs={{12,20},{14,22},{13,21},{15,23}} | collective-permute-start | bytes 393224 | tf_op jit(solution)/shard_map/ppermute | solution.py:191
  69.9 1.4 collective-permute-start.3
  70.6 0.7 collective-permute-start.5
  72.8 0.7 collective-permute-start.6
  74.4 4.0 %collective-permute-start.10 = (bf16[64,2048]{1,0:T(8,128)(2,1)S(1)}, bf16[64,2048]{1,0:T(8,128)(2,1)S(1)}, u32[]{:S(2)}, u32[]{:S(2)}) collective-permute-start(bf16[64,2048]{1,0:T(8,128)(2,1)S(1)} %get-tuple-element.27), channel_id=1, source_target_pairs={{4,10},{6,8},{20,26},{22,24},{5,11},{7,9},{21,27},{23,25}} | collective-permute-start | bytes 786440 | tf_op jit(solution)/shard_map/ppermute | solution.py:191
  75.1 31.4 %collective-permute-start.7 = (bf16[64,2048]{1,0:T(8,128)(2,1)S(1)}, bf16[64,2048]{1,0:T(8,128)(2,1)S(1)}, u32[]{:S(2)}, u32[]{:S(2)}) collective-permute-start(bf16[64,2048]{1,0:T(8,128)(2,1)S(1)} %get-tuple-element.27), channel_id=1, source_target_pairs={{4,0},{6,2},{20,16},{22,18},{5,1},{7,3},{21,17},{23,19}} | collective-permute-start | bytes 786440 | tf_op jit(solution)/shard_map/ppermute | solution.py:191
  76.4 32.8 %collective-permute-start.8 = (bf16[64,2048]{1,0:T(8,128)(2,1)S(1)}, bf16[64,2048]{1,0:T(8,128)(2,1)S(1)}, u32[]{:S(2)}, u32[]{:S(2)}) collective-permute-start(bf16[64,2048]{1,0:T(8,128)(2,1)S(1)} %get-tuple-element.27), channel_id=1, source_target_pairs={{4,2},{6,0},{20,18},{22,16},{5,3},{7,1},{21,19},{23,17}} | collective-permute-start | bytes 786440 | tf_op jit(solution)/shard_map/ppermute | solution.py:191
  77.7 31.5 %collective-permute-start.9 = (bf16[64,2048]{1,0:T(8,128)(2,1)S(1)}, bf16[64,2048]{1,0:T(8,128)(2,1)S(1)}, u32[]{:S(2)}, u32[]{:S(2)}) collective-permute-start(bf16[64,2048]{1,0:T(8,128)(2,1)S(1)} %get-tuple-element.27), channel_id=1, source_target_pairs={{4,8},{6,10},{20,24},{22,26},{5,9},{7,11},{21,25},{23,27}} | collective-permute-start | bytes 786440 | tf_op jit(solution)/shard_map/ppermute | solution.py:191
  110.7 20.0 %collective-permute-start.16 = (bf16[64,4096]{1,0:T(8,128)(2,1)S(1)}, bf16[64,4096]{1,0:T(8,128)(2,1)S(1)}, u32[]{:S(2)}, u32[]{:S(2)}) collective-permute-start(bf16[64,4096]{1,0:T(8,128)(2,1)S(1)} %get-tuple-element.33.refs_4_), channel_id=1, source_target_pairs={{0,4},{2,6},{8,12},{10,14},{16,20},{18,22},{24,28},{26,30},{1,5},{... | collective-permute-start | bytes 1572872 | tf_op jit(solution)/shard_map/ppermute | solution.py:191
  112.2 6.9 %collective-permute-start.11 = (bf16[64,1024]{1,0:T(8,128)(2,1)S(1)}, bf16[64,1024]{1,0:T(8,128)(2,1)S(1)}, u32[]{:S(2)}, u32[]{:S(2)}) collective-permute-start(bf16[64,1024]{1,0:T(8,128)(2,1)S(1)} %get-tuple-element.28.refs_0_), channel_id=1, source_target_pairs={{0,2},{2,0},{8,10},{10,8},{16,18},{18,16},{24,26},{26,24},{1,3},{3... | collective-permute-start | bytes 393224 | tf_op jit(solution)/shard_map/ppermute | solution.py:191
  119.9 10.7 %collective-permute-start.13 = (bf16[64,1024]{1,0:T(8,128)(2,1)S(1)}, bf16[64,1024]{1,0:T(8,128)(2,1)S(1)}, u32[]{:S(2)}, u32[]{:S(2)}) collective-permute-start(bf16[64,1024]{1,0:T(8,128)(2,1)S(1)} %get-tuple-element.30.after_ref.refs_0_), channel_id=1, source_target_pairs={{0,2},{2,0},{8,10},{10,8},{16,18},{18,16},{24,26},{26,24},{1,3},{3... | collective-permute-start | bytes 393224 | tf_op jit(solution)/shard_map/ppermute | solution.py:191
  123.2 7.4 %collective-permute-start.14 = (bf16[64,1024]{1,0:T(8,128)(2,1)S(1)}, bf16[64,1024]{1,0:T(8,128)(2,1)S(1)}, u32[]{:S(2)}, u32[]{:S(2)}) collective-permute-start(bf16[64,1024]{1,0:T(8,128)(2,1)S(1)} %get-tuple-element.30.after_ref.refs_0_), channel_id=1, source_target_pairs={{0,4},{2,6},{8,12},{10,14},{16,20},{18,22},{24,28},{26,30},{1,5},{... | collective-permute-start | bytes 393224 | tf_op jit(solution)/shard_map/ppermute | solution.py:191
  124.5 6.1 %collective-permute-start.15 = (bf16[64,1024]{1,0:T(8,128)(2,1)S(1)}, bf16[64,1024]{1,0:T(8,128)(2,1)S(1)}, u32[]{:S(2)}, u32[]{:S(2)}) collective-permute-start(bf16[64,1024]{1,0:T(8,128)(2,1)S(1)} %get-tuple-element.30.after_ref.refs_0_), channel_id=1, source_target_pairs={{0,6},{2,4},{8,14},{10,12},{16,22},{18,20},{24,30},{26,28},{1,7},{... | collective-permute-start | bytes 393224 | tf_op jit(solution)/shard_map/ppermute | solution.py:191
  125.8 1.3 copy-start.1
  132.1 5.0 %collective-permute-start.17 = (bf16[64,1024]{1,0:T(8,128)(2,1)S(1)}, bf16[64,1024]{1,0:T(8,128)(2,1)S(1)}, u32[]{:S(2)}, u32[]{:S(2)}) collective-permute-start(bf16[64,1024]{1,0:T(8,128)(2,1)S(1)} %shard_map.54.refs_0_), channel_id=1, source_target_pairs={{0,2},{2,0},{4,6},{6,4},{8,10},{10,8},{12,14},{14,12},{16,18},{18,... | collective-permute-start | bytes 393224 | tf_op jit(solution)/shard_map/ppermute | solution.py:191

commit v5 on v4

v5 whole, which is shorter than its diff:
```python
import functools
import jax
import jax.numpy as jnp
from jax import lax
from jax.experimental import pallas as pl
from jax.experimental.pallas import tpu as pltpu
from jax.sharding import PartitionSpec as P

F32 = jnp.float32
BF16 = jnp.bfloat16


def upper_depth(leaf, top):
    return top - 1 - sum(((leaf + 1) % 2**power == 0).astype(jnp.int32) for power in range(1, top + 1))


def first_kernel(right_ref, inverse_ref, cast_ref, inverse_out, staged, semaphores):
    weights = pltpu.make_async_copy(inverse_ref.at[1], inverse_out, semaphores.at[0])
    values = pltpu.make_async_copy(right_ref.at[1], staged, semaphores.at[1])
    values.start()
    weights.start()
    values.wait()
    cast_ref[...] = staged[...].astype(BF16)
    weights.wait()


def load_kernel(after_ref, right_ref, inverse_ref, lower_ref, *refs):
    semaphores = refs[-1]
    sources = [lower_ref.at[1], right_ref, inverse_ref.at[0], lower_ref.at[0]]
    copies = [pltpu.make_async_copy(a, b, semaphores.at[i]) for i, (a, b) in enumerate(zip(sources, refs[:-1]))]
    for copy in copies:
        copy.start()
    for copy in copies:
        copy.wait()


def place_pieces(piece_refs, target_ref, start):
    rows = len(piece_refs)
    width = piece_refs[0].shape[1]
    own = lax.axis_index("rows")
    for shift, piece_ref in enumerate(piece_refs):
        source = lax.rem(own - shift + rows, rows)
        target_ref[:, pl.ds(pl.multiple_of(start + source * width, width), width)] = piece_ref[...]


def offset_kernel(top, level, rows, block_rows_ref, right_ref, lower_ref, *refs):
    leaf = lax.axis_index("leaf")
    slot = 0 if level == top else 1
    pieces = [refs[:rows], refs[rows:2 * rows]]
    older = 2 if level > 1 else 0
    older_refs = refs[2 * rows:2 * rows + older]
    reduced_ref, joined, numbers, semaphore, picked = refs[-5:]
    width = right_ref.shape[2]
    fetch = pltpu.make_async_copy(block_rows_ref, numbers, semaphore)
    fetch.start()
    reach = 2 ** (top - level - 1) if level < top else 1
    first = leaf % 2 == 0 if level == top else ((leaf + 1) // reach) % 4 == 1
    before = (level - 1) * rows * width
    for which, wanted in enumerate((first, jnp.logical_not(first))):
        @pl.when(wanted)
        def _():
            if older:
                joined[:, :before] = older_refs[which][...]
            place_pieces(pieces[which], joined, before)
    blocks, block_width = lower_ref.shape[:2]
    highest = joined.shape[1] // block_width - 1
    fetch.wait()
    for index in range(blocks):
        number = jnp.clip(numbers[slot, index], 0, highest)
        column = pl.multiple_of(number * block_width, block_width)
        picked[:, index * block_width:(index + 1) * block_width] = joined[:, pl.ds(column, block_width)]
    weights = lower_ref[...].reshape(blocks * block_width, width)
    offset = jnp.dot(picked[...], weights, preferred_element_type=F32)
    reduced_ref[...] = (right_ref[slot] - offset).astype(BF16)


def apply_inverse(cores, piece_refs, inverse_refs, joined, store):
    quarter = inverse_refs[0].shape[-1]
    place_pieces(piece_refs, joined, 0)
    own = lax.axis_index("rhs")
    for turn, inverse_ref in enumerate(inverse_refs):
        total = jnp.dot(joined[...], inverse_ref[...], preferred_element_type=F32)
        core = lax.rem(own - turn + cores, cores)
        store(pl.ds(pl.multiple_of(core * quarter, quarter), quarter), total)


def solve_kernel(top, depth, rows, cores, *refs):
    piece_refs = refs[:rows]
    inverse_refs = refs[rows:rows + cores]
    before_ref = refs[rows + cores] if depth > 0 else None
    rounded_ref, solved_ref, joined = refs[-3:]
    active = upper_depth(lax.axis_index("leaf"), top) == depth

    def store(columns, total):
        rounded_ref[:, columns] = total.astype(BF16)
        before = jnp.zeros_like(total) if before_ref is None else before_ref[:, columns]
        solved_ref[:, columns] = jnp.where(active, total, before)

    apply_inverse(cores, piece_refs, inverse_refs, joined, store)


def last_kernel(rows, cores, *refs):
    piece_refs = refs[:rows]
    inverse_refs = refs[rows:rows + cores]
    before_ref, out_ref, joined = refs[rows + cores:]
    out_ref[1] = before_ref[...]

    def store(columns, total):
        out_ref[0, :, columns] = total

    apply_inverse(cores, piece_refs, inverse_refs, joined, store)


WHOLE = pl.BlockSpec(memory_space=pltpu.VMEM)
FAR = pl.BlockSpec(memory_space=pltpu.HBM)


def call(kernel, near, far, outs, scratch=(), flops=0):
    several = len(outs) > 1
    size = sum(a.size * a.dtype.itemsize for a in [*near, *far])
    near = [pltpu.with_memory_space_constraint(a, pltpu.VMEM) for a in near]
    far = [pltpu.with_memory_space_constraint(a, pltpu.HBM) for a in far]
    specs = [FAR if getattr(o, "memory_space", None) == pltpu.HBM else WHOLE for o in outs]
    return pl.pallas_call(
        kernel,
        in_specs=[WHOLE] * len(near) + [FAR] * len(far),
        out_specs=specs if several else specs[0],
        out_shape=list(outs) if several else outs[0],
        scratch_shapes=list(scratch),
        cost_estimate=pl.CostEstimate(flops=flops, bytes_accessed=size, transcendentals=0),
        compiler_params=pltpu.CompilerParams(vmem_limit_bytes=8 * 2**20),
    )(*near, *far)


def local(right_side, inverse_diag, lower_blocks, block_rows):
    leafs, rows, cores = (lax.axis_size(name) for name in ("leaf", "rows", "rhs"))
    top = leafs.bit_length() - 1
    count, width = right_side.shape[1:]
    full_width = rows * width
    places = ("leaf", "rows")

    def send(value, hops, shift):
        pairs = [(a * rows + r, b * rows + (r + shift) % rows) for a, b in hops for r in range(rows)]
        return lax.ppermute(value, places, pairs)

    def spread(value, hops):
        return [send(value, hops, shift) for shift in range(rows)]

    def rows_of(value, holders):
        return [value] + [send(value, [(h, h) for h in holders], shift) for shift in range(1, rows)]

    def core_columns(own):
        turns = range(1, cores)
        return [own] + [lax.ppermute(own, "rhs", [(c, (c + t) % cores) for c in range(cores)]) for t in turns]

    def holders(depth):
        return [(2 * p + 1) * 2 ** (top - depth - 1) - 1 for p in range(2**depth)]

    near = pltpu.VMEM
    half = near((count, width), BF16)
    half_f32 = near((count, width), F32)
    square = near(inverse_diag.shape[1:], BF16)
    lower = near(lower_blocks.shape[1:], BF16)
    joined = near((count, full_width), BF16)
    work = 2 * count * full_width * width
    semaphores = lambda n: pltpu.SemaphoreType.DMA((n,))

    reduced, inverse_upper = call(
        first_kernel, [], [right_side, inverse_diag], [half, square], [near((count, width), F32), semaphores(2)])
    gathered = rows_of(reduced, holders(0))
    inverse_upper = core_columns(inverse_upper)
    solved = None
    kept = []
    for depth in range(top + 1):
        if depth > 0:
            all_joined = near((count, depth * full_width), BF16)
            fetched = [pltpu.SMEM(block_rows.shape, jnp.int32), pltpu.SemaphoreType.DMA(()), joined]
            kernel = functools.partial(offset_kernel, top, depth, rows)
            weights = kept[0] if depth == top else lower_upper
            arrays = [block_rows, right, weights, *lefts, *rights, *older]
            if depth == top:
                reduced = call(kernel, arrays, [], [half], [all_joined, *fetched], work)
            else:
                reduced, mine = call(kernel, [*arrays, *kept], [], [half, all_joined], fetched, work)
            gathered = rows_of(reduced, range(leafs) if depth == top else holders(depth))
        if depth == top:
            return call(functools.partial(last_kernel, rows, cores), [*gathered, *kept[1:], solved], [],
                        [jax.ShapeDtypeStruct(right_side.shape, F32)], [joined], work)
        here = holders(depth)
        if depth + 1 < top:
            reach = 2 ** (top - depth - 2)
            ways = [[(h, h - reach) for h in here], [(h, h + reach) for h in here]]
            older = [send(mine, way, 0) for way in ways] if depth else []
        else:
            over = [(h, h + 1) for h in here]
            older = [mine, send(mine, over, 0)]
        kernel = functools.partial(solve_kernel, top, depth, rows, cores)
        arrays = [*gathered, *inverse_upper] + ([solved] if depth else []) + kept
        rounded, solved = call(kernel, arrays, [], [half, half_f32], [joined], work)
        if depth + 1 < top:
            lefts, rights = [spread(rounded, way) for way in ways]
        else:
            lefts, rights = rows_of(rounded, here), spread(rounded, over)
        if depth == 0:
            lower_upper, right, inverse_own, lower_own = call(
                load_kernel, [rounded], [right_side, inverse_diag, lower_blocks],
                [lower, near(right_side.shape, F32), square, lower], [semaphores(4)])
            kept = [lower_own, *core_columns(inverse_own)]


def solution(mesh):
    return jax.shard_map(
        local,
        mesh=mesh,
        in_specs=(
            P("leaf", "rhs", "rows"),
            P("leaf", None, ("rows", "rhs")),
            P("leaf", None, None, "rows"),
            P("leaf", None),
        ),
        out_specs=P("leaf", "rhs", "rows"),
        check_vma=False,
    )
```

time: 139 us -> 83.3 us (0.60)
  Pallas kernels: 78.5 us -> 14.5 us
  waiting for transfers between devices: 38.8 us -> 44.8 us
  starting transfers between devices: 19.9 us -> 23.4 us
    pallas_call x10 -> x9, Pallas kernels: 78.5 us -> 14.5 us  [call(): pl.pallas_call(kernel, in_specs=[WHOLE] * len(near) + [FAR] * len(far), o...]
    ppermute x2, waiting for transfers between devices: 0.01 us -> 4.16 us  [core_columns(): lax.ppermute(own, 'rhs', [(c, (c + t) % cores) for c in range(cores)])]
    ppermute x16 -> x18, starting transfers between devices: 19.3 us -> 22.4 us  [send(): return lax.ppermute(value, places, pairs)]
    ppermute x16 -> x18, waiting for transfers between devices: 38.8 us -> 40.6 us  [send(): return lax.ppermute(value, places, pairs)]
  transfers between devices with their start and end apart: 18 -> 20, of which waited for: 4 -> 9; matrix products, arithmetic and copies ran while one was open for 0% -> 0% of each run, Pallas kernels for 53% -> 1%
where the time goes in v5:
time: 83.3 us; the launch traced here: 82.9 us
  waiting for transfers between devices  44.8 us (54%)
  starting transfers between devices  23.4 us (28%)
  Pallas kernels  14.5 us (17%)
    ppermute x18, waiting for transfers between devices, send(): return lax.ppermute(value, places, pairs)  40.6 us
    ppermute x18, starting transfers between devices, send(): return lax.ppermute(value, places, pairs)  22.4 us
    pallas_call x9, Pallas kernels, call(): pl.pallas_call(kernel, in_specs=[WHOLE] * len(near) + [FAR] * len(far), o...  14.5 us
    ppermute x2, waiting for transfers between devices, core_columns(): lax.ppermute(own, 'rhs', [(c, (c + t) % cores) for c in range(cores)])  4.16 us
  transfers between devices with their start and end apart: 20, of which 9 were waited for; matrix products, arithmetic and copies ran while one was open for 0% of the time, Pallas kernels for 1%

profile of v5, /device:TPU:0, one launch (start us, length us, event | category | flops | bytes accessed | tf_op | source)
XLA Modules:
  0.0 82.9 jit_solution(16166078003278721124)
XLA Ops:
  0.0 1.7 %shard_map.46 = (bf16[64,1024]{1,0:T(8,128)(2,1)S(1)}, bf16[2048,512]{1,0:T(8,128)(2,1)S(1)}) custom-call(f32[2,64,1024]{2,1,0:T(8,128)} %right_ref.3, bf16[2,2048,512]{2,1,0:T(8,128)(2,1)} %inverse_ref.3), custom_call_target="tpu_custom_call" | custom-call | bytes 4718592 | tf_op jit(solution)/shard_map/pallas_call | solution.py:124
  1.7 0.5 collective-permute-start.1
  2.2 0.7 collective-permute-start
  2.9 0.0 collective-permute-done.refs_1_
  2.9 3.1 %collective-permute-done.1.refs_3_ = bf16[2048,512]{1,0:T(8,128)(2,1)S(1)} collective-permute-done((bf16[2048,512]{1,0:T(8,128)(2,1)S(1)}, bf16[2048,512]{1,0:T(8,128)(2,1)S(1)}, u32[]{:S(2)}, u32[]{:S(2)}) %collective-permute-start.1) | collective-permute-done | bytes 2097184 | tf_op jit(solution)/shard_map/ppermute | solution.py:154
  6.0 0.9 %shard_map.47 = (bf16[64,1024]{1,0:T(8,128)(2,1)S(1)}, f32[64,1024]{1,0:T(8,128)S(1)}) custom-call(bf16[64,1024]{1,0:T(8,128)(2,1)S(1)} %get-tuple-element.21.refs_0_, bf16[64,1024]{1,0:T(8,128)(2,1)S(1)} %collective-permute-done.refs_1_, bf16[2048,512]{1,0:T(8,128)(2,1)S(1)} %get-tuple-element.22.refs_2_, bf16[2048,512]{1,0:T(8,128)(2,1)S(1)} %collective-permute-done.1.refs_3_), custom_call_target="tpu_custom_call" | custom-call | flops 268435456 | bytes 4456448 | tf_op jit(solution)/shard_map/pallas_call | solution.py:124
  6.9 4.3 %shard_map.48 = (bf16[16,128,1024]{2,1,0:T(8,128)(2,1)S(1)}, f32[2,64,1024]{2,1,0:T(8,128)S(1)}, bf16[2048,512]{1,0:T(8,128)(2,1)S(1)}, bf16[16,128,1024]{2,1,0:T(8,128)(2,1)S(1)}) custom-call(bf16[64,1024]{1,0:T(8,128)(2,1)S(1)} %get-tuple-element.23.after_ref, f32[2,64,1024]{2,1,0:T(8,128)} %right_ref.3, bf16[2,2048,512]{2,1,0:T(8,128)(2,1)} %inverse_ref.3, ...), custom_call_target="tpu_custom_call" | custom-call | bytes 13238272 | tf_op jit(solution)/shard_map/pallas_call | solution.py:124
  11.2 0.4 collective-permute-start.6
  11.6 0.7 collective-permute-start.5
  12.3 0.7 collective-permute-start.4
  12.9 0.7 collective-permute-start.3
  13.6 0.7 collective-permute-start.2
  14.3 0.0 collective-permute-done.5.refs_3_
  14.3 0.0 collective-permute-done.4.refs_2_
  14.3 0.0 collective-permute-done.3.refs_1_
  14.3 0.0 collective-permute-done.2.refs_0_
  14.3 1.0 %collective-permute-done.6.refs_6_.refs_7_.refs_8_.refs_3_ = bf16[2048,512]{1,0:T(8,128)(2,1)S(1)} collective-permute-done((bf16[2048,512]{1,0:T(8,128)(2,1)S(1)}, bf16[2048,512]{1,0:T(8,128)(2,1)S(1)}, u32[]{:S(2)}, u32[]{:S(2)}) %collective-permute-start.6) | collective-permute-done | bytes 2097184 | tf_op jit(solution)/shard_map/ppermute | solution.py:154
  15.4 1.4 %shard_map.49 = (bf16[64,1024]{1,0:T(8,128)(2,1)S(1)}, bf16[64,2048]{1,0:T(8,128)(2,1)S(1)}) custom-call(s32[2,16]{1,0:T(2,128)S(1)} %copy-done, f32[2,64,1024]{2,1,0:T(8,128)S(1)} %get-tuple-element.24.right_ref, bf16[16,128,1024]{2,1,0:T(8,128)(2,1)S(1)} %get-tuple-element.26.lower_ref, bf16[64,1024]{1,0:T(8,128)(2,1)S(1)} %collective-permute-done.2.refs_0_, ...), custom_call_target="tpu_custom_call" | custom-call | flops 268435456 | bytes 13631616 | tf_op jit(solution)/shard_map/pallas_call | solution.py:124
  16.8 0.7 collective-permute-start.7
  17.5 0.0 collective-permute-done.7.refs_1_
  17.5 0.9 %shard_map.50 = (bf16[64,1024]{1,0:T(8,128)(2,1)S(1)}, f32[64,1024]{1,0:T(8,128)S(1)}) custom-call(bf16[64,1024]{1,0:T(8,128)(2,1)S(1)} %get-tuple-element.28.refs_0_, bf16[64,1024]{1,0:T(8,128)(2,1)S(1)} %collective-permute-done.7.refs_1_, bf16[2048,512]{1,0:T(8,128)(2,1)S(1)} %get-tuple-element.22.refs_2_, ...), custom_call_target="tpu_custom_call" | custom-call | flops 268435456 | bytes 13107200 | tf_op jit(solution)/shard_map/pallas_call | solution.py:124
  18.4 0.7 collective-permute-start.11
  19.1 0.7 collective-permute-start.13
  19.7 1.3 %collective-permute-start.12 = (bf16[64,2048]{1,0:T(8,128)(2,1)S(1)}, bf16[64,2048]{1,0:T(8,128)(2,1)S(1)}, u32[]{:S(2)}, u32[]{:S(2)}) collective-permute-start(bf16[64,2048]{1,0:T(8,128)(2,1)S(1)} %get-tuple-element.31), channel_id=1, source_target_pairs={{4,0},{6,2},{20,16},{22,18},{5,1},{7,3},{21,17},{23,19}} | collective-permute-start | bytes 786440 | tf_op jit(solution)/shard_map/ppermute | solution.py:144
  21.0 0.7 collective-permute-start.10
  21.7 1.3 %collective-permute-start.9 = (bf16[64,1024]{1,0:T(8,128)(2,1)S(1)}, bf16[64,1024]{1,0:T(8,128)(2,1)S(1)}, u32[]{:S(2)}, u32[]{:S(2)}) collective-permute-start(bf16[64,1024]{1,0:T(8,128)(2,1)S(1)} %get-tuple-element.30), channel_id=1, source_target_pairs={{4,2},{6,0},{20,18},{22,16},{5,3},{7,1},{21,19},{23,17}} | collective-permute-start | bytes 393224 | tf_op jit(solution)/shard_map/ppermute | solution.py:144
  23.0 0.0 collective-permute-done.11.refs_3_
  23.0 1.3 %collective-permute-start.8 = (bf16[64,1024]{1,0:T(8,128)(2,1)S(1)}, bf16[64,1024]{1,0:T(8,128)(2,1)S(1)}, u32[]{:S(2)}, u32[]{:S(2)}) collective-permute-start(bf16[64,1024]{1,0:T(8,128)(2,1)S(1)} %get-tuple-element.30), channel_id=1, source_target_pairs={{4,0},{6,2},{20,16},{22,18},{5,1},{7,3},{21,17},{23,19}} | collective-permute-start | bytes 393224 | tf_op jit(solution)/shard_map/ppermute | solution.py:144
  24.3 0.0 collective-permute-done.10.refs_2_
  24.3 29.9 %collective-permute-done.9.refs_1_ = bf16[64,1024]{1,0:T(8,128)(2,1)S(1)} collective-permute-done((bf16[64,1024]{1,0:T(8,128)(2,1)S(1)}, bf16[64,1024]{1,0:T(8,128)(2,1)S(1)}, u32[]{:S(2)}, u32[]{:S(2)}) %collective-permute-start.9) | collective-permute-done | bytes 131104 | tf_op jit(solution)/shard_map/ppermute | solution.py:144
  54.3 0.4 collective-permute-done.8.refs_0_
  54.7 0.0 collective-permute-done.13.refs_5_
  54.7 0.0 collective-permute-done.12.refs_4_
  54.7 1.4 %shard_map.51 = (bf16[64,1024]{1,0:T(8,128)(2,1)S(1)}, bf16[64,4096]{1,0:T(8,128)(2,1)S(1)}) custom-call(s32[2,16]{1,0:T(2,128)S(1)} %copy-done, f32[2,64,1024]{2,1,0:T(8,128)S(1)} %get-tuple-element.24.right_ref, bf16[16,128,1024]{2,1,0:T(8,128)(2,1)S(1)} %get-tuple-element.26.lower_ref, bf16[64,1024]{1,0:T(8,128)(2,1)S(1)} %collective-permute-done.8.refs_0_, ...), custom_call_target="tpu_custom_call" | custom-call | flops 268435456 | bytes 14155904 | tf_op jit(solution)/shard_map/pallas_call | solution.py:124
  56.1 1.5 %collective-permute-start.18 = (bf16[64,4096]{1,0:T(8,128)(2,1)S(1)}, bf16[64,4096]{1,0:T(8,128)(2,1)S(1)}, u32[]{:S(2)}, u32[]{:S(2)}) collective-permute-start(bf16[64,4096]{1,0:T(8,128)(2,1)S(1)} %get-tuple-element.35.refs_4_), channel_id=1, source_target_pairs={{0,4},{2,6},{8,12},{10,14},{16,20},{18,22},{24,28},{26,30},{1,5},{... | collective-permute-start | bytes 1572872 | tf_op jit(solution)/shard_map/ppermute | solution.py:144
  57.6 3.4 %collective-permute-start.14 = (bf16[64,1024]{1,0:T(8,128)(2,1)S(1)}, bf16[64,1024]{1,0:T(8,128)(2,1)S(1)}, u32[]{:S(2)}, u32[]{:S(2)}) collective-permute-start(bf16[64,1024]{1,0:T(8,128)(2,1)S(1)} %get-tuple-element.32.refs_0_), channel_id=1, source_target_pairs={{0,2},{2,0},{8,10},{10,8},{16,18},{18,16},{24,26},{26,24},{1,3},{3... | collective-permute-start | bytes 393224 | tf_op jit(solution)/shard_map/ppermute | solution.py:144
  61.1 3.4 %collective-permute-done.14.refs_1_ = bf16[64,1024]{1,0:T(8,128)(2,1)S(1)} collective-permute-done((bf16[64,1024]{1,0:T(8,128)(2,1)S(1)}, bf16[64,1024]{1,0:T(8,128)(2,1)S(1)}, u32[]{:S(2)}, u32[]{:S(2)}) %collective-permute-start.14) | collective-permute-done | bytes 131104 | tf_op jit(solution)/shard_map/ppermute | solution.py:144
  64.5 0.9 %shard_map.52 = (bf16[64,1024]{1,0:T(8,128)(2,1)S(1)}, f32[64,1024]{1,0:T(8,128)S(1)}) custom-call(bf16[64,1024]{1,0:T(8,128)(2,1)S(1)} %get-tuple-element.32.refs_0_, bf16[64,1024]{1,0:T(8,128)(2,1)S(1)} %collective-permute-done.14.refs_1_, bf16[2048,512]{1,0:T(8,128)(2,1)S(1)} %get-tuple-element.22.refs_2_, ...), custom_call_target="tpu_custom_call" | custom-call | flops 268435456 | bytes 13107200 | tf_op jit(solution)/shard_map/pallas_call | solution.py:124
  65.4 1.3 %collective-permute-start.17 = (bf16[64,1024]{1,0:T(8,128)(2,1)S(1)}, bf16[64,1024]{1,0:T(8,128)(2,1)S(1)}, u32[]{:S(2)}, u32[]{:S(2)}) collective-permute-start(bf16[64,1024]{1,0:T(8,128)(2,1)S(1)} %get-tuple-element.34.refs_0_), channel_id=1, source_target_pairs={{0,6},{2,4},{8,14},{10,12},{16,22},{18,20},{24,30},{26,28},{1,7},{... | collective-permute-start | bytes 393224 | tf_op jit(solution)/shard_map/ppermute | solution.py:144
  66.7 1.3 %collective-permute-start.16 = (bf16[64,1024]{1,0:T(8,128)(2,1)S(1)}, bf16[64,1024]{1,0:T(8,128)(2,1)S(1)}, u32[]{:S(2)}, u32[]{:S(2)}) collective-permute-start(bf16[64,1024]{1,0:T(8,128)(2,1)S(1)} %get-tuple-element.34.refs_0_), channel_id=1, source_target_pairs={{0,4},{2,6},{8,12},{10,14},{16,20},{18,22},{24,28},{26,30},{1,5},{... | collective-permute-start | bytes 393224 | tf_op jit(solution)/shard_map/ppermute | solution.py:144
  68.0 3.4 %collective-permute-start.15 = (bf16[64,1024]{1,0:T(8,128)(2,1)S(1)}, bf16[64,1024]{1,0:T(8,128)(2,1)S(1)}, u32[]{:S(2)}, u32[]{:S(2)}) collective-permute-start(bf16[64,1024]{1,0:T(8,128)(2,1)S(1)} %get-tuple-element.34.refs_0_), channel_id=1, source_target_pairs={{0,2},{2,0},{8,10},{10,8},{16,18},{18,16},{24,26},{26,24},{1,3},{3... | collective-permute-start | bytes 393224 | tf_op jit(solution)/shard_map/ppermute | solution.py:144
  71.4 0.2 collective-permute-done.17.refs_3_
  71.7 1.4 %collective-permute-done.16.refs_2_ = bf16[64,1024]{1,0:T(8,128)(2,1)S(1)} collective-permute-done((bf16[64,1024]{1,0:T(8,128)(2,1)S(1)}, bf16[64,1024]{1,0:T(8,128)(2,1)S(1)}, u32[]{:S(2)}, u32[]{:S(2)}) %collective-permute-start.16) | collective-permute-done | bytes 131104 | tf_op jit(solution)/shard_map/ppermute | solution.py:144
  73.1 1.8 %collective-permute-done.15.refs_1_ = bf16[64,1024]{1,0:T(8,128)(2,1)S(1)} collective-permute-done((bf16[64,1024]{1,0:T(8,128)(2,1)S(1)}, bf16[64,1024]{1,0:T(8,128)(2,1)S(1)}, u32[]{:S(2)}, u32[]{:S(2)}) %collective-permute-start.15) | collective-permute-done | bytes 131104 | tf_op jit(solution)/shard_map/ppermute | solution.py:144
  74.8 1.4 %shard_map.53.refs_0_ = bf16[64,1024]{1,0:T(8,128)(2,1)S(1)} custom-call(s32[2,16]{1,0:T(2,128)S(1)} %copy-done, f32[2,64,1024]{2,1,0:T(8,128)S(1)} %get-tuple-element.24.right_ref, bf16[16,128,1024]{2,1,0:T(8,128)(2,1)S(1)} %get-tuple-element.25.refs_4_.refs_5_.refs_6_.lower_ref, bf16[64,1024]{1,0:T(8,128)(2,1)S(1)} %get-tuple-element.34.refs_0_, ...), custom_call_target="tpu_custom_call" | custom-call | flops 268435456 | bytes 6291584 | tf_op jit(solution)/shard_map/pallas_call | solution.py:124
  76.3 1.6 %collective-permute-start.19 = (bf16[64,1024]{1,0:T(8,128)(2,1)S(1)}, bf16[64,1024]{1,0:T(8,128)(2,1)S(1)}, u32[]{:S(2)}, u32[]{:S(2)}) collective-permute-start(bf16[64,1024]{1,0:T(8,128)(2,1)S(1)} %shard_map.53.refs_0_), channel_id=1, source_target_pairs={{0,2},{2,0},{4,6},{6,4},{8,10},{10,8},{12,14},{14,12},{16,18},{18,... | collective-permute-start | bytes 393224 | tf_op jit(solution)/shard_map/ppermute | solution.py:144
  77.9 3.4 %collective-permute-done.19.refs_1_ = bf16[64,1024]{1,0:T(8,128)(2,1)S(1)} collective-permute-done((bf16[64,1024]{1,0:T(8,128)(2,1)S(1)}, bf16[64,1024]{1,0:T(8,128)(2,1)S(1)}, u32[]{:S(2)}, u32[]{:S(2)}) %collective-permute-start.19) | collective-permute-done | bytes 131104 | tf_op jit(solution)/shard_map/ppermute | solution.py:144
  81.3 1.7 %shard_map.54 = f32[2,64,1024]{2,1,0:T(8,128)} custom-call(bf16[64,1024]{1,0:T(8,128)(2,1)S(1)} %shard_map.53.refs_0_, bf16[64,1024]{1,0:T(8,128)(2,1)S(1)} %collective-permute-done.19.refs_1_, bf16[2048,512]{1,0:T(8,128)(2,1)S(1)} %get-tuple-element.27.refs_5_.refs_6_.refs_7_.refs_2_, ...), custom_call_target="tpu_custom_call" | custom-call | flops 268435456 | bytes 4718592 | tf_op jit(solution)/shard_map/pallas_call | solution.py:124
  (3 shorter events, 0.0 us)
Async XLA Ops:
  1.7 4.3 %collective-permute-start.1 = (bf16[2048,512]{1,0:T(8,128)(2,1)S(1)}, bf16[2048,512]{1,0:T(8,128)(2,1)S(1)}, u32[]{:S(2)}, u32[]{:S(2)}) collective-permute-start(bf16[2048,512]{1,0:T(8,128)(2,1)S(1)} %get-tuple-element.22.refs_2_), channel_id=1, source_target_pairs={{0,1},{1,0},{2,3},{3,2},{4,5},{5,4},{6,7},{7,6},{8,9},{9,8},{10,11... | collective-permute-start | bytes 6291464 | tf_op jit(solution)/shard_map/ppermute | solution.py:154
  2.2 0.7 collective-permute-start
  6.9 8.5 %copy-start = (s32[2,16]{1,0:T(2,128)S(1)}, s32[2,16]{1,0:T(2,128)}, u32[]{:S(2)}) copy-start(s32[2,16]{1,0:T(2,128)} %block_rows_ref.5) | copy-start | bytes 388
  11.2 4.2 %collective-permute-start.6 = (bf16[2048,512]{1,0:T(8,128)(2,1)S(1)}, bf16[2048,512]{1,0:T(8,128)(2,1)S(1)}, u32[]{:S(2)}, u32[]{:S(2)}) collective-permute-start(bf16[2048,512]{1,0:T(8,128)(2,1)S(1)} %get-tuple-element.27.refs_5_.refs_6_.refs_7_.refs_2_), channel_id=1, source_target_pairs={{0,1},{1,0},{2,3},{3,2},{4,5},{5,4},{6,7},{7,6},{8,9},{9,8},{10,11... | collective-permute-start | bytes 6291464 | tf_op jit(solution)/shard_map/ppermute | solution.py:154
  11.6 2.7 %collective-permute-start.5 = (bf16[64,1024]{1,0:T(8,128)(2,1)S(1)}, bf16[64,1024]{1,0:T(8,128)(2,1)S(1)}, u32[]{:S(2)}, u32[]{:S(2)}) collective-permute-start(bf16[64,1024]{1,0:T(8,128)(2,1)S(1)} %get-tuple-element.23.after_ref), channel_id=1, source_target_pairs={{12,22},{14,20},{13,23},{15,21}} | collective-permute-start | bytes 393224 | tf_op jit(solution)/shard_map/ppermute | solution.py:144
  12.3 2.0 %collective-permute-start.4 = (bf16[64,1024]{1,0:T(8,128)(2,1)S(1)}, bf16[64,1024]{1,0:T(8,128)(2,1)S(1)}, u32[]{:S(2)}, u32[]{:S(2)}) collective-permute-start(bf16[64,1024]{1,0:T(8,128)(2,1)S(1)} %get-tuple-element.23.after_ref), channel_id=1, source_target_pairs={{12,20},{14,22},{13,21},{15,23}} | collective-permute-start | bytes 393224 | tf_op jit(solution)/shard_map/ppermute | solution.py:144
  12.9 1.4 %collective-permute-start.3 = (bf16[64,1024]{1,0:T(8,128)(2,1)S(1)}, bf16[64,1024]{1,0:T(8,128)(2,1)S(1)}, u32[]{:S(2)}, u32[]{:S(2)}) collective-permute-start(bf16[64,1024]{1,0:T(8,128)(2,1)S(1)} %get-tuple-element.23.after_ref), channel_id=1, source_target_pairs={{12,6},{14,4},{13,7},{15,5}} | collective-permute-start | bytes 393224 | tf_op jit(solution)/shard_map/ppermute | solution.py:144
  13.6 0.7 collective-permute-start.2
  16.8 0.7 collective-permute-start.7
  18.4 4.6 %collective-permute-start.11 = (bf16[64,1024]{1,0:T(8,128)(2,1)S(1)}, bf16[64,1024]{1,0:T(8,128)(2,1)S(1)}, u32[]{:S(2)}, u32[]{:S(2)}) collective-permute-start(bf16[64,1024]{1,0:T(8,128)(2,1)S(1)} %get-tuple-element.30), channel_id=1, source_target_pairs={{4,10},{6,8},{20,26},{22,24},{5,11},{7,9},{21,27},{23,25}} | collective-permute-start | bytes 393224 | tf_op jit(solution)/shard_map/ppermute | solution.py:144
  19.1 35.6 %collective-permute-start.13 = (bf16[64,2048]{1,0:T(8,128)(2,1)S(1)}, bf16[64,2048]{1,0:T(8,128)(2,1)S(1)}, u32[]{:S(2)}, u32[]{:S(2)}) collective-permute-start(bf16[64,2048]{1,0:T(8,128)(2,1)S(1)} %get-tuple-element.31), channel_id=1, source_target_pairs={{4,8},{6,10},{20,24},{22,26},{5,9},{7,11},{21,25},{23,27}} | collective-permute-start | bytes 786440 | tf_op jit(solution)/shard_map/ppermute | solution.py:144
  19.7 35.0 %collective-permute-start.12 = (bf16[64,2048]{1,0:T(8,128)(2,1)S(1)}, bf16[64,2048]{1,0:T(8,128)(2,1)S(1)}, u32[]{:S(2)}, u32[]{:S(2)}) collective-permute-start(bf16[64,2048]{1,0:T(8,128)(2,1)S(1)} %get-tuple-element.31), channel_id=1, source_target_pairs={{4,0},{6,2},{20,16},{22,18},{5,1},{7,3},{21,17},{23,19}} | collective-permute-start | bytes 786440 | tf_op jit(solution)/shard_map/ppermute | solution.py:144
  21.0 3.3 %collective-permute-start.10 = (bf16[64,1024]{1,0:T(8,128)(2,1)S(1)}, bf16[64,1024]{1,0:T(8,128)(2,1)S(1)}, u32[]{:S(2)}, u32[]{:S(2)}) collective-permute-start(bf16[64,1024]{1,0:T(8,128)(2,1)S(1)} %get-tuple-element.30), channel_id=1, source_target_pairs={{4,8},{6,10},{20,24},{22,26},{5,9},{7,11},{21,25},{23,27}} | collective-permute-start | bytes 393224 | tf_op jit(solution)/shard_map/ppermute | solution.py:144
  21.7 32.5 %collective-permute-start.9 = (bf16[64,1024]{1,0:T(8,128)(2,1)S(1)}, bf16[64,1024]{1,0:T(8,128)(2,1)S(1)}, u32[]{:S(2)}, u32[]{:S(2)}) collective-permute-start(bf16[64,1024]{1,0:T(8,128)(2,1)S(1)} %get-tuple-element.30), channel_id=1, source_target_pairs={{4,2},{6,0},{20,18},{22,16},{5,3},{7,1},{21,19},{23,17}} | collective-permute-start | bytes 393224 | tf_op jit(solution)/shard_map/ppermute | solution.py:144
  23.0 31.7 %collective-permute-start.8 = (bf16[64,1024]{1,0:T(8,128)(2,1)S(1)}, bf16[64,1024]{1,0:T(8,128)(2,1)S(1)}, u32[]{:S(2)}, u32[]{:S(2)}) collective-permute-start(bf16[64,1024]{1,0:T(8,128)(2,1)S(1)} %get-tuple-element.30), channel_id=1, source_target_pairs={{4,0},{6,2},{20,16},{22,18},{5,1},{7,3},{21,17},{23,19}} | collective-permute-start | bytes 393224 | tf_op jit(solution)/shard_map/ppermute | solution.py:144
  56.1 18.7 %collective-permute-start.18 = (bf16[64,4096]{1,0:T(8,128)(2,1)S(1)}, bf16[64,4096]{1,0:T(8,128)(2,1)S(1)}, u32[]{:S(2)}, u32[]{:S(2)}) collective-permute-start(bf16[64,4096]{1,0:T(8,128)(2,1)S(1)} %get-tuple-element.35.refs_4_), channel_id=1, source_target_pairs={{0,4},{2,6},{8,12},{10,14},{16,20},{18,22},{24,28},{26,30},{1,5},{... | collective-permute-start | bytes 1572872 | tf_op jit(solution)/shard_map/ppermute | solution.py:144
  57.6 6.9 %collective-permute-start.14 = (bf16[64,1024]{1,0:T(8,128)(2,1)S(1)}, bf16[64,1024]{1,0:T(8,128)(2,1)S(1)}, u32[]{:S(2)}, u32[]{:S(2)}) collective-permute-start(bf16[64,1024]{1,0:T(8,128)(2,1)S(1)} %get-tuple-element.32.refs_0_), channel_id=1, source_target_pairs={{0,2},{2,0},{8,10},{10,8},{16,18},{18,16},{24,26},{26,24},{1,3},{3... | collective-permute-start | bytes 393224 | tf_op jit(solution)/shard_map/ppermute | solution.py:144
  65.4 6.3 %collective-permute-start.17 = (bf16[64,1024]{1,0:T(8,128)(2,1)S(1)}, bf16[64,1024]{1,0:T(8,128)(2,1)S(1)}, u32[]{:S(2)}, u32[]{:S(2)}) collective-permute-start(bf16[64,1024]{1,0:T(8,128)(2,1)S(1)} %get-tuple-element.34.refs_0_), channel_id=1, source_target_pairs={{0,6},{2,4},{8,14},{10,12},{16,22},{18,20},{24,30},{26,28},{1,7},{... | collective-permute-start | bytes 393224 | tf_op jit(solution)/shard_map/ppermute | solution.py:144
  66.7 6.4 %collective-permute-start.16 = (bf16[64,1024]{1,0:T(8,128)(2,1)S(1)}, bf16[64,1024]{1,0:T(8,128)(2,1)S(1)}, u32[]{:S(2)}, u32[]{:S(2)}) collective-permute-start(bf16[64,1024]{1,0:T(8,128)(2,1)S(1)} %get-tuple-element.34.refs_0_), channel_id=1, source_target_pairs={{0,4},{2,6},{8,12},{10,14},{16,20},{18,22},{24,28},{26,30},{1,5},{... | collective-permute-start | bytes 393224 | tf_op jit(solution)/shard_map/ppermute | solution.py:144
  68.0 6.9 %collective-permute-start.15 = (bf16[64,1024]{1,0:T(8,128)(2,1)S(1)}, bf16[64,1024]{1,0:T(8,128)(2,1)S(1)}, u32[]{:S(2)}, u32[]{:S(2)}) collective-permute-start(bf16[64,1024]{1,0:T(8,128)(2,1)S(1)} %get-tuple-element.34.refs_0_), channel_id=1, source_target_pairs={{0,2},{2,0},{8,10},{10,8},{16,18},{18,16},{24,26},{26,24},{1,3},{3... | collective-permute-start | bytes 393224 | tf_op jit(solution)/shard_map/ppermute | solution.py:144
  76.3 5.0 %collective-permute-start.19 = (bf16[64,1024]{1,0:T(8,128)(2,1)S(1)}, bf16[64,1024]{1,0:T(8,128)(2,1)S(1)}, u32[]{:S(2)}, u32[]{:S(2)}) collective-permute-start(bf16[64,1024]{1,0:T(8,128)(2,1)S(1)} %shard_map.53.refs_0_), channel_id=1, source_target_pairs={{0,2},{2,0},{4,6},{6,4},{8,10},{10,8},{12,14},{14,12},{16,18},{18,... | collective-permute-start | bytes 393224 | tf_op jit(solution)/shard_map/ppermute | solution.py:144

commit v6 on v5

v6 whole, which is shorter than its diff:
```python
import functools
import jax
import jax.numpy as jnp
from jax import lax
from jax.experimental import pallas as pl
from jax.experimental.pallas import tpu as pltpu
from jax.sharding import PartitionSpec as P

F32 = jnp.float32
BF16 = jnp.bfloat16


def upper_depth(leaf, top):
    return top - 1 - sum(((leaf + 1) % 2**power == 0).astype(jnp.int32) for power in range(1, top + 1))


def cast_kernel(right_ref, cast_ref, staged, semaphore):
    values = pltpu.make_async_copy(right_ref.at[1], staged, semaphore)
    values.start()
    values.wait()
    cast_ref[...] = staged[...].astype(BF16)


def load_kernel(after_ref, right_ref, inverse_ref, lower_ref, right_out, inverse_out, lower_out, semaphores):
    pairs = [(inverse_ref, inverse_out), (right_ref, right_out), (lower_ref, lower_out)]
    copies = [pltpu.make_async_copy(a, b, semaphores.at[i]) for i, (a, b) in enumerate(pairs)]
    for copy in copies:
        copy.start()
    for copy in copies:
        copy.wait()


def place_pieces(piece_refs, target_ref, start):
    rows = len(piece_refs)
    width = piece_refs[0].shape[1]
    own = lax.axis_index("rows")
    for shift, piece_ref in enumerate(piece_refs):
        source = lax.rem(own - shift + rows, rows)
        target_ref[:, pl.ds(pl.multiple_of(start + source * width, width), width)] = piece_ref[...]


def offset_kernel(top, level, rows, plan, block_rows_ref, right_ref, lower_ref, *refs):
    leaf = lax.axis_index("leaf")
    slot = 0 if level == top else 1
    pieces = [refs[:rows], refs[rows:2 * rows]]
    extra = refs[2 * rows:-5]
    reduced_ref, joined, numbers, semaphore, picked = refs[-5:]
    width = right_ref.shape[2]
    fetch = pltpu.make_async_copy(block_rows_ref, numbers, semaphore)
    fetch.start()
    reach = 2 ** (top - level - 1) if level < top else 1
    first = leaf % 2 == 0 if level == top else ((leaf + 1) // reach) % 4 == 1
    before = (level - 1) * rows * width
    for which, wanted in enumerate((first, jnp.logical_not(first))):
        @pl.when(wanted)
        def _():
            if plan == "crossed":
                place_pieces(pieces[1 - which], joined, 0)
            elif before:
                joined[:, :before] = extra[which][...]
            place_pieces(pieces[which], joined, before)
    blocks, block_width = lower_ref.shape[1:3]
    highest = joined.shape[1] // block_width - 1
    fetch.wait()
    for index in range(blocks):
        number = jnp.clip(numbers[slot, index], 0, highest)
        column = pl.multiple_of(number * block_width, block_width)
        picked[:, index * block_width:(index + 1) * block_width] = joined[:, pl.ds(column, block_width)]
    weights = lower_ref[slot].reshape(blocks * block_width, width)
    offset = jnp.dot(picked[...], weights, preferred_element_type=F32)
    reduced_ref[...] = (right_ref[slot] - offset).astype(BF16)
    if plan == "held":
        @pl.when(upper_depth(leaf, top) == 0)
        def _():
            reduced_ref[...] = extra[0][...]


def apply_inverse(slot, cores, piece_refs, inverse_refs, joined, store):
    quarter = inverse_refs[0].shape[-1]
    place_pieces(piece_refs, joined, 0)
    own = lax.axis_index("rhs")
    for turn, inverse_ref in enumerate(inverse_refs):
        total = jnp.dot(joined[...], inverse_ref[slot], preferred_element_type=F32)
        core = lax.rem(own - turn + cores, cores)
        store(pl.ds(pl.multiple_of(core * quarter, quarter), quarter), total)


def solve_kernel(top, depth, rows, cores, plan, *refs):
    piece_refs = refs[:rows]
    inverse_refs = refs[rows:rows + cores]
    before_ref = refs[rows + cores] if depth > 0 else None
    held_ref = refs[rows + cores + 1] if plan == "held" else None
    rounded_ref, solved_ref, joined = refs[-3:]
    leaf = lax.axis_index("leaf")
    active = upper_depth(leaf, top) == depth

    def store(columns, total):
        rounded_ref[:, columns] = total.astype(BF16)
        before = jnp.zeros_like(total) if before_ref is None else before_ref[:, columns]
        solved_ref[:, columns] = jnp.where(active, total, before)

    apply_inverse(1, cores, piece_refs, inverse_refs, joined, store)
    if plan == "held":
        @pl.when(upper_depth(leaf, top) == 0)
        def _():
            rounded_ref[...] = held_ref[...]

        @pl.when(leaf == lax.axis_size("leaf") - 1)
        def _():
            rounded_ref[...] = piece_refs[1][...]


def last_kernel(rows, cores, *refs):
    piece_refs = refs[:rows]
    inverse_refs = refs[rows:rows + cores]
    before_ref, out_ref, joined = refs[rows + cores:]
    out_ref[1] = before_ref[...]

    def store(columns, total):
        out_ref[0, :, columns] = total

    apply_inverse(0, cores, piece_refs, inverse_refs, joined, store)


WHOLE = pl.BlockSpec(memory_space=pltpu.VMEM)
FAR = pl.BlockSpec(memory_space=pltpu.HBM)


def call(kernel, near, far, outs, scratch=(), flops=0):
    several = len(outs) > 1
    size = sum(a.size * a.dtype.itemsize for a in [*near, *far])
    near = [pltpu.with_memory_space_constraint(a, pltpu.VMEM) for a in near]
    far = [pltpu.with_memory_space_constraint(a, pltpu.HBM) for a in far]
    specs = [FAR if getattr(o, "memory_space", None) == pltpu.HBM else WHOLE for o in outs]
    return pl.pallas_call(
        kernel,
        in_specs=[WHOLE] * len(near) + [FAR] * len(far),
        out_specs=specs if several else specs[0],
        out_shape=list(outs) if several else outs[0],
        scratch_shapes=list(scratch),
        cost_estimate=pl.CostEstimate(flops=flops, bytes_accessed=size, transcendentals=0),
        compiler_params=pltpu.CompilerParams(vmem_limit_bytes=8 * 2**20),
    )(*near, *far)


def local(right_side, inverse_diag, lower_blocks, block_rows):
    leafs, rows, cores = (lax.axis_size(name) for name in ("leaf", "rows", "rhs"))
    top = leafs.bit_length() - 1
    count, width = right_side.shape[1:]
    full_width = rows * width
    places = ("leaf", "rows")

    def send(value, hops, shift):
        pairs = [(a * rows + r, b * rows + (r + shift) % rows) for a, b in hops for r in range(rows)]
        return lax.ppermute(value, places, pairs)

    def spread(value, hops):
        return [send(value, hops, shift) for shift in range(rows)]

    def rows_of(value, holders, others=()):
        arrived = [value]
        for shift in range(1, rows):
            pairs = [(h * rows + r, h * rows + (r + shift) % rows) for h in holders for r in range(rows)]
            if shift == 1:
                pairs += [(a * rows + r, b * rows + r) for a, b in others for r in range(rows)]
            arrived.append(lax.ppermute(value, places, pairs))
        return arrived

    def core_columns(own):
        turns = range(1, cores)
        return [own] + [lax.ppermute(own, "rhs", [(c, (c + t) % cores) for c in range(cores)]) for t in turns]

    def holders(depth):
        return [(2 * p + 1) * 2 ** (top - depth - 1) - 1 for p in range(2**depth)]

    near = pltpu.VMEM
    half = near((count, width), BF16)
    half_f32 = near((count, width), F32)
    joined = near((count, full_width), BF16)
    work = 2 * count * full_width * width
    semaphores = lambda n: pltpu.SemaphoreType.DMA((n,))

    crossing = top == 3 and rows > 1
    spare = leafs - 1
    swapped = core_columns(inverse_diag)[1:]
    reduced = call(cast_kernel, [], [right_side], [half], [near((count, width), F32), pltpu.SemaphoreType.DMA(())])
    gathered = rows_of(reduced, holders(0))
    right, inverse_own, lower = call(
        load_kernel, [reduced], [right_side, inverse_diag, lower_blocks],
        [near(a.shape, a.dtype) for a in (right_side, inverse_diag, lower_blocks)], [semaphores(3)])
    inverses = [inverse_own, *swapped]
    solved = None
    for depth in range(top + 1):
        held = crossing and depth == 1
        crossed = crossing and depth == 2
        if depth > 0:
            all_joined = near((count, depth * full_width), BF16)
            fetched = [pltpu.SMEM(block_rows.shape, jnp.int32), pltpu.SemaphoreType.DMA(()), joined]
            plan = "held" if held else "crossed" if crossed else "plain"
            kernel = functools.partial(offset_kernel, top, depth, rows, plan)
            arrays = [block_rows, right, lower, *lefts, *rights, *older] + ([rounded] if held else [])
            if depth == top:
                reduced = call(kernel, arrays, [], [half], [all_joined, *fetched], work)
            else:
                reduced, mine = call(kernel, arrays, [], [half, all_joined], fetched, work)
            others = [(h, spare) for h in holders(0)] if held else []
            gathered = rows_of(reduced, range(leafs) if depth == top else holders(depth), others)
        if depth == top:
            return call(functools.partial(last_kernel, rows, cores), [*gathered, *inverses, solved], [],
                        [jax.ShapeDtypeStruct(right_side.shape, F32)], [joined], work)
        here = holders(depth)
        older = []
        if depth + 1 < top:
            reach = 2 ** (top - depth - 2)
            ways = [[(h, h - reach) for h in here], [(h, h + reach) for h in here]]
            if held:
                tops = [*holders(0), spare]
                ways = [ways[0] + [(h, h - reach) for h in tops], ways[1] + [(h, h - 3 * reach) for h in tops]]
            elif depth > 0:
                older = [send(mine, way, 0) for way in ways]
        else:
            over = [(h, h + 1) for h in here]
            older = [mine, send(mine, over, 0)]
        kernel = functools.partial(solve_kernel, top, depth, rows, cores, "held" if held else "plain")
        arrays = [*gathered, *inverses] + ([solved] if depth else []) + ([rounded] if held else [])
        rounded, solved = call(kernel, arrays, [], [half, half_f32], [joined], work)
        if depth + 1 < top:
            lefts, rights = [spread(rounded, way) for way in ways]
        else:
            lefts, rights = rows_of(rounded, here), spread(rounded, over)


def solution(mesh):
    return jax.shard_map(
        local,
        mesh=mesh,
        in_specs=(
            P("leaf", "rhs", "rows"),
            P("leaf", None, ("rows", "rhs")),
            P("leaf", None, None, "rows"),
            P("leaf", None),
        ),
        out_specs=P("leaf", "rhs", "rows"),
        check_vma=False,
    )
```

time: 83.3 us -> 74.1 us (0.89)
  waiting for transfers between devices: 44.8 us -> 38.8 us
  starting transfers between devices: 23.4 us -> 19.5 us
    ppermute x18 -> x11, waiting for transfers between devices: 40.6 us -> 26.3 us  [send(): return lax.ppermute(value, places, pairs)]
    ppermute x0 -> x5, waiting for transfers between devices: none -> 12.1 us  [rows_of(): arrived.append(lax.ppermute(value, places, pairs))]
    ppermute x18 -> x11, starting transfers between devices: 22.4 us -> 11.9 us  [send(): return lax.ppermute(value, places, pairs)]
    ppermute x0 -> x5, starting transfers between devices: none -> 7.14 us  [rows_of(): arrived.append(lax.ppermute(value, places, pairs))]
    ppermute x2 -> x1, waiting for transfers between devices: 4.16 us -> 0.47 us  [core_columns(): lax.ppermute(own, 'rhs', [(c, (c + t) % cores) for c in range(cores)])]
  transfers between devices with their start and end apart: 20 -> 17, of which waited for: 9 -> 10; matrix products, arithmetic and copies ran while one was open for 0% -> 0% of each run, Pallas kernels for 1% -> 9%
where the time goes in v6:
time: 74.1 us; the launch traced here: 73.7 us
  waiting for transfers between devices  38.8 us (52%)
  starting transfers between devices  19.5 us (26%)
  Pallas kernels  15.1 us (20%)
    ppermute x11, waiting for transfers between devices, send(): return lax.ppermute(value, places, pairs)  26.3 us
    pallas_call x9, Pallas kernels, call(): pl.pallas_call(kernel, in_specs=[WHOLE] * len(near) + [FAR] * len(far), o...  15.1 us
    ppermute x5, waiting for transfers between devices, rows_of(): arrived.append(lax.ppermute(value, places, pairs))  12.1 us
    ppermute x11, starting transfers between devices, send(): return lax.ppermute(value, places, pairs)  11.9 us
    ppermute x5, starting transfers between devices, rows_of(): arrived.append(lax.ppermute(value, places, pairs))  7.14 us
  transfers between devices with their start and end apart: 17, of which 10 were waited for; matrix products, arithmetic and copies ran while one was open for 0% of the time, Pallas kernels for 9%

profile of v6, /device:TPU:0, one launch (start us, length us, event | category | flops | bytes accessed | tf_op | source)
XLA Modules:
  0.0 73.7 jit_solution(11005369633542460667)
XLA Ops:
  0.0 0.5 collective-permute-start.1
  0.5 1.0 %shard_map.46.after_ref.refs_0_ = bf16[64,1024]{1,0:T(8,128)(2,1)S(1)} custom-call(f32[2,64,1024]{2,1,0:T(8,128)} %right_ref.3), custom_call_target="tpu_custom_call" | custom-call | bytes 524288 | tf_op jit(solution)/shard_map/pallas_call | solution.py:135
  1.4 0.7 collective-permute-start
  2.1 4.8 %shard_map.47 = (f32[2,64,1024]{2,1,0:T(8,128)S(1)}, bf16[2,2048,512]{2,1,0:T(8,128)(2,1)S(1)}, bf16[2,16,128,1024]{3,2,1,0:T(8,128)(2,1)S(1)}) custom-call(bf16[64,1024]{1,0:T(8,128)(2,1)S(1)} %shard_map.46.after_ref.refs_0_, f32[2,64,1024]{2,1,0:T(8,128)} %right_ref.3, bf16[2,2048,512]{2,1,0:T(8,128)(2,1)} %inverse_ref.1, bf16[2,16,128,1024]{3,2,1,0:T(8,128)(2,1)} %lower_ref.1), custom_call_target="tpu_custom_call" | custom-call | bytes 13238272 | tf_op jit(solution)/shard_map/pallas_call | solution.py:135
  7.0 0.0 collective-permute-done.refs_1_
  7.0 0.5 collective-permute-done.1.refs_3_
  7.5 0.0 copy-start
  7.5 0.9 %shard_map.48 = (bf16[64,1024]{1,0:T(8,128)(2,1)S(1)}, f32[64,1024]{1,0:T(8,128)S(1)}) custom-call(bf16[64,1024]{1,0:T(8,128)(2,1)S(1)} %shard_map.46.after_ref.refs_0_, bf16[64,1024]{1,0:T(8,128)(2,1)S(1)} %collective-permute-done.refs_1_, bf16[2,2048,512]{2,1,0:T(8,128)(2,1)S(1)} %get-tuple-element.19.refs_2_, ...), custom_call_target="tpu_custom_call" | custom-call | flops 268435456 | bytes 8650752 | tf_op jit(solution)/shard_map/pallas_call | solution.py:135
  8.3 0.7 collective-permute-start.5
  9.0 0.7 collective-permute-start.4
  9.7 0.7 collective-permute-start.3
  10.4 0.7 collective-permute-start.2
  11.0 0.0 collective-permute-done.5.refs_3_
  11.0 0.0 collective-permute-done.4.refs_2_
  11.1 0.0 collective-permute-done.3.refs_1_
  11.1 0.0 collective-permute-done.2.refs_0_
  11.1 0.0 copy-done
  11.1 2.1 %shard_map.49 = (bf16[64,1024]{1,0:T(8,128)(2,1)S(1)}, bf16[64,2048]{1,0:T(8,128)(2,1)}) custom-call(s32[2,16]{1,0:T(2,128)S(1)} %copy-done, f32[2,64,1024]{2,1,0:T(8,128)S(1)} %get-tuple-element.17.right_ref, bf16[2,16,128,1024]{3,2,1,0:T(8,128)(2,1)S(1)} %get-tuple-element.18.lower_ref, bf16[64,1024]{1,0:T(8,128)(2,1)S(1)} %collective-permute-done.2.refs_0_, ...), custom_call_target="tpu_custom_call" | custom-call | flops 268435456 | bytes 9568384 | tf_op jit(solution)/shard_map/pallas_call | solution.py:135
  13.2 0.7 collective-permute-start.6
  13.9 0.0 collective-permute-done.6.refs_1_
  13.9 0.9 %shard_map.50 = (bf16[64,1024]{1,0:T(8,128)(2,1)S(1)}, f32[64,1024]{1,0:T(8,128)S(1)}) custom-call(bf16[64,1024]{1,0:T(8,128)(2,1)S(1)} %get-tuple-element.21.refs_0_, bf16[64,1024]{1,0:T(8,128)(2,1)S(1)} %collective-permute-done.6.refs_1_, bf16[2,2048,512]{2,1,0:T(8,128)(2,1)S(1)} %get-tuple-element.19.refs_2_, ...), custom_call_target="tpu_custom_call" | custom-call | flops 268435456 | bytes 9043968 | tf_op jit(solution)/shard_map/pallas_call | solution.py:135
  14.8 1.3 %collective-permute-start.10 = (bf16[64,1024]{1,0:T(8,128)(2,1)S(1)}, bf16[64,1024]{1,0:T(8,128)(2,1)S(1)}, u32[]{:S(2)}, u32[]{:S(2)}) collective-permute-start(bf16[64,1024]{1,0:T(8,128)(2,1)S(1)} %get-tuple-element.23), channel_id=1, source_target_pairs={{4,10},{6,8},{20,26},{22,24},{12,2},{14,0},{28,18},{30,16},{5,11},... | collective-permute-start | bytes 393224 | tf_op jit(solution)/shard_map/ppermute | solution.py:155
  16.1 1.3 %collective-permute-start.9 = (bf16[64,1024]{1,0:T(8,128)(2,1)S(1)}, bf16[64,1024]{1,0:T(8,128)(2,1)S(1)}, u32[]{:S(2)}, u32[]{:S(2)}) collective-permute-start(bf16[64,1024]{1,0:T(8,128)(2,1)S(1)} %get-tuple-element.23), channel_id=1, source_target_pairs={{4,8},{6,10},{20,24},{22,26},{12,0},{14,2},{28,16},{30,18},{5,9},{... | collective-permute-start | bytes 393224 | tf_op jit(solution)/shard_map/ppermute | solution.py:155
  17.4 1.3 %collective-permute-start.8 = (bf16[64,1024]{1,0:T(8,128)(2,1)S(1)}, bf16[64,1024]{1,0:T(8,128)(2,1)S(1)}, u32[]{:S(2)}, u32[]{:S(2)}) collective-permute-start(bf16[64,1024]{1,0:T(8,128)(2,1)S(1)} %get-tuple-element.23), channel_id=1, source_target_pairs={{4,2},{6,0},{20,18},{22,16},{12,10},{14,8},{28,26},{30,24},{5,3},{... | collective-permute-start | bytes 393224 | tf_op jit(solution)/shard_map/ppermute | solution.py:155
  18.7 1.3 %collective-permute-start.7 = (bf16[64,1024]{1,0:T(8,128)(2,1)S(1)}, bf16[64,1024]{1,0:T(8,128)(2,1)S(1)}, u32[]{:S(2)}, u32[]{:S(2)}) collective-permute-start(bf16[64,1024]{1,0:T(8,128)(2,1)S(1)} %get-tuple-element.23), channel_id=1, source_target_pairs={{4,0},{6,2},{20,16},{22,18},{12,8},{14,10},{28,24},{30,26},{5,1},{... | collective-permute-start | bytes 393224 | tf_op jit(solution)/shard_map/ppermute | solution.py:155
  20.0 17.0 %collective-permute-done.10.refs_3_ = bf16[64,1024]{1,0:T(8,128)(2,1)S(1)} collective-permute-done((bf16[64,1024]{1,0:T(8,128)(2,1)S(1)}, bf16[64,1024]{1,0:T(8,128)(2,1)S(1)}, u32[]{:S(2)}, u32[]{:S(2)}) %collective-permute-start.10) | collective-permute-done | bytes 131104 | tf_op jit(solution)/shard_map/ppermute | solution.py:155
  37.0 1.4 %collective-permute-done.9.refs_2_ = bf16[64,1024]{1,0:T(8,128)(2,1)S(1)} collective-permute-done((bf16[64,1024]{1,0:T(8,128)(2,1)S(1)}, bf16[64,1024]{1,0:T(8,128)(2,1)S(1)}, u32[]{:S(2)}, u32[]{:S(2)}) %collective-permute-start.9) | collective-permute-done | bytes 131104 | tf_op jit(solution)/shard_map/ppermute | solution.py:155
  38.4 4.7 %collective-permute-done.8.refs_1_ = bf16[64,1024]{1,0:T(8,128)(2,1)S(1)} collective-permute-done((bf16[64,1024]{1,0:T(8,128)(2,1)S(1)}, bf16[64,1024]{1,0:T(8,128)(2,1)S(1)}, u32[]{:S(2)}, u32[]{:S(2)}) %collective-permute-start.8) | collective-permute-done | bytes 131104 | tf_op jit(solution)/shard_map/ppermute | solution.py:155
  43.1 1.4 %collective-permute-done.7.refs_0_ = bf16[64,1024]{1,0:T(8,128)(2,1)S(1)} collective-permute-done((bf16[64,1024]{1,0:T(8,128)(2,1)S(1)}, bf16[64,1024]{1,0:T(8,128)(2,1)S(1)}, u32[]{:S(2)}, u32[]{:S(2)}) %collective-permute-start.7) | collective-permute-done | bytes 131104 | tf_op jit(solution)/shard_map/ppermute | solution.py:155
  44.5 1.4 %shard_map.51 = (bf16[64,1024]{1,0:T(8,128)(2,1)S(1)}, bf16[64,4096]{1,0:T(8,128)(2,1)S(1)}) custom-call(s32[2,16]{1,0:T(2,128)S(1)} %copy-done, f32[2,64,1024]{2,1,0:T(8,128)S(1)} %get-tuple-element.17.right_ref, bf16[2,16,128,1024]{3,2,1,0:T(8,128)(2,1)S(1)} %get-tuple-element.18.lower_ref, bf16[64,1024]{1,0:T(8,128)(2,1)S(1)} %collective-permute-done.7.refs_0_, ...), custom_call_target="tpu_custom_call" | custom-call | flops 268435456 | bytes 9437312 | tf_op jit(solution)/shard_map/pallas_call | solution.py:135
  46.0 1.5 %collective-permute-start.15 = (bf16[64,4096]{1,0:T(8,128)(2,1)S(1)}, bf16[64,4096]{1,0:T(8,128)(2,1)S(1)}, u32[]{:S(2)}, u32[]{:S(2)}) collective-permute-start(bf16[64,4096]{1,0:T(8,128)(2,1)S(1)} %get-tuple-element.27.refs_4_), channel_id=1, source_target_pairs={{0,4},{2,6},{8,12},{10,14},{16,20},{18,22},{24,28},{26,30},{1,5},{... | collective-permute-start | bytes 1572872 | tf_op jit(solution)/shard_map/ppermute | solution.py:155
  47.4 2.5 %collective-permute-start.11 = (bf16[64,1024]{1,0:T(8,128)(2,1)S(1)}, bf16[64,1024]{1,0:T(8,128)(2,1)S(1)}, u32[]{:S(2)}, u32[]{:S(2)}) collective-permute-start(bf16[64,1024]{1,0:T(8,128)(2,1)S(1)} %get-tuple-element.24.refs_0_), channel_id=1, source_target_pairs={{0,2},{2,0},{8,10},{10,8},{16,18},{18,16},{24,26},{26,24},{1,3},{3... | collective-permute-start | bytes 393224 | tf_op jit(solution)/shard_map/ppermute | solution.py:166
  49.9 4.4 %collective-permute-done.11.refs_1_ = bf16[64,1024]{1,0:T(8,128)(2,1)S(1)} collective-permute-done((bf16[64,1024]{1,0:T(8,128)(2,1)S(1)}, bf16[64,1024]{1,0:T(8,128)(2,1)S(1)}, u32[]{:S(2)}, u32[]{:S(2)}) %collective-permute-start.11) | collective-permute-done | bytes 131104 | tf_op jit(solution)/shard_map/ppermute | solution.py:166
  54.3 0.9 %shard_map.52 = (bf16[64,1024]{1,0:T(8,128)(2,1)S(1)}, f32[64,1024]{1,0:T(8,128)S(1)}) custom-call(bf16[64,1024]{1,0:T(8,128)(2,1)S(1)} %get-tuple-element.24.refs_0_, bf16[64,1024]{1,0:T(8,128)(2,1)S(1)} %collective-permute-done.11.refs_1_, bf16[2,2048,512]{2,1,0:T(8,128)(2,1)S(1)} %get-tuple-element.19.refs_2_, ...), custom_call_target="tpu_custom_call" | custom-call | flops 268435456 | bytes 8912896 | tf_op jit(solution)/shard_map/pallas_call | solution.py:135
  55.2 1.3 %collective-permute-start.14 = (bf16[64,1024]{1,0:T(8,128)(2,1)S(1)}, bf16[64,1024]{1,0:T(8,128)(2,1)S(1)}, u32[]{:S(2)}, u32[]{:S(2)}) collective-permute-start(bf16[64,1024]{1,0:T(8,128)(2,1)S(1)} %get-tuple-element.26.refs_0_), channel_id=1, source_target_pairs={{0,6},{2,4},{8,14},{10,12},{16,22},{18,20},{24,30},{26,28},{1,7},{... | collective-permute-start | bytes 393224 | tf_op jit(solution)/shard_map/ppermute | solution.py:155
  56.5 1.3 %collective-permute-start.13 = (bf16[64,1024]{1,0:T(8,128)(2,1)S(1)}, bf16[64,1024]{1,0:T(8,128)(2,1)S(1)}, u32[]{:S(2)}, u32[]{:S(2)}) collective-permute-start(bf16[64,1024]{1,0:T(8,128)(2,1)S(1)} %get-tuple-element.26.refs_0_), channel_id=1, source_target_pairs={{0,4},{2,6},{8,12},{10,14},{16,20},{18,22},{24,28},{26,30},{1,5},{... | collective-permute-start | bytes 393224 | tf_op jit(solution)/shard_map/ppermute | solution.py:155
  57.8 2.5 %collective-permute-start.12 = (bf16[64,1024]{1,0:T(8,128)(2,1)S(1)}, bf16[64,1024]{1,0:T(8,128)(2,1)S(1)}, u32[]{:S(2)}, u32[]{:S(2)}) collective-permute-start(bf16[64,1024]{1,0:T(8,128)(2,1)S(1)} %get-tuple-element.26.refs_0_), channel_id=1, source_target_pairs={{0,2},{2,0},{8,10},{10,8},{16,18},{18,16},{24,26},{26,24},{1,3},{3... | collective-permute-start | bytes 393224 | tf_op jit(solution)/shard_map/ppermute | solution.py:166
  60.3 0.3 collective-permute-done.14.refs_3_
  60.6 1.4 %collective-permute-done.13.refs_2_ = bf16[64,1024]{1,0:T(8,128)(2,1)S(1)} collective-permute-done((bf16[64,1024]{1,0:T(8,128)(2,1)S(1)}, bf16[64,1024]{1,0:T(8,128)(2,1)S(1)}, u32[]{:S(2)}, u32[]{:S(2)}) %collective-permute-start.13) | collective-permute-done | bytes 131104 | tf_op jit(solution)/shard_map/ppermute | solution.py:155
  62.0 3.5 %collective-permute-done.12.refs_1_ = bf16[64,1024]{1,0:T(8,128)(2,1)S(1)} collective-permute-done((bf16[64,1024]{1,0:T(8,128)(2,1)S(1)}, bf16[64,1024]{1,0:T(8,128)(2,1)S(1)}, u32[]{:S(2)}, u32[]{:S(2)}) %collective-permute-start.12) | collective-permute-done | bytes 131104 | tf_op jit(solution)/shard_map/ppermute | solution.py:166
  65.5 0.0 collective-permute-done.15.refs_5_
  65.5 1.4 %shard_map.53.refs_0_ = bf16[64,1024]{1,0:T(8,128)(2,1)S(1)} custom-call(s32[2,16]{1,0:T(2,128)S(1)} %copy-done, f32[2,64,1024]{2,1,0:T(8,128)S(1)} %get-tuple-element.17.right_ref, bf16[2,16,128,1024]{3,2,1,0:T(8,128)(2,1)S(1)} %get-tuple-element.18.lower_ref, bf16[64,1024]{1,0:T(8,128)(2,1)S(1)} %get-tuple-element.26.refs_0_, ...), custom_call_target="tpu_custom_call" | custom-call | flops 268435456 | bytes 10485888 | tf_op jit(solution)/shard_map/pallas_call | solution.py:135
  67.0 0.9 %collective-permute-start.16 = (bf16[64,1024]{1,0:T(8,128)(2,1)S(1)}, bf16[64,1024]{1,0:T(8,128)(2,1)S(1)}, u32[]{:S(2)}, u32[]{:S(2)}) collective-permute-start(bf16[64,1024]{1,0:T(8,128)(2,1)S(1)} %shard_map.53.refs_0_), channel_id=1, source_target_pairs={{0,2},{2,0},{4,6},{6,4},{8,10},{10,8},{12,14},{14,12},{16,18},{18,... | collective-permute-start | bytes 393224 | tf_op jit(solution)/shard_map/ppermute | solution.py:166
  67.8 4.2 %collective-permute-done.16.refs_1_ = bf16[64,1024]{1,0:T(8,128)(2,1)S(1)} collective-permute-done((bf16[64,1024]{1,0:T(8,128)(2,1)S(1)}, bf16[64,1024]{1,0:T(8,128)(2,1)S(1)}, u32[]{:S(2)}, u32[]{:S(2)}) %collective-permute-start.16) | collective-permute-done | bytes 131104 | tf_op jit(solution)/shard_map/ppermute | solution.py:166
  72.0 1.7 %shard_map.54 = f32[2,64,1024]{2,1,0:T(8,128)} custom-call(bf16[64,1024]{1,0:T(8,128)(2,1)S(1)} %shard_map.53.refs_0_, bf16[64,1024]{1,0:T(8,128)(2,1)S(1)} %collective-permute-done.16.refs_1_, bf16[2,2048,512]{2,1,0:T(8,128)(2,1)S(1)} %get-tuple-element.19.refs_2_, bf16[2,2048,512]{2,1,0:T(8,128)(2,1)S(1)} %collective-permute-done.1.refs_3_, ...), custom_call_target="tpu_custom_call" | custom-call | flops 268435456 | bytes 8912896 | tf_op jit(solution)/shard_map/pallas_call | solution.py:135
Async XLA Ops:
  0.0 7.4 %collective-permute-start.1 = (bf16[2,2048,512]{2,1,0:T(8,128)(2,1)}, bf16[2,2048,512]{2,1,0:T(8,128)(2,1)S(1)}, u32[]{:S(2)}, u32[]{:S(2)}) collective-permute-start(bf16[2,2048,512]{2,1,0:T(8,128)(2,1)} %inverse_ref.1), channel_id=1, source_target_pairs={{0,1},{1,0},{2,3},{3,2},{4,5},{5,4},{6,7},{7,6},{8,9},{9,8},{10,11... | collective-permute-start | bytes 12582920 | tf_op jit(solution)/shard_map/ppermute | solution.py:171
  1.4 5.5 %collective-permute-start = (bf16[64,1024]{1,0:T(8,128)(2,1)S(1)}, bf16[64,1024]{1,0:T(8,128)(2,1)S(1)}, u32[]{:S(2)}, u32[]{:S(2)}) collective-permute-start(bf16[64,1024]{1,0:T(8,128)(2,1)S(1)} %shard_map.46.after_ref.refs_0_), channel_id=1, source_target_pairs={{12,14},{14,12},{13,15},{15,13}} | collective-permute-start | bytes 393224 | tf_op jit(solution)/shard_map/ppermute | solution.py:166
  7.5 3.6 %copy-start = (s32[2,16]{1,0:T(2,128)S(1)}, s32[2,16]{1,0:T(2,128)}, u32[]{:S(2)}) copy-start(s32[2,16]{1,0:T(2,128)} %block_rows_ref.5) | copy-start | bytes 388
  8.3 2.7 %collective-permute-start.5 = (bf16[64,1024]{1,0:T(8,128)(2,1)S(1)}, bf16[64,1024]{1,0:T(8,128)(2,1)S(1)}, u32[]{:S(2)}, u32[]{:S(2)}) collective-permute-start(bf16[64,1024]{1,0:T(8,128)(2,1)S(1)} %get-tuple-element.20.refs_4_.refs_5_), channel_id=1, source_target_pairs={{12,22},{14,20},{13,23},{15,21}} | collective-permute-start | bytes 393224 | tf_op jit(solution)/shard_map/ppermute | solution.py:155
  9.0 2.0 %collective-permute-start.4 = (bf16[64,1024]{1,0:T(8,128)(2,1)S(1)}, bf16[64,1024]{1,0:T(8,128)(2,1)S(1)}, u32[]{:S(2)}, u32[]{:S(2)}) collective-permute-start(bf16[64,1024]{1,0:T(8,128)(2,1)S(1)} %get-tuple-element.20.refs_4_.refs_5_), channel_id=1, source_target_pairs={{12,20},{14,22},{13,21},{15,23}} | collective-permute-start | bytes 393224 | tf_op jit(solution)/shard_map/ppermute | solution.py:155
  9.7 1.4 %collective-permute-start.3 = (bf16[64,1024]{1,0:T(8,128)(2,1)S(1)}, bf16[64,1024]{1,0:T(8,128)(2,1)S(1)}, u32[]{:S(2)}, u32[]{:S(2)}) collective-permute-start(bf16[64,1024]{1,0:T(8,128)(2,1)S(1)} %get-tuple-element.20.refs_4_.refs_5_), channel_id=1, source_target_pairs={{12,6},{14,4},{13,7},{15,5}} | collective-permute-start | bytes 393224 | tf_op jit(solution)/shard_map/ppermute | solution.py:155
  10.4 0.7 collective-permute-start.2
  13.2 0.7 collective-permute-start.6
  14.8 22.2 %collective-permute-start.10 = (bf16[64,1024]{1,0:T(8,128)(2,1)S(1)}, bf16[64,1024]{1,0:T(8,128)(2,1)S(1)}, u32[]{:S(2)}, u32[]{:S(2)}) collective-permute-start(bf16[64,1024]{1,0:T(8,128)(2,1)S(1)} %get-tuple-element.23), channel_id=1, source_target_pairs={{4,10},{6,8},{20,26},{22,24},{12,2},{14,0},{28,18},{30,16},{5,11},... | collective-permute-start | bytes 393224 | tf_op jit(solution)/shard_map/ppermute | solution.py:155
  16.1 22.3 %collective-permute-start.9 = (bf16[64,1024]{1,0:T(8,128)(2,1)S(1)}, bf16[64,1024]{1,0:T(8,128)(2,1)S(1)}, u32[]{:S(2)}, u32[]{:S(2)}) collective-permute-start(bf16[64,1024]{1,0:T(8,128)(2,1)S(1)} %get-tuple-element.23), channel_id=1, source_target_pairs={{4,8},{6,10},{20,24},{22,26},{12,0},{14,2},{28,16},{30,18},{5,9},{... | collective-permute-start | bytes 393224 | tf_op jit(solution)/shard_map/ppermute | solution.py:155
  17.4 25.7 %collective-permute-start.8 = (bf16[64,1024]{1,0:T(8,128)(2,1)S(1)}, bf16[64,1024]{1,0:T(8,128)(2,1)S(1)}, u32[]{:S(2)}, u32[]{:S(2)}) collective-permute-start(bf16[64,1024]{1,0:T(8,128)(2,1)S(1)} %get-tuple-element.23), channel_id=1, source_target_pairs={{4,2},{6,0},{20,18},{22,16},{12,10},{14,8},{28,26},{30,24},{5,3},{... | collective-permute-start | bytes 393224 | tf_op jit(solution)/shard_map/ppermute | solution.py:155
  18.7 25.8 %collective-permute-start.7 = (bf16[64,1024]{1,0:T(8,128)(2,1)S(1)}, bf16[64,1024]{1,0:T(8,128)(2,1)S(1)}, u32[]{:S(2)}, u32[]{:S(2)}) collective-permute-start(bf16[64,1024]{1,0:T(8,128)(2,1)S(1)} %get-tuple-element.23), channel_id=1, source_target_pairs={{4,0},{6,2},{20,16},{22,18},{12,8},{14,10},{28,24},{30,26},{5,1},{... | collective-permute-start | bytes 393224 | tf_op jit(solution)/shard_map/ppermute | solution.py:155
  46.0 19.6 %collective-permute-start.15 = (bf16[64,4096]{1,0:T(8,128)(2,1)S(1)}, bf16[64,4096]{1,0:T(8,128)(2,1)S(1)}, u32[]{:S(2)}, u32[]{:S(2)}) collective-permute-start(bf16[64,4096]{1,0:T(8,128)(2,1)S(1)} %get-tuple-element.27.refs_4_), channel_id=1, source_target_pairs={{0,4},{2,6},{8,12},{10,14},{16,20},{18,22},{24,28},{26,30},{1,5},{... | collective-permute-start | bytes 1572872 | tf_op jit(solution)/shard_map/ppermute | solution.py:155
  47.4 6.9 %collective-permute-start.11 = (bf16[64,1024]{1,0:T(8,128)(2,1)S(1)}, bf16[64,1024]{1,0:T(8,128)(2,1)S(1)}, u32[]{:S(2)}, u32[]{:S(2)}) collective-permute-start(bf16[64,1024]{1,0:T(8,128)(2,1)S(1)} %get-tuple-element.24.refs_0_), channel_id=1, source_target_pairs={{0,2},{2,0},{8,10},{10,8},{16,18},{18,16},{24,26},{26,24},{1,3},{3... | collective-permute-start | bytes 393224 | tf_op jit(solution)/shard_map/ppermute | solution.py:166
  55.2 5.4 %collective-permute-start.14 = (bf16[64,1024]{1,0:T(8,128)(2,1)S(1)}, bf16[64,1024]{1,0:T(8,128)(2,1)S(1)}, u32[]{:S(2)}, u32[]{:S(2)}) collective-permute-start(bf16[64,1024]{1,0:T(8,128)(2,1)S(1)} %get-tuple-element.26.refs_0_), channel_id=1, source_target_pairs={{0,6},{2,4},{8,14},{10,12},{16,22},{18,20},{24,30},{26,28},{1,7},{... | collective-permute-start | bytes 393224 | tf_op jit(solution)/shard_map/ppermute | solution.py:155
  56.5 5.5 %collective-permute-start.13 = (bf16[64,1024]{1,0:T(8,128)(2,1)S(1)}, bf16[64,1024]{1,0:T(8,128)(2,1)S(1)}, u32[]{:S(2)}, u32[]{:S(2)}) collective-permute-start(bf16[64,1024]{1,0:T(8,128)(2,1)S(1)} %get-tuple-element.26.refs_0_), channel_id=1, source_target_pairs={{0,4},{2,6},{8,12},{10,14},{16,20},{18,22},{24,28},{26,30},{1,5},{... | collective-permute-start | bytes 393224 | tf_op jit(solution)/shard_map/ppermute | solution.py:155
  57.8 7.7 %collective-permute-start.12 = (bf16[64,1024]{1,0:T(8,128)(2,1)S(1)}, bf16[64,1024]{1,0:T(8,128)(2,1)S(1)}, u32[]{:S(2)}, u32[]{:S(2)}) collective-permute-start(bf16[64,1024]{1,0:T(8,128)(2,1)S(1)} %get-tuple-element.26.refs_0_), channel_id=1, source_target_pairs={{0,2},{2,0},{8,10},{10,8},{16,18},{18,16},{24,26},{26,24},{1,3},{3... | collective-permute-start | bytes 393224 | tf_op jit(solution)/shard_map/ppermute | solution.py:166
  67.0 5.0 %collective-permute-start.16 = (bf16[64,1024]{1,0:T(8,128)(2,1)S(1)}, bf16[64,1024]{1,0:T(8,128)(2,1)S(1)}, u32[]{:S(2)}, u32[]{:S(2)}) collective-permute-start(bf16[64,1024]{1,0:T(8,128)(2,1)S(1)} %shard_map.53.refs_0_), channel_id=1, source_target_pairs={{0,2},{2,0},{4,6},{6,4},{8,10},{10,8},{12,14},{14,12},{16,18},{18,... | collective-permute-start | bytes 393224 | tf_op jit(solution)/shard_map/ppermute | solution.py:166

commit v7 on v6

v7 whole, which is shorter than its diff:
```python
import functools
import jax
import jax.numpy as jnp
from jax import lax
from jax.experimental import pallas as pl
from jax.experimental.pallas import tpu as pltpu
from jax.sharding import PartitionSpec as P

F32 = jnp.float32
BF16 = jnp.bfloat16


def upper_depth(leaf, top):
    return top - 1 - sum(((leaf + 1) % 2**power == 0).astype(jnp.int32) for power in range(1, top + 1))


def first_kernel(right_ref, inverse_ref, cast_ref, inverse_out, staged, semaphores):
    weights = pltpu.make_async_copy(inverse_ref.at[1], inverse_out, semaphores.at[0])
    values = pltpu.make_async_copy(right_ref.at[1], staged, semaphores.at[1])
    values.start()
    weights.start()
    values.wait()
    cast_ref[...] = staged[...].astype(BF16)
    weights.wait()


def load_kernel(after_ref, right_ref, lower_ref, right_out, lower_out, semaphores):
    pairs = [(lower_ref.at[1], lower_out), (right_ref, right_out)]
    copies = [pltpu.make_async_copy(a, b, semaphores.at[i]) for i, (a, b) in enumerate(pairs)]
    for copy in copies:
        copy.start()
    for copy in copies:
        copy.wait()


def place_pieces(piece_refs, target_ref, start):
    rows = len(piece_refs)
    width = piece_refs[0].shape[1]
    own = lax.axis_index("rows")
    for shift, piece_ref in enumerate(piece_refs):
        source = lax.rem(own - shift + rows, rows)
        target_ref[:, pl.ds(pl.multiple_of(start + source * width, width), width)] = piece_ref[...]


def offset_kernel(top, level, rows, plan, fetch, block_rows_ref, right_ref, lower_ref, *refs):
    leaf = lax.axis_index("leaf")
    slot = 0 if level == top else 1
    pieces = [refs[:rows], refs[rows:2 * rows]]
    if fetch:
        *refs, far_ref, reduced_ref, near_ref, joined, numbers, semaphores, picked = refs
        load = pltpu.make_async_copy(far_ref.at[0], near_ref, semaphores.at[1])
        load.start()
    else:
        *refs, reduced_ref, joined, numbers, semaphores, picked = refs
    extra = refs[2 * rows:]
    width = right_ref.shape[2]
    listed = pltpu.make_async_copy(block_rows_ref, numbers, semaphores.at[0])
    listed.start()
    reach = 2 ** (top - level - 1) if level < top else 1
    first = leaf % 2 == 0 if level == top else ((leaf + 1) // reach) % 4 == 1
    before = (level - 1) * rows * width
    for which, wanted in enumerate((first, jnp.logical_not(first))):
        @pl.when(wanted)
        def _():
            if plan == "crossed":
                place_pieces(pieces[1 - which], joined, 0)
            elif before:
                joined[:, :before] = extra[which][...]
            place_pieces(pieces[which], joined, before)
    blocks, block_width = lower_ref.shape[:2]
    highest = joined.shape[1] // block_width - 1
    listed.wait()
    for index in range(blocks):
        number = jnp.clip(numbers[slot, index], 0, highest)
        column = pl.multiple_of(number * block_width, block_width)
        picked[:, index * block_width:(index + 1) * block_width] = joined[:, pl.ds(column, block_width)]
    weights = lower_ref[...].reshape(blocks * block_width, width)
    offset = jnp.dot(picked[...], weights, preferred_element_type=F32)
    reduced_ref[...] = (right_ref[slot] - offset).astype(BF16)
    if plan == "held":
        @pl.when(upper_depth(leaf, top) == 0)
        def _():
            reduced_ref[...] = extra[0][...]

    if fetch:
        load.wait()


def apply_inverse(cores, piece_refs, inverse_refs, joined, store):
    quarter = inverse_refs[0].shape[-1]
    place_pieces(piece_refs, joined, 0)
    own = lax.axis_index("rhs")
    for turn, inverse_ref in enumerate(inverse_refs):
        total = jnp.dot(joined[...], inverse_ref[...], preferred_element_type=F32)
        core = lax.rem(own - turn + cores, cores)
        store(pl.ds(pl.multiple_of(core * quarter, quarter), quarter), total)


def solve_kernel(top, depth, rows, cores, plan, fetch, *refs):
    piece_refs = refs[:rows]
    inverse_refs = refs[rows:rows + cores]
    before_ref = refs[rows + cores] if depth > 0 else None
    held_ref = refs[rows + cores + 1] if plan == "held" else None
    if fetch:
        far_ref, rounded_ref, solved_ref, near_ref, joined, semaphore = refs[-6:]
        load = pltpu.make_async_copy(far_ref.at[0], near_ref, semaphore)
        load.start()
    else:
        rounded_ref, solved_ref, joined = refs[-3:]
    leaf = lax.axis_index("leaf")
    active = upper_depth(leaf, top) == depth

    def store(columns, total):
        rounded_ref[:, columns] = total.astype(BF16)
        before = jnp.zeros_like(total) if before_ref is None else before_ref[:, columns]
        solved_ref[:, columns] = jnp.where(active, total, before)

    apply_inverse(cores, piece_refs, inverse_refs, joined, store)
    if plan == "held":
        @pl.when(upper_depth(leaf, top) == 0)
        def _():
            rounded_ref[...] = held_ref[...]

        @pl.when(leaf == lax.axis_size("leaf") - 1)
        def _():
            rounded_ref[...] = piece_refs[1][...]

    if fetch:
        load.wait()


def last_kernel(rows, cores, *refs):
    piece_refs = refs[:rows]
    inverse_refs = refs[rows:rows + cores]
    before_ref, out_ref, joined, staged, semaphores = refs[rows + cores:]
    copies = [pltpu.make_async_copy(before_ref, out_ref.at[1], semaphores.at[0])]
    copies[0].start()

    def store(columns, total):
        staged[:, columns] = total
        copy = pltpu.make_async_copy(staged.at[:, columns], out_ref.at[0, :, columns], semaphores.at[len(copies)])
        copy.start()
        copies.append(copy)

    apply_inverse(cores, piece_refs, inverse_refs, joined, store)
    for copy in copies:
        copy.wait()


WHOLE = pl.BlockSpec(memory_space=pltpu.VMEM)
FAR = pl.BlockSpec(memory_space=pltpu.HBM)


def call(kernel, near, far, outs, scratch=(), flops=0):
    several = len(outs) > 1
    size = sum(a.size * a.dtype.itemsize for a in [*near, *far])
    near = [pltpu.with_memory_space_constraint(a, pltpu.VMEM) for a in near]
    far = [pltpu.with_memory_space_constraint(a, pltpu.HBM) for a in far]
    specs = [FAR if getattr(o, "memory_space", None) == pltpu.HBM else WHOLE for o in outs]
    return pl.pallas_call(
        kernel,
        in_specs=[WHOLE] * len(near) + [FAR] * len(far),
        out_specs=specs if several else specs[0],
        out_shape=list(outs) if several else outs[0],
        scratch_shapes=list(scratch),
        cost_estimate=pl.CostEstimate(flops=flops, bytes_accessed=size, transcendentals=0),
        compiler_params=pltpu.CompilerParams(vmem_limit_bytes=8 * 2**20),
    )(*near, *far)


def local(right_side, inverse_diag, lower_blocks, block_rows):
    leafs, rows, cores = (lax.axis_size(name) for name in ("leaf", "rows", "rhs"))
    top = leafs.bit_length() - 1
    count, width = right_side.shape[1:]
    full_width = rows * width
    places = ("leaf", "rows")

    def send(value, hops, shift):
        pairs = [(a * rows + r, b * rows + (r + shift) % rows) for a, b in hops for r in range(rows)]
        return lax.ppermute(value, places, pairs)

    def spread(value, hops):
        return [send(value, hops, shift) for shift in range(rows)]

    def rows_of(value, swaps=()):
        trading = dict([*swaps, *((b, a) for a, b in swaps)])
        arrived = [value]
        for shift in range(1, rows):
            pairs = [(h * rows + r, trading[h] * rows + r) if h in trading and shift == 1 else
                     (h * rows + r, h * rows + (r + shift) % rows) for h in range(leafs) for r in range(rows)]
            arrived.append(lax.ppermute(value, places, pairs))
        return arrived

    def ring(value, stops):
        after = dict(zip(stops, [*stops[1:], stops[0]]))
        pairs = [(h * rows + r, after[h] * rows + r if h in after else h * rows + (r + 1) % rows)
                 for h in range(leafs) for r in range(rows)]
        return lax.ppermute(value, places, pairs)

    def core_columns(own):
        turns = range(1, cores)
        return [own] + [lax.ppermute(own, "rhs", [(c, (c + t) % cores) for c in range(cores)]) for t in turns]

    def holders(depth):
        return [(2 * p + 1) * 2 ** (top - depth - 1) - 1 for p in range(2**depth)]

    near = pltpu.VMEM
    half = near((count, width), BF16)
    half_f32 = near((count, width), F32)
    joined = near((count, full_width), BF16)
    work = 2 * count * full_width * width
    semaphores = lambda n: pltpu.SemaphoreType.DMA((n,))

    crossing = top == 3 and rows == 2
    spare = leafs - 1
    square = near(inverse_diag.shape[1:], BF16)
    blocks = near(lower_blocks.shape[1:], BF16)
    reduced, own_columns = call(
        first_kernel, [], [right_side, inverse_diag], [half, square], [near((count, width), F32), semaphores(2)])
    inverses = core_columns(own_columns)
    gathered = rows_of(reduced)
    right, lower = call(
        load_kernel, [reduced], [right_side, lower_blocks], [near(right_side.shape, F32), blocks], [semaphores(2)])
    solved = None
    kept = []
    for depth in range(top + 1):
        held = crossing and depth == 1
        crossed = crossing and depth == 2
        if depth > 0:
            all_joined = near((count, depth * full_width), BF16)
            fetched = [pltpu.SMEM(block_rows.shape, jnp.int32), semaphores(2), joined]
            plan = "held" if held else "crossed" if crossed else "plain"
            kernel = functools.partial(offset_kernel, top, depth, rows, plan, depth == 1)
            arrays = [block_rows, right, kept[0] if depth == top else lower, *lefts, *rights, *older]
            arrays += ([rounded] if held else []) + ([] if depth == top else kept)
            passes = depth == top - 1 or (depth < top and not crossing)
            outs = [half] + ([blocks] if depth == 1 else []) + ([all_joined] if passes else [])
            scratch = ([] if passes else [all_joined]) + fetched
            reduced = call(kernel, arrays, [lower_blocks] if depth == 1 else [], outs, scratch, work)
            if passes:
                *reduced, mine = reduced
                reduced = reduced if depth == 1 else reduced[0]
            if depth == 1:
                reduced, lower_last = reduced
                kept = [lower_last]
            gathered = rows_of(reduced, [(h, spare) for h in holders(0)] if held else ())
        if depth == top:
            pieces = [near((count, width), F32), semaphores(cores + 1)]
            return call(functools.partial(last_kernel, rows, cores), [*gathered, *kept[1:], solved], [],
                        [pltpu.HBM(right_side.shape, F32)], [joined, *pieces], work)
        here = holders(depth)
        older = []
        if depth + 1 < top:
            reach = 2 ** (top - depth - 2)
            ways = [[(h, h - reach) for h in here], [(h, h + reach) for h in here]]
            if held:
                tops = [*holders(0), spare]
                ways = [ways[0] + [(h, h - reach) for h in tops], ways[1] + [(h, h - 3 * reach) for h in tops]]
            elif depth > 0:
                older = [send(mine, way, 0) for way in ways]
        else:
            over = [(h, h + 1) for h in here]
            older = [mine, send(mine, over, 0)]
        kernel = functools.partial(solve_kernel, top, depth, rows, cores, "held" if held else "plain", depth == 1)
        arrays = [*gathered, *inverses] + ([solved] if depth else []) + ([rounded] if held else []) + kept
        if depth == 1:
            rounded, solved, own_last = call(
                kernel, arrays, [inverse_diag], [half, half_f32, square], [joined, pltpu.SemaphoreType.DMA(())], work)
            kept += core_columns(own_last)
        else:
            rounded, solved = call(kernel, arrays, [], [half, half_f32], [joined], work)
        if crossing and depth == 0:
            (root,) = here
            cross = [[send(rounded, way, shift) for way in ways[::-1]] for shift in range(1, rows)]
            rights = [ring(rounded, [root, root + reach, root + 1])]
            lefts = [ring(rounded, [root, root - reach, root - 1])]
            rights += [pair[0] for pair in cross]
            lefts += [pair[1] for pair in cross]
        elif depth + 1 < top:
            rights, lefts = [spread(rounded, way) for way in ways[::-1]]
        else:
            rights = spread(rounded, over)
            lefts = rows_of(rounded)


def solution(mesh):
    return jax.shard_map(
        local,
        mesh=mesh,
        in_specs=(
            P("leaf", "rhs", "rows"),
            P("leaf", None, ("rows", "rhs")),
            P("leaf", None, None, "rows"),
            P("leaf", None),
        ),
        out_specs=P("leaf", "rhs", "rows"),
        check_vma=False,
    )
```

time: 74.1 us -> 78.1 us (1.054)
  waiting for transfers between devices: 38.8 us -> 43.1 us
  Pallas kernels: 15.1 us -> 14.1 us
  starting transfers between devices: 19.5 us -> 20.4 us
    ppermute x5, waiting for transfers between devices: 12.1 us -> 16.7 us  [rows_of(): arrived.append(lax.ppermute(value, places, pairs))]
    ppermute x0 -> x2, waiting for transfers between devices: none -> 2.95 us  [ring(): return lax.ppermute(value, places, pairs)]
    ppermute x11 -> x9, waiting for transfers between devices: 26.3 us -> 23.4 us  [send(): return lax.ppermute(value, places, pairs)]
    ppermute x0 -> x2, starting transfers between devices: none -> 2.15 us  [ring(): return lax.ppermute(value, places, pairs)]
    ppermute x11 -> x9, starting transfers between devices: 11.9 us -> 10.7 us  [send(): return lax.ppermute(value, places, pairs)]
    pallas_call x9, Pallas kernels: 15.1 us -> 14.1 us  [call(): pl.pallas_call(kernel, in_specs=[WHOLE] * len(near) + [FAR] * len(far), o...]
  transfers between devices with their start and end apart: 17 -> 18, of which waited for: 10 -> 12; matrix products, arithmetic and copies ran while one was open for 0% -> 0% of each run, Pallas kernels for 9% -> 4%
where the time goes in v7:
time: 78.1 us; the launch traced here: 77.7 us
  waiting for transfers between devices  43.1 us (55%)
  starting transfers between devices  20.4 us (26%)
  Pallas kernels  14.1 us (18%)
    ppermute x9, waiting for transfers between devices, send(): return lax.ppermute(value, places, pairs)  23.4 us
    ppermute x5, waiting for transfers between devices, rows_of(): arrived.append(lax.ppermute(value, places, pairs))  16.7 us
    pallas_call x9, Pallas kernels, call(): pl.pallas_call(kernel, in_specs=[WHOLE] * len(near) + [FAR] * len(far), o...  14.1 us
    ppermute x9, starting transfers between devices, send(): return lax.ppermute(value, places, pairs)  10.7 us
    ppermute x5, starting transfers between devices, rows_of(): arrived.append(lax.ppermute(value, places, pairs))  6.92 us
    ppermute x2, waiting for transfers between devices, ring(): return lax.ppermute(value, places, pairs)  2.95 us
    ppermute x2, starting transfers between devices, ring(): return lax.ppermute(value, places, pairs)  2.15 us
  transfers between devices with their start and end apart: 18, of which 12 were waited for; matrix products, arithmetic and copies ran while one was open for 0% of the time, Pallas kernels for 4%

profile of v7, /device:TPU:0, one launch (start us, length us, event | category | flops | bytes accessed | tf_op | source)
XLA Modules:
  0.0 77.7 jit_solution(2913501798338486225)
XLA Ops:
  0.0 1.7 %shard_map.46 = (bf16[64,1024]{1,0:T(8,128)(2,1)S(1)}, bf16[2048,512]{1,0:T(8,128)(2,1)S(1)}) custom-call(f32[2,64,1024]{2,1,0:T(8,128)} %right_ref.3, bf16[2,2048,512]{2,1,0:T(8,128)(2,1)} %refs_7_.1), custom_call_target="tpu_custom_call" | custom-call | bytes 4718592 | tf_op jit(solution)/shard_map/pallas_call | solution.py:160
  1.7 0.5 collective-permute-start.1
  2.2 2.6 %collective-permute-start = (bf16[64,1024]{1,0:T(8,128)(2,1)S(1)}, bf16[64,1024]{1,0:T(8,128)(2,1)S(1)}, u32[]{:S(2)}, u32[]{:S(2)}) collective-permute-start(bf16[64,1024]{1,0:T(8,128)(2,1)S(1)} %get-tuple-element.20.after_ref.refs_0_), channel_id=1, source_target_pairs={{0,2},{2,0},{4,6},{6,4},{8,10},{10,8},{12,14},{14,12},{16,18},{18,... | collective-permute-start | bytes 393224 | tf_op jit(solution)/shard_map/ppermute | solution.py:191
  4.8 4.1 %collective-permute-done.refs_1_ = bf16[64,1024]{1,0:T(8,128)(2,1)S(1)} collective-permute-done((bf16[64,1024]{1,0:T(8,128)(2,1)S(1)}, bf16[64,1024]{1,0:T(8,128)(2,1)S(1)}, u32[]{:S(2)}, u32[]{:S(2)}) %collective-permute-start) | collective-permute-done | bytes 131104 | tf_op jit(solution)/shard_map/ppermute | solution.py:191
  8.9 0.0 collective-permute-done.1.refs_3_
  8.9 0.9 %shard_map.48 = (bf16[64,1024]{1,0:T(8,128)(2,1)S(1)}, f32[64,1024]{1,0:T(8,128)S(1)}) custom-call(bf16[64,1024]{1,0:T(8,128)(2,1)S(1)} %get-tuple-element.20.after_ref.refs_0_, bf16[64,1024]{1,0:T(8,128)(2,1)S(1)} %collective-permute-done.refs_1_, bf16[2048,512]{1,0:T(8,128)(2,1)S(1)} %get-tuple-element.23.refs_2_, ...), custom_call_target="tpu_custom_call" | custom-call | flops 268435456 | bytes 4456448 | tf_op jit(solution)/shard_map/pallas_call | solution.py:160
  9.8 0.0 copy-start
  9.8 0.7 collective-permute-start.5
  10.5 1.8 %collective-permute-start.4 = (bf16[64,1024]{1,0:T(8,128)(2,1)S(1)}, bf16[64,1024]{1,0:T(8,128)(2,1)S(1)}, u32[]{:S(2)}, u32[]{:S(2)}) collective-permute-start(bf16[64,1024]{1,0:T(8,128)(2,1)S(1)} %get-tuple-element.24.refs_4_.refs_5_), channel_id=1, source_target_pairs={{0,2},{2,0},{4,6},{6,4},{8,10},{10,8},{12,20},{14,22},{16,12},{18,... | collective-permute-start | bytes 393224 | tf_op jit(solution)/shard_map/ppermute | solution.py:198
  12.3 0.7 collective-permute-start.3
  13.0 0.3 collective-permute-start.2
  13.3 2.3 %shard_map.47 = (f32[2,64,1024]{2,1,0:T(8,128)S(1)}, bf16[16,128,1024]{2,1,0:T(8,128)(2,1)S(1)}) custom-call(bf16[64,1024]{1,0:T(8,128)(2,1)S(1)} %get-tuple-element.20.after_ref.refs_0_, f32[2,64,1024]{2,1,0:T(8,128)} %right_ref.3, bf16[2,16,128,1024]{3,2,1,0:T(8,128)(2,1)} %refs_5_.1), custom_call_target="tpu_custom_call" | custom-call | bytes 9043968 | tf_op jit(solution)/shard_map/pallas_call | solution.py:160
  15.6 0.0 collective-permute-done.5.refs_3_
  15.6 0.9 %collective-permute-done.4.refs_2_ = bf16[64,1024]{1,0:T(8,128)(2,1)S(1)} collective-permute-done((bf16[64,1024]{1,0:T(8,128)(2,1)S(1)}, bf16[64,1024]{1,0:T(8,128)(2,1)S(1)}, u32[]{:S(2)}, u32[]{:S(2)}) %collective-permute-start.4) | collective-permute-done | bytes 131104 | tf_op jit(solution)/shard_map/ppermute | solution.py:198
  16.6 0.0 collective-permute-done.3.refs_1_
  16.6 2.0 %collective-permute-done.2.refs_0_ = bf16[64,1024]{1,0:T(8,128)(2,1)S(1)} collective-permute-done((bf16[64,1024]{1,0:T(8,128)(2,1)S(1)}, bf16[64,1024]{1,0:T(8,128)(2,1)S(1)}, u32[]{:S(2)}, u32[]{:S(2)}) %collective-permute-start.2) | collective-permute-done | bytes 131104 | tf_op jit(solution)/shard_map/ppermute | solution.py:198
  18.6 0.0 copy-done
  18.6 2.2 %shard_map.49 = (bf16[64,1024]{1,0:T(8,128)(2,1)S(1)}, bf16[16,128,1024]{2,1,0:T(8,128)(2,1)S(1)}) custom-call(s32[2,16]{1,0:T(2,128)S(1)} %copy-done, f32[2,64,1024]{2,1,0:T(8,128)S(1)} %get-tuple-element.21.right_ref, bf16[16,128,1024]{2,1,0:T(8,128)(2,1)S(1)} %get-tuple-element.22.lower_ref, bf16[64,1024]{1,0:T(8,128)(2,1)S(1)} %collective-permute-done.2.refs_0_, ...), custom_call_target="tpu_custom_call" | custom-call | flops 268435456 | bytes 13762688 | tf_op jit(solution)/shard_map/pallas_call | solution.py:160
  20.8 1.6 %collective-permute-start.6 = (bf16[64,1024]{1,0:T(8,128)(2,1)S(1)}, bf16[64,1024]{1,0:T(8,128)(2,1)S(1)}, u32[]{:S(2)}, u32[]{:S(2)}) collective-permute-start(bf16[64,1024]{1,0:T(8,128)(2,1)S(1)} %get-tuple-element.26.refs_0_), channel_id=1, source_target_pairs={{0,2},{2,0},{4,6},{6,4},{8,10},{10,8},{12,28},{14,30},{16,18},{18,... | collective-permute-start | bytes 393224 | tf_op jit(solution)/shard_map/ppermute | solution.py:191
  22.4 3.4 %collective-permute-done.6.refs_1_ = bf16[64,1024]{1,0:T(8,128)(2,1)S(1)} collective-permute-done((bf16[64,1024]{1,0:T(8,128)(2,1)S(1)}, bf16[64,1024]{1,0:T(8,128)(2,1)S(1)}, u32[]{:S(2)}, u32[]{:S(2)}) %collective-permute-start.6) | collective-permute-done | bytes 131104 | tf_op jit(solution)/shard_map/ppermute | solution.py:191
  25.8 1.7 %shard_map.50 = (bf16[64,1024]{1,0:T(8,128)(2,1)S(1)}, f32[64,1024]{1,0:T(8,128)S(1)}, bf16[2048,512]{1,0:T(8,128)(2,1)S(1)}) custom-call(bf16[64,1024]{1,0:T(8,128)(2,1)S(1)} %get-tuple-element.26.refs_0_, bf16[64,1024]{1,0:T(8,128)(2,1)S(1)} %collective-permute-done.6.refs_1_, bf16[2048,512]{1,0:T(8,128)(2,1)S(1)} %get-tuple-element.23.refs_2_, ...), custom_call_target="tpu_custom_call" | custom-call | flops 268435456 | bytes 13238272 | tf_op jit(solution)/shard_map/pallas_call | solution.py:160
  27.6 0.1 collective-permute-start.11
  27.7 1.3 %collective-permute-start.10 = (bf16[64,1024]{1,0:T(8,128)(2,1)S(1)}, bf16[64,1024]{1,0:T(8,128)(2,1)S(1)}, u32[]{:S(2)}, u32[]{:S(2)}) collective-permute-start(bf16[64,1024]{1,0:T(8,128)(2,1)S(1)} %get-tuple-element.28), channel_id=1, source_target_pairs={{4,10},{6,8},{20,26},{22,24},{12,2},{14,0},{28,18},{30,16},{5,11},... | collective-permute-start | bytes 393224 | tf_op jit(solution)/shard_map/ppermute | solution.py:180
  29.0 1.3 %collective-permute-start.9 = (bf16[64,1024]{1,0:T(8,128)(2,1)S(1)}, bf16[64,1024]{1,0:T(8,128)(2,1)S(1)}, u32[]{:S(2)}, u32[]{:S(2)}) collective-permute-start(bf16[64,1024]{1,0:T(8,128)(2,1)S(1)} %get-tuple-element.28), channel_id=1, source_target_pairs={{4,8},{6,10},{20,24},{22,26},{12,0},{14,2},{28,16},{30,18},{5,9},{... | collective-permute-start | bytes 393224 | tf_op jit(solution)/shard_map/ppermute | solution.py:180
  30.3 1.3 %collective-permute-start.8 = (bf16[64,1024]{1,0:T(8,128)(2,1)S(1)}, bf16[64,1024]{1,0:T(8,128)(2,1)S(1)}, u32[]{:S(2)}, u32[]{:S(2)}) collective-permute-start(bf16[64,1024]{1,0:T(8,128)(2,1)S(1)} %get-tuple-element.28), channel_id=1, source_target_pairs={{4,2},{6,0},{20,18},{22,16},{12,10},{14,8},{28,26},{30,24},{5,3},{... | collective-permute-start | bytes 393224 | tf_op jit(solution)/shard_map/ppermute | solution.py:180
  31.6 1.3 %collective-permute-start.7 = (bf16[64,1024]{1,0:T(8,128)(2,1)S(1)}, bf16[64,1024]{1,0:T(8,128)(2,1)S(1)}, u32[]{:S(2)}, u32[]{:S(2)}) collective-permute-start(bf16[64,1024]{1,0:T(8,128)(2,1)S(1)} %get-tuple-element.28), channel_id=1, source_target_pairs={{4,0},{6,2},{20,16},{22,18},{12,8},{14,10},{28,24},{30,26},{5,1},{... | collective-permute-start | bytes 393224 | tf_op jit(solution)/shard_map/ppermute | solution.py:180
  32.9 8.6 %collective-permute-done.10.refs_3_ = bf16[64,1024]{1,0:T(8,128)(2,1)S(1)} collective-permute-done((bf16[64,1024]{1,0:T(8,128)(2,1)S(1)}, bf16[64,1024]{1,0:T(8,128)(2,1)S(1)}, u32[]{:S(2)}, u32[]{:S(2)}) %collective-permute-start.10) | collective-permute-done | bytes 131104 | tf_op jit(solution)/shard_map/ppermute | solution.py:180
  41.4 2.7 %collective-permute-done.9.refs_2_ = bf16[64,1024]{1,0:T(8,128)(2,1)S(1)} collective-permute-done((bf16[64,1024]{1,0:T(8,128)(2,1)S(1)}, bf16[64,1024]{1,0:T(8,128)(2,1)S(1)}, u32[]{:S(2)}, u32[]{:S(2)}) %collective-permute-start.9) | collective-permute-done | bytes 131104 | tf_op jit(solution)/shard_map/ppermute | solution.py:180
  44.2 2.7 %collective-permute-done.8.refs_1_ = bf16[64,1024]{1,0:T(8,128)(2,1)S(1)} collective-permute-done((bf16[64,1024]{1,0:T(8,128)(2,1)S(1)}, bf16[64,1024]{1,0:T(8,128)(2,1)S(1)}, u32[]{:S(2)}, u32[]{:S(2)}) %collective-permute-start.8) | collective-permute-done | bytes 131104 | tf_op jit(solution)/shard_map/ppermute | solution.py:180
  46.8 2.8 %collective-permute-done.7.refs_0_ = bf16[64,1024]{1,0:T(8,128)(2,1)S(1)} collective-permute-done((bf16[64,1024]{1,0:T(8,128)(2,1)S(1)}, bf16[64,1024]{1,0:T(8,128)(2,1)S(1)}, u32[]{:S(2)}, u32[]{:S(2)}) %collective-permute-start.7) | collective-permute-done | bytes 131104 | tf_op jit(solution)/shard_map/ppermute | solution.py:180
  49.7 0.0 collective-permute-done.11.refs_6_.refs_7_.refs_3_
  49.7 1.4 %shard_map.51 = (bf16[64,1024]{1,0:T(8,128)(2,1)S(1)}, bf16[64,4096]{1,0:T(8,128)(2,1)S(1)}) custom-call(s32[2,16]{1,0:T(2,128)S(1)} %copy-done, f32[2,64,1024]{2,1,0:T(8,128)S(1)} %get-tuple-element.21.right_ref, bf16[16,128,1024]{2,1,0:T(8,128)(2,1)S(1)} %get-tuple-element.22.lower_ref, bf16[64,1024]{1,0:T(8,128)(2,1)S(1)} %collective-permute-done.7.refs_0_, ...), custom_call_target="tpu_custom_call" | custom-call | flops 268435456 | bytes 13631616 | tf_op jit(solution)/shard_map/pallas_call | solution.py:160
  51.1 1.5 %collective-permute-start.16 = (bf16[64,4096]{1,0:T(8,128)(2,1)S(1)}, bf16[64,4096]{1,0:T(8,128)(2,1)S(1)}, u32[]{:S(2)}, u32[]{:S(2)}) collective-permute-start(bf16[64,4096]{1,0:T(8,128)(2,1)S(1)} %get-tuple-element.33.refs_4_), channel_id=1, source_target_pairs={{0,4},{2,6},{8,12},{10,14},{16,20},{18,22},{24,28},{26,30},{1,5},{... | collective-permute-start | bytes 1572872 | tf_op jit(solution)/shard_map/ppermute | solution.py:180
  52.6 0.6 collective-permute-start.12
  53.2 4.8 %collective-permute-done.12.refs_1_ = bf16[64,1024]{1,0:T(8,128)(2,1)S(1)} collective-permute-done((bf16[64,1024]{1,0:T(8,128)(2,1)S(1)}, bf16[64,1024]{1,0:T(8,128)(2,1)S(1)}, u32[]{:S(2)}, u32[]{:S(2)}) %collective-permute-start.12) | collective-permute-done | bytes 131104 | tf_op jit(solution)/shard_map/ppermute | solution.py:191
  58.0 0.9 %shard_map.52 = (bf16[64,1024]{1,0:T(8,128)(2,1)S(1)}, f32[64,1024]{1,0:T(8,128)S(1)}) custom-call(bf16[64,1024]{1,0:T(8,128)(2,1)S(1)} %get-tuple-element.30.refs_0_, bf16[64,1024]{1,0:T(8,128)(2,1)S(1)} %collective-permute-done.12.refs_1_, bf16[2048,512]{1,0:T(8,128)(2,1)S(1)} %get-tuple-element.23.refs_2_, ...), custom_call_target="tpu_custom_call" | custom-call | flops 268435456 | bytes 13107200 | tf_op jit(solution)/shard_map/pallas_call | solution.py:160
  58.9 1.4 %collective-permute-start.15 = (bf16[64,1024]{1,0:T(8,128)(2,1)S(1)}, bf16[64,1024]{1,0:T(8,128)(2,1)S(1)}, u32[]{:S(2)}, u32[]{:S(2)}) collective-permute-start(bf16[64,1024]{1,0:T(8,128)(2,1)S(1)} %get-tuple-element.32.refs_0_), channel_id=1, source_target_pairs={{0,6},{2,4},{8,14},{10,12},{16,22},{18,20},{24,30},{26,28},{1,7},{... | collective-permute-start | bytes 393224 | tf_op jit(solution)/shard_map/ppermute | solution.py:180
  60.3 1.3 %collective-permute-start.14 = (bf16[64,1024]{1,0:T(8,128)(2,1)S(1)}, bf16[64,1024]{1,0:T(8,128)(2,1)S(1)}, u32[]{:S(2)}, u32[]{:S(2)}) collective-permute-start(bf16[64,1024]{1,0:T(8,128)(2,1)S(1)} %get-tuple-element.32.refs_0_), channel_id=1, source_target_pairs={{0,4},{2,6},{8,12},{10,14},{16,20},{18,22},{24,28},{26,30},{1,5},{... | collective-permute-start | bytes 393224 | tf_op jit(solution)/shard_map/ppermute | solution.py:180
  61.6 1.5 %collective-permute-start.13 = (bf16[64,1024]{1,0:T(8,128)(2,1)S(1)}, bf16[64,1024]{1,0:T(8,128)(2,1)S(1)}, u32[]{:S(2)}, u32[]{:S(2)}) collective-permute-start(bf16[64,1024]{1,0:T(8,128)(2,1)S(1)} %get-tuple-element.32.refs_0_), channel_id=1, source_target_pairs={{0,2},{2,0},{4,6},{6,4},{8,10},{10,8},{12,14},{14,12},{16,18},{18,... | collective-permute-start | bytes 393224 | tf_op jit(solution)/shard_map/ppermute | solution.py:191
  63.1 4.5 %collective-permute-done.15.refs_3_ = bf16[64,1024]{1,0:T(8,128)(2,1)S(1)} collective-permute-done((bf16[64,1024]{1,0:T(8,128)(2,1)S(1)}, bf16[64,1024]{1,0:T(8,128)(2,1)S(1)}, u32[]{:S(2)}, u32[]{:S(2)}) %collective-permute-start.15) | collective-permute-done | bytes 131104 | tf_op jit(solution)/shard_map/ppermute | solution.py:180
  67.7 2.1 %collective-permute-done.14.refs_2_ = bf16[64,1024]{1,0:T(8,128)(2,1)S(1)} collective-permute-done((bf16[64,1024]{1,0:T(8,128)(2,1)S(1)}, bf16[64,1024]{1,0:T(8,128)(2,1)S(1)}, u32[]{:S(2)}, u32[]{:S(2)}) %collective-permute-start.14) | collective-permute-done | bytes 131104 | tf_op jit(solution)/shard_map/ppermute | solution.py:180
  69.7 0.0 collective-permute-done.13.refs_1_
  69.7 0.0 collective-permute-done.16.refs_5_
  69.7 1.4 %shard_map.53.refs_0_ = bf16[64,1024]{1,0:T(8,128)(2,1)S(1)} custom-call(s32[2,16]{1,0:T(2,128)S(1)} %copy-done, f32[2,64,1024]{2,1,0:T(8,128)S(1)} %get-tuple-element.21.right_ref, bf16[16,128,1024]{2,1,0:T(8,128)(2,1)S(1)} %get-tuple-element.25.refs_6_.refs_4_.refs_5_.lower_ref, bf16[64,1024]{1,0:T(8,128)(2,1)S(1)} %get-tuple-element.32.refs_0_, ...), custom_call_target="tpu_custom_call" | custom-call | flops 268435456 | bytes 6291584 | tf_op jit(solution)/shard_map/pallas_call | solution.py:160
  71.2 0.6 collective-permute-start.17
  71.8 4.5 %collective-permute-done.17.refs_1_ = bf16[64,1024]{1,0:T(8,128)(2,1)S(1)} collective-permute-done((bf16[64,1024]{1,0:T(8,128)(2,1)S(1)}, bf16[64,1024]{1,0:T(8,128)(2,1)S(1)}, u32[]{:S(2)}, u32[]{:S(2)}) %collective-permute-start.17) | collective-permute-done | bytes 131104 | tf_op jit(solution)/shard_map/ppermute | solution.py:191
  76.2 1.5 %shard_map.54 = f32[2,64,1024]{2,1,0:T(8,128)} custom-call(bf16[64,1024]{1,0:T(8,128)(2,1)S(1)} %shard_map.53.refs_0_, bf16[64,1024]{1,0:T(8,128)(2,1)S(1)} %collective-permute-done.17.refs_1_, bf16[2048,512]{1,0:T(8,128)(2,1)S(1)} %get-tuple-element.29.refs_5_.refs_6_.refs_2_, bf16[2048,512]{1,0:T(8,128)(2,1)S(1)} %collective-permute-done.11.refs_6_.refs_7_.refs_3_, ...), custom_call_target="tpu_custom_call" | custom-call | flops 268435456 | bytes 4718592 | tf_op jit(solution)/shard_map/pallas_call | solution.py:160
Async XLA Ops:
  1.7 7.2 %collective-permute-start.1 = (bf16[2048,512]{1,0:T(8,128)(2,1)S(1)}, bf16[2048,512]{1,0:T(8,128)(2,1)S(1)}, u32[]{:S(2)}, u32[]{:S(2)}) collective-permute-start(bf16[2048,512]{1,0:T(8,128)(2,1)S(1)} %get-tuple-element.23.refs_2_), channel_id=1, source_target_pairs={{0,1},{1,0},{2,3},{3,2},{4,5},{5,4},{6,7},{7,6},{8,9},{9,8},{10,11... | collective-permute-start | bytes 6291464 | tf_op jit(solution)/shard_map/ppermute | solution.py:202
  2.2 6.7 %collective-permute-start = (bf16[64,1024]{1,0:T(8,128)(2,1)S(1)}, bf16[64,1024]{1,0:T(8,128)(2,1)S(1)}, u32[]{:S(2)}, u32[]{:S(2)}) collective-permute-start(bf16[64,1024]{1,0:T(8,128)(2,1)S(1)} %get-tuple-element.20.after_ref.refs_0_), channel_id=1, source_target_pairs={{0,2},{2,0},{4,6},{6,4},{8,10},{10,8},{12,14},{14,12},{16,18},{18,... | collective-permute-start | bytes 393224 | tf_op jit(solution)/shard_map/ppermute | solution.py:191
  9.8 8.8 %copy-start = (s32[2,16]{1,0:T(2,128)S(1)}, s32[2,16]{1,0:T(2,128)}, u32[]{:S(2)}) copy-start(s32[2,16]{1,0:T(2,128)} %block_rows_ref.5) | copy-start | bytes 388
  9.8 5.8 %collective-permute-start.5 = (bf16[64,1024]{1,0:T(8,128)(2,1)S(1)}, bf16[64,1024]{1,0:T(8,128)(2,1)S(1)}, u32[]{:S(2)}, u32[]{:S(2)}) collective-permute-start(bf16[64,1024]{1,0:T(8,128)(2,1)S(1)} %get-tuple-element.24.refs_4_.refs_5_), channel_id=1, source_target_pairs={{12,22},{14,20},{13,23},{15,21}} | collective-permute-start | bytes 393224 | tf_op jit(solution)/shard_map/ppermute | solution.py:180
  10.5 6.1 %collective-permute-start.4 = (bf16[64,1024]{1,0:T(8,128)(2,1)S(1)}, bf16[64,1024]{1,0:T(8,128)(2,1)S(1)}, u32[]{:S(2)}, u32[]{:S(2)}) collective-permute-start(bf16[64,1024]{1,0:T(8,128)(2,1)S(1)} %get-tuple-element.24.refs_4_.refs_5_), channel_id=1, source_target_pairs={{0,2},{2,0},{4,6},{6,4},{8,10},{10,8},{12,20},{14,22},{16,12},{18,... | collective-permute-start | bytes 393224 | tf_op jit(solution)/shard_map/ppermute | solution.py:198
  12.3 4.3 %collective-permute-start.3 = (bf16[64,1024]{1,0:T(8,128)(2,1)S(1)}, bf16[64,1024]{1,0:T(8,128)(2,1)S(1)}, u32[]{:S(2)}, u32[]{:S(2)}) collective-permute-start(bf16[64,1024]{1,0:T(8,128)(2,1)S(1)} %get-tuple-element.24.refs_4_.refs_5_), channel_id=1, source_target_pairs={{12,6},{14,4},{13,7},{15,5}} | collective-permute-start | bytes 393224 | tf_op jit(solution)/shard_map/ppermute | solution.py:180
  13.0 5.6 %collective-permute-start.2 = (bf16[64,1024]{1,0:T(8,128)(2,1)S(1)}, bf16[64,1024]{1,0:T(8,128)(2,1)S(1)}, u32[]{:S(2)}, u32[]{:S(2)}) collective-permute-start(bf16[64,1024]{1,0:T(8,128)(2,1)S(1)} %get-tuple-element.24.refs_4_.refs_5_), channel_id=1, source_target_pairs={{0,2},{2,0},{4,8},{6,10},{8,12},{10,14},{12,4},{14,6},{16,18},{18,... | collective-permute-start | bytes 393224 | tf_op jit(solution)/shard_map/ppermute | solution.py:198
  20.8 5.0 %collective-permute-start.6 = (bf16[64,1024]{1,0:T(8,128)(2,1)S(1)}, bf16[64,1024]{1,0:T(8,128)(2,1)S(1)}, u32[]{:S(2)}, u32[]{:S(2)}) collective-permute-start(bf16[64,1024]{1,0:T(8,128)(2,1)S(1)} %get-tuple-element.26.refs_0_), channel_id=1, source_target_pairs={{0,2},{2,0},{4,6},{6,4},{8,10},{10,8},{12,28},{14,30},{16,18},{18,... | collective-permute-start | bytes 393224 | tf_op jit(solution)/shard_map/ppermute | solution.py:191
  27.6 22.1 %collective-permute-start.11 = (bf16[2048,512]{1,0:T(8,128)(2,1)S(1)}, bf16[2048,512]{1,0:T(8,128)(2,1)S(1)}, u32[]{:S(2)}, u32[]{:S(2)}) collective-permute-start(bf16[2048,512]{1,0:T(8,128)(2,1)S(1)} %get-tuple-element.29.refs_5_.refs_6_.refs_2_), channel_id=1, source_target_pairs={{0,1},{1,0},{2,3},{3,2},{4,5},{5,4},{6,7},{7,6},{8,9},{9,8},{10,11... | collective-permute-start | bytes 6291464 | tf_op jit(solution)/shard_map/ppermute | solution.py:202
  27.7 13.8 %collective-permute-start.10 = (bf16[64,1024]{1,0:T(8,128)(2,1)S(1)}, bf16[64,1024]{1,0:T(8,128)(2,1)S(1)}, u32[]{:S(2)}, u32[]{:S(2)}) collective-permute-start(bf16[64,1024]{1,0:T(8,128)(2,1)S(1)} %get-tuple-element.28), channel_id=1, source_target_pairs={{4,10},{6,8},{20,26},{22,24},{12,2},{14,0},{28,18},{30,16},{5,11},... | collective-permute-start | bytes 393224 | tf_op jit(solution)/shard_map/ppermute | solution.py:180
  29.0 15.2 %collective-permute-start.9 = (bf16[64,1024]{1,0:T(8,128)(2,1)S(1)}, bf16[64,1024]{1,0:T(8,128)(2,1)S(1)}, u32[]{:S(2)}, u32[]{:S(2)}) collective-permute-start(bf16[64,1024]{1,0:T(8,128)(2,1)S(1)} %get-tuple-element.28), channel_id=1, source_target_pairs={{4,8},{6,10},{20,24},{22,26},{12,0},{14,2},{28,16},{30,18},{5,9},{... | collective-permute-start | bytes 393224 | tf_op jit(solution)/shard_map/ppermute | solution.py:180
  30.3 16.6 %collective-permute-start.8 = (bf16[64,1024]{1,0:T(8,128)(2,1)S(1)}, bf16[64,1024]{1,0:T(8,128)(2,1)S(1)}, u32[]{:S(2)}, u32[]{:S(2)}) collective-permute-start(bf16[64,1024]{1,0:T(8,128)(2,1)S(1)} %get-tuple-element.28), channel_id=1, source_target_pairs={{4,2},{6,0},{20,18},{22,16},{12,10},{14,8},{28,26},{30,24},{5,3},{... | collective-permute-start | bytes 393224 | tf_op jit(solution)/shard_map/ppermute | solution.py:180
  31.6 18.1 %collective-permute-start.7 = (bf16[64,1024]{1,0:T(8,128)(2,1)S(1)}, bf16[64,1024]{1,0:T(8,128)(2,1)S(1)}, u32[]{:S(2)}, u32[]{:S(2)}) collective-permute-start(bf16[64,1024]{1,0:T(8,128)(2,1)S(1)} %get-tuple-element.28), channel_id=1, source_target_pairs={{4,0},{6,2},{20,16},{22,18},{12,8},{14,10},{28,24},{30,26},{5,1},{... | collective-permute-start | bytes 393224 | tf_op jit(solution)/shard_map/ppermute | solution.py:180
  51.1 18.6 %collective-permute-start.16 = (bf16[64,4096]{1,0:T(8,128)(2,1)S(1)}, bf16[64,4096]{1,0:T(8,128)(2,1)S(1)}, u32[]{:S(2)}, u32[]{:S(2)}) collective-permute-start(bf16[64,4096]{1,0:T(8,128)(2,1)S(1)} %get-tuple-element.33.refs_4_), channel_id=1, source_target_pairs={{0,4},{2,6},{8,12},{10,14},{16,20},{18,22},{24,28},{26,30},{1,5},{... | collective-permute-start | bytes 1572872 | tf_op jit(solution)/shard_map/ppermute | solution.py:180
  52.6 5.4 %collective-permute-start.12 = (bf16[64,1024]{1,0:T(8,128)(2,1)S(1)}, bf16[64,1024]{1,0:T(8,128)(2,1)S(1)}, u32[]{:S(2)}, u32[]{:S(2)}) collective-permute-start(bf16[64,1024]{1,0:T(8,128)(2,1)S(1)} %get-tuple-element.30.refs_0_), channel_id=1, source_target_pairs={{0,2},{2,0},{4,6},{6,4},{8,10},{10,8},{12,14},{14,12},{16,18},{18,... | collective-permute-start | bytes 393224 | tf_op jit(solution)/shard_map/ppermute | solution.py:191
  58.9 8.8 %collective-permute-start.15 = (bf16[64,1024]{1,0:T(8,128)(2,1)S(1)}, bf16[64,1024]{1,0:T(8,128)(2,1)S(1)}, u32[]{:S(2)}, u32[]{:S(2)}) collective-permute-start(bf16[64,1024]{1,0:T(8,128)(2,1)S(1)} %get-tuple-element.32.refs_0_), channel_id=1, source_target_pairs={{0,6},{2,4},{8,14},{10,12},{16,22},{18,20},{24,30},{26,28},{1,7},{... | collective-permute-start | bytes 393224 | tf_op jit(solution)/shard_map/ppermute | solution.py:180
  60.3 9.5 %collective-permute-start.14 = (bf16[64,1024]{1,0:T(8,128)(2,1)S(1)}, bf16[64,1024]{1,0:T(8,128)(2,1)S(1)}, u32[]{:S(2)}, u32[]{:S(2)}) collective-permute-start(bf16[64,1024]{1,0:T(8,128)(2,1)S(1)} %get-tuple-element.32.refs_0_), channel_id=1, source_target_pairs={{0,4},{2,6},{8,12},{10,14},{16,20},{18,22},{24,28},{26,30},{1,5},{... | collective-permute-start | bytes 393224 | tf_op jit(solution)/shard_map/ppermute | solution.py:180
  61.6 8.1 %collective-permute-start.13 = (bf16[64,1024]{1,0:T(8,128)(2,1)S(1)}, bf16[64,1024]{1,0:T(8,128)(2,1)S(1)}, u32[]{:S(2)}, u32[]{:S(2)}) collective-permute-start(bf16[64,1024]{1,0:T(8,128)(2,1)S(1)} %get-tuple-element.32.refs_0_), channel_id=1, source_target_pairs={{0,2},{2,0},{4,6},{6,4},{8,10},{10,8},{12,14},{14,12},{16,18},{18,... | collective-permute-start | bytes 393224 | tf_op jit(solution)/shard_map/ppermute | solution.py:191
  71.2 5.0 %collective-permute-start.17 = (bf16[64,1024]{1,0:T(8,128)(2,1)S(1)}, bf16[64,1024]{1,0:T(8,128)(2,1)S(1)}, u32[]{:S(2)}, u32[]{:S(2)}) collective-permute-start(bf16[64,1024]{1,0:T(8,128)(2,1)S(1)} %shard_map.53.refs_0_), channel_id=1, source_target_pairs={{0,2},{2,0},{4,6},{6,4},{8,10},{10,8},{12,14},{14,12},{16,18},{18,... | collective-permute-start | bytes 393224 | tf_op jit(solution)/shard_map/ppermute | solution.py:191

commit v8 on v6

--- a/solution.py
+++ b/solution.py
@@ -21,9 +21,9 @@
     cast_ref[...] = staged[...].astype(BF16)
 
 
-def load_kernel(after_ref, right_ref, inverse_ref, lower_ref, right_out, inverse_out, lower_out, semaphores):
-    pairs = [(inverse_ref, inverse_out), (right_ref, right_out), (lower_ref, lower_out)]
-    copies = [pltpu.make_async_copy(a, b, semaphores.at[i]) for i, (a, b) in enumerate(pairs)]
+def load_kernel(count, after_ref, *refs):
+    semaphores = refs[-1]
+    copies = [pltpu.make_async_copy(refs[i], refs[count + i], semaphores.at[i]) for i in range(count)]
     for copy in copies:
         copy.start()
     for copy in copies:
@@ -42,26 +42,47 @@
 def offset_kernel(top, level, rows, plan, block_rows_ref, right_ref, lower_ref, *refs):
     leaf = lax.axis_index("leaf")
     slot = 0 if level == top else 1
-    pieces = [refs[:rows], refs[rows:2 * rows]]
-    extra = refs[2 * rows:-5]
-    reduced_ref, joined, numbers, semaphore, picked = refs[-5:]
+    *refs, reduced_ref, joined, numbers, semaphore, picked = refs
+    if level == top:
+        pieces = [refs[1:2 * rows:2], refs[:2 * rows:2]]
+    else:
+        pieces = [refs[:2 * rows:2][::-1], refs[1:2 * rows:2][::-1]]
+    extra = refs[2 * rows:]
     width = right_ref.shape[2]
-    fetch = pltpu.make_async_copy(block_rows_ref, numbers, semaphore)
-    fetch.start()
+    full = rows * width
+    listed = pltpu.make_async_copy(block_rows_ref, numbers, semaphore)
+    listed.start()
     reach = 2 ** (top - level - 1) if level < top else 1
     first = leaf % 2 == 0 if level == top else ((leaf + 1) // reach) % 4 == 1
-    before = (level - 1) * rows * width
+    before = (level - 1) * full
     for which, wanted in enumerate((first, jnp.logical_not(first))):
         @pl.when(wanted)
         def _():
             if plan == "crossed":
                 place_pieces(pieces[1 - which], joined, 0)
-            elif before:
+            elif plan != "traded" and before:
                 joined[:, :before] = extra[which][...]
             place_pieces(pieces[which], joined, before)
+    if plan == "traded":
+        mine_ref, both_ref, passed_ref, *roots = extra
+
+        @pl.when(leaf % 2 == 0)
+        def _():
+            joined[:, :before] = mine_ref[...]
+
+        for which, place in enumerate((1, 3)):
+            @pl.when((leaf % 4 == 1) & ((leaf + 1) // 2 % 4 == place))
+            def _():
+                place_pieces(roots[which::2][::-1], joined, 0)
+                joined[:, full:before] = both_ref[...]
+
+        @pl.when(leaf % 4 == 3)
+        def _():
+            joined[:, :full] = both_ref[...]
+            joined[:, full:before] = passed_ref[...]
     blocks, block_width = lower_ref.shape[1:3]
     highest = joined.shape[1] // block_width - 1
-    fetch.wait()
+    listed.wait()
     for index in range(blocks):
         number = jnp.clip(numbers[slot, index], 0, highest)
         column = pl.multiple_of(number * block_width, block_width)
@@ -69,8 +90,8 @@
     weights = lower_ref[slot].reshape(blocks * block_width, width)
     offset = jnp.dot(picked[...], weights, preferred_element_type=F32)
     reduced_ref[...] = (right_ref[slot] - offset).astype(BF16)
-    if plan == "held":
-        @pl.when(upper_depth(leaf, top) == 0)
+    if plan in ("held", "crossed"):
+        @pl.when(upper_depth(leaf, top) == 0 if plan == "held" else leaf % 2 == 1)
         def _():
             reduced_ref[...] = extra[0][...]
 
@@ -113,13 +134,19 @@
 def last_kernel(rows, cores, *refs):
     piece_refs = refs[:rows]
     inverse_refs = refs[rows:rows + cores]
-    before_ref, out_ref, joined = refs[rows + cores:]
-    out_ref[1] = before_ref[...]
+    before_ref, out_ref, joined, staged, semaphores = refs[rows + cores:]
+    copies = [pltpu.make_async_copy(before_ref, out_ref.at[1], semaphores.at[0])]
+    copies[0].start()
 
     def store(columns, total):
-        out_ref[0, :, columns] = total
+        staged[:, columns] = total
+        copy = pltpu.make_async_copy(staged.at[:, columns], out_ref.at[0, :, columns], semaphores.at[len(copies)])
+        copy.start()
+        copies.append(copy)
 
     apply_inverse(0, cores, piece_refs, inverse_refs, joined, store)
+    for copy in copies:
+        copy.wait()
 
 
 WHOLE = pl.BlockSpec(memory_space=pltpu.VMEM)
@@ -157,14 +184,20 @@
     def spread(value, hops):
         return [send(value, hops, shift) for shift in range(rows)]
 
-    def rows_of(value, holders, others=()):
+    def rows_of(value, swaps=()):
+        trading = dict([*swaps, *((b, a) for a, b in swaps)])
         arrived = [value]
         for shift in range(1, rows):
-            pairs = [(h * rows + r, h * rows + (r + shift) % rows) for h in holders for r in range(rows)]
-            if shift == 1:
-                pairs += [(a * rows + r, b * rows + r) for a, b in others for r in range(rows)]
+            pairs = [(h * rows + r, trading[h] * rows + r) if h in trading and shift == 1 else
+                     (h * rows + r, h * rows + (r + shift) % rows) for h in range(leafs) for r in range(rows)]
             arrived.append(lax.ppermute(value, places, pairs))
         return arrived
+
+    def ring(value, stops):
+        after = dict(zip(stops, [*stops[1:], stops[0]]))
+        pairs = [(h * rows + r, after[h] * rows + r if h in after else h * rows + (r + 1) % rows)
+                 for h in range(leafs) for r in range(rows)]
+        return lax.ppermute(value, places, pairs)
 
     def core_columns(own):
         turns = range(1, cores)
@@ -180,15 +213,20 @@
     work = 2 * count * full_width * width
     semaphores = lambda n: pltpu.SemaphoreType.DMA((n,))
 
-    crossing = top == 3 and rows > 1
+    crossing = top == 3 and rows == 2
     spare = leafs - 1
     swapped = core_columns(inverse_diag)[1:]
+
+    def load(after, arrays):
+        outs = [near(a.shape, a.dtype) for a in arrays]
+        return call(functools.partial(load_kernel, len(arrays)), [after], arrays, outs, [semaphores(len(arrays))])
+
+    def paired(lefts, rights):
+        return [piece for pair in zip(lefts[::-1], rights[::-1]) for piece in pair]
+
     reduced = call(cast_kernel, [], [right_side], [half], [near((count, width), F32), pltpu.SemaphoreType.DMA(())])
-    gathered = rows_of(reduced, holders(0))
-    right, inverse_own, lower = call(
-        load_kernel, [reduced], [right_side, inverse_diag, lower_blocks],
-        [near(a.shape, a.dtype) for a in (right_side, inverse_diag, lower_blocks)], [semaphores(3)])
-    inverses = [inverse_own, *swapped]
+    gathered = rows_of(reduced)
+    inverses = [load(reduced, [inverse_diag]), *swapped]
     solved = None
     for depth in range(top + 1):
         held = crossing and depth == 1
@@ -196,18 +234,20 @@
         if depth > 0:
             all_joined = near((count, depth * full_width), BF16)
             fetched = [pltpu.SMEM(block_rows.shape, jnp.int32), pltpu.SemaphoreType.DMA(()), joined]
-            plan = "held" if held else "crossed" if crossed else "plain"
+            plan = "held" if held else "crossed" if crossed else "traded" if crossing else "plain"
             kernel = functools.partial(offset_kernel, top, depth, rows, plan)
-            arrays = [block_rows, right, lower, *lefts, *rights, *older] + ([rounded] if held else [])
-            if depth == top:
+            extra = older + ([rounded] if held or crossed else [])
+            pieces = paired(rights[::-1], lefts[::-1]) if depth == top else paired(lefts, rights)
+            arrays = [block_rows, right, lower, *pieces, *extra]
+            if depth < top and not held:
+                reduced, mine = call(kernel, arrays, [], [half, all_joined], fetched, work)
+            else:
                 reduced = call(kernel, arrays, [], [half], [all_joined, *fetched], work)
-            else:
-                reduced, mine = call(kernel, arrays, [], [half, all_joined], fetched, work)
-            others = [(h, spare) for h in holders(0)] if held else []
-            gathered = rows_of(reduced, range(leafs) if depth == top else holders(depth), others)
+            gathered = rows_of(reduced, [(h, spare) for h in holders(0)] if held else ())
         if depth == top:
+            staged = [near((count, width), F32), semaphores(cores + 1)]
             return call(functools.partial(last_kernel, rows, cores), [*gathered, *inverses, solved], [],
-                        [jax.ShapeDtypeStruct(right_side.shape, F32)], [joined], work)
+                        [pltpu.HBM(right_side.shape, F32)], [joined, *staged], work)
         here = holders(depth)
         older = []
         if depth + 1 < top:
@@ -220,14 +260,27 @@
                 older = [send(mine, way, 0) for way in ways]
         else:
             over = [(h, h + 1) for h in here]
-            older = [mine, send(mine, over, 0)]
+            older = [] if crossing else [mine, send(mine, over, 0)]
         kernel = functools.partial(solve_kernel, top, depth, rows, cores, "held" if held else "plain")
         arrays = [*gathered, *inverses] + ([solved] if depth else []) + ([rounded] if held else [])
-        rounded, solved = call(kernel, arrays, [], [half, half_f32], [joined], work)
-        if depth + 1 < top:
+        if crossed:
+            both_full = near((count, full_width), BF16)
+            rounded, solved, both = call(kernel, arrays, [], [half, half_f32, both_full], (), work)
+            passed = send(both, [(h, h + 2) for h in holders(1)], 0)
+            older = [mine, both, passed, *roots]
+        else:
+            rounded, solved = call(kernel, arrays, [], [half, half_f32], [joined], work)
+        if crossing and depth == 0:
+            (root,) = here
+            lefts = [ring(rounded, [root, root - reach, root - 1]), send(rounded, ways[0], 1)]
+            rights = [ring(rounded, [root, root + reach, root + 1]), send(rounded, ways[1], 1)]
+            roots = paired(lefts, rights)
+        elif depth + 1 < top:
             lefts, rights = [spread(rounded, way) for way in ways]
         else:
-            lefts, rights = rows_of(rounded, here), spread(rounded, over)
+            lefts, rights = rows_of(rounded), spread(rounded, over)
+        if depth == 0:
+            right, lower = load(rounded, [right_side, lower_blocks])
 
 
 def solution(mesh):

time: 74.1 us -> 68 us (0.918)
  waiting for transfers between devices: 38.8 us -> 30.6 us
  starting transfers between devices: 19.5 us -> 21.7 us
    ppermute x11 -> x9, waiting for transfers between devices: 26.3 us -> 15.5 us  [send(): return lax.ppermute(value, places, pairs)]
    ppermute x0 -> x2, starting transfers between devices: none -> 2.29 us  [ring(): return lax.ppermute(value, places, pairs)]
    ppermute x0 -> x2, waiting for transfers between devices: none -> 1.58 us  [ring(): return lax.ppermute(value, places, pairs)]
    ppermute x5, waiting for transfers between devices: 12.1 us -> 13.5 us  [rows_of(): arrived.append(lax.ppermute(value, places, pairs))]
    ppermute x11 -> x9, starting transfers between devices: 11.9 us -> 12.2 us  [send(): return lax.ppermute(value, places, pairs)]
    pallas_call x9 -> x10, Pallas kernels: 15.1 us -> 15.2 us  [call(): pl.pallas_call(kernel, in_specs=[WHOLE] * len(near) + [FAR] * len(far), o...]
  transfers between devices with their start and end apart: 17 -> 17, of which waited for: 10 -> 10; matrix products, arithmetic and copies ran while one was open for 0% -> 0% of each run, Pallas kernels for 9% -> 10%
where the time goes in v8:
time: 68 us; the launch traced here: 67.7 us
  waiting for transfers between devices  30.6 us (45%)
  starting transfers between devices  21.7 us (32%)
  Pallas kernels  15.2 us (22%)
    ppermute x9, waiting for transfers between devices, send(): return lax.ppermute(value, places, pairs)  15.5 us
    pallas_call x10, Pallas kernels, call(): pl.pallas_call(kernel, in_specs=[WHOLE] * len(near) + [FAR] * len(far), o...  15.2 us
    ppermute x5, waiting for transfers between devices, rows_of(): arrived.append(lax.ppermute(value, places, pairs))  13.5 us
    ppermute x9, starting transfers between devices, send(): return lax.ppermute(value, places, pairs)  12.2 us
    ppermute x5, starting transfers between devices, rows_of(): arrived.append(lax.ppermute(value, places, pairs))  6.76 us
    ppermute x2, starting transfers between devices, ring(): return lax.ppermute(value, places, pairs)  2.29 us
    ppermute x2, waiting for transfers between devices, ring(): return lax.ppermute(value, places, pairs)  1.58 us
  transfers between devices with their start and end apart: 17, of which 10 were waited for; matrix products, arithmetic and copies ran while one was open for 0% of the time, Pallas kernels for 10%

profile of v8, /device:TPU:0, one launch (start us, length us, event | category | flops | bytes accessed | tf_op | source)
XLA Modules:
  0.0 67.7 jit_solution(498667486804935397)
XLA Ops:
  0.0 0.5 collective-permute-start.1
  0.5 1.0 %shard_map.46.after_ref.refs_0_ = bf16[64,1024]{1,0:T(8,128)(2,1)S(1)} custom-call(f32[2,64,1024]{2,1,0:T(8,128)} %refs_0_.3), custom_call_target="tpu_custom_call" | custom-call | bytes 524288 | tf_op jit(solution)/shard_map/pallas_call | solution.py:162
  1.4 2.6 %collective-permute-start = (bf16[64,1024]{1,0:T(8,128)(2,1)S(1)}, bf16[64,1024]{1,0:T(8,128)(2,1)S(1)}, u32[]{:S(2)}, u32[]{:S(2)}) collective-permute-start(bf16[64,1024]{1,0:T(8,128)(2,1)S(1)} %shard_map.46.after_ref.refs_0_), channel_id=1, source_target_pairs={{0,2},{2,0},{4,6},{6,4},{8,10},{10,8},{12,14},{14,12},{16,18},{18,... | collective-permute-start | bytes 393224 | tf_op jit(solution)/shard_map/ppermute | solution.py:193
  4.0 2.2 %shard_map.47.refs_2_ = bf16[2,2048,512]{2,1,0:T(8,128)(2,1)S(1)} custom-call(bf16[64,1024]{1,0:T(8,128)(2,1)S(1)} %shard_map.46.after_ref.refs_0_, bf16[2,2048,512]{2,1,0:T(8,128)(2,1)} %refs_0_.2), custom_call_target="tpu_custom_call" | custom-call | bytes 4325376 | tf_op jit(solution)/shard_map/pallas_call | solution.py:162
  6.2 2.0 %collective-permute-done.refs_1_ = bf16[64,1024]{1,0:T(8,128)(2,1)S(1)} collective-permute-done((bf16[64,1024]{1,0:T(8,128)(2,1)S(1)}, bf16[64,1024]{1,0:T(8,128)(2,1)S(1)}, u32[]{:S(2)}, u32[]{:S(2)}) %collective-permute-start) | collective-permute-done | bytes 131104 | tf_op jit(solution)/shard_map/ppermute | solution.py:193
  8.2 0.0 collective-permute-done.1.refs_3_
  8.2 0.9 %shard_map.48 = (bf16[64,1024]{1,0:T(8,128)(2,1)S(1)}, f32[64,1024]{1,0:T(8,128)S(1)}) custom-call(bf16[64,1024]{1,0:T(8,128)(2,1)S(1)} %shard_map.46.after_ref.refs_0_, bf16[64,1024]{1,0:T(8,128)(2,1)S(1)} %collective-permute-done.refs_1_, bf16[2,2048,512]{2,1,0:T(8,128)(2,1)S(1)} %shard_map.47.refs_2_, bf16[2,2048,512]{2,1,0:T(8,128)(2,1)S(1)} %collective-permute-done.1.refs_3_), custom_call_target="tpu_custom_call" | custom-call | flops 268435456 | bytes 8650752 | tf_op jit(solution)/shard_map/pallas_call | solution.py:162
  9.1 0.0 copy-start
  9.1 2.2 %collective-permute-start.5 = (bf16[64,1024]{1,0:T(8,128)(2,1)S(1)}, bf16[64,1024]{1,0:T(8,128)(2,1)S(1)}, u32[]{:S(2)}, u32[]{:S(2)}) collective-permute-start(bf16[64,1024]{1,0:T(8,128)(2,1)S(1)} %get-tuple-element.16.after_ref.refs_4_.refs_5_), channel_id=1, source_target_pairs={{0,2},{2,0},{4,6},{6,4},{8,10},{10,8},{12,20},{14,22},{16,12},{18,... | collective-permute-start | bytes 393224 | tf_op jit(solution)/shard_map/ppermute | solution.py:200
  11.3 0.1 collective-permute-start.4
  11.4 0.7 collective-permute-start.3
  12.0 0.7 collective-permute-start.2
  12.7 3.6 %shard_map.49 = (f32[2,64,1024]{2,1,0:T(8,128)S(1)}, bf16[2,16,128,1024]{3,2,1,0:T(8,128)(2,1)S(1)}) custom-call(bf16[64,1024]{1,0:T(8,128)(2,1)S(1)} %get-tuple-element.16.after_ref.refs_4_.refs_5_, f32[2,64,1024]{2,1,0:T(8,128)} %refs_0_.3, bf16[2,16,128,1024]{3,2,1,0:T(8,128)(2,1)} %refs_1_.1), custom_call_target="tpu_custom_call" | custom-call | bytes 9043968 | tf_op jit(solution)/shard_map/pallas_call | solution.py:162
  16.3 0.0 collective-permute-done.5.refs_3_.refs_10_
  16.3 1.6 %collective-permute-done.4.refs_2_.refs_9_ = bf16[64,1024]{1,0:T(8,128)(2,1)S(1)} collective-permute-done((bf16[64,1024]{1,0:T(8,128)(2,1)S(1)}, bf16[64,1024]{1,0:T(8,128)(2,1)S(1)}, u32[]{:S(2)}, u32[]{:S(2)}) %collective-permute-start.4) | collective-permute-done | bytes 131104 | tf_op jit(solution)/shard_map/ppermute | solution.py:200
  17.9 0.0 collective-permute-done.3.refs_1_.refs_8_
  17.9 0.0 collective-permute-done.2.refs_0_.refs_7_
  17.9 0.0 copy-done
  17.9 1.4 %shard_map.50.refs_0_ = bf16[64,1024]{1,0:T(8,128)(2,1)S(1)} custom-call(s32[2,16]{1,0:T(2,128)S(1)} %copy-done, f32[2,64,1024]{2,1,0:T(8,128)S(1)} %get-tuple-element.17.right_ref, bf16[2,16,128,1024]{3,2,1,0:T(8,128)(2,1)S(1)} %get-tuple-element.18.lower_ref, bf16[64,1024]{1,0:T(8,128)(2,1)S(1)} %collective-permute-done.2.refs_0_.refs_7_, ...), custom_call_target="tpu_custom_call" | custom-call | flops 268435456 | bytes 9568384 | tf_op jit(solution)/shard_map/pallas_call | solution.py:162
  19.3 1.8 %collective-permute-start.6 = (bf16[64,1024]{1,0:T(8,128)(2,1)S(1)}, bf16[64,1024]{1,0:T(8,128)(2,1)S(1)}, u32[]{:S(2)}, u32[]{:S(2)}) collective-permute-start(bf16[64,1024]{1,0:T(8,128)(2,1)S(1)} %shard_map.50.refs_0_), channel_id=1, source_target_pairs={{0,2},{2,0},{4,6},{6,4},{8,10},{10,8},{12,28},{14,30},{16,18},{18,... | collective-permute-start | bytes 393224 | tf_op jit(solution)/shard_map/ppermute | solution.py:193
  21.1 3.3 %collective-permute-done.6.refs_1_ = bf16[64,1024]{1,0:T(8,128)(2,1)S(1)} collective-permute-done((bf16[64,1024]{1,0:T(8,128)(2,1)S(1)}, bf16[64,1024]{1,0:T(8,128)(2,1)S(1)}, u32[]{:S(2)}, u32[]{:S(2)}) %collective-permute-start.6) | collective-permute-done | bytes 131104 | tf_op jit(solution)/shard_map/ppermute | solution.py:193
  24.4 0.9 %shard_map.51 = (bf16[64,1024]{1,0:T(8,128)(2,1)S(1)}, f32[64,1024]{1,0:T(8,128)S(1)}) custom-call(bf16[64,1024]{1,0:T(8,128)(2,1)S(1)} %shard_map.50.refs_0_, bf16[64,1024]{1,0:T(8,128)(2,1)S(1)} %collective-permute-done.6.refs_1_, bf16[2,2048,512]{2,1,0:T(8,128)(2,1)S(1)} %shard_map.47.refs_2_, bf16[2,2048,512]{2,1,0:T(8,128)(2,1)S(1)} %collective-permute-done.1.refs_3_, ...), custom_call_target="tpu_custom_call" | custom-call | flops 268435456 | bytes 9043968 | tf_op jit(solution)/shard_map/pallas_call | solution.py:162
  25.3 1.3 %collective-permute-start.10 = (bf16[64,1024]{1,0:T(8,128)(2,1)S(1)}, bf16[64,1024]{1,0:T(8,128)(2,1)S(1)}, u32[]{:S(2)}, u32[]{:S(2)}) collective-permute-start(bf16[64,1024]{1,0:T(8,128)(2,1)S(1)} %get-tuple-element.20.refs_4_), channel_id=1, source_target_pairs={{4,8},{6,10},{20,24},{22,26},{12,0},{14,2},{28,16},{30,18},{5,9},{... | collective-permute-start | bytes 393224 | tf_op jit(solution)/shard_map/ppermute | solution.py:182
  26.6 1.3 %collective-permute-start.9 = (bf16[64,1024]{1,0:T(8,128)(2,1)S(1)}, bf16[64,1024]{1,0:T(8,128)(2,1)S(1)}, u32[]{:S(2)}, u32[]{:S(2)}) collective-permute-start(bf16[64,1024]{1,0:T(8,128)(2,1)S(1)} %get-tuple-element.20.refs_4_), channel_id=1, source_target_pairs={{4,0},{6,2},{20,16},{22,18},{12,8},{14,10},{28,24},{30,26},{5,1},{... | collective-permute-start | bytes 393224 | tf_op jit(solution)/shard_map/ppermute | solution.py:182
  27.9 1.3 %collective-permute-start.8 = (bf16[64,1024]{1,0:T(8,128)(2,1)S(1)}, bf16[64,1024]{1,0:T(8,128)(2,1)S(1)}, u32[]{:S(2)}, u32[]{:S(2)}) collective-permute-start(bf16[64,1024]{1,0:T(8,128)(2,1)S(1)} %get-tuple-element.20.refs_4_), channel_id=1, source_target_pairs={{4,10},{6,8},{20,26},{22,24},{12,2},{14,0},{28,18},{30,16},{5,11},... | collective-permute-start | bytes 393224 | tf_op jit(solution)/shard_map/ppermute | solution.py:182
  29.2 1.3 %collective-permute-start.7 = (bf16[64,1024]{1,0:T(8,128)(2,1)S(1)}, bf16[64,1024]{1,0:T(8,128)(2,1)S(1)}, u32[]{:S(2)}, u32[]{:S(2)}) collective-permute-start(bf16[64,1024]{1,0:T(8,128)(2,1)S(1)} %get-tuple-element.20.refs_4_), channel_id=1, source_target_pairs={{4,2},{6,0},{20,18},{22,16},{12,10},{14,8},{28,26},{30,24},{5,3},{... | collective-permute-start | bytes 393224 | tf_op jit(solution)/shard_map/ppermute | solution.py:182
  30.5 6.1 %collective-permute-done.10.refs_3_ = bf16[64,1024]{1,0:T(8,128)(2,1)S(1)} collective-permute-done((bf16[64,1024]{1,0:T(8,128)(2,1)S(1)}, bf16[64,1024]{1,0:T(8,128)(2,1)S(1)}, u32[]{:S(2)}, u32[]{:S(2)}) %collective-permute-start.10) | collective-permute-done | bytes 131104 | tf_op jit(solution)/shard_map/ppermute | solution.py:182
  36.6 4.3 %collective-permute-done.9.refs_2_ = bf16[64,1024]{1,0:T(8,128)(2,1)S(1)} collective-permute-done((bf16[64,1024]{1,0:T(8,128)(2,1)S(1)}, bf16[64,1024]{1,0:T(8,128)(2,1)S(1)}, u32[]{:S(2)}, u32[]{:S(2)}) %collective-permute-start.9) | collective-permute-done | bytes 131104 | tf_op jit(solution)/shard_map/ppermute | solution.py:182
  41.0 0.0 collective-permute-done.8.refs_1_
  41.0 2.5 %collective-permute-done.7.refs_0_ = bf16[64,1024]{1,0:T(8,128)(2,1)S(1)} collective-permute-done((bf16[64,1024]{1,0:T(8,128)(2,1)S(1)}, bf16[64,1024]{1,0:T(8,128)(2,1)S(1)}, u32[]{:S(2)}, u32[]{:S(2)}) %collective-permute-start.7) | collective-permute-done | bytes 131104 | tf_op jit(solution)/shard_map/ppermute | solution.py:182
  43.4 1.4 %shard_map.52 = (bf16[64,1024]{1,0:T(8,128)(2,1)S(1)}, bf16[64,4096]{1,0:T(8,128)(2,1)S(1)}) custom-call(s32[2,16]{1,0:T(2,128)S(1)} %copy-done, f32[2,64,1024]{2,1,0:T(8,128)S(1)} %get-tuple-element.17.right_ref, bf16[2,16,128,1024]{3,2,1,0:T(8,128)(2,1)S(1)} %get-tuple-element.18.lower_ref, bf16[64,1024]{1,0:T(8,128)(2,1)S(1)} %collective-permute-done.7.refs_0_, ...), custom_call_target="tpu_custom_call" | custom-call | flops 268435456 | bytes 9568384 | tf_op jit(solution)/shard_map/pallas_call | solution.py:162
  44.9 0.6 collective-permute-start.11
  45.4 4.5 %collective-permute-done.11.refs_1_ = bf16[64,1024]{1,0:T(8,128)(2,1)S(1)} collective-permute-done((bf16[64,1024]{1,0:T(8,128)(2,1)S(1)}, bf16[64,1024]{1,0:T(8,128)(2,1)S(1)}, u32[]{:S(2)}, u32[]{:S(2)}) %collective-permute-start.11) | collective-permute-done | bytes 131104 | tf_op jit(solution)/shard_map/ppermute | solution.py:193
  49.9 0.9 %shard_map.53 = (bf16[64,1024]{1,0:T(8,128)(2,1)S(1)}, f32[64,1024]{1,0:T(8,128)S(1)}, bf16[64,2048]{1,0:T(8,128)(2,1)S(1)}) custom-call(bf16[64,1024]{1,0:T(8,128)(2,1)S(1)} %get-tuple-element.21.refs_0_, bf16[64,1024]{1,0:T(8,128)(2,1)S(1)} %collective-permute-done.11.refs_1_, bf16[2,2048,512]{2,1,0:T(8,128)(2,1)S(1)} %shard_map.47.refs_2_, ...), custom_call_target="tpu_custom_call" | custom-call | flops 268435456 | bytes 8912896 | tf_op jit(solution)/shard_map/pallas_call | solution.py:162
  50.8 0.7 collective-permute-start.15
  51.5 0.6 collective-permute-start.14
  52.0 3.8 %collective-permute-start.13 = (bf16[64,1024]{1,0:T(8,128)(2,1)S(1)}, bf16[64,1024]{1,0:T(8,128)(2,1)S(1)}, u32[]{:S(2)}, u32[]{:S(2)}) collective-permute-start(bf16[64,1024]{1,0:T(8,128)(2,1)S(1)} %get-tuple-element.23.refs_1_), channel_id=1, source_target_pairs={{0,6},{2,4},{8,14},{10,12},{16,22},{18,20},{24,30},{26,28},{1,7},{... | collective-permute-start | bytes 393224 | tf_op jit(solution)/shard_map/ppermute | solution.py:182
  55.8 1.3 %collective-permute-start.12 = (bf16[64,1024]{1,0:T(8,128)(2,1)S(1)}, bf16[64,1024]{1,0:T(8,128)(2,1)S(1)}, u32[]{:S(2)}, u32[]{:S(2)}) collective-permute-start(bf16[64,1024]{1,0:T(8,128)(2,1)S(1)} %get-tuple-element.23.refs_1_), channel_id=1, source_target_pairs={{0,4},{2,6},{8,12},{10,14},{16,20},{18,22},{24,28},{26,30},{1,5},{... | collective-permute-start | bytes 393224 | tf_op jit(solution)/shard_map/ppermute | solution.py:182
  57.1 0.0 collective-permute-done.14.refs_3_
  57.1 1.2 %collective-permute-done.13.refs_2_ = bf16[64,1024]{1,0:T(8,128)(2,1)S(1)} collective-permute-done((bf16[64,1024]{1,0:T(8,128)(2,1)S(1)}, bf16[64,1024]{1,0:T(8,128)(2,1)S(1)}, u32[]{:S(2)}, u32[]{:S(2)}) %collective-permute-start.13) | collective-permute-done | bytes 131104 | tf_op jit(solution)/shard_map/ppermute | solution.py:182
  58.3 1.4 %collective-permute-done.12.refs_0_ = bf16[64,1024]{1,0:T(8,128)(2,1)S(1)} collective-permute-done((bf16[64,1024]{1,0:T(8,128)(2,1)S(1)}, bf16[64,1024]{1,0:T(8,128)(2,1)S(1)}, u32[]{:S(2)}, u32[]{:S(2)}) %collective-permute-start.12) | collective-permute-done | bytes 131104 | tf_op jit(solution)/shard_map/ppermute | solution.py:182
  59.7 0.0 collective-permute-done.15.refs_6_
  59.7 1.4 %shard_map.54.refs_0_ = bf16[64,1024]{1,0:T(8,128)(2,1)S(1)} custom-call(s32[2,16]{1,0:T(2,128)S(1)} %copy-done, f32[2,64,1024]{2,1,0:T(8,128)S(1)} %get-tuple-element.17.right_ref, bf16[2,16,128,1024]{3,2,1,0:T(8,128)(2,1)S(1)} %get-tuple-element.18.lower_ref, bf16[64,1024]{1,0:T(8,128)(2,1)S(1)} %collective-permute-done.12.refs_0_, ...), custom_call_target="tpu_custom_call" | custom-call | flops 268435456 | bytes 11010176 | tf_op jit(solution)/shard_map/pallas_call | solution.py:162
  61.1 1.2 %collective-permute-start.16 = (bf16[64,1024]{1,0:T(8,128)(2,1)S(1)}, bf16[64,1024]{1,0:T(8,128)(2,1)S(1)}, u32[]{:S(2)}, u32[]{:S(2)}) collective-permute-start(bf16[64,1024]{1,0:T(8,128)(2,1)S(1)} %shard_map.54.refs_0_), channel_id=1, source_target_pairs={{0,2},{2,0},{4,6},{6,4},{8,10},{10,8},{12,14},{14,12},{16,18},{18,... | collective-permute-start | bytes 393224 | tf_op jit(solution)/shard_map/ppermute | solution.py:193
  62.4 3.8 %collective-permute-done.16.refs_1_ = bf16[64,1024]{1,0:T(8,128)(2,1)S(1)} collective-permute-done((bf16[64,1024]{1,0:T(8,128)(2,1)S(1)}, bf16[64,1024]{1,0:T(8,128)(2,1)S(1)}, u32[]{:S(2)}, u32[]{:S(2)}) %collective-permute-start.16) | collective-permute-done | bytes 131104 | tf_op jit(solution)/shard_map/ppermute | solution.py:193
  66.1 1.6 %shard_map.55 = f32[2,64,1024]{2,1,0:T(8,128)} custom-call(bf16[64,1024]{1,0:T(8,128)(2,1)S(1)} %shard_map.54.refs_0_, bf16[64,1024]{1,0:T(8,128)(2,1)S(1)} %collective-permute-done.16.refs_1_, bf16[2,2048,512]{2,1,0:T(8,128)(2,1)S(1)} %shard_map.47.refs_2_, bf16[2,2048,512]{2,1,0:T(8,128)(2,1)S(1)} %collective-permute-done.1.refs_3_, ...), custom_call_target="tpu_custom_call" | custom-call | flops 268435456 | bytes 8912896 | tf_op jit(solution)/shard_map/pallas_call | solution.py:162
Async XLA Ops:
  0.0 8.2 %collective-permute-start.1 = (bf16[2,2048,512]{2,1,0:T(8,128)(2,1)}, bf16[2,2048,512]{2,1,0:T(8,128)(2,1)S(1)}, u32[]{:S(2)}, u32[]{:S(2)}) collective-permute-start(bf16[2,2048,512]{2,1,0:T(8,128)(2,1)} %refs_0_.2), channel_id=1, source_target_pairs={{0,1},{1,0},{2,3},{3,2},{4,5},{5,4},{6,7},{7,6},{8,9},{9,8},{10,11... | collective-permute-start | bytes 12582920 | tf_op jit(solution)/shard_map/ppermute | solution.py:204
  1.4 6.8 %collective-permute-start = (bf16[64,1024]{1,0:T(8,128)(2,1)S(1)}, bf16[64,1024]{1,0:T(8,128)(2,1)S(1)}, u32[]{:S(2)}, u32[]{:S(2)}) collective-permute-start(bf16[64,1024]{1,0:T(8,128)(2,1)S(1)} %shard_map.46.after_ref.refs_0_), channel_id=1, source_target_pairs={{0,2},{2,0},{4,6},{6,4},{8,10},{10,8},{12,14},{14,12},{16,18},{18,... | collective-permute-start | bytes 393224 | tf_op jit(solution)/shard_map/ppermute | solution.py:193
  9.1 8.8 %copy-start = (s32[2,16]{1,0:T(2,128)S(1)}, s32[2,16]{1,0:T(2,128)}, u32[]{:S(2)}) copy-start(s32[2,16]{1,0:T(2,128)} %block_rows_ref.5) | copy-start | bytes 388
  9.1 7.2 %collective-permute-start.5 = (bf16[64,1024]{1,0:T(8,128)(2,1)S(1)}, bf16[64,1024]{1,0:T(8,128)(2,1)S(1)}, u32[]{:S(2)}, u32[]{:S(2)}) collective-permute-start(bf16[64,1024]{1,0:T(8,128)(2,1)S(1)} %get-tuple-element.16.after_ref.refs_4_.refs_5_), channel_id=1, source_target_pairs={{0,2},{2,0},{4,6},{6,4},{8,10},{10,8},{12,20},{14,22},{16,12},{18,... | collective-permute-start | bytes 393224 | tf_op jit(solution)/shard_map/ppermute | solution.py:200
  11.3 6.6 %collective-permute-start.4 = (bf16[64,1024]{1,0:T(8,128)(2,1)S(1)}, bf16[64,1024]{1,0:T(8,128)(2,1)S(1)}, u32[]{:S(2)}, u32[]{:S(2)}) collective-permute-start(bf16[64,1024]{1,0:T(8,128)(2,1)S(1)} %get-tuple-element.16.after_ref.refs_4_.refs_5_), channel_id=1, source_target_pairs={{0,2},{2,0},{4,8},{6,10},{8,12},{10,14},{12,4},{14,6},{16,18},{18,... | collective-permute-start | bytes 393224 | tf_op jit(solution)/shard_map/ppermute | solution.py:200
  11.4 6.5 %collective-permute-start.3 = (bf16[64,1024]{1,0:T(8,128)(2,1)S(1)}, bf16[64,1024]{1,0:T(8,128)(2,1)S(1)}, u32[]{:S(2)}, u32[]{:S(2)}) collective-permute-start(bf16[64,1024]{1,0:T(8,128)(2,1)S(1)} %get-tuple-element.16.after_ref.refs_4_.refs_5_), channel_id=1, source_target_pairs={{12,22},{14,20},{13,23},{15,21}} | collective-permute-start | bytes 393224 | tf_op jit(solution)/shard_map/ppermute | solution.py:182
  12.0 5.9 %collective-permute-start.2 = (bf16[64,1024]{1,0:T(8,128)(2,1)S(1)}, bf16[64,1024]{1,0:T(8,128)(2,1)S(1)}, u32[]{:S(2)}, u32[]{:S(2)}) collective-permute-start(bf16[64,1024]{1,0:T(8,128)(2,1)S(1)} %get-tuple-element.16.after_ref.refs_4_.refs_5_), channel_id=1, source_target_pairs={{12,6},{14,4},{13,7},{15,5}} | collective-permute-start | bytes 393224 | tf_op jit(solution)/shard_map/ppermute | solution.py:182
  19.3 5.1 %collective-permute-start.6 = (bf16[64,1024]{1,0:T(8,128)(2,1)S(1)}, bf16[64,1024]{1,0:T(8,128)(2,1)S(1)}, u32[]{:S(2)}, u32[]{:S(2)}) collective-permute-start(bf16[64,1024]{1,0:T(8,128)(2,1)S(1)} %shard_map.50.refs_0_), channel_id=1, source_target_pairs={{0,2},{2,0},{4,6},{6,4},{8,10},{10,8},{12,28},{14,30},{16,18},{18,... | collective-permute-start | bytes 393224 | tf_op jit(solution)/shard_map/ppermute | solution.py:193
  25.3 11.3 %collective-permute-start.10 = (bf16[64,1024]{1,0:T(8,128)(2,1)S(1)}, bf16[64,1024]{1,0:T(8,128)(2,1)S(1)}, u32[]{:S(2)}, u32[]{:S(2)}) collective-permute-start(bf16[64,1024]{1,0:T(8,128)(2,1)S(1)} %get-tuple-element.20.refs_4_), channel_id=1, source_target_pairs={{4,8},{6,10},{20,24},{22,26},{12,0},{14,2},{28,16},{30,18},{5,9},{... | collective-permute-start | bytes 393224 | tf_op jit(solution)/shard_map/ppermute | solution.py:182
  26.6 14.4 %collective-permute-start.9 = (bf16[64,1024]{1,0:T(8,128)(2,1)S(1)}, bf16[64,1024]{1,0:T(8,128)(2,1)S(1)}, u32[]{:S(2)}, u32[]{:S(2)}) collective-permute-start(bf16[64,1024]{1,0:T(8,128)(2,1)S(1)} %get-tuple-element.20.refs_4_), channel_id=1, source_target_pairs={{4,0},{6,2},{20,16},{22,18},{12,8},{14,10},{28,24},{30,26},{5,1},{... | collective-permute-start | bytes 393224 | tf_op jit(solution)/shard_map/ppermute | solution.py:182
  27.9 13.1 %collective-permute-start.8 = (bf16[64,1024]{1,0:T(8,128)(2,1)S(1)}, bf16[64,1024]{1,0:T(8,128)(2,1)S(1)}, u32[]{:S(2)}, u32[]{:S(2)}) collective-permute-start(bf16[64,1024]{1,0:T(8,128)(2,1)S(1)} %get-tuple-element.20.refs_4_), channel_id=1, source_target_pairs={{4,10},{6,8},{20,26},{22,24},{12,2},{14,0},{28,18},{30,16},{5,11},... | collective-permute-start | bytes 393224 | tf_op jit(solution)/shard_map/ppermute | solution.py:182
  29.2 14.2 %collective-permute-start.7 = (bf16[64,1024]{1,0:T(8,128)(2,1)S(1)}, bf16[64,1024]{1,0:T(8,128)(2,1)S(1)}, u32[]{:S(2)}, u32[]{:S(2)}) collective-permute-start(bf16[64,1024]{1,0:T(8,128)(2,1)S(1)} %get-tuple-element.20.refs_4_), channel_id=1, source_target_pairs={{4,2},{6,0},{20,18},{22,16},{12,10},{14,8},{28,26},{30,24},{5,3},{... | collective-permute-start | bytes 393224 | tf_op jit(solution)/shard_map/ppermute | solution.py:182
  44.9 5.0 %collective-permute-start.11 = (bf16[64,1024]{1,0:T(8,128)(2,1)S(1)}, bf16[64,1024]{1,0:T(8,128)(2,1)S(1)}, u32[]{:S(2)}, u32[]{:S(2)}) collective-permute-start(bf16[64,1024]{1,0:T(8,128)(2,1)S(1)} %get-tuple-element.21.refs_0_), channel_id=1, source_target_pairs={{0,2},{2,0},{4,6},{6,4},{8,10},{10,8},{12,14},{14,12},{16,18},{18,... | collective-permute-start | bytes 393224 | tf_op jit(solution)/shard_map/ppermute | solution.py:193
  50.8 8.9 %collective-permute-start.15 = (bf16[64,2048]{1,0:T(8,128)(2,1)S(1)}, bf16[64,2048]{1,0:T(8,128)(2,1)S(1)}, u32[]{:S(2)}, u32[]{:S(2)}) collective-permute-start(bf16[64,2048]{1,0:T(8,128)(2,1)S(1)} %get-tuple-element.25.refs_5_), channel_id=1, source_target_pairs={{4,12},{6,14},{20,28},{22,30},{5,13},{7,15},{21,29},{23,31}} | collective-permute-start | bytes 786440 | tf_op jit(solution)/shard_map/ppermute | solution.py:182
  51.5 5.7 %collective-permute-start.14 = (bf16[64,1024]{1,0:T(8,128)(2,1)S(1)}, bf16[64,1024]{1,0:T(8,128)(2,1)S(1)}, u32[]{:S(2)}, u32[]{:S(2)}) collective-permute-start(bf16[64,1024]{1,0:T(8,128)(2,1)S(1)} %get-tuple-element.23.refs_1_), channel_id=1, source_target_pairs={{0,2},{2,0},{4,6},{6,4},{8,10},{10,8},{12,14},{14,12},{16,18},{18,... | collective-permute-start | bytes 393224 | tf_op jit(solution)/shard_map/ppermute | solution.py:193
  52.0 6.3 %collective-permute-start.13 = (bf16[64,1024]{1,0:T(8,128)(2,1)S(1)}, bf16[64,1024]{1,0:T(8,128)(2,1)S(1)}, u32[]{:S(2)}, u32[]{:S(2)}) collective-permute-start(bf16[64,1024]{1,0:T(8,128)(2,1)S(1)} %get-tuple-element.23.refs_1_), channel_id=1, source_target_pairs={{0,6},{2,4},{8,14},{10,12},{16,22},{18,20},{24,30},{26,28},{1,7},{... | collective-permute-start | bytes 393224 | tf_op jit(solution)/shard_map/ppermute | solution.py:182
  55.8 3.9 %collective-permute-start.12 = (bf16[64,1024]{1,0:T(8,128)(2,1)S(1)}, bf16[64,1024]{1,0:T(8,128)(2,1)S(1)}, u32[]{:S(2)}, u32[]{:S(2)}) collective-permute-start(bf16[64,1024]{1,0:T(8,128)(2,1)S(1)} %get-tuple-element.23.refs_1_), channel_id=1, source_target_pairs={{0,4},{2,6},{8,12},{10,14},{16,20},{18,22},{24,28},{26,30},{1,5},{... | collective-permute-start | bytes 393224 | tf_op jit(solution)/shard_map/ppermute | solution.py:182
  61.1 5.0 %collective-permute-start.16 = (bf16[64,1024]{1,0:T(8,128)(2,1)S(1)}, bf16[64,1024]{1,0:T(8,128)(2,1)S(1)}, u32[]{:S(2)}, u32[]{:S(2)}) collective-permute-start(bf16[64,1024]{1,0:T(8,128)(2,1)S(1)} %shard_map.54.refs_0_), channel_id=1, source_target_pairs={{0,2},{2,0},{4,6},{6,4},{8,10},{10,8},{12,14},{14,12},{16,18},{18,... | collective-permute-start | bytes 393224 | tf_op jit(solution)/shard_map/ppermute | solution.py:193

commit v9 on v8

--- a/solution.py
+++ b/solution.py
@@ -42,7 +42,12 @@
 def offset_kernel(top, level, rows, plan, block_rows_ref, right_ref, lower_ref, *refs):
     leaf = lax.axis_index("leaf")
     slot = 0 if level == top else 1
-    *refs, reduced_ref, joined, numbers, semaphore, picked = refs
+    if plan == "rooted":
+        *refs, reduced_ref, piece_ref, joined, numbers, semaphore, picked = refs
+    else:
+        *refs, reduced_ref, joined, numbers, semaphore, picked = refs
+    if plan in ("crossed", "traded"):
+        late_ref, *refs = refs
     if level == top:
         pieces = [refs[1:2 * rows:2], refs[:2 * rows:2]]
     else:
@@ -58,28 +63,18 @@
     for which, wanted in enumerate((first, jnp.logical_not(first))):
         @pl.when(wanted)
         def _():
-            if plan == "crossed":
-                place_pieces(pieces[1 - which], joined, 0)
-            elif plan != "traded" and before:
+            if plan == "rooted":
+                piece_ref[...] = pieces[which][0][...]
+            elif plan == "plain" and before:
                 joined[:, :before] = extra[which][...]
             place_pieces(pieces[which], joined, before)
-    if plan == "traded":
-        mine_ref, both_ref, passed_ref, *roots = extra
-
-        @pl.when(leaf % 2 == 0)
-        def _():
-            joined[:, :before] = mine_ref[...]
-
-        for which, place in enumerate((1, 3)):
-            @pl.when((leaf % 4 == 1) & ((leaf + 1) // 2 % 4 == place))
+    if plan == "crossed":
+        place_pieces([extra[0], late_ref], joined, 0)
+    elif plan == "traded":
+        for wanted, ref in ((leaf % 2 == 0, extra[0]), (leaf % 4 == 1, extra[1]), (leaf % 4 == 3, late_ref)):
+            @pl.when(wanted)
             def _():
-                place_pieces(roots[which::2][::-1], joined, 0)
-                joined[:, full:before] = both_ref[...]
-
-        @pl.when(leaf % 4 == 3)
-        def _():
-            joined[:, :full] = both_ref[...]
-            joined[:, full:before] = passed_ref[...]
+                joined[:, :before] = ref[...]
     blocks, block_width = lower_ref.shape[1:3]
     highest = joined.shape[1] // block_width - 1
     listed.wait()
@@ -90,10 +85,10 @@
     weights = lower_ref[slot].reshape(blocks * block_width, width)
     offset = jnp.dot(picked[...], weights, preferred_element_type=F32)
     reduced_ref[...] = (right_ref[slot] - offset).astype(BF16)
-    if plan in ("held", "crossed"):
-        @pl.when(upper_depth(leaf, top) == 0 if plan == "held" else leaf % 2 == 1)
+    if plan == "crossed":
+        @pl.when(leaf % 2 == 1)
         def _():
-            reduced_ref[...] = extra[0][...]
+            reduced_ref[...] = extra[1][...]
 
 
 def apply_inverse(slot, cores, piece_refs, inverse_refs, joined, store):
@@ -110,8 +105,11 @@
     piece_refs = refs[:rows]
     inverse_refs = refs[rows:rows + cores]
     before_ref = refs[rows + cores] if depth > 0 else None
-    held_ref = refs[rows + cores + 1] if plan == "held" else None
-    rounded_ref, solved_ref, joined = refs[-3:]
+    if plan == "crossed":
+        own_ref, *root_refs = refs[rows + cores + 1:-4]
+        rounded_ref, solved_ref, both_ref, joined = refs[-4:]
+    else:
+        rounded_ref, solved_ref, joined = refs[-3:]
     leaf = lax.axis_index("leaf")
     active = upper_depth(leaf, top) == depth
 
@@ -121,14 +119,12 @@
         solved_ref[:, columns] = jnp.where(active, total, before)
 
     apply_inverse(1, cores, piece_refs, inverse_refs, joined, store)
-    if plan == "held":
-        @pl.when(upper_depth(leaf, top) == 0)
-        def _():
-            rounded_ref[...] = held_ref[...]
-
-        @pl.when(leaf == lax.axis_size("leaf") - 1)
-        def _():
-            rounded_ref[...] = piece_refs[1][...]
+    if plan == "crossed":
+        for which, place in enumerate((1, 3)):
+            @pl.when((leaf % 4 == 1) & ((leaf + 1) // 2 % 4 == place))
+            def _():
+                place_pieces([own_ref, root_refs[which]], both_ref, 0)
+                both_ref[:, joined.shape[1]:] = joined[...]
 
 
 def last_kernel(rows, cores, *refs):
@@ -184,17 +180,15 @@
     def spread(value, hops):
         return [send(value, hops, shift) for shift in range(rows)]
 
-    def rows_of(value, swaps=()):
-        trading = dict([*swaps, *((b, a) for a, b in swaps)])
+    def rows_of(value):
         arrived = [value]
         for shift in range(1, rows):
-            pairs = [(h * rows + r, trading[h] * rows + r) if h in trading and shift == 1 else
-                     (h * rows + r, h * rows + (r + shift) % rows) for h in range(leafs) for r in range(rows)]
+            pairs = [(h * rows + r, h * rows + (r + shift) % rows) for h in range(leafs) for r in range(rows)]
             arrived.append(lax.ppermute(value, places, pairs))
         return arrived
 
-    def ring(value, stops):
-        after = dict(zip(stops, [*stops[1:], stops[0]]))
+    def ring(value, *rings):
+        after = {a: b for stops in rings for a, b in zip(stops, [*stops[1:], stops[0]])}
         pairs = [(h * rows + r, after[h] * rows + r if h in after else h * rows + (r + 1) % rows)
                  for h in range(leafs) for r in range(rows)]
         return lax.ppermute(value, places, pairs)
@@ -214,7 +208,6 @@
     semaphores = lambda n: pltpu.SemaphoreType.DMA((n,))
 
     crossing = top == 3 and rows == 2
-    spare = leafs - 1
     swapped = core_columns(inverse_diag)[1:]
 
     def load(after, arrays):
@@ -227,23 +220,31 @@
     reduced = call(cast_kernel, [], [right_side], [half], [near((count, width), F32), pltpu.SemaphoreType.DMA(())])
     gathered = rows_of(reduced)
     inverses = [load(reduced, [inverse_diag]), *swapped]
+    plans = ["rooted", "crossed", "traded"] if crossing else ["plain"] * top
+    plans = ["plain", *plans]
+    older = []
     solved = None
-    for depth in range(top + 1):
-        held = crossing and depth == 1
-        crossed = crossing and depth == 2
+    for depth, plan in enumerate(plans):
         if depth > 0:
             all_joined = near((count, depth * full_width), BF16)
             fetched = [pltpu.SMEM(block_rows.shape, jnp.int32), pltpu.SemaphoreType.DMA(()), joined]
-            plan = "held" if held else "crossed" if crossed else "traded" if crossing else "plain"
             kernel = functools.partial(offset_kernel, top, depth, rows, plan)
-            extra = older + ([rounded] if held or crossed else [])
             pieces = paired(rights[::-1], lefts[::-1]) if depth == top else paired(lefts, rights)
-            arrays = [block_rows, right, lower, *pieces, *extra]
-            if depth < top and not held:
+            if plan == "crossed":
+                older = [late, *pieces, relayed, rounded]
+            elif plan == "traded":
+                older = [passed, *pieces, mine, both]
+            else:
+                older = [*pieces, *older]
+            arrays = [block_rows, right, lower, *older]
+            if plan == "rooted":
+                reduced, own_root = call(kernel, arrays, [], [half, half], [all_joined, *fetched], work)
+            elif depth < top:
                 reduced, mine = call(kernel, arrays, [], [half, all_joined], fetched, work)
             else:
                 reduced = call(kernel, arrays, [], [half], [all_joined, *fetched], work)
-            gathered = rows_of(reduced, [(h, spare) for h in holders(0)] if held else ())
+        if depth > 0:
+            gathered = rows_of(reduced)
         if depth == top:
             staged = [near((count, width), F32), semaphores(cores + 1)]
             return call(functools.partial(last_kernel, rows, cores), [*gathered, *inverses, solved], [],
@@ -253,30 +254,31 @@
         if depth + 1 < top:
             reach = 2 ** (top - depth - 2)
             ways = [[(h, h - reach) for h in here], [(h, h + reach) for h in here]]
-            if held:
-                tops = [*holders(0), spare]
-                ways = [ways[0] + [(h, h - reach) for h in tops], ways[1] + [(h, h - 3 * reach) for h in tops]]
+            if plan == "rooted":
+                sides = [ring(own_root, *way) for way in ways]
+                relayed = jnp.where(lax.axis_index("leaf") % 4 == 0, *sides)
             elif depth > 0:
                 older = [send(mine, way, 0) for way in ways]
         else:
             over = [(h, h + 1) for h in here]
             older = [] if crossing else [mine, send(mine, over, 0)]
-        kernel = functools.partial(solve_kernel, top, depth, rows, cores, "held" if held else "plain")
-        arrays = [*gathered, *inverses] + ([solved] if depth else []) + ([rounded] if held else [])
-        if crossed:
-            both_full = near((count, full_width), BF16)
-            rounded, solved, both = call(kernel, arrays, [], [half, half_f32, both_full], (), work)
+        kernel = functools.partial(solve_kernel, top, depth, rows, cores, plan)
+        arrays = [*gathered, *inverses] + ([solved] if depth else [])
+        if plan == "crossed":
+            rounded, solved, both = call(kernel, [*arrays, own_root, *roots], [],
+                                         [half, half_f32, all_joined], [joined], work)
             passed = send(both, [(h, h + 2) for h in holders(1)], 0)
-            older = [mine, both, passed, *roots]
         else:
             rounded, solved = call(kernel, arrays, [], [half, half_f32], [joined], work)
         if crossing and depth == 0:
             (root,) = here
             lefts = [ring(rounded, [root, root - reach, root - 1]), send(rounded, ways[0], 1)]
             rights = [ring(rounded, [root, root + reach, root + 1]), send(rounded, ways[1], 1)]
-            roots = paired(lefts, rights)
+            roots = [lefts[1], rights[1]]
         elif depth + 1 < top:
             lefts, rights = [spread(rounded, way) for way in ways]
+            if plan == "rooted":
+                late = rows_of(relayed)[1]
         else:
             lefts, rights = rows_of(rounded), spread(rounded, over)
         if depth == 0:

time: 68 us -> 73.4 us (1.079)
  waiting for transfers between devices: 30.6 us -> 20.7 us
  starting transfers between devices: 21.7 us -> 31.4 us
  local copies, waits for them, and re-layouts: 0.01 us -> 5.68 us
    ppermute x9, waiting for transfers between devices: 15.5 us -> 9.6 us  [send(): return lax.ppermute(value, places, pairs)]
    unnamed x2 -> x16, local copies, waits for them, and re-layouts: 0.01 us -> 5.68 us
    ppermute x5 -> x6, starting transfers between devices: 6.76 us -> 10.9 us  [rows_of(): arrived.append(lax.ppermute(value, places, pairs))]
    ppermute x5 -> x6, waiting for transfers between devices: 13.5 us -> 9.44 us  [rows_of(): arrived.append(lax.ppermute(value, places, pairs))]
    ppermute x2 -> x4, starting transfers between devices: 2.29 us -> 6.26 us  [ring(): return lax.ppermute(value, places, pairs)]
    ppermute x9, starting transfers between devices: 12.2 us -> 13.8 us  [send(): return lax.ppermute(value, places, pairs)]
    ppermute x2 -> x4, waiting for transfers between devices: 1.58 us -> 1.62 us  [ring(): return lax.ppermute(value, places, pairs)]
  transfers between devices with their start and end apart: 17 -> 20, of which waited for: 10 -> 9; matrix products, arithmetic and copies ran while one was open for 0% -> 0% of each run, Pallas kernels for 10% -> 10%
where the time goes in v9:
time: 73.4 us; the launch traced here: 73.1 us
  starting transfers between devices  31.4 us (43%)
  waiting for transfers between devices  20.7 us (28%)
  Pallas kernels  15.1 us (21%)
  local copies, waits for them, and re-layouts  5.68 us (8%)
    pallas_call x10, Pallas kernels, call(): pl.pallas_call(kernel, in_specs=[WHOLE] * len(near) + [FAR] * len(far), o...  15.1 us
    ppermute x9, starting transfers between devices, send(): return lax.ppermute(value, places, pairs)  13.8 us
    ppermute x6, starting transfers between devices, rows_of(): arrived.append(lax.ppermute(value, places, pairs))  10.9 us
    ppermute x9, waiting for transfers between devices, send(): return lax.ppermute(value, places, pairs)  9.6 us
    ppermute x6, waiting for transfers between devices, rows_of(): arrived.append(lax.ppermute(value, places, pairs))  9.44 us
    ppermute x4, starting transfers between devices, ring(): return lax.ppermute(value, places, pairs)  6.26 us
    unnamed x16, local copies, waits for them, and re-layouts  5.68 us
    ppermute x4, waiting for transfers between devices, ring(): return lax.ppermute(value, places, pairs)  1.62 us
  transfers between devices with their start and end apart: 20, of which 9 were waited for; matrix products, arithmetic and copies ran while one was open for 0% of the time, Pallas kernels for 10%

profile of v9, /device:TPU:0, one launch (start us, length us, event | category | flops | bytes accessed | tf_op | source)
XLA Modules:
  0.0 73.1 jit_solution(2237280108849756632)
XLA Ops:
  0.0 0.5 collective-permute-start.1
  0.5 1.0 %shard_map.46.after_ref.refs_0_ = bf16[64,1024]{1,0:T(8,128)(2,1)S(1)} custom-call(f32[2,64,1024]{2,1,0:T(8,128)} %refs_0_.3), custom_call_target="tpu_custom_call" | custom-call | bytes 524288 | tf_op jit(solution)/shard_map/pallas_call | solution.py:158
  1.4 2.6 %collective-permute-start = (bf16[64,1024]{1,0:T(8,128)(2,1)S(1)}, bf16[64,1024]{1,0:T(8,128)(2,1)S(1)}, u32[]{:S(2)}, u32[]{:S(2)}) collective-permute-start(bf16[64,1024]{1,0:T(8,128)(2,1)S(1)} %shard_map.46.after_ref.refs_0_), channel_id=1, source_target_pairs={{0,2},{2,0},{4,6},{6,4},{8,10},{10,8},{12,14},{14,12},{16,18},{18,... | collective-permute-start | bytes 393224 | tf_op jit(solution)/shard_map/ppermute | solution.py:187
  4.0 2.2 %shard_map.47.refs_2_ = bf16[2,2048,512]{2,1,0:T(8,128)(2,1)S(1)} custom-call(bf16[64,1024]{1,0:T(8,128)(2,1)S(1)} %shard_map.46.after_ref.refs_0_, bf16[2,2048,512]{2,1,0:T(8,128)(2,1)} %refs_0_.2), custom_call_target="tpu_custom_call" | custom-call | bytes 4325376 | tf_op jit(solution)/shard_map/pallas_call | solution.py:158
  6.2 2.0 %collective-permute-done.refs_1_ = bf16[64,1024]{1,0:T(8,128)(2,1)S(1)} collective-permute-done((bf16[64,1024]{1,0:T(8,128)(2,1)S(1)}, bf16[64,1024]{1,0:T(8,128)(2,1)S(1)}, u32[]{:S(2)}, u32[]{:S(2)}) %collective-permute-start) | collective-permute-done | bytes 131104 | tf_op jit(solution)/shard_map/ppermute | solution.py:187
  8.2 0.0 collective-permute-done.1.refs_3_
  8.2 0.8 %shard_map.48 = (bf16[64,1024]{1,0:T(8,128)(2,1)S(1)}, f32[64,1024]{1,0:T(8,128)S(1)}) custom-call(bf16[64,1024]{1,0:T(8,128)(2,1)S(1)} %shard_map.46.after_ref.refs_0_, bf16[64,1024]{1,0:T(8,128)(2,1)S(1)} %collective-permute-done.refs_1_, bf16[2,2048,512]{2,1,0:T(8,128)(2,1)S(1)} %shard_map.47.refs_2_, bf16[2,2048,512]{2,1,0:T(8,128)(2,1)S(1)} %collective-permute-done.1.refs_3_), custom_call_target="tpu_custom_call" | custom-call | flops 268435456 | bytes 8650752 | tf_op jit(solution)/shard_map/pallas_call | solution.py:158
  9.0 1.1 %copy-done.5 = bf16[2,2048,512]{2,1,0:T(8,128)(2,1)} copy-done((bf16[2,2048,512]{2,1,0:T(8,128)(2,1)}, bf16[2,2048,512]{2,1,0:T(8,128)(2,1)S(1)}, u32[]{:S(2)}) %copy-start.5) | copy-done | bytes 4194328
  10.1 2.1 %collective-permute-start.5 = (bf16[64,1024]{1,0:T(8,128)(2,1)S(1)}, bf16[64,1024]{1,0:T(8,128)(2,1)S(1)}, u32[]{:S(2)}, u32[]{:S(2)}) collective-permute-start(bf16[64,1024]{1,0:T(8,128)(2,1)S(1)} %get-tuple-element.18.after_ref), channel_id=1, source_target_pairs={{0,2},{2,0},{4,6},{6,4},{8,10},{10,8},{12,20},{14,22},{16,12},{18,... | collective-permute-start | bytes 393224 | tf_op jit(solution)/shard_map/ppermute | solution.py:194
  12.3 0.0 collective-permute-start.4
  12.3 0.7 collective-permute-start.3
  13.0 0.7 collective-permute-start.2
  13.7 3.6 %shard_map.49 = (f32[2,64,1024]{2,1,0:T(8,128)S(1)}, bf16[2,16,128,1024]{3,2,1,0:T(8,128)(2,1)S(1)}) custom-call(bf16[64,1024]{1,0:T(8,128)(2,1)S(1)} %get-tuple-element.18.after_ref, f32[2,64,1024]{2,1,0:T(8,128)} %refs_0_.3, bf16[2,16,128,1024]{3,2,1,0:T(8,128)(2,1)} %refs_1_.1), custom_call_target="tpu_custom_call" | custom-call | bytes 9043968 | tf_op jit(solution)/shard_map/pallas_call | solution.py:158
  17.3 0.0 collective-permute-done.5.refs_3_
  17.3 1.6 %collective-permute-done.4.refs_2_ = bf16[64,1024]{1,0:T(8,128)(2,1)S(1)} collective-permute-done((bf16[64,1024]{1,0:T(8,128)(2,1)S(1)}, bf16[64,1024]{1,0:T(8,128)(2,1)S(1)}, u32[]{:S(2)}, u32[]{:S(2)}) %collective-permute-start.4) | collective-permute-done | bytes 131104 | tf_op jit(solution)/shard_map/ppermute | solution.py:194
  18.9 0.0 collective-permute-done.3.refs_1_.refs_7_
  18.9 0.0 collective-permute-done.2.refs_0_.refs_6_
  18.9 1.4 %shard_map.50 = (bf16[64,1024]{1,0:T(8,128)(2,1)S(1)}, bf16[64,1024]{1,0:T(8,128)(2,1)S(1)}) custom-call(s32[2,16]{1,0:T(2,128)S(1)} %copy-done.7, f32[2,64,1024]{2,1,0:T(8,128)S(1)} %get-tuple-element.19.right_ref, bf16[2,16,128,1024]{3,2,1,0:T(8,128)(2,1)S(1)} %get-tuple-element.20.lower_ref, bf16[64,1024]{1,0:T(8,128)(2,1)S(1)} %collective-permute-done.2.refs_0_.refs_6_, ...), custom_call_target="tpu_custom_call" | custom-call | flops 268435456 | bytes 9437312 | tf_op jit(solution)/shard_map/pallas_call | solution.py:158
  20.3 0.2 copy-done.3
  20.5 2.0 %collective-permute-start.9 = (bf16[64,1024]{1,0:T(8,128)(2,1)S(1)}, bf16[64,1024]{1,0:T(8,128)(2,1)S(1)}, u32[]{:S(2)}, u32[]{:S(2)}) collective-permute-start(bf16[64,1024]{1,0:T(8,128)(2,1)S(1)} %get-tuple-element.22.refs_0_), channel_id=1, source_target_pairs={{0,2},{2,0},{4,6},{6,4},{8,10},{10,8},{12,14},{14,12},{16,18},{18,... | collective-permute-start | bytes 393224 | tf_op jit(solution)/shard_map/ppermute | solution.py:187
  22.5 0.0 collective-permute-start.7
  22.6 4.0 %collective-permute-start.6 = (bf16[64,1024]{1,0:T(8,128)(2,1)S(1)}, bf16[64,1024]{1,0:T(8,128)(2,1)S(1)}, u32[]{:S(2)}, u32[]{:S(2)}) collective-permute-start(bf16[64,1024]{1,0:T(8,128)(2,1)S(1)} %get-tuple-element.21.refs_5_), channel_id=1, source_target_pairs={{0,4},{2,6},{4,0},{6,2},{8,10},{10,8},{12,14},{14,12},{16,20},{18,... | collective-permute-start | bytes 393224 | tf_op jit(solution)/shard_map/ppermute | solution.py:194
  26.6 0.3 collective-permute-done.9.refs_1_
  26.9 2.2 %copy-done.1 = bf16[2,2048,512]{2,1,0:T(8,128)(2,1)S(1)} copy-done((bf16[2,2048,512]{2,1,0:T(8,128)(2,1)S(1)}, bf16[2,2048,512]{2,1,0:T(8,128)(2,1)}, u32[]{:S(2)}) %copy-start.1) | copy-done | bytes 4194328
  29.1 2.2 %copy-done.6 = bf16[2,2048,512]{2,1,0:T(8,128)(2,1)S(1)} copy-done((bf16[2,2048,512]{2,1,0:T(8,128)(2,1)S(1)}, bf16[2,2048,512]{2,1,0:T(8,128)(2,1)}, u32[]{:S(2)}) %copy-start.6) | copy-done | bytes 4194328
  31.3 0.8 %shard_map.51 = (bf16[64,1024]{1,0:T(8,128)(2,1)S(1)}, f32[64,1024]{1,0:T(8,128)S(1)}) custom-call(bf16[64,1024]{1,0:T(8,128)(2,1)S(1)} %get-tuple-element.22.refs_0_, bf16[64,1024]{1,0:T(8,128)(2,1)S(1)} %collective-permute-done.9.refs_1_, bf16[2,2048,512]{2,1,0:T(8,128)(2,1)S(1)} %copy-done.1, bf16[2,2048,512]{2,1,0:T(8,128)(2,1)S(1)} %copy-done.6, ...), custom_call_target="tpu_custom_call" | custom-call | flops 268435456 | bytes 8912896 | tf_op jit(solution)/shard_map/pallas_call | solution.py:158
  32.1 0.8 %collective-permute-start.13 = (bf16[64,1024]{1,0:T(8,128)(2,1)S(1)}, bf16[64,1024]{1,0:T(8,128)(2,1)S(1)}, u32[]{:S(2)}, u32[]{:S(2)}) collective-permute-start(bf16[64,1024]{1,0:T(8,128)(2,1)S(1)} %get-tuple-element.24.refs_6_), channel_id=1, source_target_pairs={{4,8},{6,10},{20,24},{22,26},{5,9},{7,11},{21,25},{23,27}} | collective-permute-start | bytes 393224 | tf_op jit(solution)/shard_map/ppermute | solution.py:178
  32.9 1.4 %collective-permute-start.12 = (bf16[64,1024]{1,0:T(8,128)(2,1)S(1)}, bf16[64,1024]{1,0:T(8,128)(2,1)S(1)}, u32[]{:S(2)}, u32[]{:S(2)}) collective-permute-start(bf16[64,1024]{1,0:T(8,128)(2,1)S(1)} %get-tuple-element.24.refs_6_), channel_id=1, source_target_pairs={{4,0},{6,2},{20,16},{22,18},{5,1},{7,3},{21,17},{23,19}} | collective-permute-start | bytes 393224 | tf_op jit(solution)/shard_map/ppermute | solution.py:178
  34.4 0.7 collective-permute-start.11
  35.0 0.0 collective-permute-done.7
  35.1 1.3 %collective-permute-start.10 = (bf16[64,1024]{1,0:T(8,128)(2,1)S(1)}, bf16[64,1024]{1,0:T(8,128)(2,1)S(1)}, u32[]{:S(2)}, u32[]{:S(2)}) collective-permute-start(bf16[64,1024]{1,0:T(8,128)(2,1)S(1)} %get-tuple-element.24.refs_6_), channel_id=1, source_target_pairs={{4,2},{6,0},{20,18},{22,16},{5,3},{7,1},{21,19},{23,17}} | collective-permute-start | bytes 393224 | tf_op jit(solution)/shard_map/ppermute | solution.py:178
  36.4 2.1 %collective-permute-start.8 = (bf16[64,1024]{1,0:T(8,128)(2,1)S(1)}, bf16[64,1024]{1,0:T(8,128)(2,1)S(1)}, u32[]{:S(2)}, u32[]{:S(2)}) collective-permute-start(bf16[64,1024]{1,0:T(8,128)(2,1)S(1)} %broadcast_select_fusion.refs_5_), channel_id=1, source_target_pairs={{0,2},{2,0},{4,6},{6,4},{8,10},{10,8},{12,14},{14,12},{16,18},{18,... | collective-permute-start | bytes 393224 | tf_op jit(solution)/shard_map/ppermute | solution.py:187
  38.5 5.0 %collective-permute-done.12.refs_3_ = bf16[64,1024]{1,0:T(8,128)(2,1)S(1)} collective-permute-done((bf16[64,1024]{1,0:T(8,128)(2,1)S(1)}, bf16[64,1024]{1,0:T(8,128)(2,1)S(1)}, u32[]{:S(2)}, u32[]{:S(2)}) %collective-permute-start.12) | collective-permute-done | bytes 131104 | tf_op jit(solution)/shard_map/ppermute | solution.py:178
  43.5 2.0 %collective-permute-done.10.refs_1_ = bf16[64,1024]{1,0:T(8,128)(2,1)S(1)} collective-permute-done((bf16[64,1024]{1,0:T(8,128)(2,1)S(1)}, bf16[64,1024]{1,0:T(8,128)(2,1)S(1)}, u32[]{:S(2)}, u32[]{:S(2)}) %collective-permute-start.10) | collective-permute-done | bytes 131104 | tf_op jit(solution)/shard_map/ppermute | solution.py:178
  45.5 1.4 %shard_map.52 = (bf16[64,1024]{1,0:T(8,128)(2,1)S(1)}, bf16[64,4096]{1,0:T(8,128)(2,1)S(1)}) custom-call(s32[2,16]{1,0:T(2,128)S(1)} %copy-done.7, f32[2,64,1024]{2,1,0:T(8,128)S(1)} %get-tuple-element.19.right_ref, bf16[2,16,128,1024]{3,2,1,0:T(8,128)(2,1)S(1)} %copy-done.4, bf16[64,1024]{1,0:T(8,128)(2,1)S(1)} %collective-permute-done.8.refs_0_, ...), custom_call_target="tpu_custom_call" | custom-call | flops 268435456 | bytes 9830528 | tf_op jit(solution)/shard_map/pallas_call | solution.py:158
  47.0 1.3 %collective-permute-start.14 = (bf16[64,1024]{1,0:T(8,128)(2,1)S(1)}, bf16[64,1024]{1,0:T(8,128)(2,1)S(1)}, u32[]{:S(2)}, u32[]{:S(2)}) collective-permute-start(bf16[64,1024]{1,0:T(8,128)(2,1)S(1)} %get-tuple-element.25.refs_0_), channel_id=1, source_target_pairs={{0,2},{2,0},{4,6},{6,4},{8,10},{10,8},{12,14},{14,12},{16,18},{18,... | collective-permute-start | bytes 393224 | tf_op jit(solution)/shard_map/ppermute | solution.py:187
  48.3 3.7 %collective-permute-done.14.refs_1_ = bf16[64,1024]{1,0:T(8,128)(2,1)S(1)} collective-permute-done((bf16[64,1024]{1,0:T(8,128)(2,1)S(1)}, bf16[64,1024]{1,0:T(8,128)(2,1)S(1)}, u32[]{:S(2)}, u32[]{:S(2)}) %collective-permute-start.14) | collective-permute-done | bytes 131104 | tf_op jit(solution)/shard_map/ppermute | solution.py:187
  52.0 0.9 %shard_map.53 = (bf16[64,1024]{1,0:T(8,128)(2,1)S(1)}, f32[64,1024]{1,0:T(8,128)S(1)}, bf16[64,4096]{1,0:T(8,128)(2,1)S(1)}) custom-call(bf16[64,1024]{1,0:T(8,128)(2,1)S(1)} %get-tuple-element.25.refs_0_, bf16[64,1024]{1,0:T(8,128)(2,1)S(1)} %collective-permute-done.14.refs_1_, bf16[2,2048,512]{2,1,0:T(8,128)(2,1)S(1)} %copy-done.2, ...), custom_call_target="tpu_custom_call" | custom-call | flops 268435456 | bytes 9306112 | tf_op jit(solution)/shard_map/pallas_call | solution.py:158
  52.9 0.7 collective-permute-start.15
  53.6 1.4 %collective-permute-start.18 = (bf16[64,1024]{1,0:T(8,128)(2,1)S(1)}, bf16[64,1024]{1,0:T(8,128)(2,1)S(1)}, u32[]{:S(2)}, u32[]{:S(2)}) collective-permute-start(bf16[64,1024]{1,0:T(8,128)(2,1)S(1)} %get-tuple-element.28.refs_2_), channel_id=1, source_target_pairs={{0,2},{2,0},{4,6},{6,4},{8,10},{10,8},{12,14},{14,12},{16,18},{18,... | collective-permute-start | bytes 393224 | tf_op jit(solution)/shard_map/ppermute | solution.py:187
  54.9 6.2 %collective-permute-start.17 = (bf16[64,1024]{1,0:T(8,128)(2,1)S(1)}, bf16[64,1024]{1,0:T(8,128)(2,1)S(1)}, u32[]{:S(2)}, u32[]{:S(2)}) collective-permute-start(bf16[64,1024]{1,0:T(8,128)(2,1)S(1)} %get-tuple-element.28.refs_2_), channel_id=1, source_target_pairs={{0,6},{2,4},{8,14},{10,12},{16,22},{18,20},{24,30},{26,28},{1,7},{... | collective-permute-start | bytes 393224 | tf_op jit(solution)/shard_map/ppermute | solution.py:178
  61.1 1.4 %collective-permute-start.16 = (bf16[64,1024]{1,0:T(8,128)(2,1)S(1)}, bf16[64,1024]{1,0:T(8,128)(2,1)S(1)}, u32[]{:S(2)}, u32[]{:S(2)}) collective-permute-start(bf16[64,1024]{1,0:T(8,128)(2,1)S(1)} %get-tuple-element.28.refs_2_), channel_id=1, source_target_pairs={{0,4},{2,6},{8,12},{10,14},{16,20},{18,22},{24,28},{26,30},{1,5},{... | collective-permute-start | bytes 393224 | tf_op jit(solution)/shard_map/ppermute | solution.py:178
  62.5 1.1 %collective-permute-done.17.refs_3_ = bf16[64,1024]{1,0:T(8,128)(2,1)S(1)} collective-permute-done((bf16[64,1024]{1,0:T(8,128)(2,1)S(1)}, bf16[64,1024]{1,0:T(8,128)(2,1)S(1)}, u32[]{:S(2)}, u32[]{:S(2)}) %collective-permute-start.17) | collective-permute-done | bytes 131104 | tf_op jit(solution)/shard_map/ppermute | solution.py:178
  63.6 1.4 %collective-permute-done.16.refs_1_ = bf16[64,1024]{1,0:T(8,128)(2,1)S(1)} collective-permute-done((bf16[64,1024]{1,0:T(8,128)(2,1)S(1)}, bf16[64,1024]{1,0:T(8,128)(2,1)S(1)}, u32[]{:S(2)}, u32[]{:S(2)}) %collective-permute-start.16) | collective-permute-done | bytes 131104 | tf_op jit(solution)/shard_map/ppermute | solution.py:178
  65.1 1.4 %shard_map.54.refs_0_ = bf16[64,1024]{1,0:T(8,128)(2,1)S(1)} custom-call(s32[2,16]{1,0:T(2,128)S(1)} %copy-done.7, f32[2,64,1024]{2,1,0:T(8,128)S(1)} %get-tuple-element.19.right_ref, bf16[2,16,128,1024]{3,2,1,0:T(8,128)(2,1)S(1)} %copy-done.4, bf16[64,4096]{1,0:T(8,128)(2,1)S(1)} %collective-permute-done.15.refs_0_, ...), custom_call_target="tpu_custom_call" | custom-call | flops 268435456 | bytes 11010176 | tf_op jit(solution)/shard_map/pallas_call | solution.py:158
  66.5 1.5 %collective-permute-start.19 = (bf16[64,1024]{1,0:T(8,128)(2,1)S(1)}, bf16[64,1024]{1,0:T(8,128)(2,1)S(1)}, u32[]{:S(2)}, u32[]{:S(2)}) collective-permute-start(bf16[64,1024]{1,0:T(8,128)(2,1)S(1)} %shard_map.54.refs_0_), channel_id=1, source_target_pairs={{0,2},{2,0},{4,6},{6,4},{8,10},{10,8},{12,14},{14,12},{16,18},{18,... | collective-permute-start | bytes 393224 | tf_op jit(solution)/shard_map/ppermute | solution.py:187
  68.0 3.5 %collective-permute-done.19.refs_1_ = bf16[64,1024]{1,0:T(8,128)(2,1)S(1)} collective-permute-done((bf16[64,1024]{1,0:T(8,128)(2,1)S(1)}, bf16[64,1024]{1,0:T(8,128)(2,1)S(1)}, u32[]{:S(2)}, u32[]{:S(2)}) %collective-permute-start.19) | collective-permute-done | bytes 131104 | tf_op jit(solution)/shard_map/ppermute | solution.py:187
  71.5 1.5 %shard_map.55 = f32[2,64,1024]{2,1,0:T(8,128)} custom-call(bf16[64,1024]{1,0:T(8,128)(2,1)S(1)} %shard_map.54.refs_0_, bf16[64,1024]{1,0:T(8,128)(2,1)S(1)} %collective-permute-done.19.refs_1_, bf16[2,2048,512]{2,1,0:T(8,128)(2,1)S(1)} %copy-done.2, bf16[2,2048,512]{2,1,0:T(8,128)(2,1)S(1)} %copy-done.6, f32[64,1024]{1,0:T(8,128)S(1)} %get-tuple-element.30.refs_4_), custom_call_target="tpu_custom_call" | custom-call | flops 268435456 | bytes 8912896 | tf_op jit(solution)/shard_map/pallas_call | solution.py:158
  (19 shorter events, 0.1 us)
Async XLA Ops:
  0.0 8.2 %collective-permute-start.1 = (bf16[2,2048,512]{2,1,0:T(8,128)(2,1)}, bf16[2,2048,512]{2,1,0:T(8,128)(2,1)S(1)}, u32[]{:S(2)}, u32[]{:S(2)}) collective-permute-start(bf16[2,2048,512]{2,1,0:T(8,128)(2,1)} %refs_0_.2), channel_id=1, source_target_pairs={{0,1},{1,0},{2,3},{3,2},{4,5},{5,4},{6,7},{7,6},{8,9},{9,8},{10,11... | collective-permute-start | bytes 12582920 | tf_op jit(solution)/shard_map/ppermute | solution.py:198
  1.4 6.8 %collective-permute-start = (bf16[64,1024]{1,0:T(8,128)(2,1)S(1)}, bf16[64,1024]{1,0:T(8,128)(2,1)S(1)}, u32[]{:S(2)}, u32[]{:S(2)}) collective-permute-start(bf16[64,1024]{1,0:T(8,128)(2,1)S(1)} %shard_map.46.after_ref.refs_0_), channel_id=1, source_target_pairs={{0,2},{2,0},{4,6},{6,4},{8,10},{10,8},{12,14},{14,12},{16,18},{18,... | collective-permute-start | bytes 393224 | tf_op jit(solution)/shard_map/ppermute | solution.py:187
  6.2 2.8 %copy-start = (bf16[2,2048,512]{2,1,0:T(8,128)(2,1)}, bf16[2,2048,512]{2,1,0:T(8,128)(2,1)S(1)}, u32[]{:S(2)}) copy-start(bf16[2,2048,512]{2,1,0:T(8,128)(2,1)S(1)} %shard_map.47.refs_2_) | copy-start | bytes 12582916
  8.2 1.9 %copy-start.5 = (bf16[2,2048,512]{2,1,0:T(8,128)(2,1)}, bf16[2,2048,512]{2,1,0:T(8,128)(2,1)S(1)}, u32[]{:S(2)}) copy-start(bf16[2,2048,512]{2,1,0:T(8,128)(2,1)S(1)} %collective-permute-done.1.refs_3_) | copy-start | bytes 12582916
  10.1 8.8 %copy-start.7 = (s32[2,16]{1,0:T(2,128)S(1)}, s32[2,16]{1,0:T(2,128)}, u32[]{:S(2)}) copy-start(s32[2,16]{1,0:T(2,128)} %block_rows_ref.5) | copy-start | bytes 388
  10.1 7.1 %collective-permute-start.5 = (bf16[64,1024]{1,0:T(8,128)(2,1)S(1)}, bf16[64,1024]{1,0:T(8,128)(2,1)S(1)}, u32[]{:S(2)}, u32[]{:S(2)}) collective-permute-start(bf16[64,1024]{1,0:T(8,128)(2,1)S(1)} %get-tuple-element.18.after_ref), channel_id=1, source_target_pairs={{0,2},{2,0},{4,6},{6,4},{8,10},{10,8},{12,20},{14,22},{16,12},{18,... | collective-permute-start | bytes 393224 | tf_op jit(solution)/shard_map/ppermute | solution.py:194
  12.3 6.6 %collective-permute-start.4 = (bf16[64,1024]{1,0:T(8,128)(2,1)S(1)}, bf16[64,1024]{1,0:T(8,128)(2,1)S(1)}, u32[]{:S(2)}, u32[]{:S(2)}) collective-permute-start(bf16[64,1024]{1,0:T(8,128)(2,1)S(1)} %get-tuple-element.18.after_ref), channel_id=1, source_target_pairs={{0,2},{2,0},{4,8},{6,10},{8,12},{10,14},{12,4},{14,6},{16,18},{18,... | collective-permute-start | bytes 393224 | tf_op jit(solution)/shard_map/ppermute | solution.py:194
  12.3 6.6 %collective-permute-start.3 = (bf16[64,1024]{1,0:T(8,128)(2,1)S(1)}, bf16[64,1024]{1,0:T(8,128)(2,1)S(1)}, u32[]{:S(2)}, u32[]{:S(2)}) collective-permute-start(bf16[64,1024]{1,0:T(8,128)(2,1)S(1)} %get-tuple-element.18.after_ref), channel_id=1, source_target_pairs={{12,22},{14,20},{13,23},{15,21}} | collective-permute-start | bytes 393224 | tf_op jit(solution)/shard_map/ppermute | solution.py:178
  13.0 5.9 %collective-permute-start.2 = (bf16[64,1024]{1,0:T(8,128)(2,1)S(1)}, bf16[64,1024]{1,0:T(8,128)(2,1)S(1)}, u32[]{:S(2)}, u32[]{:S(2)}) collective-permute-start(bf16[64,1024]{1,0:T(8,128)(2,1)S(1)} %get-tuple-element.18.after_ref), channel_id=1, source_target_pairs={{12,6},{14,4},{13,7},{15,5}} | collective-permute-start | bytes 393224 | tf_op jit(solution)/shard_map/ppermute | solution.py:178
  17.2 3.3 %copy-start.3 = (bf16[2,16,128,1024]{3,2,1,0:T(8,128)(2,1)}, bf16[2,16,128,1024]{3,2,1,0:T(8,128)(2,1)S(1)}, u32[]{:S(2)}) copy-start(bf16[2,16,128,1024]{3,2,1,0:T(8,128)(2,1)S(1)} %get-tuple-element.20.lower_ref) | copy-start | bytes 25165828
  20.5 6.4 %collective-permute-start.9 = (bf16[64,1024]{1,0:T(8,128)(2,1)S(1)}, bf16[64,1024]{1,0:T(8,128)(2,1)S(1)}, u32[]{:S(2)}, u32[]{:S(2)}) collective-permute-start(bf16[64,1024]{1,0:T(8,128)(2,1)S(1)} %get-tuple-element.22.refs_0_), channel_id=1, source_target_pairs={{0,2},{2,0},{4,6},{6,4},{8,10},{10,8},{12,14},{14,12},{16,18},{18,... | collective-permute-start | bytes 393224 | tf_op jit(solution)/shard_map/ppermute | solution.py:187
  22.5 12.5 %collective-permute-start.7 = (bf16[64,1024]{1,0:T(8,128)(2,1)S(1)}, bf16[64,1024]{1,0:T(8,128)(2,1)S(1)}, u32[]{:S(2)}, u32[]{:S(2)}) collective-permute-start(bf16[64,1024]{1,0:T(8,128)(2,1)S(1)} %get-tuple-element.21.refs_5_), channel_id=1, source_target_pairs={{0,2},{2,0},{4,8},{6,10},{8,4},{10,6},{12,14},{14,12},{16,18},{18,... | collective-permute-start | bytes 393224 | tf_op jit(solution)/shard_map/ppermute | solution.py:194
  22.6 13.8 %collective-permute-start.6 = (bf16[64,1024]{1,0:T(8,128)(2,1)S(1)}, bf16[64,1024]{1,0:T(8,128)(2,1)S(1)}, u32[]{:S(2)}, u32[]{:S(2)}) collective-permute-start(bf16[64,1024]{1,0:T(8,128)(2,1)S(1)} %get-tuple-element.21.refs_5_), channel_id=1, source_target_pairs={{0,4},{2,6},{4,0},{6,2},{8,10},{10,8},{12,14},{14,12},{16,20},{18,... | collective-permute-start | bytes 393224 | tf_op jit(solution)/shard_map/ppermute | solution.py:194
  26.9 2.2 %copy-start.1 = (bf16[2,2048,512]{2,1,0:T(8,128)(2,1)S(1)}, bf16[2,2048,512]{2,1,0:T(8,128)(2,1)}, u32[]{:S(2)}) copy-start(bf16[2,2048,512]{2,1,0:T(8,128)(2,1)} %copy-done) | copy-start | bytes 12582916
  29.1 2.2 %copy-start.6 = (bf16[2,2048,512]{2,1,0:T(8,128)(2,1)S(1)}, bf16[2,2048,512]{2,1,0:T(8,128)(2,1)}, u32[]{:S(2)}) copy-start(bf16[2,2048,512]{2,1,0:T(8,128)(2,1)} %copy-done.5) | copy-start | bytes 12582916
  31.3 14.2 %copy-start.4 = (bf16[2,16,128,1024]{3,2,1,0:T(8,128)(2,1)S(1)}, bf16[2,16,128,1024]{3,2,1,0:T(8,128)(2,1)}, u32[]{:S(2)}) copy-start(bf16[2,16,128,1024]{3,2,1,0:T(8,128)(2,1)} %copy-done.3) | copy-start | bytes 25165828
  32.1 6.3 %collective-permute-start.13 = (bf16[64,1024]{1,0:T(8,128)(2,1)S(1)}, bf16[64,1024]{1,0:T(8,128)(2,1)S(1)}, u32[]{:S(2)}, u32[]{:S(2)}) collective-permute-start(bf16[64,1024]{1,0:T(8,128)(2,1)S(1)} %get-tuple-element.24.refs_6_), channel_id=1, source_target_pairs={{4,8},{6,10},{20,24},{22,26},{5,9},{7,11},{21,25},{23,27}} | collective-permute-start | bytes 393224 | tf_op jit(solution)/shard_map/ppermute | solution.py:178
  32.9 10.5 %collective-permute-start.12 = (bf16[64,1024]{1,0:T(8,128)(2,1)S(1)}, bf16[64,1024]{1,0:T(8,128)(2,1)S(1)}, u32[]{:S(2)}, u32[]{:S(2)}) collective-permute-start(bf16[64,1024]{1,0:T(8,128)(2,1)S(1)} %get-tuple-element.24.refs_6_), channel_id=1, source_target_pairs={{4,0},{6,2},{20,16},{22,18},{5,1},{7,3},{21,17},{23,19}} | collective-permute-start | bytes 393224 | tf_op jit(solution)/shard_map/ppermute | solution.py:178
  34.4 9.1 %collective-permute-start.11 = (bf16[64,1024]{1,0:T(8,128)(2,1)S(1)}, bf16[64,1024]{1,0:T(8,128)(2,1)S(1)}, u32[]{:S(2)}, u32[]{:S(2)}) collective-permute-start(bf16[64,1024]{1,0:T(8,128)(2,1)S(1)} %get-tuple-element.24.refs_6_), channel_id=1, source_target_pairs={{4,10},{6,8},{20,26},{22,24},{5,11},{7,9},{21,27},{23,25}} | collective-permute-start | bytes 393224 | tf_op jit(solution)/shard_map/ppermute | solution.py:178
  35.1 10.5 %collective-permute-start.10 = (bf16[64,1024]{1,0:T(8,128)(2,1)S(1)}, bf16[64,1024]{1,0:T(8,128)(2,1)S(1)}, u32[]{:S(2)}, u32[]{:S(2)}) collective-permute-start(bf16[64,1024]{1,0:T(8,128)(2,1)S(1)} %get-tuple-element.24.refs_6_), channel_id=1, source_target_pairs={{4,2},{6,0},{20,18},{22,16},{5,3},{7,1},{21,19},{23,17}} | collective-permute-start | bytes 393224 | tf_op jit(solution)/shard_map/ppermute | solution.py:178
  36.4 15.6 %copy-start.2 = (bf16[2,2048,512]{2,1,0:T(8,128)(2,1)S(1)}, bf16[2,2048,512]{2,1,0:T(8,128)(2,1)}, u32[]{:S(2)}) copy-start(bf16[2,2048,512]{2,1,0:T(8,128)(2,1)} %copy-done) | copy-start | bytes 12582916
  36.4 9.1 %collective-permute-start.8 = (bf16[64,1024]{1,0:T(8,128)(2,1)S(1)}, bf16[64,1024]{1,0:T(8,128)(2,1)S(1)}, u32[]{:S(2)}, u32[]{:S(2)}) collective-permute-start(bf16[64,1024]{1,0:T(8,128)(2,1)S(1)} %broadcast_select_fusion.refs_5_), channel_id=1, source_target_pairs={{0,2},{2,0},{4,6},{6,4},{8,10},{10,8},{12,14},{14,12},{16,18},{18,... | collective-permute-start | bytes 393224 | tf_op jit(solution)/shard_map/ppermute | solution.py:187
  47.0 5.0 %collective-permute-start.14 = (bf16[64,1024]{1,0:T(8,128)(2,1)S(1)}, bf16[64,1024]{1,0:T(8,128)(2,1)S(1)}, u32[]{:S(2)}, u32[]{:S(2)}) collective-permute-start(bf16[64,1024]{1,0:T(8,128)(2,1)S(1)} %get-tuple-element.25.refs_0_), channel_id=1, source_target_pairs={{0,2},{2,0},{4,6},{6,4},{8,10},{10,8},{12,14},{14,12},{16,18},{18,... | collective-permute-start | bytes 393224 | tf_op jit(solution)/shard_map/ppermute | solution.py:187
  52.9 12.2 %collective-permute-start.15 = (bf16[64,4096]{1,0:T(8,128)(2,1)S(1)}, bf16[64,4096]{1,0:T(8,128)(2,1)S(1)}, u32[]{:S(2)}, u32[]{:S(2)}) collective-permute-start(bf16[64,4096]{1,0:T(8,128)(2,1)S(1)} %get-tuple-element.27.refs_6_), channel_id=1, source_target_pairs={{4,12},{6,14},{20,28},{22,30},{5,13},{7,15},{21,29},{23,31}} | collective-permute-start | bytes 1572872 | tf_op jit(solution)/shard_map/ppermute | solution.py:178
  53.6 8.9 %collective-permute-start.18 = (bf16[64,1024]{1,0:T(8,128)(2,1)S(1)}, bf16[64,1024]{1,0:T(8,128)(2,1)S(1)}, u32[]{:S(2)}, u32[]{:S(2)}) collective-permute-start(bf16[64,1024]{1,0:T(8,128)(2,1)S(1)} %get-tuple-element.28.refs_2_), channel_id=1, source_target_pairs={{0,2},{2,0},{4,6},{6,4},{8,10},{10,8},{12,14},{14,12},{16,18},{18,... | collective-permute-start | bytes 393224 | tf_op jit(solution)/shard_map/ppermute | solution.py:187
  54.9 8.7 %collective-permute-start.17 = (bf16[64,1024]{1,0:T(8,128)(2,1)S(1)}, bf16[64,1024]{1,0:T(8,128)(2,1)S(1)}, u32[]{:S(2)}, u32[]{:S(2)}) collective-permute-start(bf16[64,1024]{1,0:T(8,128)(2,1)S(1)} %get-tuple-element.28.refs_2_), channel_id=1, source_target_pairs={{0,6},{2,4},{8,14},{10,12},{16,22},{18,20},{24,30},{26,28},{1,7},{... | collective-permute-start | bytes 393224 | tf_op jit(solution)/shard_map/ppermute | solution.py:178
  61.1 3.9 %collective-permute-start.16 = (bf16[64,1024]{1,0:T(8,128)(2,1)S(1)}, bf16[64,1024]{1,0:T(8,128)(2,1)S(1)}, u32[]{:S(2)}, u32[]{:S(2)}) collective-permute-start(bf16[64,1024]{1,0:T(8,128)(2,1)S(1)} %get-tuple-element.28.refs_2_), channel_id=1, source_target_pairs={{0,4},{2,6},{8,12},{10,14},{16,20},{18,22},{24,28},{26,30},{1,5},{... | collective-permute-start | bytes 393224 | tf_op jit(solution)/shard_map/ppermute | solution.py:178
  66.5 5.0 %collective-permute-start.19 = (bf16[64,1024]{1,0:T(8,128)(2,1)S(1)}, bf16[64,1024]{1,0:T(8,128)(2,1)S(1)}, u32[]{:S(2)}, u32[]{:S(2)}) collective-permute-start(bf16[64,1024]{1,0:T(8,128)(2,1)S(1)} %shard_map.54.refs_0_), channel_id=1, source_target_pairs={{0,2},{2,0},{4,6},{6,4},{8,10},{10,8},{12,14},{14,12},{16,18},{18,... | collective-permute-start | bytes 393224 | tf_op jit(solution)/shard_map/ppermute | solution.py:187

commit v10 on v9

--- a/solution.py
+++ b/solution.py
@@ -30,6 +30,16 @@
         copy.wait()
 
 
+def choose_kernel(first_ref, second_ref, own_ref, out_ref):
+    leaf = lax.axis_index("leaf")
+    first = (leaf % 4 == 0) | (leaf == lax.axis_size("leaf") - 1)
+    second = leaf % 4 == 2
+    for wanted, ref in ((first, first_ref), (second, second_ref), (jnp.logical_not(first | second), own_ref)):
+        @pl.when(wanted)
+        def _():
+            out_ref[...] = ref[...]
+
+
 def place_pieces(piece_refs, target_ref, start):
     rows = len(piece_refs)
     width = piece_refs[0].shape[1]
@@ -46,10 +56,12 @@
         *refs, reduced_ref, piece_ref, joined, numbers, semaphore, picked = refs
     else:
         *refs, reduced_ref, joined, numbers, semaphore, picked = refs
-    if plan in ("crossed", "traded"):
+    if plan == "crossed":
         late_ref, *refs = refs
     if level == top:
         pieces = [refs[1:2 * rows:2], refs[:2 * rows:2]]
+        if plan == "traded":
+            pieces[1] = pieces[1][::-1]
     else:
         pieces = [refs[:2 * rows:2][::-1], refs[1:2 * rows:2][::-1]]
     extra = refs[2 * rows:]
@@ -65,16 +77,20 @@
         def _():
             if plan == "rooted":
                 piece_ref[...] = pieces[which][0][...]
+            elif plan == "traded" and which == 0:
+                joined[:, :before] = extra[0][...]
+            elif plan == "traded":
+                place_pieces(extra[1:1 + rows], joined, 0)
+                place_pieces(pieces[0], joined, full)
             elif plan == "plain" and before:
                 joined[:, :before] = extra[which][...]
             place_pieces(pieces[which], joined, before)
-    if plan == "crossed":
+    if plan == "rooted":
+        @pl.when(upper_depth(leaf, top) == 0)
+        def _():
+            piece_ref[...] = extra[0][...]
+    elif plan == "crossed":
         place_pieces([extra[0], late_ref], joined, 0)
-    elif plan == "traded":
-        for wanted, ref in ((leaf % 2 == 0, extra[0]), (leaf % 4 == 1, extra[1]), (leaf % 4 == 3, late_ref)):
-            @pl.when(wanted)
-            def _():
-                joined[:, :before] = ref[...]
     blocks, block_width = lower_ref.shape[1:3]
     highest = joined.shape[1] // block_width - 1
     listed.wait()
@@ -104,27 +120,22 @@
 def solve_kernel(top, depth, rows, cores, plan, *refs):
     piece_refs = refs[:rows]
     inverse_refs = refs[rows:rows + cores]
-    before_ref = refs[rows + cores] if depth > 0 else None
-    if plan == "crossed":
-        own_ref, *root_refs = refs[rows + cores + 1:-4]
-        rounded_ref, solved_ref, both_ref, joined = refs[-4:]
-    else:
-        rounded_ref, solved_ref, joined = refs[-3:]
+    before_ref, held_ref = refs[rows + cores:rows + cores + 2]
+    rounded_ref, solved_ref, joined = refs[-3:]
     leaf = lax.axis_index("leaf")
     active = upper_depth(leaf, top) == depth
 
     def store(columns, total):
         rounded_ref[:, columns] = total.astype(BF16)
-        before = jnp.zeros_like(total) if before_ref is None else before_ref[:, columns]
+        before = before_ref[:, columns] if depth > 0 else jnp.zeros_like(total)
         solved_ref[:, columns] = jnp.where(active, total, before)
 
     apply_inverse(1, cores, piece_refs, inverse_refs, joined, store)
     if plan == "crossed":
-        for which, place in enumerate((1, 3)):
-            @pl.when((leaf % 4 == 1) & ((leaf + 1) // 2 % 4 == place))
+        for wanted, ref in ((leaf % 4 == 1, held_ref), (leaf % 4 == 3, piece_refs[1])):
+            @pl.when(wanted)
             def _():
-                place_pieces([own_ref, root_refs[which]], both_ref, 0)
-                both_ref[:, joined.shape[1]:] = joined[...]
+                rounded_ref[...] = ref[...]
 
 
 def last_kernel(rows, cores, *refs):
@@ -187,9 +198,9 @@
             arrived.append(lax.ppermute(value, places, pairs))
         return arrived
 
-    def ring(value, *rings):
+    def ring(value, rings, shift=0):
         after = {a: b for stops in rings for a, b in zip(stops, [*stops[1:], stops[0]])}
-        pairs = [(h * rows + r, after[h] * rows + r if h in after else h * rows + (r + 1) % rows)
+        pairs = [(h * rows + r, after[h] * rows + (r + shift) % rows if h in after else h * rows + (r + 1) % rows)
                  for h in range(leafs) for r in range(rows)]
         return lax.ppermute(value, places, pairs)
 
@@ -225,60 +236,62 @@
     older = []
     solved = None
     for depth, plan in enumerate(plans):
+        here = holders(min(depth, top - 1))
         if depth > 0:
             all_joined = near((count, depth * full_width), BF16)
             fetched = [pltpu.SMEM(block_rows.shape, jnp.int32), pltpu.SemaphoreType.DMA(()), joined]
             kernel = functools.partial(offset_kernel, top, depth, rows, plan)
             pieces = paired(rights[::-1], lefts[::-1]) if depth == top else paired(lefts, rights)
-            if plan == "crossed":
-                older = [late, *pieces, relayed, rounded]
+            if plan == "rooted":
+                pieces = [*pieces, rounded]
+            elif plan == "crossed":
+                pieces = [late, *pieces, relayed, rounded]
             elif plan == "traded":
-                older = [passed, *pieces, mine, both]
+                rights = rights[::-1]
+                pieces = [rights[0], lefts[0], rights[1], lefts[1], mine, relayed, late]
             else:
-                older = [*pieces, *older]
-            arrays = [block_rows, right, lower, *older]
+                pieces = [*pieces, *older]
+            arrays = [block_rows, right, lower, *pieces]
             if plan == "rooted":
                 reduced, own_root = call(kernel, arrays, [], [half, half], [all_joined, *fetched], work)
             elif depth < top:
                 reduced, mine = call(kernel, arrays, [], [half, all_joined], fetched, work)
             else:
                 reduced = call(kernel, arrays, [], [half], [all_joined, *fetched], work)
-        if depth > 0:
-            gathered = rows_of(reduced)
+            if plan == "crossed":
+                gathered = [reduced, ring(reduced, [(h, h + 2) for h in holders(1)])]
+            else:
+                gathered = rows_of(reduced)
         if depth == top:
             staged = [near((count, width), F32), semaphores(cores + 1)]
             return call(functools.partial(last_kernel, rows, cores), [*gathered, *inverses, solved], [],
                         [pltpu.HBM(right_side.shape, F32)], [joined, *staged], work)
-        here = holders(depth)
         older = []
         if depth + 1 < top:
             reach = 2 ** (top - depth - 2)
             ways = [[(h, h - reach) for h in here], [(h, h + reach) for h in here]]
             if plan == "rooted":
-                sides = [ring(own_root, *way) for way in ways]
-                relayed = jnp.where(lax.axis_index("leaf") % 4 == 0, *sides)
+                others = [(h, leafs - 1) for h in holders(0)]
+                first_side, second_side = ring(own_root, ways[0] + others), ring(own_root, ways[1])
+                relayed = call(choose_kernel, [first_side, second_side, own_root], [], [half])
             elif depth > 0:
                 older = [send(mine, way, 0) for way in ways]
         else:
             over = [(h, h + 1) for h in here]
             older = [] if crossing else [mine, send(mine, over, 0)]
         kernel = functools.partial(solve_kernel, top, depth, rows, cores, plan)
-        arrays = [*gathered, *inverses] + ([solved] if depth else [])
-        if plan == "crossed":
-            rounded, solved, both = call(kernel, [*arrays, own_root, *roots], [],
-                                         [half, half_f32, all_joined], [joined], work)
-            passed = send(both, [(h, h + 2) for h in holders(1)], 0)
-        else:
-            rounded, solved = call(kernel, arrays, [], [half, half_f32], [joined], work)
+        arrays = [*gathered, *inverses] + ([solved, rounded] if depth else [])
+        rounded, solved = call(kernel, arrays, [], [half, half_f32], [joined], work)
         if crossing and depth == 0:
             (root,) = here
-            lefts = [ring(rounded, [root, root - reach, root - 1]), send(rounded, ways[0], 1)]
-            rights = [ring(rounded, [root, root + reach, root + 1]), send(rounded, ways[1], 1)]
-            roots = [lefts[1], rights[1]]
+            lefts = [ring(rounded, [(root, root - reach, root - 1)]), send(rounded, ways[0], 1)]
+            rights = [ring(rounded, [(root, root + reach, root + 1)]), send(rounded, ways[1], 1)]
         elif depth + 1 < top:
             lefts, rights = [spread(rounded, way) for way in ways]
             if plan == "rooted":
                 late = rows_of(relayed)[1]
+        elif crossing:
+            lefts, rights = rows_of(rounded), [ring(rounded, over, shift) for shift in range(rows)]
         else:
             lefts, rights = rows_of(rounded), spread(rounded, over)
         if depth == 0:

time: 73.4 us -> 64.3 us (0.88)
  starting transfers between devices: 31.4 us -> 24.3 us
  local copies, waits for them, and re-layouts: 5.68 us -> 0.01 us
  waiting for transfers between devices: 20.7 us -> 24.3 us
    ppermute x9 -> x6, starting transfers between devices: 13.8 us -> 5.25 us  [send(): return lax.ppermute(value, places, pairs)]
    ppermute x4 -> x7, waiting for transfers between devices: 1.62 us -> 9.12 us  [ring(): return lax.ppermute(value, places, pairs)]
    unnamed x16 -> x2, local copies, waits for them, and re-layouts: 5.68 us -> 0.01 us
    ppermute x4 -> x7, starting transfers between devices: 6.26 us -> 9.68 us  [ring(): return lax.ppermute(value, places, pairs)]
    ppermute x9 -> x6, waiting for transfers between devices: 9.6 us -> 7.66 us  [send(): return lax.ppermute(value, places, pairs)]
    ppermute x6 -> x5, waiting for transfers between devices: 9.44 us -> 7.51 us  [rows_of(): arrived.append(lax.ppermute(value, places, pairs))]
    ppermute x6 -> x5, starting transfers between devices: 10.9 us -> 8.97 us  [rows_of(): arrived.append(lax.ppermute(value, places, pairs))]
    pallas_call x10 -> x11, Pallas kernels: 15.1 us -> 15.2 us  [call(): pl.pallas_call(kernel, in_specs=[WHOLE] * len(near) + [FAR] * len(far), o...]
  transfers between devices with their start and end apart: 20 -> 19, of which waited for: 9 -> 10; matrix products, arithmetic and copies ran while one was open for 0% -> 0% of each run, Pallas kernels for 10% -> 12%
where the time goes in v10:
time: 64.3 us; the launch traced here: 64 us
  starting transfers between devices  24.3 us (38%)
  waiting for transfers between devices  24.3 us (38%)
  Pallas kernels  15.2 us (24%)
    pallas_call x11, Pallas kernels, call(): pl.pallas_call(kernel, in_specs=[WHOLE] * len(near) + [FAR] * len(far), o...  15.2 us
    ppermute x7, starting transfers between devices, ring(): return lax.ppermute(value, places, pairs)  9.68 us
    ppermute x7, waiting for transfers between devices, ring(): return lax.ppermute(value, places, pairs)  9.12 us
    ppermute x5, starting transfers between devices, rows_of(): arrived.append(lax.ppermute(value, places, pairs))  8.97 us
    ppermute x6, waiting for transfers between devices, send(): return lax.ppermute(value, places, pairs)  7.66 us
    ppermute x5, waiting for transfers between devices, rows_of(): arrived.append(lax.ppermute(value, places, pairs))  7.51 us
    ppermute x6, starting transfers between devices, send(): return lax.ppermute(value, places, pairs)  5.25 us
  transfers between devices with their start and end apart: 19, of which 10 were waited for; matrix products, arithmetic and copies ran while one was open for 0% of the time, Pallas kernels for 12%

profile of v10, /device:TPU:0, one launch (start us, length us, event | category | flops | bytes accessed | tf_op | source)
XLA Modules:
  0.0 64.0 jit_solution(18314758548854693776)
XLA Ops:
  0.0 0.5 collective-permute-start.1
  0.5 1.0 %shard_map.46.after_ref.refs_0_ = bf16[64,1024]{1,0:T(8,128)(2,1)S(1)} custom-call(f32[2,64,1024]{2,1,0:T(8,128)} %refs_0_.3), custom_call_target="tpu_custom_call" | custom-call | bytes 524288 | tf_op jit(solution)/shard_map/pallas_call | solution.py:169
  1.4 2.6 %collective-permute-start = (bf16[64,1024]{1,0:T(8,128)(2,1)S(1)}, bf16[64,1024]{1,0:T(8,128)(2,1)S(1)}, u32[]{:S(2)}, u32[]{:S(2)}) collective-permute-start(bf16[64,1024]{1,0:T(8,128)(2,1)S(1)} %shard_map.46.after_ref.refs_0_), channel_id=1, source_target_pairs={{0,2},{2,0},{4,6},{6,4},{8,10},{10,8},{12,14},{14,12},{16,18},{18,... | collective-permute-start | bytes 393224 | tf_op jit(solution)/shard_map/ppermute | solution.py:198
  4.0 2.2 %shard_map.47.refs_2_ = bf16[2,2048,512]{2,1,0:T(8,128)(2,1)S(1)} custom-call(bf16[64,1024]{1,0:T(8,128)(2,1)S(1)} %shard_map.46.after_ref.refs_0_, bf16[2,2048,512]{2,1,0:T(8,128)(2,1)} %refs_0_.2), custom_call_target="tpu_custom_call" | custom-call | bytes 4325376 | tf_op jit(solution)/shard_map/pallas_call | solution.py:169
  6.2 2.0 %collective-permute-done.refs_1_ = bf16[64,1024]{1,0:T(8,128)(2,1)S(1)} collective-permute-done((bf16[64,1024]{1,0:T(8,128)(2,1)S(1)}, bf16[64,1024]{1,0:T(8,128)(2,1)S(1)}, u32[]{:S(2)}, u32[]{:S(2)}) %collective-permute-start) | collective-permute-done | bytes 131104 | tf_op jit(solution)/shard_map/ppermute | solution.py:198
  8.2 0.0 collective-permute-done.1.refs_3_
  8.2 0.9 %shard_map.48 = (bf16[64,1024]{1,0:T(8,128)(2,1)S(1)}, f32[64,1024]{1,0:T(8,128)S(1)}) custom-call(bf16[64,1024]{1,0:T(8,128)(2,1)S(1)} %shard_map.46.after_ref.refs_0_, bf16[64,1024]{1,0:T(8,128)(2,1)S(1)} %collective-permute-done.refs_1_, bf16[2,2048,512]{2,1,0:T(8,128)(2,1)S(1)} %shard_map.47.refs_2_, bf16[2,2048,512]{2,1,0:T(8,128)(2,1)S(1)} %collective-permute-done.1.refs_3_), custom_call_target="tpu_custom_call" | custom-call | flops 268435456 | bytes 8650752 | tf_op jit(solution)/shard_map/pallas_call | solution.py:169
  9.1 2.2 %collective-permute-start.5 = (bf16[64,1024]{1,0:T(8,128)(2,1)S(1)}, bf16[64,1024]{1,0:T(8,128)(2,1)S(1)}, u32[]{:S(2)}, u32[]{:S(2)}) collective-permute-start(bf16[64,1024]{1,0:T(8,128)(2,1)S(1)} %get-tuple-element.17.after_ref.refs_4_.refs_5_), channel_id=1, source_target_pairs={{0,2},{2,0},{4,6},{6,4},{8,10},{10,8},{12,20},{14,22},{16,12},{18,... | collective-permute-start | bytes 393224 | tf_op jit(solution)/shard_map/ppermute | solution.py:205
  11.3 0.1 collective-permute-start.4
  11.4 0.7 %collective-permute-start.3 = (bf16[64,1024]{1,0:T(8,128)(2,1)S(1)}, bf16[64,1024]{1,0:T(8,128)(2,1)S(1)}, u32[]{:S(2)}, u32[]{:S(2)}) collective-permute-start(bf16[64,1024]{1,0:T(8,128)(2,1)S(1)} %get-tuple-element.17.after_ref.refs_4_.refs_5_), channel_id=1, source_target_pairs={{12,22},{14,20},{13,23},{15,21}} | collective-permute-start | bytes 393224 | tf_op jit(solution)/shard_map/ppermute | solution.py:189
  12.0 0.7 %collective-permute-start.2 = (bf16[64,1024]{1,0:T(8,128)(2,1)S(1)}, bf16[64,1024]{1,0:T(8,128)(2,1)S(1)}, u32[]{:S(2)}, u32[]{:S(2)}) collective-permute-start(bf16[64,1024]{1,0:T(8,128)(2,1)S(1)} %get-tuple-element.17.after_ref.refs_4_.refs_5_), channel_id=1, source_target_pairs={{12,6},{14,4},{13,7},{15,5}} | collective-permute-start | bytes 393224 | tf_op jit(solution)/shard_map/ppermute | solution.py:189
  12.7 3.6 %shard_map.49 = (f32[2,64,1024]{2,1,0:T(8,128)S(1)}, bf16[2,16,128,1024]{3,2,1,0:T(8,128)(2,1)S(1)}) custom-call(bf16[64,1024]{1,0:T(8,128)(2,1)S(1)} %get-tuple-element.17.after_ref.refs_4_.refs_5_, f32[2,64,1024]{2,1,0:T(8,128)} %refs_0_.3, bf16[2,16,128,1024]{3,2,1,0:T(8,128)(2,1)} %refs_1_.1), custom_call_target="tpu_custom_call" | custom-call | bytes 9043968 | tf_op jit(solution)/shard_map/pallas_call | solution.py:169
  16.3 0.0 collective-permute-done.5.refs_3_
  16.3 1.6 %collective-permute-done.4.refs_2_ = bf16[64,1024]{1,0:T(8,128)(2,1)S(1)} collective-permute-done((bf16[64,1024]{1,0:T(8,128)(2,1)S(1)}, bf16[64,1024]{1,0:T(8,128)(2,1)S(1)}, u32[]{:S(2)}, u32[]{:S(2)}) %collective-permute-start.4) | collective-permute-done | bytes 131104 | tf_op jit(solution)/shard_map/ppermute | solution.py:205
  17.9 0.0 collective-permute-done.3.refs_1_
  17.9 0.0 collective-permute-done.2.refs_0_
  17.9 1.4 %shard_map.50 = (bf16[64,1024]{1,0:T(8,128)(2,1)S(1)}, bf16[64,1024]{1,0:T(8,128)(2,1)S(1)}) custom-call(s32[2,16]{1,0:T(2,128)S(1)} %copy-done, f32[2,64,1024]{2,1,0:T(8,128)S(1)} %get-tuple-element.18.right_ref, bf16[2,16,128,1024]{3,2,1,0:T(8,128)(2,1)S(1)} %get-tuple-element.19.lower_ref, bf16[64,1024]{1,0:T(8,128)(2,1)S(1)} %collective-permute-done.2.refs_0_, ...), custom_call_target="tpu_custom_call" | custom-call | flops 268435456 | bytes 9568384 | tf_op jit(solution)/shard_map/pallas_call | solution.py:169
  19.3 1.8 %collective-permute-start.9 = (bf16[64,1024]{1,0:T(8,128)(2,1)S(1)}, bf16[64,1024]{1,0:T(8,128)(2,1)S(1)}, u32[]{:S(2)}, u32[]{:S(2)}) collective-permute-start(bf16[64,1024]{1,0:T(8,128)(2,1)S(1)} %get-tuple-element.21.refs_0_), channel_id=1, source_target_pairs={{0,2},{2,0},{4,6},{6,4},{8,10},{10,8},{12,14},{14,12},{16,18},{18,... | collective-permute-start | bytes 393224 | tf_op jit(solution)/shard_map/ppermute | solution.py:198
  21.1 0.3 collective-permute-start.7
  21.4 4.1 %collective-permute-start.6 = (bf16[64,1024]{1,0:T(8,128)(2,1)S(1)}, bf16[64,1024]{1,0:T(8,128)(2,1)S(1)}, u32[]{:S(2)}, u32[]{:S(2)}) collective-permute-start(bf16[64,1024]{1,0:T(8,128)(2,1)S(1)} %get-tuple-element.20.own_ref), channel_id=1, source_target_pairs={{0,4},{2,6},{4,0},{6,2},{8,10},{10,8},{12,28},{14,30},{16,20},{18,... | collective-permute-start | bytes 393224 | tf_op jit(solution)/shard_map/ppermute | solution.py:205
  25.5 0.3 collective-permute-done.9.refs_1_
  25.8 0.9 %shard_map.52 = (bf16[64,1024]{1,0:T(8,128)(2,1)S(1)}, f32[64,1024]{1,0:T(8,128)S(1)}) custom-call(bf16[64,1024]{1,0:T(8,128)(2,1)S(1)} %get-tuple-element.21.refs_0_, bf16[64,1024]{1,0:T(8,128)(2,1)S(1)} %collective-permute-done.9.refs_1_, bf16[2,2048,512]{2,1,0:T(8,128)(2,1)S(1)} %shard_map.47.refs_2_, ...), custom_call_target="tpu_custom_call" | custom-call | flops 268435456 | bytes 9043968 | tf_op jit(solution)/shard_map/pallas_call | solution.py:169
  26.7 0.7 %collective-permute-start.13 = (bf16[64,1024]{1,0:T(8,128)(2,1)S(1)}, bf16[64,1024]{1,0:T(8,128)(2,1)S(1)}, u32[]{:S(2)}, u32[]{:S(2)}) collective-permute-start(bf16[64,1024]{1,0:T(8,128)(2,1)S(1)} %get-tuple-element.23.refs_6_.refs_5_), channel_id=1, source_target_pairs={{4,8},{6,10},{20,24},{22,26},{5,9},{7,11},{21,25},{23,27}} | collective-permute-start | bytes 393224 | tf_op jit(solution)/shard_map/ppermute | solution.py:189
  27.4 1.3 %collective-permute-start.12 = (bf16[64,1024]{1,0:T(8,128)(2,1)S(1)}, bf16[64,1024]{1,0:T(8,128)(2,1)S(1)}, u32[]{:S(2)}, u32[]{:S(2)}) collective-permute-start(bf16[64,1024]{1,0:T(8,128)(2,1)S(1)} %get-tuple-element.23.refs_6_.refs_5_), channel_id=1, source_target_pairs={{4,0},{6,2},{20,16},{22,18},{5,1},{7,3},{21,17},{23,19}} | collective-permute-start | bytes 393224 | tf_op jit(solution)/shard_map/ppermute | solution.py:189
  28.7 0.7 %collective-permute-start.11 = (bf16[64,1024]{1,0:T(8,128)(2,1)S(1)}, bf16[64,1024]{1,0:T(8,128)(2,1)S(1)}, u32[]{:S(2)}, u32[]{:S(2)}) collective-permute-start(bf16[64,1024]{1,0:T(8,128)(2,1)S(1)} %get-tuple-element.23.refs_6_.refs_5_), channel_id=1, source_target_pairs={{4,10},{6,8},{20,26},{22,24},{5,11},{7,9},{21,27},{23,25}} | collective-permute-start | bytes 393224 | tf_op jit(solution)/shard_map/ppermute | solution.py:189
  29.3 0.0 collective-permute-done.7.second_ref
  29.3 1.3 %collective-permute-start.10 = (bf16[64,1024]{1,0:T(8,128)(2,1)S(1)}, bf16[64,1024]{1,0:T(8,128)(2,1)S(1)}, u32[]{:S(2)}, u32[]{:S(2)}) collective-permute-start(bf16[64,1024]{1,0:T(8,128)(2,1)S(1)} %get-tuple-element.23.refs_6_.refs_5_), channel_id=1, source_target_pairs={{4,2},{6,0},{20,18},{22,16},{5,3},{7,1},{21,19},{23,17}} | collective-permute-start | bytes 393224 | tf_op jit(solution)/shard_map/ppermute | solution.py:189
  30.6 0.0 collective-permute-done.6.first_ref
  30.7 1.5 %collective-permute-start.8 = (bf16[64,1024]{1,0:T(8,128)(2,1)S(1)}, bf16[64,1024]{1,0:T(8,128)(2,1)S(1)}, u32[]{:S(2)}, u32[]{:S(2)}) collective-permute-start(bf16[64,1024]{1,0:T(8,128)(2,1)S(1)} %shard_map.51.refs_5_), channel_id=1, source_target_pairs={{0,2},{2,0},{4,6},{6,4},{8,10},{10,8},{12,14},{14,12},{16,18},{18,... | collective-permute-start | bytes 393224 | tf_op jit(solution)/shard_map/ppermute | solution.py:198
  32.2 0.0 collective-permute-done.13.refs_4_
  32.2 5.4 %collective-permute-done.12.refs_3_ = bf16[64,1024]{1,0:T(8,128)(2,1)S(1)} collective-permute-done((bf16[64,1024]{1,0:T(8,128)(2,1)S(1)}, bf16[64,1024]{1,0:T(8,128)(2,1)S(1)}, u32[]{:S(2)}, u32[]{:S(2)}) %collective-permute-start.12) | collective-permute-done | bytes 131104 | tf_op jit(solution)/shard_map/ppermute | solution.py:189
  37.6 0.0 collective-permute-done.11.refs_2_
  37.6 2.3 %collective-permute-done.10.refs_1_ = bf16[64,1024]{1,0:T(8,128)(2,1)S(1)} collective-permute-done((bf16[64,1024]{1,0:T(8,128)(2,1)S(1)}, bf16[64,1024]{1,0:T(8,128)(2,1)S(1)}, u32[]{:S(2)}, u32[]{:S(2)}) %collective-permute-start.10) | collective-permute-done | bytes 131104 | tf_op jit(solution)/shard_map/ppermute | solution.py:189
  39.9 0.0 collective-permute-done.8.refs_0_.refs_6_
  39.9 1.4 %shard_map.53 = (bf16[64,1024]{1,0:T(8,128)(2,1)S(1)}, bf16[64,4096]{1,0:T(8,128)(2,1)S(1)}) custom-call(s32[2,16]{1,0:T(2,128)S(1)} %copy-done, f32[2,64,1024]{2,1,0:T(8,128)S(1)} %get-tuple-element.18.right_ref, bf16[2,16,128,1024]{3,2,1,0:T(8,128)(2,1)S(1)} %get-tuple-element.19.lower_ref, bf16[64,1024]{1,0:T(8,128)(2,1)S(1)} %collective-permute-done.8.refs_0_.refs_6_, ...), custom_call_target="tpu_custom_call" | custom-call | flops 268435456 | bytes 9830528 | tf_op jit(solution)/shard_map/pallas_call | solution.py:169
  41.3 1.3 %collective-permute-start.14 = (bf16[64,1024]{1,0:T(8,128)(2,1)S(1)}, bf16[64,1024]{1,0:T(8,128)(2,1)S(1)}, u32[]{:S(2)}, u32[]{:S(2)}) collective-permute-start(bf16[64,1024]{1,0:T(8,128)(2,1)S(1)} %get-tuple-element.24.refs_0_), channel_id=1, source_target_pairs={{0,2},{2,0},{4,12},{6,14},{8,10},{10,8},{12,4},{14,6},{16,18},{18,... | collective-permute-start | bytes 393224 | tf_op jit(solution)/shard_map/ppermute | solution.py:205
  42.6 3.8 %collective-permute-done.14.refs_1_ = bf16[64,1024]{1,0:T(8,128)(2,1)S(1)} collective-permute-done((bf16[64,1024]{1,0:T(8,128)(2,1)S(1)}, bf16[64,1024]{1,0:T(8,128)(2,1)S(1)}, u32[]{:S(2)}, u32[]{:S(2)}) %collective-permute-start.14) | collective-permute-done | bytes 131104 | tf_op jit(solution)/shard_map/ppermute | solution.py:205
  46.3 0.9 %shard_map.54 = (bf16[64,1024]{1,0:T(8,128)(2,1)S(1)}, f32[64,1024]{1,0:T(8,128)S(1)}) custom-call(bf16[64,1024]{1,0:T(8,128)(2,1)S(1)} %get-tuple-element.24.refs_0_, bf16[64,1024]{1,0:T(8,128)(2,1)S(1)} %collective-permute-done.14.refs_1_, bf16[2,2048,512]{2,1,0:T(8,128)(2,1)S(1)} %shard_map.47.refs_2_, ...), custom_call_target="tpu_custom_call" | custom-call | flops 268435456 | bytes 9043968 | tf_op jit(solution)/shard_map/pallas_call | solution.py:169
  47.2 1.8 %collective-permute-start.17 = (bf16[64,1024]{1,0:T(8,128)(2,1)S(1)}, bf16[64,1024]{1,0:T(8,128)(2,1)S(1)}, u32[]{:S(2)}, u32[]{:S(2)}) collective-permute-start(bf16[64,1024]{1,0:T(8,128)(2,1)S(1)} %get-tuple-element.26.refs_1_), channel_id=1, source_target_pairs={{0,2},{2,0},{4,6},{6,4},{8,10},{10,8},{12,14},{14,12},{16,18},{18,... | collective-permute-start | bytes 393224 | tf_op jit(solution)/shard_map/ppermute | solution.py:198
  49.0 1.0 %collective-permute-start.16 = (bf16[64,1024]{1,0:T(8,128)(2,1)S(1)}, bf16[64,1024]{1,0:T(8,128)(2,1)S(1)}, u32[]{:S(2)}, u32[]{:S(2)}) collective-permute-start(bf16[64,1024]{1,0:T(8,128)(2,1)S(1)} %get-tuple-element.26.refs_1_), channel_id=1, source_target_pairs={{0,4},{2,6},{4,0},{6,2},{8,12},{10,14},{12,8},{14,10},{16,20},{18,... | collective-permute-start | bytes 393224 | tf_op jit(solution)/shard_map/ppermute | solution.py:205
  50.1 0.7 %collective-permute-start.15 = (bf16[64,1024]{1,0:T(8,128)(2,1)S(1)}, bf16[64,1024]{1,0:T(8,128)(2,1)S(1)}, u32[]{:S(2)}, u32[]{:S(2)}) collective-permute-start(bf16[64,1024]{1,0:T(8,128)(2,1)S(1)} %get-tuple-element.26.refs_1_), channel_id=1, source_target_pairs={{0,6},{2,4},{4,2},{6,0},{8,14},{10,12},{12,10},{14,8},{16,22},{18,... | collective-permute-start | bytes 393224 | tf_op jit(solution)/shard_map/ppermute | solution.py:205
  50.8 1.5 %collective-permute-done.17.refs_3_ = bf16[64,1024]{1,0:T(8,128)(2,1)S(1)} collective-permute-done((bf16[64,1024]{1,0:T(8,128)(2,1)S(1)}, bf16[64,1024]{1,0:T(8,128)(2,1)S(1)}, u32[]{:S(2)}, u32[]{:S(2)}) %collective-permute-start.17) | collective-permute-done | bytes 131104 | tf_op jit(solution)/shard_map/ppermute | solution.py:198
  52.3 1.7 %collective-permute-done.16.refs_2_ = bf16[64,1024]{1,0:T(8,128)(2,1)S(1)} collective-permute-done((bf16[64,1024]{1,0:T(8,128)(2,1)S(1)}, bf16[64,1024]{1,0:T(8,128)(2,1)S(1)}, u32[]{:S(2)}, u32[]{:S(2)}) %collective-permute-start.16) | collective-permute-done | bytes 131104 | tf_op jit(solution)/shard_map/ppermute | solution.py:205
  54.0 2.0 %collective-permute-done.15.refs_0_ = bf16[64,1024]{1,0:T(8,128)(2,1)S(1)} collective-permute-done((bf16[64,1024]{1,0:T(8,128)(2,1)S(1)}, bf16[64,1024]{1,0:T(8,128)(2,1)S(1)}, u32[]{:S(2)}, u32[]{:S(2)}) %collective-permute-start.15) | collective-permute-done | bytes 131104 | tf_op jit(solution)/shard_map/ppermute | solution.py:205
  56.0 1.4 %shard_map.55.refs_0_ = bf16[64,1024]{1,0:T(8,128)(2,1)S(1)} custom-call(s32[2,16]{1,0:T(2,128)S(1)} %copy-done, f32[2,64,1024]{2,1,0:T(8,128)S(1)} %get-tuple-element.18.right_ref, bf16[2,16,128,1024]{3,2,1,0:T(8,128)(2,1)S(1)} %get-tuple-element.19.lower_ref, bf16[64,1024]{1,0:T(8,128)(2,1)S(1)} %collective-permute-done.15.refs_0_, ...), custom_call_target="tpu_custom_call" | custom-call | flops 268435456 | bytes 10223744 | tf_op jit(solution)/shard_map/pallas_call | solution.py:169
  57.5 1.3 %collective-permute-start.18 = (bf16[64,1024]{1,0:T(8,128)(2,1)S(1)}, bf16[64,1024]{1,0:T(8,128)(2,1)S(1)}, u32[]{:S(2)}, u32[]{:S(2)}) collective-permute-start(bf16[64,1024]{1,0:T(8,128)(2,1)S(1)} %shard_map.55.refs_0_), channel_id=1, source_target_pairs={{0,2},{2,0},{4,6},{6,4},{8,10},{10,8},{12,14},{14,12},{16,18},{18,... | collective-permute-start | bytes 393224 | tf_op jit(solution)/shard_map/ppermute | solution.py:198
  58.7 3.8 %collective-permute-done.18.refs_1_ = bf16[64,1024]{1,0:T(8,128)(2,1)S(1)} collective-permute-done((bf16[64,1024]{1,0:T(8,128)(2,1)S(1)}, bf16[64,1024]{1,0:T(8,128)(2,1)S(1)}, u32[]{:S(2)}, u32[]{:S(2)}) %collective-permute-start.18) | collective-permute-done | bytes 131104 | tf_op jit(solution)/shard_map/ppermute | solution.py:198
  62.5 1.6 %shard_map.56 = f32[2,64,1024]{2,1,0:T(8,128)} custom-call(bf16[64,1024]{1,0:T(8,128)(2,1)S(1)} %shard_map.55.refs_0_, bf16[64,1024]{1,0:T(8,128)(2,1)S(1)} %collective-permute-done.18.refs_1_, bf16[2,2048,512]{2,1,0:T(8,128)(2,1)S(1)} %shard_map.47.refs_2_, bf16[2,2048,512]{2,1,0:T(8,128)(2,1)S(1)} %collective-permute-done.1.refs_3_, ...), custom_call_target="tpu_custom_call" | custom-call | flops 268435456 | bytes 8912896 | tf_op jit(solution)/shard_map/pallas_call | solution.py:169
  (3 shorter events, 0.0 us)
Async XLA Ops:
  0.0 8.2 %collective-permute-start.1 = (bf16[2,2048,512]{2,1,0:T(8,128)(2,1)}, bf16[2,2048,512]{2,1,0:T(8,128)(2,1)S(1)}, u32[]{:S(2)}, u32[]{:S(2)}) collective-permute-start(bf16[2,2048,512]{2,1,0:T(8,128)(2,1)} %refs_0_.2), channel_id=1, source_target_pairs={{0,1},{1,0},{2,3},{3,2},{4,5},{5,4},{6,7},{7,6},{8,9},{9,8},{10,11... | collective-permute-start | bytes 12582920 | tf_op jit(solution)/shard_map/ppermute | solution.py:209
  1.4 6.8 %collective-permute-start = (bf16[64,1024]{1,0:T(8,128)(2,1)S(1)}, bf16[64,1024]{1,0:T(8,128)(2,1)S(1)}, u32[]{:S(2)}, u32[]{:S(2)}) collective-permute-start(bf16[64,1024]{1,0:T(8,128)(2,1)S(1)} %shard_map.46.after_ref.refs_0_), channel_id=1, source_target_pairs={{0,2},{2,0},{4,6},{6,4},{8,10},{10,8},{12,14},{14,12},{16,18},{18,... | collective-permute-start | bytes 393224 | tf_op jit(solution)/shard_map/ppermute | solution.py:198
  9.1 8.8 %copy-start = (s32[2,16]{1,0:T(2,128)S(1)}, s32[2,16]{1,0:T(2,128)}, u32[]{:S(2)}) copy-start(s32[2,16]{1,0:T(2,128)} %block_rows_ref.5) | copy-start | bytes 388
  9.1 7.2 %collective-permute-start.5 = (bf16[64,1024]{1,0:T(8,128)(2,1)S(1)}, bf16[64,1024]{1,0:T(8,128)(2,1)S(1)}, u32[]{:S(2)}, u32[]{:S(2)}) collective-permute-start(bf16[64,1024]{1,0:T(8,128)(2,1)S(1)} %get-tuple-element.17.after_ref.refs_4_.refs_5_), channel_id=1, source_target_pairs={{0,2},{2,0},{4,6},{6,4},{8,10},{10,8},{12,20},{14,22},{16,12},{18,... | collective-permute-start | bytes 393224 | tf_op jit(solution)/shard_map/ppermute | solution.py:205
  11.3 6.6 %collective-permute-start.4 = (bf16[64,1024]{1,0:T(8,128)(2,1)S(1)}, bf16[64,1024]{1,0:T(8,128)(2,1)S(1)}, u32[]{:S(2)}, u32[]{:S(2)}) collective-permute-start(bf16[64,1024]{1,0:T(8,128)(2,1)S(1)} %get-tuple-element.17.after_ref.refs_4_.refs_5_), channel_id=1, source_target_pairs={{0,2},{2,0},{4,8},{6,10},{8,12},{10,14},{12,4},{14,6},{16,18},{18,... | collective-permute-start | bytes 393224 | tf_op jit(solution)/shard_map/ppermute | solution.py:205
  11.4 6.5 %collective-permute-start.3 = (bf16[64,1024]{1,0:T(8,128)(2,1)S(1)}, bf16[64,1024]{1,0:T(8,128)(2,1)S(1)}, u32[]{:S(2)}, u32[]{:S(2)}) collective-permute-start(bf16[64,1024]{1,0:T(8,128)(2,1)S(1)} %get-tuple-element.17.after_ref.refs_4_.refs_5_), channel_id=1, source_target_pairs={{12,22},{14,20},{13,23},{15,21}} | collective-permute-start | bytes 393224 | tf_op jit(solution)/shard_map/ppermute | solution.py:189
  12.0 5.9 %collective-permute-start.2 = (bf16[64,1024]{1,0:T(8,128)(2,1)S(1)}, bf16[64,1024]{1,0:T(8,128)(2,1)S(1)}, u32[]{:S(2)}, u32[]{:S(2)}) collective-permute-start(bf16[64,1024]{1,0:T(8,128)(2,1)S(1)} %get-tuple-element.17.after_ref.refs_4_.refs_5_), channel_id=1, source_target_pairs={{12,6},{14,4},{13,7},{15,5}} | collective-permute-start | bytes 393224 | tf_op jit(solution)/shard_map/ppermute | solution.py:189
  19.3 6.5 %collective-permute-start.9 = (bf16[64,1024]{1,0:T(8,128)(2,1)S(1)}, bf16[64,1024]{1,0:T(8,128)(2,1)S(1)}, u32[]{:S(2)}, u32[]{:S(2)}) collective-permute-start(bf16[64,1024]{1,0:T(8,128)(2,1)S(1)} %get-tuple-element.21.refs_0_), channel_id=1, source_target_pairs={{0,2},{2,0},{4,6},{6,4},{8,10},{10,8},{12,14},{14,12},{16,18},{18,... | collective-permute-start | bytes 393224 | tf_op jit(solution)/shard_map/ppermute | solution.py:198
  21.1 8.2 %collective-permute-start.7 = (bf16[64,1024]{1,0:T(8,128)(2,1)S(1)}, bf16[64,1024]{1,0:T(8,128)(2,1)S(1)}, u32[]{:S(2)}, u32[]{:S(2)}) collective-permute-start(bf16[64,1024]{1,0:T(8,128)(2,1)S(1)} %get-tuple-element.20.own_ref), channel_id=1, source_target_pairs={{0,2},{2,0},{4,8},{6,10},{8,4},{10,6},{12,14},{14,12},{16,18},{18,... | collective-permute-start | bytes 393224 | tf_op jit(solution)/shard_map/ppermute | solution.py:205
  21.4 9.2 %collective-permute-start.6 = (bf16[64,1024]{1,0:T(8,128)(2,1)S(1)}, bf16[64,1024]{1,0:T(8,128)(2,1)S(1)}, u32[]{:S(2)}, u32[]{:S(2)}) collective-permute-start(bf16[64,1024]{1,0:T(8,128)(2,1)S(1)} %get-tuple-element.20.own_ref), channel_id=1, source_target_pairs={{0,4},{2,6},{4,0},{6,2},{8,10},{10,8},{12,28},{14,30},{16,20},{18,... | collective-permute-start | bytes 393224 | tf_op jit(solution)/shard_map/ppermute | solution.py:205
  26.7 5.5 %collective-permute-start.13 = (bf16[64,1024]{1,0:T(8,128)(2,1)S(1)}, bf16[64,1024]{1,0:T(8,128)(2,1)S(1)}, u32[]{:S(2)}, u32[]{:S(2)}) collective-permute-start(bf16[64,1024]{1,0:T(8,128)(2,1)S(1)} %get-tuple-element.23.refs_6_.refs_5_), channel_id=1, source_target_pairs={{4,8},{6,10},{20,24},{22,26},{5,9},{7,11},{21,25},{23,27}} | collective-permute-start | bytes 393224 | tf_op jit(solution)/shard_map/ppermute | solution.py:189
  27.4 10.3 %collective-permute-start.12 = (bf16[64,1024]{1,0:T(8,128)(2,1)S(1)}, bf16[64,1024]{1,0:T(8,128)(2,1)S(1)}, u32[]{:S(2)}, u32[]{:S(2)}) collective-permute-start(bf16[64,1024]{1,0:T(8,128)(2,1)S(1)} %get-tuple-element.23.refs_6_.refs_5_), channel_id=1, source_target_pairs={{4,0},{6,2},{20,16},{22,18},{5,1},{7,3},{21,17},{23,19}} | collective-permute-start | bytes 393224 | tf_op jit(solution)/shard_map/ppermute | solution.py:189
  28.7 9.0 %collective-permute-start.11 = (bf16[64,1024]{1,0:T(8,128)(2,1)S(1)}, bf16[64,1024]{1,0:T(8,128)(2,1)S(1)}, u32[]{:S(2)}, u32[]{:S(2)}) collective-permute-start(bf16[64,1024]{1,0:T(8,128)(2,1)S(1)} %get-tuple-element.23.refs_6_.refs_5_), channel_id=1, source_target_pairs={{4,10},{6,8},{20,26},{22,24},{5,11},{7,9},{21,27},{23,25}} | collective-permute-start | bytes 393224 | tf_op jit(solution)/shard_map/ppermute | solution.py:189
  29.3 10.5 %collective-permute-start.10 = (bf16[64,1024]{1,0:T(8,128)(2,1)S(1)}, bf16[64,1024]{1,0:T(8,128)(2,1)S(1)}, u32[]{:S(2)}, u32[]{:S(2)}) collective-permute-start(bf16[64,1024]{1,0:T(8,128)(2,1)S(1)} %get-tuple-element.23.refs_6_.refs_5_), channel_id=1, source_target_pairs={{4,2},{6,0},{20,18},{22,16},{5,3},{7,1},{21,19},{23,17}} | collective-permute-start | bytes 393224 | tf_op jit(solution)/shard_map/ppermute | solution.py:189
  30.7 9.2 %collective-permute-start.8 = (bf16[64,1024]{1,0:T(8,128)(2,1)S(1)}, bf16[64,1024]{1,0:T(8,128)(2,1)S(1)}, u32[]{:S(2)}, u32[]{:S(2)}) collective-permute-start(bf16[64,1024]{1,0:T(8,128)(2,1)S(1)} %shard_map.51.refs_5_), channel_id=1, source_target_pairs={{0,2},{2,0},{4,6},{6,4},{8,10},{10,8},{12,14},{14,12},{16,18},{18,... | collective-permute-start | bytes 393224 | tf_op jit(solution)/shard_map/ppermute | solution.py:198
  41.3 5.0 %collective-permute-start.14 = (bf16[64,1024]{1,0:T(8,128)(2,1)S(1)}, bf16[64,1024]{1,0:T(8,128)(2,1)S(1)}, u32[]{:S(2)}, u32[]{:S(2)}) collective-permute-start(bf16[64,1024]{1,0:T(8,128)(2,1)S(1)} %get-tuple-element.24.refs_0_), channel_id=1, source_target_pairs={{0,2},{2,0},{4,12},{6,14},{8,10},{10,8},{12,4},{14,6},{16,18},{18,... | collective-permute-start | bytes 393224 | tf_op jit(solution)/shard_map/ppermute | solution.py:205
  47.2 5.0 %collective-permute-start.17 = (bf16[64,1024]{1,0:T(8,128)(2,1)S(1)}, bf16[64,1024]{1,0:T(8,128)(2,1)S(1)}, u32[]{:S(2)}, u32[]{:S(2)}) collective-permute-start(bf16[64,1024]{1,0:T(8,128)(2,1)S(1)} %get-tuple-element.26.refs_1_), channel_id=1, source_target_pairs={{0,2},{2,0},{4,6},{6,4},{8,10},{10,8},{12,14},{14,12},{16,18},{18,... | collective-permute-start | bytes 393224 | tf_op jit(solution)/shard_map/ppermute | solution.py:198
  49.0 5.0 %collective-permute-start.16 = (bf16[64,1024]{1,0:T(8,128)(2,1)S(1)}, bf16[64,1024]{1,0:T(8,128)(2,1)S(1)}, u32[]{:S(2)}, u32[]{:S(2)}) collective-permute-start(bf16[64,1024]{1,0:T(8,128)(2,1)S(1)} %get-tuple-element.26.refs_1_), channel_id=1, source_target_pairs={{0,4},{2,6},{4,0},{6,2},{8,12},{10,14},{12,8},{14,10},{16,20},{18,... | collective-permute-start | bytes 393224 | tf_op jit(solution)/shard_map/ppermute | solution.py:205
  50.1 6.0 %collective-permute-start.15 = (bf16[64,1024]{1,0:T(8,128)(2,1)S(1)}, bf16[64,1024]{1,0:T(8,128)(2,1)S(1)}, u32[]{:S(2)}, u32[]{:S(2)}) collective-permute-start(bf16[64,1024]{1,0:T(8,128)(2,1)S(1)} %get-tuple-element.26.refs_1_), channel_id=1, source_target_pairs={{0,6},{2,4},{4,2},{6,0},{8,14},{10,12},{12,10},{14,8},{16,22},{18,... | collective-permute-start | bytes 393224 | tf_op jit(solution)/shard_map/ppermute | solution.py:205
  57.5 5.0 %collective-permute-start.18 = (bf16[64,1024]{1,0:T(8,128)(2,1)S(1)}, bf16[64,1024]{1,0:T(8,128)(2,1)S(1)}, u32[]{:S(2)}, u32[]{:S(2)}) collective-permute-start(bf16[64,1024]{1,0:T(8,128)(2,1)S(1)} %shard_map.55.refs_0_), channel_id=1, source_target_pairs={{0,2},{2,0},{4,6},{6,4},{8,10},{10,8},{12,14},{14,12},{16,18},{18,... | collective-permute-start | bytes 393224 | tf_op jit(solution)/shard_map/ppermute | solution.py:198

commit v11 on v10

--- a/solution.py
+++ b/solution.py
@@ -191,18 +191,31 @@
     def spread(value, hops):
         return [send(value, hops, shift) for shift in range(rows)]
 
-    def rows_of(value):
-        arrived = [value]
-        for shift in range(1, rows):
-            pairs = [(h * rows + r, h * rows + (r + shift) % rows) for h in range(leafs) for r in range(rows)]
-            arrived.append(lax.ppermute(value, places, pairs))
-        return arrived
-
-    def ring(value, rings, shift=0):
+    def permute(value, target):
+        pairs = []
+        for place in range(leafs * rows):
+            goal = target(*divmod(place, rows))
+            for core in range(cores):
+                if goal is None:
+                    pairs.append((place * cores + core, place * cores + (core + 1) % cores))
+                else:
+                    pairs.append((place * cores + core, (goal[0] * rows + goal[1]) * cores + core))
+        return lax.ppermute(value, ("leaf", "rows", "rhs"), pairs)
+
+    def rows_of(value, traders=None):
+        traders = range(leafs) if traders is None else traders
+        return [value] + [permute(value, lambda h, r: (h, (r + shift) % rows) if h in traders else None)
+                          for shift in range(1, rows)]
+
+    def ring(value, rings, shift=0, traders=()):
         after = {a: b for stops in rings for a, b in zip(stops, [*stops[1:], stops[0]])}
-        pairs = [(h * rows + r, after[h] * rows + (r + shift) % rows if h in after else h * rows + (r + 1) % rows)
-                 for h in range(leafs) for r in range(rows)]
-        return lax.ppermute(value, places, pairs)
+
+        def target(h, r):
+            if h in after:
+                return after[h], (r + shift) % rows
+            return (h, (r + 1) % rows) if h in traders else None
+
+        return permute(value, target)
 
     def core_columns(own):
         turns = range(1, cores)
@@ -229,7 +242,7 @@
         return [piece for pair in zip(lefts[::-1], rights[::-1]) for piece in pair]
 
     reduced = call(cast_kernel, [], [right_side], [half], [near((count, width), F32), pltpu.SemaphoreType.DMA(())])
-    gathered = rows_of(reduced)
+    gathered = rows_of(reduced, holders(0))
     inverses = [load(reduced, [inverse_diag]), *swapped]
     plans = ["rooted", "crossed", "traded"] if crossing else ["plain"] * top
     plans = ["plain", *plans]
@@ -259,9 +272,9 @@
             else:
                 reduced = call(kernel, arrays, [], [half], [all_joined, *fetched], work)
             if plan == "crossed":
-                gathered = [reduced, ring(reduced, [(h, h + 2) for h in holders(1)])]
+                gathered = [reduced, ring(reduced, [(h, h + 2) for h in holders(1)], 0, here)]
             else:
-                gathered = rows_of(reduced)
+                gathered = rows_of(reduced, here if depth < top else None)
         if depth == top:
             staged = [near((count, width), F32), semaphores(cores + 1)]
             return call(functools.partial(last_kernel, rows, cores), [*gathered, *inverses, solved], [],
@@ -284,8 +297,8 @@
         rounded, solved = call(kernel, arrays, [], [half, half_f32], [joined], work)
         if crossing and depth == 0:
             (root,) = here
-            lefts = [ring(rounded, [(root, root - reach, root - 1)]), send(rounded, ways[0], 1)]
-            rights = [ring(rounded, [(root, root + reach, root + 1)]), send(rounded, ways[1], 1)]
+            lefts = [ring(rounded, [(root, root - reach, root - 1)]), ring(rounded, ways[0], 1)]
+            rights = [ring(rounded, [(root, root + reach, root + 1)]), ring(rounded, ways[1], 1)]
         elif depth + 1 < top:
             lefts, rights = [spread(rounded, way) for way in ways]
             if plan == "rooted":

time: 64.3 us -> 62.7 us (0.975)
  starting transfers between devices: 24.3 us -> 21.1 us
  waiting for transfers between devices: 24.3 us -> 25.9 us
    ppermute x12 -> x14, starting transfers between devices: 18.6 us -> 16.7 us  [permute(): return lax.ppermute(value, ('leaf', 'rows', 'rhs'), pairs)]
    ppermute x6 -> x4, starting transfers between devices: 5.25 us -> 3.92 us  [send(): return lax.ppermute(value, places, pairs)]
    ppermute x12 -> x14, waiting for transfers between devices: 16.6 us -> 17.8 us  [permute(): return lax.ppermute(value, ('leaf', 'rows', 'rhs'), pairs)]
    ppermute x6 -> x4, waiting for transfers between devices: 7.66 us -> 8.17 us  [send(): return lax.ppermute(value, places, pairs)]
  transfers between devices with their start and end apart: 19 -> 19, of which waited for: 10 -> 7; matrix products, arithmetic and copies ran while one was open for 0% -> 0% of each run, Pallas kernels for 12% -> 12%
where the time goes in v11:
time: 62.7 us; the launch traced here: 62.4 us
  waiting for transfers between devices  25.9 us (41%)
  starting transfers between devices  21.1 us (34%)
  Pallas kernels  15.3 us (24%)
    ppermute x14, waiting for transfers between devices, permute(): return lax.ppermute(value, ('leaf', 'rows', 'rhs'), pairs)  17.8 us
    ppermute x14, starting transfers between devices, permute(): return lax.ppermute(value, ('leaf', 'rows', 'rhs'), pairs)  16.7 us
    pallas_call x11, Pallas kernels, call(): pl.pallas_call(kernel, in_specs=[WHOLE] * len(near) + [FAR] * len(far), o...  15.3 us
    ppermute x4, waiting for transfers between devices, send(): return lax.ppermute(value, places, pairs)  8.17 us
    ppermute x4, starting transfers between devices, send(): return lax.ppermute(value, places, pairs)  3.92 us
  transfers between devices with their start and end apart: 19, of which 7 were waited for; matrix products, arithmetic and copies ran while one was open for 0% of the time, Pallas kernels for 12%

profile of v11, /device:TPU:0, one launch (start us, length us, event | category | flops | bytes accessed | tf_op | source)
XLA Modules:
  0.0 62.4 jit_solution(15723052419396606166)
XLA Ops:
  0.0 0.5 collective-permute-start.1
  0.5 1.0 %shard_map.46.after_ref.refs_0_ = bf16[64,1024]{1,0:T(8,128)(2,1)S(1)} custom-call(f32[2,64,1024]{2,1,0:T(8,128)} %refs_0_.3), custom_call_target="tpu_custom_call" | custom-call | bytes 524288 | tf_op jit(solution)/shard_map/pallas_call | solution.py:169
  1.4 0.1 collective-permute-start
  1.6 2.2 %shard_map.47.refs_2_ = bf16[2,2048,512]{2,1,0:T(8,128)(2,1)S(1)} custom-call(bf16[64,1024]{1,0:T(8,128)(2,1)S(1)} %shard_map.46.after_ref.refs_0_, bf16[2,2048,512]{2,1,0:T(8,128)(2,1)} %refs_0_.2), custom_call_target="tpu_custom_call" | custom-call | bytes 4325376 | tf_op jit(solution)/shard_map/pallas_call | solution.py:169
  3.8 3.7 %collective-permute-done.refs_1_ = bf16[64,1024]{1,0:T(8,128)(2,1)S(1)} collective-permute-done((bf16[64,1024]{1,0:T(8,128)(2,1)S(1)}, bf16[64,1024]{1,0:T(8,128)(2,1)S(1)}, u32[]{:S(2)}, u32[]{:S(2)}) %collective-permute-start) | collective-permute-done | bytes 131104 | tf_op jit(solution)/shard_map/ppermute | solution.py:203
  7.4 0.0 collective-permute-done.1.refs_3_
  7.5 0.9 %shard_map.48 = (bf16[64,1024]{1,0:T(8,128)(2,1)S(1)}, f32[64,1024]{1,0:T(8,128)S(1)}) custom-call(bf16[64,1024]{1,0:T(8,128)(2,1)S(1)} %shard_map.46.after_ref.refs_0_, bf16[64,1024]{1,0:T(8,128)(2,1)S(1)} %collective-permute-done.refs_1_, bf16[2,2048,512]{2,1,0:T(8,128)(2,1)S(1)} %shard_map.47.refs_2_, bf16[2,2048,512]{2,1,0:T(8,128)(2,1)S(1)} %collective-permute-done.1.refs_3_), custom_call_target="tpu_custom_call" | custom-call | flops 268435456 | bytes 8650752 | tf_op jit(solution)/shard_map/pallas_call | solution.py:169
  8.3 0.4 collective-permute-start.5
  8.8 0.1 collective-permute-start.4
  8.9 0.4 collective-permute-start.3
  9.3 0.1 collective-permute-start.2
  9.4 3.6 %shard_map.49 = (f32[2,64,1024]{2,1,0:T(8,128)S(1)}, bf16[2,16,128,1024]{3,2,1,0:T(8,128)(2,1)S(1)}) custom-call(bf16[64,1024]{1,0:T(8,128)(2,1)S(1)} %get-tuple-element.17.after_ref.refs_4_.refs_5_, f32[2,64,1024]{2,1,0:T(8,128)} %refs_0_.3, bf16[2,16,128,1024]{3,2,1,0:T(8,128)(2,1)} %refs_1_.1), custom_call_target="tpu_custom_call" | custom-call | bytes 9043968 | tf_op jit(solution)/shard_map/pallas_call | solution.py:169
  13.0 0.0 collective-permute-done.5.refs_3_
  13.0 0.0 collective-permute-done.4.refs_2_
  13.0 0.0 collective-permute-done.3.refs_1_
  13.0 0.0 collective-permute-done.2.refs_0_
  13.1 1.4 %shard_map.50 = (bf16[64,1024]{1,0:T(8,128)(2,1)S(1)}, bf16[64,1024]{1,0:T(8,128)(2,1)S(1)}) custom-call(s32[2,16]{1,0:T(2,128)S(1)} %copy-done, f32[2,64,1024]{2,1,0:T(8,128)S(1)} %get-tuple-element.18.right_ref, bf16[2,16,128,1024]{3,2,1,0:T(8,128)(2,1)S(1)} %get-tuple-element.19.lower_ref, bf16[64,1024]{1,0:T(8,128)(2,1)S(1)} %collective-permute-done.2.refs_0_, ...), custom_call_target="tpu_custom_call" | custom-call | flops 268435456 | bytes 9568384 | tf_op jit(solution)/shard_map/pallas_call | solution.py:169
  14.5 0.4 collective-permute-start.9
  14.9 0.1 collective-permute-start.7
  15.1 8.6 %collective-permute-start.6 = (bf16[64,1024]{1,0:T(8,128)(2,1)S(1)}, bf16[64,1024]{1,0:T(8,128)(2,1)S(1)}, u32[]{:S(2)}, u32[]{:S(2)}) collective-permute-start(bf16[64,1024]{1,0:T(8,128)(2,1)S(1)} %get-tuple-element.20.own_ref), channel_id=1, source_target_pairs={{0,4},{1,5},{2,6},{3,7},{4,0},{5,1},{6,2},{7,3},{8,9},{9,8},{10,11... | collective-permute-start | bytes 393224 | tf_op jit(solution)/shard_map/ppermute | solution.py:203
  23.7 0.0 collective-permute-done.9.refs_1_
  23.7 0.9 %shard_map.52 = (bf16[64,1024]{1,0:T(8,128)(2,1)S(1)}, f32[64,1024]{1,0:T(8,128)S(1)}) custom-call(bf16[64,1024]{1,0:T(8,128)(2,1)S(1)} %get-tuple-element.21.refs_0_, bf16[64,1024]{1,0:T(8,128)(2,1)S(1)} %collective-permute-done.9.refs_1_, bf16[2,2048,512]{2,1,0:T(8,128)(2,1)S(1)} %shard_map.47.refs_2_, ...), custom_call_target="tpu_custom_call" | custom-call | flops 268435456 | bytes 9043968 | tf_op jit(solution)/shard_map/pallas_call | solution.py:169
  24.6 0.7 %collective-permute-start.13 = (bf16[64,1024]{1,0:T(8,128)(2,1)S(1)}, bf16[64,1024]{1,0:T(8,128)(2,1)S(1)}, u32[]{:S(2)}, u32[]{:S(2)}) collective-permute-start(bf16[64,1024]{1,0:T(8,128)(2,1)S(1)} %get-tuple-element.23.refs_6_.refs_5_), channel_id=1, source_target_pairs={{4,8},{6,10},{20,24},{22,26},{5,9},{7,11},{21,25},{23,27}} | collective-permute-start | bytes 393224 | tf_op jit(solution)/shard_map/ppermute | solution.py:189
  25.2 1.3 %collective-permute-start.12 = (bf16[64,1024]{1,0:T(8,128)(2,1)S(1)}, bf16[64,1024]{1,0:T(8,128)(2,1)S(1)}, u32[]{:S(2)}, u32[]{:S(2)}) collective-permute-start(bf16[64,1024]{1,0:T(8,128)(2,1)S(1)} %get-tuple-element.23.refs_6_.refs_5_), channel_id=1, source_target_pairs={{4,0},{6,2},{20,16},{22,18},{5,1},{7,3},{21,17},{23,19}} | collective-permute-start | bytes 393224 | tf_op jit(solution)/shard_map/ppermute | solution.py:189
  26.5 0.7 %collective-permute-start.11 = (bf16[64,1024]{1,0:T(8,128)(2,1)S(1)}, bf16[64,1024]{1,0:T(8,128)(2,1)S(1)}, u32[]{:S(2)}, u32[]{:S(2)}) collective-permute-start(bf16[64,1024]{1,0:T(8,128)(2,1)S(1)} %get-tuple-element.23.refs_6_.refs_5_), channel_id=1, source_target_pairs={{4,10},{6,8},{20,26},{22,24},{5,11},{7,9},{21,27},{23,25}} | collective-permute-start | bytes 393224 | tf_op jit(solution)/shard_map/ppermute | solution.py:189
  27.2 0.0 collective-permute-done.7.second_ref
  27.2 1.3 %collective-permute-start.10 = (bf16[64,1024]{1,0:T(8,128)(2,1)S(1)}, bf16[64,1024]{1,0:T(8,128)(2,1)S(1)}, u32[]{:S(2)}, u32[]{:S(2)}) collective-permute-start(bf16[64,1024]{1,0:T(8,128)(2,1)S(1)} %get-tuple-element.23.refs_6_.refs_5_), channel_id=1, source_target_pairs={{4,2},{6,0},{20,18},{22,16},{5,3},{7,1},{21,19},{23,17}} | collective-permute-start | bytes 393224 | tf_op jit(solution)/shard_map/ppermute | solution.py:189
  28.5 0.0 collective-permute-done.6.first_ref
  28.6 1.6 %collective-permute-start.8 = (bf16[64,1024]{1,0:T(8,128)(2,1)S(1)}, bf16[64,1024]{1,0:T(8,128)(2,1)S(1)}, u32[]{:S(2)}, u32[]{:S(2)}) collective-permute-start(bf16[64,1024]{1,0:T(8,128)(2,1)S(1)} %shard_map.51.refs_5_), channel_id=1, source_target_pairs={{0,2},{1,3},{2,0},{3,1},{4,6},{5,7},{6,4},{7,5},{8,10},{9,11},{10,... | collective-permute-start | bytes 393224 | tf_op jit(solution)/shard_map/ppermute | solution.py:203
  30.2 0.0 collective-permute-done.13.refs_4_
  30.2 4.4 %collective-permute-done.12.refs_3_ = bf16[64,1024]{1,0:T(8,128)(2,1)S(1)} collective-permute-done((bf16[64,1024]{1,0:T(8,128)(2,1)S(1)}, bf16[64,1024]{1,0:T(8,128)(2,1)S(1)}, u32[]{:S(2)}, u32[]{:S(2)}) %collective-permute-start.12) | collective-permute-done | bytes 131104 | tf_op jit(solution)/shard_map/ppermute | solution.py:189
  34.6 0.0 collective-permute-done.11.refs_2_
  34.6 3.8 %collective-permute-done.10.refs_1_ = bf16[64,1024]{1,0:T(8,128)(2,1)S(1)} collective-permute-done((bf16[64,1024]{1,0:T(8,128)(2,1)S(1)}, bf16[64,1024]{1,0:T(8,128)(2,1)S(1)}, u32[]{:S(2)}, u32[]{:S(2)}) %collective-permute-start.10) | collective-permute-done | bytes 131104 | tf_op jit(solution)/shard_map/ppermute | solution.py:189
  38.4 0.0 collective-permute-done.8.refs_0_.refs_6_
  38.4 1.4 %shard_map.53 = (bf16[64,1024]{1,0:T(8,128)(2,1)S(1)}, bf16[64,4096]{1,0:T(8,128)(2,1)S(1)}) custom-call(s32[2,16]{1,0:T(2,128)S(1)} %copy-done, f32[2,64,1024]{2,1,0:T(8,128)S(1)} %get-tuple-element.18.right_ref, bf16[2,16,128,1024]{3,2,1,0:T(8,128)(2,1)S(1)} %get-tuple-element.19.lower_ref, bf16[64,1024]{1,0:T(8,128)(2,1)S(1)} %collective-permute-done.8.refs_0_.refs_6_, ...), custom_call_target="tpu_custom_call" | custom-call | flops 268435456 | bytes 9830528 | tf_op jit(solution)/shard_map/pallas_call | solution.py:169
  39.8 0.7 %collective-permute-start.14 = (bf16[64,1024]{1,0:T(8,128)(2,1)S(1)}, bf16[64,1024]{1,0:T(8,128)(2,1)S(1)}, u32[]{:S(2)}, u32[]{:S(2)}) collective-permute-start(bf16[64,1024]{1,0:T(8,128)(2,1)S(1)} %get-tuple-element.24.refs_0_), channel_id=1, source_target_pairs={{0,2},{1,3},{2,0},{3,1},{4,12},{5,13},{6,14},{7,15},{8,10},{9,11},... | collective-permute-start | bytes 393224 | tf_op jit(solution)/shard_map/ppermute | solution.py:203
  40.5 4.6 %collective-permute-done.14.refs_1_ = bf16[64,1024]{1,0:T(8,128)(2,1)S(1)} collective-permute-done((bf16[64,1024]{1,0:T(8,128)(2,1)S(1)}, bf16[64,1024]{1,0:T(8,128)(2,1)S(1)}, u32[]{:S(2)}, u32[]{:S(2)}) %collective-permute-start.14) | collective-permute-done | bytes 131104 | tf_op jit(solution)/shard_map/ppermute | solution.py:203
  45.1 0.9 %shard_map.54 = (bf16[64,1024]{1,0:T(8,128)(2,1)S(1)}, f32[64,1024]{1,0:T(8,128)S(1)}) custom-call(bf16[64,1024]{1,0:T(8,128)(2,1)S(1)} %get-tuple-element.24.refs_0_, bf16[64,1024]{1,0:T(8,128)(2,1)S(1)} %collective-permute-done.14.refs_1_, bf16[2,2048,512]{2,1,0:T(8,128)(2,1)S(1)} %shard_map.47.refs_2_, ...), custom_call_target="tpu_custom_call" | custom-call | flops 268435456 | bytes 9043968 | tf_op jit(solution)/shard_map/pallas_call | solution.py:169
  46.0 0.5 collective-permute-start.17
  46.4 1.6 %collective-permute-start.16 = (bf16[64,1024]{1,0:T(8,128)(2,1)S(1)}, bf16[64,1024]{1,0:T(8,128)(2,1)S(1)}, u32[]{:S(2)}, u32[]{:S(2)}) collective-permute-start(bf16[64,1024]{1,0:T(8,128)(2,1)S(1)} %get-tuple-element.26.refs_1_), channel_id=1, source_target_pairs={{0,4},{1,5},{2,6},{3,7},{4,0},{5,1},{6,2},{7,3},{8,12},{9,13},{10,... | collective-permute-start | bytes 393224 | tf_op jit(solution)/shard_map/ppermute | solution.py:203
  48.1 1.5 %collective-permute-start.15 = (bf16[64,1024]{1,0:T(8,128)(2,1)S(1)}, bf16[64,1024]{1,0:T(8,128)(2,1)S(1)}, u32[]{:S(2)}, u32[]{:S(2)}) collective-permute-start(bf16[64,1024]{1,0:T(8,128)(2,1)S(1)} %get-tuple-element.26.refs_1_), channel_id=1, source_target_pairs={{0,6},{1,7},{2,4},{3,5},{4,2},{5,3},{6,0},{7,1},{8,14},{9,15},{10,... | collective-permute-start | bytes 393224 | tf_op jit(solution)/shard_map/ppermute | solution.py:203
  49.5 2.9 %collective-permute-done.17.refs_3_ = bf16[64,1024]{1,0:T(8,128)(2,1)S(1)} collective-permute-done((bf16[64,1024]{1,0:T(8,128)(2,1)S(1)}, bf16[64,1024]{1,0:T(8,128)(2,1)S(1)}, u32[]{:S(2)}, u32[]{:S(2)}) %collective-permute-start.17) | collective-permute-done | bytes 131104 | tf_op jit(solution)/shard_map/ppermute | solution.py:203
  52.4 0.0 collective-permute-done.16.refs_2_
  52.4 2.0 %collective-permute-done.15.refs_0_ = bf16[64,1024]{1,0:T(8,128)(2,1)S(1)} collective-permute-done((bf16[64,1024]{1,0:T(8,128)(2,1)S(1)}, bf16[64,1024]{1,0:T(8,128)(2,1)S(1)}, u32[]{:S(2)}, u32[]{:S(2)}) %collective-permute-start.15) | collective-permute-done | bytes 131104 | tf_op jit(solution)/shard_map/ppermute | solution.py:203
  54.4 1.4 %shard_map.55.refs_0_ = bf16[64,1024]{1,0:T(8,128)(2,1)S(1)} custom-call(s32[2,16]{1,0:T(2,128)S(1)} %copy-done, f32[2,64,1024]{2,1,0:T(8,128)S(1)} %get-tuple-element.18.right_ref, bf16[2,16,128,1024]{3,2,1,0:T(8,128)(2,1)S(1)} %get-tuple-element.19.lower_ref, bf16[64,1024]{1,0:T(8,128)(2,1)S(1)} %collective-permute-done.15.refs_0_, ...), custom_call_target="tpu_custom_call" | custom-call | flops 268435456 | bytes 10223744 | tf_op jit(solution)/shard_map/pallas_call | solution.py:169
  55.9 0.4 collective-permute-start.18
  56.3 4.6 %collective-permute-done.18.refs_1_ = bf16[64,1024]{1,0:T(8,128)(2,1)S(1)} collective-permute-done((bf16[64,1024]{1,0:T(8,128)(2,1)S(1)}, bf16[64,1024]{1,0:T(8,128)(2,1)S(1)}, u32[]{:S(2)}, u32[]{:S(2)}) %collective-permute-start.18) | collective-permute-done | bytes 131104 | tf_op jit(solution)/shard_map/ppermute | solution.py:203
  60.9 1.6 %shard_map.56 = f32[2,64,1024]{2,1,0:T(8,128)} custom-call(bf16[64,1024]{1,0:T(8,128)(2,1)S(1)} %shard_map.55.refs_0_, bf16[64,1024]{1,0:T(8,128)(2,1)S(1)} %collective-permute-done.18.refs_1_, bf16[2,2048,512]{2,1,0:T(8,128)(2,1)S(1)} %shard_map.47.refs_2_, bf16[2,2048,512]{2,1,0:T(8,128)(2,1)S(1)} %collective-permute-done.1.refs_3_, ...), custom_call_target="tpu_custom_call" | custom-call | flops 268435456 | bytes 8912896 | tf_op jit(solution)/shard_map/pallas_call | solution.py:169
  (3 shorter events, 0.0 us)
Async XLA Ops:
  0.0 7.4 %collective-permute-start.1 = (bf16[2,2048,512]{2,1,0:T(8,128)(2,1)}, bf16[2,2048,512]{2,1,0:T(8,128)(2,1)S(1)}, u32[]{:S(2)}, u32[]{:S(2)}) collective-permute-start(bf16[2,2048,512]{2,1,0:T(8,128)(2,1)} %refs_0_.2), channel_id=1, source_target_pairs={{0,1},{1,0},{2,3},{3,2},{4,5},{5,4},{6,7},{7,6},{8,9},{9,8},{10,11... | collective-permute-start | bytes 12582920 | tf_op jit(solution)/shard_map/ppermute | solution.py:222
  1.4 6.0 %collective-permute-start = (bf16[64,1024]{1,0:T(8,128)(2,1)S(1)}, bf16[64,1024]{1,0:T(8,128)(2,1)S(1)}, u32[]{:S(2)}, u32[]{:S(2)}) collective-permute-start(bf16[64,1024]{1,0:T(8,128)(2,1)S(1)} %shard_map.46.after_ref.refs_0_), channel_id=1, source_target_pairs={{0,1},{1,0},{2,3},{3,2},{4,5},{5,4},{6,7},{7,6},{8,9},{9,8},{10,11... | collective-permute-start | bytes 393224 | tf_op jit(solution)/shard_map/ppermute | solution.py:203
  8.3 4.7 %copy-start = (s32[2,16]{1,0:T(2,128)S(1)}, s32[2,16]{1,0:T(2,128)}, u32[]{:S(2)}) copy-start(s32[2,16]{1,0:T(2,128)} %block_rows_ref.5) | copy-start | bytes 388
  8.3 4.7 %collective-permute-start.5 = (bf16[64,1024]{1,0:T(8,128)(2,1)S(1)}, bf16[64,1024]{1,0:T(8,128)(2,1)S(1)}, u32[]{:S(2)}, u32[]{:S(2)}) collective-permute-start(bf16[64,1024]{1,0:T(8,128)(2,1)S(1)} %get-tuple-element.17.after_ref.refs_4_.refs_5_), channel_id=1, source_target_pairs={{0,1},{1,0},{2,3},{3,2},{4,5},{5,4},{6,7},{7,6},{8,9},{9,8},{10,11... | collective-permute-start | bytes 393224 | tf_op jit(solution)/shard_map/ppermute | solution.py:203
  8.8 4.3 %collective-permute-start.4 = (bf16[64,1024]{1,0:T(8,128)(2,1)S(1)}, bf16[64,1024]{1,0:T(8,128)(2,1)S(1)}, u32[]{:S(2)}, u32[]{:S(2)}) collective-permute-start(bf16[64,1024]{1,0:T(8,128)(2,1)S(1)} %get-tuple-element.17.after_ref.refs_4_.refs_5_), channel_id=1, source_target_pairs={{0,1},{1,0},{2,3},{3,2},{4,8},{5,9},{6,10},{7,11},{8,12},{9,13},{1... | collective-permute-start | bytes 393224 | tf_op jit(solution)/shard_map/ppermute | solution.py:203
  8.9 4.1 %collective-permute-start.3 = (bf16[64,1024]{1,0:T(8,128)(2,1)S(1)}, bf16[64,1024]{1,0:T(8,128)(2,1)S(1)}, u32[]{:S(2)}, u32[]{:S(2)}) collective-permute-start(bf16[64,1024]{1,0:T(8,128)(2,1)S(1)} %get-tuple-element.17.after_ref.refs_4_.refs_5_), channel_id=1, source_target_pairs={{0,1},{1,0},{2,3},{3,2},{4,5},{5,4},{6,7},{7,6},{8,9},{9,8},{10,11... | collective-permute-start | bytes 393224 | tf_op jit(solution)/shard_map/ppermute | solution.py:203
  9.3 3.8 %collective-permute-start.2 = (bf16[64,1024]{1,0:T(8,128)(2,1)S(1)}, bf16[64,1024]{1,0:T(8,128)(2,1)S(1)}, u32[]{:S(2)}, u32[]{:S(2)}) collective-permute-start(bf16[64,1024]{1,0:T(8,128)(2,1)S(1)} %get-tuple-element.17.after_ref.refs_4_.refs_5_), channel_id=1, source_target_pairs={{0,1},{1,0},{2,3},{3,2},{4,14},{5,15},{6,12},{7,13},{8,9},{9,8},{1... | collective-permute-start | bytes 393224 | tf_op jit(solution)/shard_map/ppermute | solution.py:203
  14.5 9.2 %collective-permute-start.9 = (bf16[64,1024]{1,0:T(8,128)(2,1)S(1)}, bf16[64,1024]{1,0:T(8,128)(2,1)S(1)}, u32[]{:S(2)}, u32[]{:S(2)}) collective-permute-start(bf16[64,1024]{1,0:T(8,128)(2,1)S(1)} %get-tuple-element.21.refs_0_), channel_id=1, source_target_pairs={{0,1},{1,0},{2,3},{3,2},{4,6},{5,7},{6,4},{7,5},{8,9},{9,8},{10,11... | collective-permute-start | bytes 393224 | tf_op jit(solution)/shard_map/ppermute | solution.py:203
  14.9 12.3 %collective-permute-start.7 = (bf16[64,1024]{1,0:T(8,128)(2,1)S(1)}, bf16[64,1024]{1,0:T(8,128)(2,1)S(1)}, u32[]{:S(2)}, u32[]{:S(2)}) collective-permute-start(bf16[64,1024]{1,0:T(8,128)(2,1)S(1)} %get-tuple-element.20.own_ref), channel_id=1, source_target_pairs={{0,1},{1,0},{2,3},{3,2},{4,8},{5,9},{6,10},{7,11},{8,4},{9,5},{10,... | collective-permute-start | bytes 393224 | tf_op jit(solution)/shard_map/ppermute | solution.py:203
  15.1 13.5 %collective-permute-start.6 = (bf16[64,1024]{1,0:T(8,128)(2,1)S(1)}, bf16[64,1024]{1,0:T(8,128)(2,1)S(1)}, u32[]{:S(2)}, u32[]{:S(2)}) collective-permute-start(bf16[64,1024]{1,0:T(8,128)(2,1)S(1)} %get-tuple-element.20.own_ref), channel_id=1, source_target_pairs={{0,4},{1,5},{2,6},{3,7},{4,0},{5,1},{6,2},{7,3},{8,9},{9,8},{10,11... | collective-permute-start | bytes 393224 | tf_op jit(solution)/shard_map/ppermute | solution.py:203
  24.6 5.6 %collective-permute-start.13 = (bf16[64,1024]{1,0:T(8,128)(2,1)S(1)}, bf16[64,1024]{1,0:T(8,128)(2,1)S(1)}, u32[]{:S(2)}, u32[]{:S(2)}) collective-permute-start(bf16[64,1024]{1,0:T(8,128)(2,1)S(1)} %get-tuple-element.23.refs_6_.refs_5_), channel_id=1, source_target_pairs={{4,8},{6,10},{20,24},{22,26},{5,9},{7,11},{21,25},{23,27}} | collective-permute-start | bytes 393224 | tf_op jit(solution)/shard_map/ppermute | solution.py:189
  25.2 9.3 %collective-permute-start.12 = (bf16[64,1024]{1,0:T(8,128)(2,1)S(1)}, bf16[64,1024]{1,0:T(8,128)(2,1)S(1)}, u32[]{:S(2)}, u32[]{:S(2)}) collective-permute-start(bf16[64,1024]{1,0:T(8,128)(2,1)S(1)} %get-tuple-element.23.refs_6_.refs_5_), channel_id=1, source_target_pairs={{4,0},{6,2},{20,16},{22,18},{5,1},{7,3},{21,17},{23,19}} | collective-permute-start | bytes 393224 | tf_op jit(solution)/shard_map/ppermute | solution.py:189
  26.5 8.0 %collective-permute-start.11 = (bf16[64,1024]{1,0:T(8,128)(2,1)S(1)}, bf16[64,1024]{1,0:T(8,128)(2,1)S(1)}, u32[]{:S(2)}, u32[]{:S(2)}) collective-permute-start(bf16[64,1024]{1,0:T(8,128)(2,1)S(1)} %get-tuple-element.23.refs_6_.refs_5_), channel_id=1, source_target_pairs={{4,10},{6,8},{20,26},{22,24},{5,11},{7,9},{21,27},{23,25}} | collective-permute-start | bytes 393224 | tf_op jit(solution)/shard_map/ppermute | solution.py:189
  27.2 11.1 %collective-permute-start.10 = (bf16[64,1024]{1,0:T(8,128)(2,1)S(1)}, bf16[64,1024]{1,0:T(8,128)(2,1)S(1)}, u32[]{:S(2)}, u32[]{:S(2)}) collective-permute-start(bf16[64,1024]{1,0:T(8,128)(2,1)S(1)} %get-tuple-element.23.refs_6_.refs_5_), channel_id=1, source_target_pairs={{4,2},{6,0},{20,18},{22,16},{5,3},{7,1},{21,19},{23,17}} | collective-permute-start | bytes 393224 | tf_op jit(solution)/shard_map/ppermute | solution.py:189
  28.6 9.8 %collective-permute-start.8 = (bf16[64,1024]{1,0:T(8,128)(2,1)S(1)}, bf16[64,1024]{1,0:T(8,128)(2,1)S(1)}, u32[]{:S(2)}, u32[]{:S(2)}) collective-permute-start(bf16[64,1024]{1,0:T(8,128)(2,1)S(1)} %shard_map.51.refs_5_), channel_id=1, source_target_pairs={{0,2},{1,3},{2,0},{3,1},{4,6},{5,7},{6,4},{7,5},{8,10},{9,11},{10,... | collective-permute-start | bytes 393224 | tf_op jit(solution)/shard_map/ppermute | solution.py:203
  39.8 5.3 %collective-permute-start.14 = (bf16[64,1024]{1,0:T(8,128)(2,1)S(1)}, bf16[64,1024]{1,0:T(8,128)(2,1)S(1)}, u32[]{:S(2)}, u32[]{:S(2)}) collective-permute-start(bf16[64,1024]{1,0:T(8,128)(2,1)S(1)} %get-tuple-element.24.refs_0_), channel_id=1, source_target_pairs={{0,2},{1,3},{2,0},{3,1},{4,12},{5,13},{6,14},{7,15},{8,10},{9,11},... | collective-permute-start | bytes 393224 | tf_op jit(solution)/shard_map/ppermute | solution.py:203
  46.0 6.4 %collective-permute-start.17 = (bf16[64,1024]{1,0:T(8,128)(2,1)S(1)}, bf16[64,1024]{1,0:T(8,128)(2,1)S(1)}, u32[]{:S(2)}, u32[]{:S(2)}) collective-permute-start(bf16[64,1024]{1,0:T(8,128)(2,1)S(1)} %get-tuple-element.26.refs_1_), channel_id=1, source_target_pairs={{0,2},{1,3},{2,0},{3,1},{4,6},{5,7},{6,4},{7,5},{8,10},{9,11},{10,... | collective-permute-start | bytes 393224 | tf_op jit(solution)/shard_map/ppermute | solution.py:203
  46.4 6.0 %collective-permute-start.16 = (bf16[64,1024]{1,0:T(8,128)(2,1)S(1)}, bf16[64,1024]{1,0:T(8,128)(2,1)S(1)}, u32[]{:S(2)}, u32[]{:S(2)}) collective-permute-start(bf16[64,1024]{1,0:T(8,128)(2,1)S(1)} %get-tuple-element.26.refs_1_), channel_id=1, source_target_pairs={{0,4},{1,5},{2,6},{3,7},{4,0},{5,1},{6,2},{7,3},{8,12},{9,13},{10,... | collective-permute-start | bytes 393224 | tf_op jit(solution)/shard_map/ppermute | solution.py:203
  48.1 6.4 %collective-permute-start.15 = (bf16[64,1024]{1,0:T(8,128)(2,1)S(1)}, bf16[64,1024]{1,0:T(8,128)(2,1)S(1)}, u32[]{:S(2)}, u32[]{:S(2)}) collective-permute-start(bf16[64,1024]{1,0:T(8,128)(2,1)S(1)} %get-tuple-element.26.refs_1_), channel_id=1, source_target_pairs={{0,6},{1,7},{2,4},{3,5},{4,2},{5,3},{6,0},{7,1},{8,14},{9,15},{10,... | collective-permute-start | bytes 393224 | tf_op jit(solution)/shard_map/ppermute | solution.py:203
  55.9 5.0 %collective-permute-start.18 = (bf16[64,1024]{1,0:T(8,128)(2,1)S(1)}, bf16[64,1024]{1,0:T(8,128)(2,1)S(1)}, u32[]{:S(2)}, u32[]{:S(2)}) collective-permute-start(bf16[64,1024]{1,0:T(8,128)(2,1)S(1)} %shard_map.55.refs_0_), channel_id=1, source_target_pairs={{0,2},{1,3},{2,0},{3,1},{4,6},{5,7},{6,4},{7,5},{8,10},{9,11},{10,... | collective-permute-start | bytes 393224 | tf_op jit(solution)/shard_map/ppermute | solution.py:203

commit v12 on v11

--- a/solution.py
+++ b/solution.py
@@ -53,9 +53,9 @@
     leaf = lax.axis_index("leaf")
     slot = 0 if level == top else 1
     if plan == "rooted":
-        *refs, reduced_ref, piece_ref, joined, numbers, semaphore, picked = refs
+        *refs, reduced_ref, piece_ref, joined, picked = refs
     else:
-        *refs, reduced_ref, joined, numbers, semaphore, picked = refs
+        *refs, reduced_ref, joined, picked = refs
     if plan == "crossed":
         late_ref, *refs = refs
     if level == top:
@@ -67,8 +67,6 @@
     extra = refs[2 * rows:]
     width = right_ref.shape[2]
     full = rows * width
-    listed = pltpu.make_async_copy(block_rows_ref, numbers, semaphore)
-    listed.start()
     reach = 2 ** (top - level - 1) if level < top else 1
     first = leaf % 2 == 0 if level == top else ((leaf + 1) // reach) % 4 == 1
     before = (level - 1) * full
@@ -93,7 +91,7 @@
         place_pieces([extra[0], late_ref], joined, 0)
     blocks, block_width = lower_ref.shape[1:3]
     highest = joined.shape[1] // block_width - 1
-    listed.wait()
+    numbers = block_rows_ref[...]
     for index in range(blocks):
         number = jnp.clip(numbers[slot, index], 0, highest)
         column = pl.multiple_of(number * block_width, block_width)
@@ -107,20 +105,50 @@
             reduced_ref[...] = extra[1][...]
 
 
-def apply_inverse(slot, cores, piece_refs, inverse_refs, joined, store):
+def begin_kernel(slot, rows, cores, piece_ref, *refs):
+    inverse_refs, part_ref = refs[:cores], refs[cores]
+    width = piece_ref.shape[1]
     quarter = inverse_refs[0].shape[-1]
-    place_pieces(piece_refs, joined, 0)
-    own = lax.axis_index("rhs")
-    for turn, inverse_ref in enumerate(inverse_refs):
-        total = jnp.dot(joined[...], inverse_ref[slot], preferred_element_type=F32)
-        core = lax.rem(own - turn + cores, cores)
-        store(pl.ds(pl.multiple_of(core * quarter, quarter), quarter), total)
-
-
-def solve_kernel(top, depth, rows, cores, plan, *refs):
+    own = lax.axis_index("rows")
+    for which in range(rows):
+        @pl.when(own == which)
+        def _():
+            for turn, inverse_ref in enumerate(inverse_refs):
+                weights = inverse_ref[slot, which * width:(which + 1) * width, :]
+                part_ref[:, turn * quarter:(turn + 1) * quarter] = jnp.dot(
+                    piece_ref[...], weights, preferred_element_type=F32)
+
+
+def apply_inverse(slot, cores, piece_refs, inverse_refs, part_ref, joined, store, turns=None):
+    rows = len(piece_refs)
+    width = piece_refs[0].shape[1]
+    quarter = inverse_refs[0].shape[-1]
+    own = lax.axis_index("rows")
+    if part_ref is None and turns in (None, [0]):
+        place_pieces(piece_refs, joined, 0)
+    for turn in range(cores) if turns is None else turns:
+        inverse_ref = inverse_refs[turn]
+        core = lax.rem(lax.axis_index("rhs") - turn + cores, cores)
+        columns = pl.ds(pl.multiple_of(core * quarter, quarter), quarter)
+        if part_ref is None:
+            store(columns, jnp.dot(joined[...], inverse_ref[slot], preferred_element_type=F32))
+            continue
+        for which in range(rows):
+            @pl.when(own == which)
+            def _():
+                total = part_ref[:, turn * quarter:(turn + 1) * quarter]
+                for shift in range(1, rows):
+                    source = (which - shift) % rows
+                    weights = inverse_ref[slot, source * width:(source + 1) * width, :]
+                    total = total + jnp.dot(piece_refs[shift][...], weights, preferred_element_type=F32)
+                store(columns, total)
+
+
+def solve_kernel(top, depth, rows, cores, plan, split, *refs):
     piece_refs = refs[:rows]
     inverse_refs = refs[rows:rows + cores]
-    before_ref, held_ref = refs[rows + cores:rows + cores + 2]
+    before_ref, held_ref, part_ref = refs[rows + cores:rows + cores + 3]
+    part_ref = part_ref if split else None
     rounded_ref, solved_ref, joined = refs[-3:]
     leaf = lax.axis_index("leaf")
     active = upper_depth(leaf, top) == depth
@@ -130,7 +158,7 @@
         before = before_ref[:, columns] if depth > 0 else jnp.zeros_like(total)
         solved_ref[:, columns] = jnp.where(active, total, before)
 
-    apply_inverse(1, cores, piece_refs, inverse_refs, joined, store)
+    apply_inverse(1, cores, piece_refs, inverse_refs, part_ref, joined, store)
     if plan == "crossed":
         for wanted, ref in ((leaf % 4 == 1, held_ref), (leaf % 4 == 3, piece_refs[1])):
             @pl.when(wanted)
@@ -138,20 +166,26 @@
                 rounded_ref[...] = ref[...]
 
 
-def last_kernel(rows, cores, *refs):
+def last_kernel(rows, cores, split, *refs):
     piece_refs = refs[:rows]
     inverse_refs = refs[rows:rows + cores]
-    before_ref, out_ref, joined, staged, semaphores = refs[rows + cores:]
+    before_ref, *part, out_ref, joined, staged, semaphores = refs[rows + cores:]
+    part_ref = part[0] if split else None
     copies = [pltpu.make_async_copy(before_ref, out_ref.at[1], semaphores.at[0])]
     copies[0].start()
 
+    quarter = inverse_refs[0].shape[-1]
+
     def store(columns, total):
         staged[:, columns] = total
-        copy = pltpu.make_async_copy(staged.at[:, columns], out_ref.at[0, :, columns], semaphores.at[len(copies)])
-        copy.start()
-        copies.append(copy)
-
-    apply_inverse(0, cores, piece_refs, inverse_refs, joined, store)
+
+    for turn in range(cores):
+        core = lax.rem(lax.axis_index("rhs") - turn + cores, cores)
+        columns = pl.ds(pl.multiple_of(core * quarter, quarter), quarter)
+        apply_inverse(0, cores, piece_refs, inverse_refs, part_ref, joined, store, [turn])
+        copies.append(pltpu.make_async_copy(
+            staged.at[:, columns], out_ref.at[0, :, columns], semaphores.at[turn + 1]))
+        copies[-1].start()
     for copy in copies:
         copy.wait()
 
@@ -252,7 +286,6 @@
         here = holders(min(depth, top - 1))
         if depth > 0:
             all_joined = near((count, depth * full_width), BF16)
-            fetched = [pltpu.SMEM(block_rows.shape, jnp.int32), pltpu.SemaphoreType.DMA(()), joined]
             kernel = functools.partial(offset_kernel, top, depth, rows, plan)
             pieces = paired(rights[::-1], lefts[::-1]) if depth == top else paired(lefts, rights)
             if plan == "rooted":
@@ -266,18 +299,23 @@
                 pieces = [*pieces, *older]
             arrays = [block_rows, right, lower, *pieces]
             if plan == "rooted":
-                reduced, own_root = call(kernel, arrays, [], [half, half], [all_joined, *fetched], work)
+                reduced, own_root = call(kernel, arrays, [], [half, half], [all_joined, joined], work)
             elif depth < top:
-                reduced, mine = call(kernel, arrays, [], [half, all_joined], fetched, work)
+                reduced, mine = call(kernel, arrays, [], [half, all_joined], [joined], work)
             else:
-                reduced = call(kernel, arrays, [], [half], [all_joined, *fetched], work)
+                reduced = call(kernel, arrays, [], [half], [all_joined, joined], work)
             if plan == "crossed":
                 gathered = [reduced, ring(reduced, [(h, h + 2) for h in holders(1)], 0, here)]
             else:
                 gathered = rows_of(reduced, here if depth < top else None)
+        split = crossing and depth > 1
+        part = []
+        if split:
+            kernel = functools.partial(begin_kernel, 0 if depth == top else 1, rows, cores)
+            part = [call(kernel, [reduced, *inverses], [], [half_f32], (), work // rows)]
         if depth == top:
             staged = [near((count, width), F32), semaphores(cores + 1)]
-            return call(functools.partial(last_kernel, rows, cores), [*gathered, *inverses, solved], [],
+            return call(functools.partial(last_kernel, rows, cores, split), [*gathered, *inverses, solved, *part], [],
                         [pltpu.HBM(right_side.shape, F32)], [joined, *staged], work)
         older = []
         if depth + 1 < top:
@@ -292,8 +330,8 @@
         else:
             over = [(h, h + 1) for h in here]
             older = [] if crossing else [mine, send(mine, over, 0)]
-        kernel = functools.partial(solve_kernel, top, depth, rows, cores, plan)
-        arrays = [*gathered, *inverses] + ([solved, rounded] if depth else [])
+        kernel = functools.partial(solve_kernel, top, depth, rows, cores, plan, split)
+        arrays = [*gathered, *inverses] + ([solved, rounded, *part] if depth else [])
         rounded, solved = call(kernel, arrays, [], [half, half_f32], [joined], work)
         if crossing and depth == 0:
             (root,) = here

time: 62.7 us -> 60.9 us (0.971)
  Pallas kernels: 15.3 us -> 14.4 us
  waiting for transfers between devices: 25.9 us -> 25 us
    ppermute x14, waiting for transfers between devices: 17.8 us -> 16.8 us  [permute(): return lax.ppermute(value, ('leaf', 'rows', 'rhs'), pairs)]
    pallas_call x11 -> x13, Pallas kernels: 15.3 us -> 14.4 us  [call(): pl.pallas_call(kernel, in_specs=[WHOLE] * len(near) + [FAR] * len(far), o...]
  transfers between devices with their start and end apart: 19 -> 19, of which waited for: 7 -> 7; matrix products, arithmetic and copies ran while one was open for 0% -> 0% of each run, Pallas kernels for 12% -> 14%
where the time goes in v12:
time: 60.9 us; the launch traced here: 60.6 us
  waiting for transfers between devices  25 us (41%)
  starting transfers between devices  21 us (34%)
  Pallas kernels  14.4 us (24%)
    ppermute x14, waiting for transfers between devices, permute(): return lax.ppermute(value, ('leaf', 'rows', 'rhs'), pairs)  16.8 us
    ppermute x14, starting transfers between devices, permute(): return lax.ppermute(value, ('leaf', 'rows', 'rhs'), pairs)  16.7 us
    pallas_call x13, Pallas kernels, call(): pl.pallas_call(kernel, in_specs=[WHOLE] * len(near) + [FAR] * len(far), o...  14.4 us
    ppermute x4, waiting for transfers between devices, send(): return lax.ppermute(value, places, pairs)  8.17 us
    ppermute x4, starting transfers between devices, send(): return lax.ppermute(value, places, pairs)  3.92 us
  transfers between devices with their start and end apart: 19, of which 7 were waited for; matrix products, arithmetic and copies ran while one was open for 0% of the time, Pallas kernels for 14%

profile of v12, /device:TPU:0, one launch (start us, length us, event | category | flops | bytes accessed | tf_op | source)
XLA Modules:
  0.0 60.6 jit_solution(13419432450821311821)
XLA Ops:
  0.0 0.5 collective-permute-start.1
  0.5 1.0 %shard_map.46.after_ref.refs_0_ = bf16[64,1024]{1,0:T(8,128)(2,1)S(1)} custom-call(f32[2,64,1024]{2,1,0:T(8,128)} %refs_0_.3), custom_call_target="tpu_custom_call" | custom-call | bytes 524288 | tf_op jit(solution)/shard_map/pallas_call | solution.py:203
  1.4 0.1 collective-permute-start
  1.6 2.2 %shard_map.47.refs_2_.refs_0_ = bf16[2,2048,512]{2,1,0:T(8,128)(2,1)S(1)} custom-call(bf16[64,1024]{1,0:T(8,128)(2,1)S(1)} %shard_map.46.after_ref.refs_0_, bf16[2,2048,512]{2,1,0:T(8,128)(2,1)} %refs_0_.2), custom_call_target="tpu_custom_call" | custom-call | bytes 4325376 | tf_op jit(solution)/shard_map/pallas_call | solution.py:203
  3.8 3.7 %collective-permute-done.refs_1_ = bf16[64,1024]{1,0:T(8,128)(2,1)S(1)} collective-permute-done((bf16[64,1024]{1,0:T(8,128)(2,1)S(1)}, bf16[64,1024]{1,0:T(8,128)(2,1)S(1)}, u32[]{:S(2)}, u32[]{:S(2)}) %collective-permute-start) | collective-permute-done | bytes 131104 | tf_op jit(solution)/shard_map/ppermute | solution.py:237
  7.4 0.0 collective-permute-done.1.refs_3_.refs_1_
  7.5 0.9 %shard_map.48 = (bf16[64,1024]{1,0:T(8,128)(2,1)S(1)}, f32[64,1024]{1,0:T(8,128)S(1)}) custom-call(bf16[64,1024]{1,0:T(8,128)(2,1)S(1)} %shard_map.46.after_ref.refs_0_, bf16[64,1024]{1,0:T(8,128)(2,1)S(1)} %collective-permute-done.refs_1_, bf16[2,2048,512]{2,1,0:T(8,128)(2,1)S(1)} %shard_map.47.refs_2_.refs_0_, ...), custom_call_target="tpu_custom_call" | custom-call | flops 268435456 | bytes 8650752 | tf_op jit(solution)/shard_map/pallas_call | solution.py:203
  8.3 0.4 collective-permute-start.5
  8.8 0.1 collective-permute-start.4
  8.9 0.4 collective-permute-start.3
  9.3 0.1 collective-permute-start.2
  9.4 3.6 %shard_map.49 = (f32[2,64,1024]{2,1,0:T(8,128)S(1)}, bf16[2,16,128,1024]{3,2,1,0:T(8,128)(2,1)S(1)}) custom-call(bf16[64,1024]{1,0:T(8,128)(2,1)S(1)} %get-tuple-element.17.after_ref.refs_4_.refs_5_, f32[2,64,1024]{2,1,0:T(8,128)} %refs_0_.3, bf16[2,16,128,1024]{3,2,1,0:T(8,128)(2,1)} %refs_1_.1), custom_call_target="tpu_custom_call" | custom-call | bytes 9043968 | tf_op jit(solution)/shard_map/pallas_call | solution.py:203
  13.0 0.0 collective-permute-done.5.refs_3_
  13.0 0.0 collective-permute-done.4.refs_2_
  13.0 0.0 collective-permute-done.3.refs_1_
  13.0 0.0 collective-permute-done.2.refs_0_
  13.1 1.0 %shard_map.50 = (bf16[64,1024]{1,0:T(8,128)(2,1)S(1)}, bf16[64,1024]{1,0:T(8,128)(2,1)S(1)}) custom-call(s32[2,16]{1,0:T(2,128)S(1)} %copy-done, f32[2,64,1024]{2,1,0:T(8,128)S(1)} %get-tuple-element.18.right_ref, bf16[2,16,128,1024]{3,2,1,0:T(8,128)(2,1)S(1)} %get-tuple-element.19.lower_ref, bf16[64,1024]{1,0:T(8,128)(2,1)S(1)} %collective-permute-done.2.refs_0_, ...), custom_call_target="tpu_custom_call" | custom-call | flops 268435456 | bytes 9568384 | tf_op jit(solution)/shard_map/pallas_call | solution.py:203
  14.1 0.4 collective-permute-start.9
  14.5 0.1 collective-permute-start.7
  14.7 8.6 %collective-permute-start.6 = (bf16[64,1024]{1,0:T(8,128)(2,1)S(1)}, bf16[64,1024]{1,0:T(8,128)(2,1)S(1)}, u32[]{:S(2)}, u32[]{:S(2)}) collective-permute-start(bf16[64,1024]{1,0:T(8,128)(2,1)S(1)} %get-tuple-element.20.own_ref), channel_id=1, source_target_pairs={{0,4},{1,5},{2,6},{3,7},{4,0},{5,1},{6,2},{7,3},{8,9},{9,8},{10,11... | collective-permute-start | bytes 393224 | tf_op jit(solution)/shard_map/ppermute | solution.py:237
  23.3 0.0 collective-permute-done.9.refs_1_
  23.3 0.9 %shard_map.52 = (bf16[64,1024]{1,0:T(8,128)(2,1)S(1)}, f32[64,1024]{1,0:T(8,128)S(1)}) custom-call(bf16[64,1024]{1,0:T(8,128)(2,1)S(1)} %get-tuple-element.21.refs_0_, bf16[64,1024]{1,0:T(8,128)(2,1)S(1)} %collective-permute-done.9.refs_1_, bf16[2,2048,512]{2,1,0:T(8,128)(2,1)S(1)} %shard_map.47.refs_2_.refs_0_, ...), custom_call_target="tpu_custom_call" | custom-call | flops 268435456 | bytes 9043968 | tf_op jit(solution)/shard_map/pallas_call | solution.py:203
  24.1 0.7 %collective-permute-start.13 = (bf16[64,1024]{1,0:T(8,128)(2,1)S(1)}, bf16[64,1024]{1,0:T(8,128)(2,1)S(1)}, u32[]{:S(2)}, u32[]{:S(2)}) collective-permute-start(bf16[64,1024]{1,0:T(8,128)(2,1)S(1)} %get-tuple-element.23.refs_6_.refs_5_), channel_id=1, source_target_pairs={{4,8},{6,10},{20,24},{22,26},{5,9},{7,11},{21,25},{23,27}} | collective-permute-start | bytes 393224 | tf_op jit(solution)/shard_map/ppermute | solution.py:223
  24.8 1.3 %collective-permute-start.12 = (bf16[64,1024]{1,0:T(8,128)(2,1)S(1)}, bf16[64,1024]{1,0:T(8,128)(2,1)S(1)}, u32[]{:S(2)}, u32[]{:S(2)}) collective-permute-start(bf16[64,1024]{1,0:T(8,128)(2,1)S(1)} %get-tuple-element.23.refs_6_.refs_5_), channel_id=1, source_target_pairs={{4,0},{6,2},{20,16},{22,18},{5,1},{7,3},{21,17},{23,19}} | collective-permute-start | bytes 393224 | tf_op jit(solution)/shard_map/ppermute | solution.py:223
  26.1 0.7 %collective-permute-start.11 = (bf16[64,1024]{1,0:T(8,128)(2,1)S(1)}, bf16[64,1024]{1,0:T(8,128)(2,1)S(1)}, u32[]{:S(2)}, u32[]{:S(2)}) collective-permute-start(bf16[64,1024]{1,0:T(8,128)(2,1)S(1)} %get-tuple-element.23.refs_6_.refs_5_), channel_id=1, source_target_pairs={{4,10},{6,8},{20,26},{22,24},{5,11},{7,9},{21,27},{23,25}} | collective-permute-start | bytes 393224 | tf_op jit(solution)/shard_map/ppermute | solution.py:223
  26.8 0.0 collective-permute-done.7.second_ref
  26.8 1.3 %collective-permute-start.10 = (bf16[64,1024]{1,0:T(8,128)(2,1)S(1)}, bf16[64,1024]{1,0:T(8,128)(2,1)S(1)}, u32[]{:S(2)}, u32[]{:S(2)}) collective-permute-start(bf16[64,1024]{1,0:T(8,128)(2,1)S(1)} %get-tuple-element.23.refs_6_.refs_5_), channel_id=1, source_target_pairs={{4,2},{6,0},{20,18},{22,16},{5,3},{7,1},{21,19},{23,17}} | collective-permute-start | bytes 393224 | tf_op jit(solution)/shard_map/ppermute | solution.py:223
  28.1 0.0 collective-permute-done.6.first_ref
  28.2 1.6 %collective-permute-start.8 = (bf16[64,1024]{1,0:T(8,128)(2,1)S(1)}, bf16[64,1024]{1,0:T(8,128)(2,1)S(1)}, u32[]{:S(2)}, u32[]{:S(2)}) collective-permute-start(bf16[64,1024]{1,0:T(8,128)(2,1)S(1)} %shard_map.51.refs_5_), channel_id=1, source_target_pairs={{0,2},{1,3},{2,0},{3,1},{4,6},{5,7},{6,4},{7,5},{8,10},{9,11},{10,... | collective-permute-start | bytes 393224 | tf_op jit(solution)/shard_map/ppermute | solution.py:237
  29.8 4.4 %collective-permute-done.12.refs_3_ = bf16[64,1024]{1,0:T(8,128)(2,1)S(1)} collective-permute-done((bf16[64,1024]{1,0:T(8,128)(2,1)S(1)}, bf16[64,1024]{1,0:T(8,128)(2,1)S(1)}, u32[]{:S(2)}, u32[]{:S(2)}) %collective-permute-start.12) | collective-permute-done | bytes 131104 | tf_op jit(solution)/shard_map/ppermute | solution.py:223
  34.1 0.0 collective-permute-done.11.refs_2_
  34.1 3.8 %collective-permute-done.10.refs_1_ = bf16[64,1024]{1,0:T(8,128)(2,1)S(1)} collective-permute-done((bf16[64,1024]{1,0:T(8,128)(2,1)S(1)}, bf16[64,1024]{1,0:T(8,128)(2,1)S(1)}, u32[]{:S(2)}, u32[]{:S(2)}) %collective-permute-start.10) | collective-permute-done | bytes 131104 | tf_op jit(solution)/shard_map/ppermute | solution.py:223
  37.9 0.0 collective-permute-done.8.refs_0_.refs_6_
  37.9 1.0 %shard_map.53 = (bf16[64,1024]{1,0:T(8,128)(2,1)S(1)}, bf16[64,4096]{1,0:T(8,128)(2,1)S(1)}) custom-call(s32[2,16]{1,0:T(2,128)S(1)} %copy-done, f32[2,64,1024]{2,1,0:T(8,128)S(1)} %get-tuple-element.18.right_ref, bf16[2,16,128,1024]{3,2,1,0:T(8,128)(2,1)S(1)} %get-tuple-element.19.lower_ref, bf16[64,1024]{1,0:T(8,128)(2,1)S(1)} %collective-permute-done.8.refs_0_.refs_6_, ...), custom_call_target="tpu_custom_call" | custom-call | flops 268435456 | bytes 9830528 | tf_op jit(solution)/shard_map/pallas_call | solution.py:203
  38.9 0.7 %collective-permute-start.14 = (bf16[64,1024]{1,0:T(8,128)(2,1)S(1)}, bf16[64,1024]{1,0:T(8,128)(2,1)S(1)}, u32[]{:S(2)}, u32[]{:S(2)}) collective-permute-start(bf16[64,1024]{1,0:T(8,128)(2,1)S(1)} %get-tuple-element.24.piece_ref.refs_0_), channel_id=1, source_target_pairs={{0,2},{1,3},{2,0},{3,1},{4,12},{5,13},{6,14},{7,15},{8,10},{9,11},... | collective-permute-start | bytes 393224 | tf_op jit(solution)/shard_map/ppermute | solution.py:237
  39.6 0.5 shard_map.54.refs_6_
  40.1 4.1 %collective-permute-done.14.refs_1_ = bf16[64,1024]{1,0:T(8,128)(2,1)S(1)} collective-permute-done((bf16[64,1024]{1,0:T(8,128)(2,1)S(1)}, bf16[64,1024]{1,0:T(8,128)(2,1)S(1)}, u32[]{:S(2)}, u32[]{:S(2)}) %collective-permute-start.14) | collective-permute-done | bytes 131104 | tf_op jit(solution)/shard_map/ppermute | solution.py:237
  44.2 0.6 %shard_map.55 = (bf16[64,1024]{1,0:T(8,128)(2,1)S(1)}, f32[64,1024]{1,0:T(8,128)S(1)}) custom-call(bf16[64,1024]{1,0:T(8,128)(2,1)S(1)} %get-tuple-element.24.piece_ref.refs_0_, bf16[64,1024]{1,0:T(8,128)(2,1)S(1)} %collective-permute-done.14.refs_1_, bf16[2,2048,512]{2,1,0:T(8,128)(2,1)S(1)} %shard_map.47.refs_2_.refs_0_, ...), custom_call_target="tpu_custom_call" | custom-call | flops 268435456 | bytes 9306112 | tf_op jit(solution)/shard_map/pallas_call | solution.py:203
  44.8 0.4 collective-permute-start.17
  45.3 1.6 %collective-permute-start.16 = (bf16[64,1024]{1,0:T(8,128)(2,1)S(1)}, bf16[64,1024]{1,0:T(8,128)(2,1)S(1)}, u32[]{:S(2)}, u32[]{:S(2)}) collective-permute-start(bf16[64,1024]{1,0:T(8,128)(2,1)S(1)} %get-tuple-element.26.refs_1_), channel_id=1, source_target_pairs={{0,4},{1,5},{2,6},{3,7},{4,0},{5,1},{6,2},{7,3},{8,12},{9,13},{10,... | collective-permute-start | bytes 393224 | tf_op jit(solution)/shard_map/ppermute | solution.py:237
  46.9 1.5 %collective-permute-start.15 = (bf16[64,1024]{1,0:T(8,128)(2,1)S(1)}, bf16[64,1024]{1,0:T(8,128)(2,1)S(1)}, u32[]{:S(2)}, u32[]{:S(2)}) collective-permute-start(bf16[64,1024]{1,0:T(8,128)(2,1)S(1)} %get-tuple-element.26.refs_1_), channel_id=1, source_target_pairs={{0,6},{1,7},{2,4},{3,5},{4,2},{5,3},{6,0},{7,1},{8,14},{9,15},{10,... | collective-permute-start | bytes 393224 | tf_op jit(solution)/shard_map/ppermute | solution.py:237
  48.4 2.9 %collective-permute-done.17.refs_3_ = bf16[64,1024]{1,0:T(8,128)(2,1)S(1)} collective-permute-done((bf16[64,1024]{1,0:T(8,128)(2,1)S(1)}, bf16[64,1024]{1,0:T(8,128)(2,1)S(1)}, u32[]{:S(2)}, u32[]{:S(2)}) %collective-permute-start.17) | collective-permute-done | bytes 131104 | tf_op jit(solution)/shard_map/ppermute | solution.py:237
  51.3 2.0 %collective-permute-done.15.refs_0_ = bf16[64,1024]{1,0:T(8,128)(2,1)S(1)} collective-permute-done((bf16[64,1024]{1,0:T(8,128)(2,1)S(1)}, bf16[64,1024]{1,0:T(8,128)(2,1)S(1)}, u32[]{:S(2)}, u32[]{:S(2)}) %collective-permute-start.15) | collective-permute-done | bytes 131104 | tf_op jit(solution)/shard_map/ppermute | solution.py:237
  53.3 1.0 %shard_map.56.piece_ref.refs_0_ = bf16[64,1024]{1,0:T(8,128)(2,1)S(1)} custom-call(s32[2,16]{1,0:T(2,128)S(1)} %copy-done, f32[2,64,1024]{2,1,0:T(8,128)S(1)} %get-tuple-element.18.right_ref, bf16[2,16,128,1024]{3,2,1,0:T(8,128)(2,1)S(1)} %get-tuple-element.19.lower_ref, bf16[64,1024]{1,0:T(8,128)(2,1)S(1)} %collective-permute-done.15.refs_0_, ...), custom_call_target="tpu_custom_call" | custom-call | flops 268435456 | bytes 10223744 | tf_op jit(solution)/shard_map/pallas_call | solution.py:203
  54.3 0.4 collective-permute-start.18
  54.7 0.5 shard_map.57.refs_5_
  55.2 4.1 %collective-permute-done.18.refs_1_ = bf16[64,1024]{1,0:T(8,128)(2,1)S(1)} collective-permute-done((bf16[64,1024]{1,0:T(8,128)(2,1)S(1)}, bf16[64,1024]{1,0:T(8,128)(2,1)S(1)}, u32[]{:S(2)}, u32[]{:S(2)}) %collective-permute-start.18) | collective-permute-done | bytes 131104 | tf_op jit(solution)/shard_map/ppermute | solution.py:237
  59.3 1.3 %shard_map.58 = f32[2,64,1024]{2,1,0:T(8,128)} custom-call(bf16[64,1024]{1,0:T(8,128)(2,1)S(1)} %shard_map.56.piece_ref.refs_0_, bf16[64,1024]{1,0:T(8,128)(2,1)S(1)} %collective-permute-done.18.refs_1_, bf16[2,2048,512]{2,1,0:T(8,128)(2,1)S(1)} %shard_map.47.refs_2_.refs_0_, bf16[2,2048,512]{2,1,0:T(8,128)(2,1)S(1)} %collective-permute-done.1.refs_3_.refs_1_, ...), custom_call_target="tpu_custom_call" | custom-call | flops 268435456 | bytes 9175040 | tf_op jit(solution)/shard_map/pallas_call | solution.py:203
  (5 shorter events, 0.0 us)
Async XLA Ops:
  0.0 7.4 %collective-permute-start.1 = (bf16[2,2048,512]{2,1,0:T(8,128)(2,1)}, bf16[2,2048,512]{2,1,0:T(8,128)(2,1)S(1)}, u32[]{:S(2)}, u32[]{:S(2)}) collective-permute-start(bf16[2,2048,512]{2,1,0:T(8,128)(2,1)} %refs_0_.2), channel_id=1, source_target_pairs={{0,1},{1,0},{2,3},{3,2},{4,5},{5,4},{6,7},{7,6},{8,9},{9,8},{10,11... | collective-permute-start | bytes 12582920 | tf_op jit(solution)/shard_map/ppermute | solution.py:256
  1.4 6.0 %collective-permute-start = (bf16[64,1024]{1,0:T(8,128)(2,1)S(1)}, bf16[64,1024]{1,0:T(8,128)(2,1)S(1)}, u32[]{:S(2)}, u32[]{:S(2)}) collective-permute-start(bf16[64,1024]{1,0:T(8,128)(2,1)S(1)} %shard_map.46.after_ref.refs_0_), channel_id=1, source_target_pairs={{0,1},{1,0},{2,3},{3,2},{4,5},{5,4},{6,7},{7,6},{8,9},{9,8},{10,11... | collective-permute-start | bytes 393224 | tf_op jit(solution)/shard_map/ppermute | solution.py:237
  8.3 4.7 %copy-start = (s32[2,16]{1,0:T(2,128)S(1)}, s32[2,16]{1,0:T(2,128)}, u32[]{:S(2)}) copy-start(s32[2,16]{1,0:T(2,128)} %block_rows_ref.5) | copy-start | bytes 388
  8.3 4.7 %collective-permute-start.5 = (bf16[64,1024]{1,0:T(8,128)(2,1)S(1)}, bf16[64,1024]{1,0:T(8,128)(2,1)S(1)}, u32[]{:S(2)}, u32[]{:S(2)}) collective-permute-start(bf16[64,1024]{1,0:T(8,128)(2,1)S(1)} %get-tuple-element.17.after_ref.refs_4_.refs_5_), channel_id=1, source_target_pairs={{0,1},{1,0},{2,3},{3,2},{4,5},{5,4},{6,7},{7,6},{8,9},{9,8},{10,11... | collective-permute-start | bytes 393224 | tf_op jit(solution)/shard_map/ppermute | solution.py:237
  8.8 4.3 %collective-permute-start.4 = (bf16[64,1024]{1,0:T(8,128)(2,1)S(1)}, bf16[64,1024]{1,0:T(8,128)(2,1)S(1)}, u32[]{:S(2)}, u32[]{:S(2)}) collective-permute-start(bf16[64,1024]{1,0:T(8,128)(2,1)S(1)} %get-tuple-element.17.after_ref.refs_4_.refs_5_), channel_id=1, source_target_pairs={{0,1},{1,0},{2,3},{3,2},{4,8},{5,9},{6,10},{7,11},{8,12},{9,13},{1... | collective-permute-start | bytes 393224 | tf_op jit(solution)/shard_map/ppermute | solution.py:237
  8.9 4.1 %collective-permute-start.3 = (bf16[64,1024]{1,0:T(8,128)(2,1)S(1)}, bf16[64,1024]{1,0:T(8,128)(2,1)S(1)}, u32[]{:S(2)}, u32[]{:S(2)}) collective-permute-start(bf16[64,1024]{1,0:T(8,128)(2,1)S(1)} %get-tuple-element.17.after_ref.refs_4_.refs_5_), channel_id=1, source_target_pairs={{0,1},{1,0},{2,3},{3,2},{4,5},{5,4},{6,7},{7,6},{8,9},{9,8},{10,11... | collective-permute-start | bytes 393224 | tf_op jit(solution)/shard_map/ppermute | solution.py:237
  9.3 3.8 %collective-permute-start.2 = (bf16[64,1024]{1,0:T(8,128)(2,1)S(1)}, bf16[64,1024]{1,0:T(8,128)(2,1)S(1)}, u32[]{:S(2)}, u32[]{:S(2)}) collective-permute-start(bf16[64,1024]{1,0:T(8,128)(2,1)S(1)} %get-tuple-element.17.after_ref.refs_4_.refs_5_), channel_id=1, source_target_pairs={{0,1},{1,0},{2,3},{3,2},{4,14},{5,15},{6,12},{7,13},{8,9},{9,8},{1... | collective-permute-start | bytes 393224 | tf_op jit(solution)/shard_map/ppermute | solution.py:237
  14.1 9.2 %collective-permute-start.9 = (bf16[64,1024]{1,0:T(8,128)(2,1)S(1)}, bf16[64,1024]{1,0:T(8,128)(2,1)S(1)}, u32[]{:S(2)}, u32[]{:S(2)}) collective-permute-start(bf16[64,1024]{1,0:T(8,128)(2,1)S(1)} %get-tuple-element.21.refs_0_), channel_id=1, source_target_pairs={{0,1},{1,0},{2,3},{3,2},{4,6},{5,7},{6,4},{7,5},{8,9},{9,8},{10,11... | collective-permute-start | bytes 393224 | tf_op jit(solution)/shard_map/ppermute | solution.py:237
  14.5 12.3 %collective-permute-start.7 = (bf16[64,1024]{1,0:T(8,128)(2,1)S(1)}, bf16[64,1024]{1,0:T(8,128)(2,1)S(1)}, u32[]{:S(2)}, u32[]{:S(2)}) collective-permute-start(bf16[64,1024]{1,0:T(8,128)(2,1)S(1)} %get-tuple-element.20.own_ref), channel_id=1, source_target_pairs={{0,1},{1,0},{2,3},{3,2},{4,8},{5,9},{6,10},{7,11},{8,4},{9,5},{10,... | collective-permute-start | bytes 393224 | tf_op jit(solution)/shard_map/ppermute | solution.py:237
  14.7 13.5 %collective-permute-start.6 = (bf16[64,1024]{1,0:T(8,128)(2,1)S(1)}, bf16[64,1024]{1,0:T(8,128)(2,1)S(1)}, u32[]{:S(2)}, u32[]{:S(2)}) collective-permute-start(bf16[64,1024]{1,0:T(8,128)(2,1)S(1)} %get-tuple-element.20.own_ref), channel_id=1, source_target_pairs={{0,4},{1,5},{2,6},{3,7},{4,0},{5,1},{6,2},{7,3},{8,9},{9,8},{10,11... | collective-permute-start | bytes 393224 | tf_op jit(solution)/shard_map/ppermute | solution.py:237
  24.1 5.6 %collective-permute-start.13 = (bf16[64,1024]{1,0:T(8,128)(2,1)S(1)}, bf16[64,1024]{1,0:T(8,128)(2,1)S(1)}, u32[]{:S(2)}, u32[]{:S(2)}) collective-permute-start(bf16[64,1024]{1,0:T(8,128)(2,1)S(1)} %get-tuple-element.23.refs_6_.refs_5_), channel_id=1, source_target_pairs={{4,8},{6,10},{20,24},{22,26},{5,9},{7,11},{21,25},{23,27}} | collective-permute-start | bytes 393224 | tf_op jit(solution)/shard_map/ppermute | solution.py:223
  24.8 9.3 %collective-permute-start.12 = (bf16[64,1024]{1,0:T(8,128)(2,1)S(1)}, bf16[64,1024]{1,0:T(8,128)(2,1)S(1)}, u32[]{:S(2)}, u32[]{:S(2)}) collective-permute-start(bf16[64,1024]{1,0:T(8,128)(2,1)S(1)} %get-tuple-element.23.refs_6_.refs_5_), channel_id=1, source_target_pairs={{4,0},{6,2},{20,16},{22,18},{5,1},{7,3},{21,17},{23,19}} | collective-permute-start | bytes 393224 | tf_op jit(solution)/shard_map/ppermute | solution.py:223
  26.1 8.0 %collective-permute-start.11 = (bf16[64,1024]{1,0:T(8,128)(2,1)S(1)}, bf16[64,1024]{1,0:T(8,128)(2,1)S(1)}, u32[]{:S(2)}, u32[]{:S(2)}) collective-permute-start(bf16[64,1024]{1,0:T(8,128)(2,1)S(1)} %get-tuple-element.23.refs_6_.refs_5_), channel_id=1, source_target_pairs={{4,10},{6,8},{20,26},{22,24},{5,11},{7,9},{21,27},{23,25}} | collective-permute-start | bytes 393224 | tf_op jit(solution)/shard_map/ppermute | solution.py:223
  26.8 11.1 %collective-permute-start.10 = (bf16[64,1024]{1,0:T(8,128)(2,1)S(1)}, bf16[64,1024]{1,0:T(8,128)(2,1)S(1)}, u32[]{:S(2)}, u32[]{:S(2)}) collective-permute-start(bf16[64,1024]{1,0:T(8,128)(2,1)S(1)} %get-tuple-element.23.refs_6_.refs_5_), channel_id=1, source_target_pairs={{4,2},{6,0},{20,18},{22,16},{5,3},{7,1},{21,19},{23,17}} | collective-permute-start | bytes 393224 | tf_op jit(solution)/shard_map/ppermute | solution.py:223
  28.2 9.8 %collective-permute-start.8 = (bf16[64,1024]{1,0:T(8,128)(2,1)S(1)}, bf16[64,1024]{1,0:T(8,128)(2,1)S(1)}, u32[]{:S(2)}, u32[]{:S(2)}) collective-permute-start(bf16[64,1024]{1,0:T(8,128)(2,1)S(1)} %shard_map.51.refs_5_), channel_id=1, source_target_pairs={{0,2},{1,3},{2,0},{3,1},{4,6},{5,7},{6,4},{7,5},{8,10},{9,11},{10,... | collective-permute-start | bytes 393224 | tf_op jit(solution)/shard_map/ppermute | solution.py:237
  38.9 5.3 %collective-permute-start.14 = (bf16[64,1024]{1,0:T(8,128)(2,1)S(1)}, bf16[64,1024]{1,0:T(8,128)(2,1)S(1)}, u32[]{:S(2)}, u32[]{:S(2)}) collective-permute-start(bf16[64,1024]{1,0:T(8,128)(2,1)S(1)} %get-tuple-element.24.piece_ref.refs_0_), channel_id=1, source_target_pairs={{0,2},{1,3},{2,0},{3,1},{4,12},{5,13},{6,14},{7,15},{8,10},{9,11},... | collective-permute-start | bytes 393224 | tf_op jit(solution)/shard_map/ppermute | solution.py:237
  44.8 6.4 %collective-permute-start.17 = (bf16[64,1024]{1,0:T(8,128)(2,1)S(1)}, bf16[64,1024]{1,0:T(8,128)(2,1)S(1)}, u32[]{:S(2)}, u32[]{:S(2)}) collective-permute-start(bf16[64,1024]{1,0:T(8,128)(2,1)S(1)} %get-tuple-element.26.refs_1_), channel_id=1, source_target_pairs={{0,2},{1,3},{2,0},{3,1},{4,6},{5,7},{6,4},{7,5},{8,10},{9,11},{10,... | collective-permute-start | bytes 393224 | tf_op jit(solution)/shard_map/ppermute | solution.py:237
  45.3 6.0 %collective-permute-start.16 = (bf16[64,1024]{1,0:T(8,128)(2,1)S(1)}, bf16[64,1024]{1,0:T(8,128)(2,1)S(1)}, u32[]{:S(2)}, u32[]{:S(2)}) collective-permute-start(bf16[64,1024]{1,0:T(8,128)(2,1)S(1)} %get-tuple-element.26.refs_1_), channel_id=1, source_target_pairs={{0,4},{1,5},{2,6},{3,7},{4,0},{5,1},{6,2},{7,3},{8,12},{9,13},{10,... | collective-permute-start | bytes 393224 | tf_op jit(solution)/shard_map/ppermute | solution.py:237
  46.9 6.4 %collective-permute-start.15 = (bf16[64,1024]{1,0:T(8,128)(2,1)S(1)}, bf16[64,1024]{1,0:T(8,128)(2,1)S(1)}, u32[]{:S(2)}, u32[]{:S(2)}) collective-permute-start(bf16[64,1024]{1,0:T(8,128)(2,1)S(1)} %get-tuple-element.26.refs_1_), channel_id=1, source_target_pairs={{0,6},{1,7},{2,4},{3,5},{4,2},{5,3},{6,0},{7,1},{8,14},{9,15},{10,... | collective-permute-start | bytes 393224 | tf_op jit(solution)/shard_map/ppermute | solution.py:237
  54.3 5.0 %collective-permute-start.18 = (bf16[64,1024]{1,0:T(8,128)(2,1)S(1)}, bf16[64,1024]{1,0:T(8,128)(2,1)S(1)}, u32[]{:S(2)}, u32[]{:S(2)}) collective-permute-start(bf16[64,1024]{1,0:T(8,128)(2,1)S(1)} %shard_map.56.piece_ref.refs_0_), channel_id=1, source_target_pairs={{0,2},{1,3},{2,0},{3,1},{4,6},{5,7},{6,4},{7,5},{8,10},{9,11},{10,... | collective-permute-start | bytes 393224 | tf_op jit(solution)/shard_map/ppermute | solution.py:237

commit v13 on v12

--- a/solution.py
+++ b/solution.py
@@ -61,7 +61,14 @@
     if level == top:
         pieces = [refs[1:2 * rows:2], refs[:2 * rows:2]]
         if plan == "traded":
-            pieces[1] = pieces[1][::-1]
+            r0, l0, l1, r1 = refs[:4]
+            pieces = [[l0, l1], [r0, r1]]
+    elif plan == "rooted":
+        r1, r0, l1, l0 = refs[:4]
+        pieces = [[l0, l1], [r0, r1]]
+    elif plan == "crossed":
+        r1, r0, l1, l0 = refs[:4]
+        pieces = [[l0, l1], [r0, r1]]
     else:
         pieces = [refs[:2 * rows:2][::-1], refs[1:2 * rows:2][::-1]]
     extra = refs[2 * rows:]
@@ -289,12 +296,11 @@
             kernel = functools.partial(offset_kernel, top, depth, rows, plan)
             pieces = paired(rights[::-1], lefts[::-1]) if depth == top else paired(lefts, rights)
             if plan == "rooted":
-                pieces = [*pieces, rounded]
+                pieces = [rights[1], rights[0], lefts[1], lefts[0], rounded]
             elif plan == "crossed":
-                pieces = [late, *pieces, relayed, rounded]
+                pieces = [late, rights[1], rights[0], lefts[1], lefts[0], relayed, rounded]
             elif plan == "traded":
-                rights = rights[::-1]
-                pieces = [rights[0], lefts[0], rights[1], lefts[1], mine, relayed, late]
+                pieces = [rights[0], lefts[0], lefts[1], rights[1], mine, relayed, late]
             else:
                 pieces = [*pieces, *older]
             arrays = [block_rows, right, lower, *pieces]

time: 60.9 us -> 59 us (0.969)
  waiting for transfers between devices: 25 us -> 20.9 us
  starting transfers between devices: 21 us -> 22.9 us
    ppermute x4, waiting for transfers between devices: 8.17 us -> 4.93 us  [send(): return lax.ppermute(value, places, pairs)]
    ppermute x14, starting transfers between devices: 16.7 us -> 18.5 us  [permute(): return lax.ppermute(value, ('leaf', 'rows', 'rhs'), pairs)]
    ppermute x14, waiting for transfers between devices: 16.8 us -> 15.9 us  [permute(): return lax.ppermute(value, ('leaf', 'rows', 'rhs'), pairs)]
  transfers between devices with their start and end apart: 19 -> 19, of which waited for: 7 -> 9; matrix products, arithmetic and copies ran while one was open for 0% -> 0% of each run, Pallas kernels for 14% -> 15%
where the time goes in v13:
time: 59 us; the launch traced here: 58.3 us
  starting transfers between devices  22.9 us (39%)
  waiting for transfers between devices  20.9 us (35%)
  Pallas kernels  14.4 us (24%)
    ppermute x14, starting transfers between devices, permute(): return lax.ppermute(value, ('leaf', 'rows', 'rhs'), pairs)  18.5 us
    ppermute x14, waiting for transfers between devices, permute(): return lax.ppermute(value, ('leaf', 'rows', 'rhs'), pairs)  15.9 us
    pallas_call x13, Pallas kernels, call(): pl.pallas_call(kernel, in_specs=[WHOLE] * len(near) + [FAR] * len(far), o...  14.4 us
    ppermute x4, waiting for transfers between devices, send(): return lax.ppermute(value, places, pairs)  4.93 us
    ppermute x4, starting transfers between devices, send(): return lax.ppermute(value, places, pairs)  3.92 us
  transfers between devices with their start and end apart: 19, of which 9 were waited for; matrix products, arithmetic and copies ran while one was open for 0% of the time, Pallas kernels for 15%

profile of v13, /device:TPU:0, one launch (start us, length us, event | category | flops | bytes accessed | tf_op | source)
XLA Modules:
  0.0 58.3 jit_solution(9158069628214035785)
XLA Ops:
  0.0 0.5 collective-permute-start.1
  0.5 1.0 %shard_map.46.after_ref.refs_0_ = bf16[64,1024]{1,0:T(8,128)(2,1)S(1)} custom-call(f32[2,64,1024]{2,1,0:T(8,128)} %refs_0_.3), custom_call_target="tpu_custom_call" | custom-call | bytes 524288 | tf_op jit(solution)/shard_map/pallas_call | solution.py:210
  1.4 0.1 collective-permute-start
  1.6 2.2 %shard_map.47.refs_2_.refs_0_ = bf16[2,2048,512]{2,1,0:T(8,128)(2,1)S(1)} custom-call(bf16[64,1024]{1,0:T(8,128)(2,1)S(1)} %shard_map.46.after_ref.refs_0_, bf16[2,2048,512]{2,1,0:T(8,128)(2,1)} %refs_0_.2), custom_call_target="tpu_custom_call" | custom-call | bytes 4325376 | tf_op jit(solution)/shard_map/pallas_call | solution.py:210
  3.8 3.7 %collective-permute-done.refs_1_ = bf16[64,1024]{1,0:T(8,128)(2,1)S(1)} collective-permute-done((bf16[64,1024]{1,0:T(8,128)(2,1)S(1)}, bf16[64,1024]{1,0:T(8,128)(2,1)S(1)}, u32[]{:S(2)}, u32[]{:S(2)}) %collective-permute-start) | collective-permute-done | bytes 131104 | tf_op jit(solution)/shard_map/ppermute | solution.py:244
  7.4 0.0 collective-permute-done.1.refs_3_.refs_1_
  7.5 0.9 %shard_map.48 = (bf16[64,1024]{1,0:T(8,128)(2,1)S(1)}, f32[64,1024]{1,0:T(8,128)S(1)}) custom-call(bf16[64,1024]{1,0:T(8,128)(2,1)S(1)} %shard_map.46.after_ref.refs_0_, bf16[64,1024]{1,0:T(8,128)(2,1)S(1)} %collective-permute-done.refs_1_, bf16[2,2048,512]{2,1,0:T(8,128)(2,1)S(1)} %shard_map.47.refs_2_.refs_0_, ...), custom_call_target="tpu_custom_call" | custom-call | flops 268435456 | bytes 8650752 | tf_op jit(solution)/shard_map/pallas_call | solution.py:210
  8.3 0.4 collective-permute-start.5
  8.8 0.1 collective-permute-start.4
  8.9 0.4 collective-permute-start.3
  9.3 0.1 collective-permute-start.2
  9.4 3.6 %shard_map.49 = (f32[2,64,1024]{2,1,0:T(8,128)S(1)}, bf16[2,16,128,1024]{3,2,1,0:T(8,128)(2,1)S(1)}) custom-call(bf16[64,1024]{1,0:T(8,128)(2,1)S(1)} %get-tuple-element.17.after_ref.refs_4_.refs_5_, f32[2,64,1024]{2,1,0:T(8,128)} %refs_0_.3, bf16[2,16,128,1024]{3,2,1,0:T(8,128)(2,1)} %refs_1_.1), custom_call_target="tpu_custom_call" | custom-call | bytes 9043968 | tf_op jit(solution)/shard_map/pallas_call | solution.py:210
  13.0 0.0 collective-permute-done.5.refs_3_
  13.0 0.0 collective-permute-done.4.refs_2_
  13.1 0.0 collective-permute-done.2.refs_0_
  13.1 1.0 %shard_map.50 = (bf16[64,1024]{1,0:T(8,128)(2,1)S(1)}, bf16[64,1024]{1,0:T(8,128)(2,1)S(1)}) custom-call(s32[2,16]{1,0:T(2,128)S(1)} %copy-done, f32[2,64,1024]{2,1,0:T(8,128)S(1)} %get-tuple-element.18.right_ref, bf16[2,16,128,1024]{3,2,1,0:T(8,128)(2,1)S(1)} %get-tuple-element.19.lower_ref, bf16[64,1024]{1,0:T(8,128)(2,1)S(1)} %collective-permute-done.2.refs_0_, ...), custom_call_target="tpu_custom_call" | custom-call | flops 268435456 | bytes 9568384 | tf_op jit(solution)/shard_map/pallas_call | solution.py:210
  14.1 0.4 collective-permute-start.9
  14.5 0.1 collective-permute-start.7
  14.7 8.2 %collective-permute-start.6 = (bf16[64,1024]{1,0:T(8,128)(2,1)S(1)}, bf16[64,1024]{1,0:T(8,128)(2,1)S(1)}, u32[]{:S(2)}, u32[]{:S(2)}) collective-permute-start(bf16[64,1024]{1,0:T(8,128)(2,1)S(1)} %get-tuple-element.20.own_ref), channel_id=1, source_target_pairs={{0,4},{1,5},{2,6},{3,7},{4,0},{5,1},{6,2},{7,3},{8,9},{9,8},{10,11... | collective-permute-start | bytes 393224 | tf_op jit(solution)/shard_map/ppermute | solution.py:244
  22.8 0.0 collective-permute-done.9.refs_1_
  22.8 0.9 %shard_map.52 = (bf16[64,1024]{1,0:T(8,128)(2,1)S(1)}, f32[64,1024]{1,0:T(8,128)S(1)}) custom-call(bf16[64,1024]{1,0:T(8,128)(2,1)S(1)} %get-tuple-element.21.refs_0_, bf16[64,1024]{1,0:T(8,128)(2,1)S(1)} %collective-permute-done.9.refs_1_, bf16[2,2048,512]{2,1,0:T(8,128)(2,1)S(1)} %shard_map.47.refs_2_.refs_0_, ...), custom_call_target="tpu_custom_call" | custom-call | flops 268435456 | bytes 9043968 | tf_op jit(solution)/shard_map/pallas_call | solution.py:210
  23.7 1.3 %collective-permute-start.13 = (bf16[64,1024]{1,0:T(8,128)(2,1)S(1)}, bf16[64,1024]{1,0:T(8,128)(2,1)S(1)}, u32[]{:S(2)}, u32[]{:S(2)}) collective-permute-start(bf16[64,1024]{1,0:T(8,128)(2,1)S(1)} %get-tuple-element.23.refs_6_.refs_5_), channel_id=1, source_target_pairs={{4,0},{6,2},{20,16},{22,18},{5,1},{7,3},{21,17},{23,19}} | collective-permute-start | bytes 393224 | tf_op jit(solution)/shard_map/ppermute | solution.py:230
  25.0 1.3 %collective-permute-start.12 = (bf16[64,1024]{1,0:T(8,128)(2,1)S(1)}, bf16[64,1024]{1,0:T(8,128)(2,1)S(1)}, u32[]{:S(2)}, u32[]{:S(2)}) collective-permute-start(bf16[64,1024]{1,0:T(8,128)(2,1)S(1)} %get-tuple-element.23.refs_6_.refs_5_), channel_id=1, source_target_pairs={{4,2},{6,0},{20,18},{22,16},{5,3},{7,1},{21,19},{23,17}} | collective-permute-start | bytes 393224 | tf_op jit(solution)/shard_map/ppermute | solution.py:230
  26.3 0.7 %collective-permute-start.11 = (bf16[64,1024]{1,0:T(8,128)(2,1)S(1)}, bf16[64,1024]{1,0:T(8,128)(2,1)S(1)}, u32[]{:S(2)}, u32[]{:S(2)}) collective-permute-start(bf16[64,1024]{1,0:T(8,128)(2,1)S(1)} %get-tuple-element.23.refs_6_.refs_5_), channel_id=1, source_target_pairs={{4,8},{6,10},{20,24},{22,26},{5,9},{7,11},{21,25},{23,27}} | collective-permute-start | bytes 393224 | tf_op jit(solution)/shard_map/ppermute | solution.py:230
  27.0 0.7 %collective-permute-start.10 = (bf16[64,1024]{1,0:T(8,128)(2,1)S(1)}, bf16[64,1024]{1,0:T(8,128)(2,1)S(1)}, u32[]{:S(2)}, u32[]{:S(2)}) collective-permute-start(bf16[64,1024]{1,0:T(8,128)(2,1)S(1)} %get-tuple-element.23.refs_6_.refs_5_), channel_id=1, source_target_pairs={{4,10},{6,8},{20,26},{22,24},{5,11},{7,9},{21,27},{23,25}} | collective-permute-start | bytes 393224 | tf_op jit(solution)/shard_map/ppermute | solution.py:230
  27.7 0.0 collective-permute-done.6.first_ref
  27.7 1.2 %collective-permute-start.8 = (bf16[64,1024]{1,0:T(8,128)(2,1)S(1)}, bf16[64,1024]{1,0:T(8,128)(2,1)S(1)}, u32[]{:S(2)}, u32[]{:S(2)}) collective-permute-start(bf16[64,1024]{1,0:T(8,128)(2,1)S(1)} %shard_map.51.refs_5_), channel_id=1, source_target_pairs={{0,2},{1,3},{2,0},{3,1},{4,6},{5,7},{6,4},{7,5},{8,10},{9,11},{10,... | collective-permute-start | bytes 393224 | tf_op jit(solution)/shard_map/ppermute | solution.py:244
  28.9 3.1 %collective-permute-done.13.refs_4_ = bf16[64,1024]{1,0:T(8,128)(2,1)S(1)} collective-permute-done((bf16[64,1024]{1,0:T(8,128)(2,1)S(1)}, bf16[64,1024]{1,0:T(8,128)(2,1)S(1)}, u32[]{:S(2)}, u32[]{:S(2)}) %collective-permute-start.13) | collective-permute-done | bytes 131104 | tf_op jit(solution)/shard_map/ppermute | solution.py:230
  32.0 1.8 %collective-permute-done.12.refs_3_ = bf16[64,1024]{1,0:T(8,128)(2,1)S(1)} collective-permute-done((bf16[64,1024]{1,0:T(8,128)(2,1)S(1)}, bf16[64,1024]{1,0:T(8,128)(2,1)S(1)}, u32[]{:S(2)}, u32[]{:S(2)}) %collective-permute-start.12) | collective-permute-done | bytes 131104 | tf_op jit(solution)/shard_map/ppermute | solution.py:230
  33.8 0.0 collective-permute-done.11.refs_2_
  33.9 0.0 collective-permute-done.10.refs_1_
  33.9 0.9 %collective-permute-done.8.refs_0_.refs_6_ = bf16[64,1024]{1,0:T(8,128)(2,1)S(1)} collective-permute-done((bf16[64,1024]{1,0:T(8,128)(2,1)S(1)}, bf16[64,1024]{1,0:T(8,128)(2,1)S(1)}, u32[]{:S(2)}, u32[]{:S(2)}) %collective-permute-start.8) | collective-permute-done | bytes 131104 | tf_op jit(solution)/shard_map/ppermute | solution.py:244
  34.8 1.0 %shard_map.53 = (bf16[64,1024]{1,0:T(8,128)(2,1)S(1)}, bf16[64,4096]{1,0:T(8,128)(2,1)S(1)}) custom-call(s32[2,16]{1,0:T(2,128)S(1)} %copy-done, f32[2,64,1024]{2,1,0:T(8,128)S(1)} %get-tuple-element.18.right_ref, bf16[2,16,128,1024]{3,2,1,0:T(8,128)(2,1)S(1)} %get-tuple-element.19.lower_ref, bf16[64,1024]{1,0:T(8,128)(2,1)S(1)} %collective-permute-done.8.refs_0_.refs_6_, ...), custom_call_target="tpu_custom_call" | custom-call | flops 268435456 | bytes 9830528 | tf_op jit(solution)/shard_map/pallas_call | solution.py:210
  35.8 1.6 %collective-permute-start.14 = (bf16[64,1024]{1,0:T(8,128)(2,1)S(1)}, bf16[64,1024]{1,0:T(8,128)(2,1)S(1)}, u32[]{:S(2)}, u32[]{:S(2)}) collective-permute-start(bf16[64,1024]{1,0:T(8,128)(2,1)S(1)} %get-tuple-element.24.piece_ref.refs_0_), channel_id=1, source_target_pairs={{0,2},{1,3},{2,0},{3,1},{4,12},{5,13},{6,14},{7,15},{8,10},{9,11},... | collective-permute-start | bytes 393224 | tf_op jit(solution)/shard_map/ppermute | solution.py:244
  37.4 0.5 shard_map.54.refs_6_
  37.8 3.0 %collective-permute-done.14.refs_1_ = bf16[64,1024]{1,0:T(8,128)(2,1)S(1)} collective-permute-done((bf16[64,1024]{1,0:T(8,128)(2,1)S(1)}, bf16[64,1024]{1,0:T(8,128)(2,1)S(1)}, u32[]{:S(2)}, u32[]{:S(2)}) %collective-permute-start.14) | collective-permute-done | bytes 131104 | tf_op jit(solution)/shard_map/ppermute | solution.py:244
  40.8 0.6 %shard_map.55 = (bf16[64,1024]{1,0:T(8,128)(2,1)S(1)}, f32[64,1024]{1,0:T(8,128)S(1)}) custom-call(bf16[64,1024]{1,0:T(8,128)(2,1)S(1)} %get-tuple-element.24.piece_ref.refs_0_, bf16[64,1024]{1,0:T(8,128)(2,1)S(1)} %collective-permute-done.14.refs_1_, bf16[2,2048,512]{2,1,0:T(8,128)(2,1)S(1)} %shard_map.47.refs_2_.refs_0_, ...), custom_call_target="tpu_custom_call" | custom-call | flops 268435456 | bytes 9306112 | tf_op jit(solution)/shard_map/pallas_call | solution.py:210
  41.5 3.7 %collective-permute-start.17 = (bf16[64,1024]{1,0:T(8,128)(2,1)S(1)}, bf16[64,1024]{1,0:T(8,128)(2,1)S(1)}, u32[]{:S(2)}, u32[]{:S(2)}) collective-permute-start(bf16[64,1024]{1,0:T(8,128)(2,1)S(1)} %get-tuple-element.26.refs_1_), channel_id=1, source_target_pairs={{0,6},{1,7},{2,4},{3,5},{4,2},{5,3},{6,0},{7,1},{8,14},{9,15},{10,... | collective-permute-start | bytes 393224 | tf_op jit(solution)/shard_map/ppermute | solution.py:244
  45.2 0.9 %collective-permute-start.16 = (bf16[64,1024]{1,0:T(8,128)(2,1)S(1)}, bf16[64,1024]{1,0:T(8,128)(2,1)S(1)}, u32[]{:S(2)}, u32[]{:S(2)}) collective-permute-start(bf16[64,1024]{1,0:T(8,128)(2,1)S(1)} %get-tuple-element.26.refs_1_), channel_id=1, source_target_pairs={{0,2},{1,3},{2,0},{3,1},{4,6},{5,7},{6,4},{7,5},{8,10},{9,11},{10,... | collective-permute-start | bytes 393224 | tf_op jit(solution)/shard_map/ppermute | solution.py:244
  46.0 0.0 collective-permute-start.15
  46.0 2.1 %collective-permute-done.17.refs_3_ = bf16[64,1024]{1,0:T(8,128)(2,1)S(1)} collective-permute-done((bf16[64,1024]{1,0:T(8,128)(2,1)S(1)}, bf16[64,1024]{1,0:T(8,128)(2,1)S(1)}, u32[]{:S(2)}, u32[]{:S(2)}) %collective-permute-start.17) | collective-permute-done | bytes 131104 | tf_op jit(solution)/shard_map/ppermute | solution.py:244
  48.2 2.0 %collective-permute-done.16.refs_2_ = bf16[64,1024]{1,0:T(8,128)(2,1)S(1)} collective-permute-done((bf16[64,1024]{1,0:T(8,128)(2,1)S(1)}, bf16[64,1024]{1,0:T(8,128)(2,1)S(1)}, u32[]{:S(2)}, u32[]{:S(2)}) %collective-permute-start.16) | collective-permute-done | bytes 131104 | tf_op jit(solution)/shard_map/ppermute | solution.py:244
  50.1 0.9 %collective-permute-done.15.refs_0_ = bf16[64,1024]{1,0:T(8,128)(2,1)S(1)} collective-permute-done((bf16[64,1024]{1,0:T(8,128)(2,1)S(1)}, bf16[64,1024]{1,0:T(8,128)(2,1)S(1)}, u32[]{:S(2)}, u32[]{:S(2)}) %collective-permute-start.15) | collective-permute-done | bytes 131104 | tf_op jit(solution)/shard_map/ppermute | solution.py:244
  51.0 1.0 %shard_map.56.piece_ref.refs_0_ = bf16[64,1024]{1,0:T(8,128)(2,1)S(1)} custom-call(s32[2,16]{1,0:T(2,128)S(1)} %copy-done, f32[2,64,1024]{2,1,0:T(8,128)S(1)} %get-tuple-element.18.right_ref, bf16[2,16,128,1024]{3,2,1,0:T(8,128)(2,1)S(1)} %get-tuple-element.19.lower_ref, bf16[64,1024]{1,0:T(8,128)(2,1)S(1)} %collective-permute-done.15.refs_0_, ...), custom_call_target="tpu_custom_call" | custom-call | flops 268435456 | bytes 10223744 | tf_op jit(solution)/shard_map/pallas_call | solution.py:210
  52.0 1.2 %collective-permute-start.18 = (bf16[64,1024]{1,0:T(8,128)(2,1)S(1)}, bf16[64,1024]{1,0:T(8,128)(2,1)S(1)}, u32[]{:S(2)}, u32[]{:S(2)}) collective-permute-start(bf16[64,1024]{1,0:T(8,128)(2,1)S(1)} %shard_map.56.piece_ref.refs_0_), channel_id=1, source_target_pairs={{0,2},{1,3},{2,0},{3,1},{4,6},{5,7},{6,4},{7,5},{8,10},{9,11},{10,... | collective-permute-start | bytes 393224 | tf_op jit(solution)/shard_map/ppermute | solution.py:244
  53.2 0.5 shard_map.57.refs_5_
  53.7 3.3 %collective-permute-done.18.refs_1_ = bf16[64,1024]{1,0:T(8,128)(2,1)S(1)} collective-permute-done((bf16[64,1024]{1,0:T(8,128)(2,1)S(1)}, bf16[64,1024]{1,0:T(8,128)(2,1)S(1)}, u32[]{:S(2)}, u32[]{:S(2)}) %collective-permute-start.18) | collective-permute-done | bytes 131104 | tf_op jit(solution)/shard_map/ppermute | solution.py:244
  57.0 1.3 %shard_map.58 = f32[2,64,1024]{2,1,0:T(8,128)} custom-call(bf16[64,1024]{1,0:T(8,128)(2,1)S(1)} %shard_map.56.piece_ref.refs_0_, bf16[64,1024]{1,0:T(8,128)(2,1)S(1)} %collective-permute-done.18.refs_1_, bf16[2,2048,512]{2,1,0:T(8,128)(2,1)S(1)} %shard_map.47.refs_2_.refs_0_, bf16[2,2048,512]{2,1,0:T(8,128)(2,1)S(1)} %collective-permute-done.1.refs_3_.refs_1_, ...), custom_call_target="tpu_custom_call" | custom-call | flops 268435456 | bytes 9175040 | tf_op jit(solution)/shard_map/pallas_call | solution.py:210
  (5 shorter events, 0.0 us)
Async XLA Ops:
  0.0 7.4 %collective-permute-start.1 = (bf16[2,2048,512]{2,1,0:T(8,128)(2,1)}, bf16[2,2048,512]{2,1,0:T(8,128)(2,1)S(1)}, u32[]{:S(2)}, u32[]{:S(2)}) collective-permute-start(bf16[2,2048,512]{2,1,0:T(8,128)(2,1)} %refs_0_.2), channel_id=1, source_target_pairs={{0,1},{1,0},{2,3},{3,2},{4,5},{5,4},{6,7},{7,6},{8,9},{9,8},{10,11... | collective-permute-start | bytes 12582920 | tf_op jit(solution)/shard_map/ppermute | solution.py:263
  1.4 6.0 %collective-permute-start = (bf16[64,1024]{1,0:T(8,128)(2,1)S(1)}, bf16[64,1024]{1,0:T(8,128)(2,1)S(1)}, u32[]{:S(2)}, u32[]{:S(2)}) collective-permute-start(bf16[64,1024]{1,0:T(8,128)(2,1)S(1)} %shard_map.46.after_ref.refs_0_), channel_id=1, source_target_pairs={{0,1},{1,0},{2,3},{3,2},{4,5},{5,4},{6,7},{7,6},{8,9},{9,8},{10,11... | collective-permute-start | bytes 393224 | tf_op jit(solution)/shard_map/ppermute | solution.py:244
  8.3 4.7 %copy-start = (s32[2,16]{1,0:T(2,128)S(1)}, s32[2,16]{1,0:T(2,128)}, u32[]{:S(2)}) copy-start(s32[2,16]{1,0:T(2,128)} %block_rows_ref.5) | copy-start | bytes 388
  8.3 4.7 %collective-permute-start.5 = (bf16[64,1024]{1,0:T(8,128)(2,1)S(1)}, bf16[64,1024]{1,0:T(8,128)(2,1)S(1)}, u32[]{:S(2)}, u32[]{:S(2)}) collective-permute-start(bf16[64,1024]{1,0:T(8,128)(2,1)S(1)} %get-tuple-element.17.after_ref.refs_4_.refs_5_), channel_id=1, source_target_pairs={{0,1},{1,0},{2,3},{3,2},{4,8},{5,9},{6,10},{7,11},{8,12},{9,13},{1... | collective-permute-start | bytes 393224 | tf_op jit(solution)/shard_map/ppermute | solution.py:244
  8.8 4.3 %collective-permute-start.4 = (bf16[64,1024]{1,0:T(8,128)(2,1)S(1)}, bf16[64,1024]{1,0:T(8,128)(2,1)S(1)}, u32[]{:S(2)}, u32[]{:S(2)}) collective-permute-start(bf16[64,1024]{1,0:T(8,128)(2,1)S(1)} %get-tuple-element.17.after_ref.refs_4_.refs_5_), channel_id=1, source_target_pairs={{0,1},{1,0},{2,3},{3,2},{4,14},{5,15},{6,12},{7,13},{8,9},{9,8},{1... | collective-permute-start | bytes 393224 | tf_op jit(solution)/shard_map/ppermute | solution.py:244
  8.9 4.1 %collective-permute-start.3 = (bf16[64,1024]{1,0:T(8,128)(2,1)S(1)}, bf16[64,1024]{1,0:T(8,128)(2,1)S(1)}, u32[]{:S(2)}, u32[]{:S(2)}) collective-permute-start(bf16[64,1024]{1,0:T(8,128)(2,1)S(1)} %get-tuple-element.17.after_ref.refs_4_.refs_5_), channel_id=1, source_target_pairs={{0,1},{1,0},{2,3},{3,2},{4,5},{5,4},{6,7},{7,6},{8,9},{9,8},{10,11... | collective-permute-start | bytes 393224 | tf_op jit(solution)/shard_map/ppermute | solution.py:244
  9.3 3.8 %collective-permute-start.2 = (bf16[64,1024]{1,0:T(8,128)(2,1)S(1)}, bf16[64,1024]{1,0:T(8,128)(2,1)S(1)}, u32[]{:S(2)}, u32[]{:S(2)}) collective-permute-start(bf16[64,1024]{1,0:T(8,128)(2,1)S(1)} %get-tuple-element.17.after_ref.refs_4_.refs_5_), channel_id=1, source_target_pairs={{0,1},{1,0},{2,3},{3,2},{4,5},{5,4},{6,7},{7,6},{8,9},{9,8},{10,11... | collective-permute-start | bytes 393224 | tf_op jit(solution)/shard_map/ppermute | solution.py:244
  14.1 8.7 %collective-permute-start.9 = (bf16[64,1024]{1,0:T(8,128)(2,1)S(1)}, bf16[64,1024]{1,0:T(8,128)(2,1)S(1)}, u32[]{:S(2)}, u32[]{:S(2)}) collective-permute-start(bf16[64,1024]{1,0:T(8,128)(2,1)S(1)} %get-tuple-element.21.refs_0_), channel_id=1, source_target_pairs={{0,1},{1,0},{2,3},{3,2},{4,6},{5,7},{6,4},{7,5},{8,9},{9,8},{10,11... | collective-permute-start | bytes 393224 | tf_op jit(solution)/shard_map/ppermute | solution.py:244
  14.5 12.5 %collective-permute-start.7 = (bf16[64,1024]{1,0:T(8,128)(2,1)S(1)}, bf16[64,1024]{1,0:T(8,128)(2,1)S(1)}, u32[]{:S(2)}, u32[]{:S(2)}) collective-permute-start(bf16[64,1024]{1,0:T(8,128)(2,1)S(1)} %get-tuple-element.20.own_ref), channel_id=1, source_target_pairs={{0,1},{1,0},{2,3},{3,2},{4,8},{5,9},{6,10},{7,11},{8,4},{9,5},{10,... | collective-permute-start | bytes 393224 | tf_op jit(solution)/shard_map/ppermute | solution.py:244
  14.7 13.0 %collective-permute-start.6 = (bf16[64,1024]{1,0:T(8,128)(2,1)S(1)}, bf16[64,1024]{1,0:T(8,128)(2,1)S(1)}, u32[]{:S(2)}, u32[]{:S(2)}) collective-permute-start(bf16[64,1024]{1,0:T(8,128)(2,1)S(1)} %get-tuple-element.20.own_ref), channel_id=1, source_target_pairs={{0,4},{1,5},{2,6},{3,7},{4,0},{5,1},{6,2},{7,3},{8,9},{9,8},{10,11... | collective-permute-start | bytes 393224 | tf_op jit(solution)/shard_map/ppermute | solution.py:244
  23.7 8.3 %collective-permute-start.13 = (bf16[64,1024]{1,0:T(8,128)(2,1)S(1)}, bf16[64,1024]{1,0:T(8,128)(2,1)S(1)}, u32[]{:S(2)}, u32[]{:S(2)}) collective-permute-start(bf16[64,1024]{1,0:T(8,128)(2,1)S(1)} %get-tuple-element.23.refs_6_.refs_5_), channel_id=1, source_target_pairs={{4,0},{6,2},{20,16},{22,18},{5,1},{7,3},{21,17},{23,19}} | collective-permute-start | bytes 393224 | tf_op jit(solution)/shard_map/ppermute | solution.py:230
  25.0 8.8 %collective-permute-start.12 = (bf16[64,1024]{1,0:T(8,128)(2,1)S(1)}, bf16[64,1024]{1,0:T(8,128)(2,1)S(1)}, u32[]{:S(2)}, u32[]{:S(2)}) collective-permute-start(bf16[64,1024]{1,0:T(8,128)(2,1)S(1)} %get-tuple-element.23.refs_6_.refs_5_), channel_id=1, source_target_pairs={{4,2},{6,0},{20,18},{22,16},{5,3},{7,1},{21,19},{23,17}} | collective-permute-start | bytes 393224 | tf_op jit(solution)/shard_map/ppermute | solution.py:230
  26.3 7.5 %collective-permute-start.11 = (bf16[64,1024]{1,0:T(8,128)(2,1)S(1)}, bf16[64,1024]{1,0:T(8,128)(2,1)S(1)}, u32[]{:S(2)}, u32[]{:S(2)}) collective-permute-start(bf16[64,1024]{1,0:T(8,128)(2,1)S(1)} %get-tuple-element.23.refs_6_.refs_5_), channel_id=1, source_target_pairs={{4,8},{6,10},{20,24},{22,26},{5,9},{7,11},{21,25},{23,27}} | collective-permute-start | bytes 393224 | tf_op jit(solution)/shard_map/ppermute | solution.py:230
  27.0 6.9 %collective-permute-start.10 = (bf16[64,1024]{1,0:T(8,128)(2,1)S(1)}, bf16[64,1024]{1,0:T(8,128)(2,1)S(1)}, u32[]{:S(2)}, u32[]{:S(2)}) collective-permute-start(bf16[64,1024]{1,0:T(8,128)(2,1)S(1)} %get-tuple-element.23.refs_6_.refs_5_), channel_id=1, source_target_pairs={{4,10},{6,8},{20,26},{22,24},{5,11},{7,9},{21,27},{23,25}} | collective-permute-start | bytes 393224 | tf_op jit(solution)/shard_map/ppermute | solution.py:230
  27.7 7.1 %collective-permute-start.8 = (bf16[64,1024]{1,0:T(8,128)(2,1)S(1)}, bf16[64,1024]{1,0:T(8,128)(2,1)S(1)}, u32[]{:S(2)}, u32[]{:S(2)}) collective-permute-start(bf16[64,1024]{1,0:T(8,128)(2,1)S(1)} %shard_map.51.refs_5_), channel_id=1, source_target_pairs={{0,2},{1,3},{2,0},{3,1},{4,6},{5,7},{6,4},{7,5},{8,10},{9,11},{10,... | collective-permute-start | bytes 393224 | tf_op jit(solution)/shard_map/ppermute | solution.py:244
  35.8 5.0 %collective-permute-start.14 = (bf16[64,1024]{1,0:T(8,128)(2,1)S(1)}, bf16[64,1024]{1,0:T(8,128)(2,1)S(1)}, u32[]{:S(2)}, u32[]{:S(2)}) collective-permute-start(bf16[64,1024]{1,0:T(8,128)(2,1)S(1)} %get-tuple-element.24.piece_ref.refs_0_), channel_id=1, source_target_pairs={{0,2},{1,3},{2,0},{3,1},{4,12},{5,13},{6,14},{7,15},{8,10},{9,11},... | collective-permute-start | bytes 393224 | tf_op jit(solution)/shard_map/ppermute | solution.py:244
  41.5 6.7 %collective-permute-start.17 = (bf16[64,1024]{1,0:T(8,128)(2,1)S(1)}, bf16[64,1024]{1,0:T(8,128)(2,1)S(1)}, u32[]{:S(2)}, u32[]{:S(2)}) collective-permute-start(bf16[64,1024]{1,0:T(8,128)(2,1)S(1)} %get-tuple-element.26.refs_1_), channel_id=1, source_target_pairs={{0,6},{1,7},{2,4},{3,5},{4,2},{5,3},{6,0},{7,1},{8,14},{9,15},{10,... | collective-permute-start | bytes 393224 | tf_op jit(solution)/shard_map/ppermute | solution.py:244
  45.2 5.0 %collective-permute-start.16 = (bf16[64,1024]{1,0:T(8,128)(2,1)S(1)}, bf16[64,1024]{1,0:T(8,128)(2,1)S(1)}, u32[]{:S(2)}, u32[]{:S(2)}) collective-permute-start(bf16[64,1024]{1,0:T(8,128)(2,1)S(1)} %get-tuple-element.26.refs_1_), channel_id=1, source_target_pairs={{0,2},{1,3},{2,0},{3,1},{4,6},{5,7},{6,4},{7,5},{8,10},{9,11},{10,... | collective-permute-start | bytes 393224 | tf_op jit(solution)/shard_map/ppermute | solution.py:244
  46.0 5.0 %collective-permute-start.15 = (bf16[64,1024]{1,0:T(8,128)(2,1)S(1)}, bf16[64,1024]{1,0:T(8,128)(2,1)S(1)}, u32[]{:S(2)}, u32[]{:S(2)}) collective-permute-start(bf16[64,1024]{1,0:T(8,128)(2,1)S(1)} %get-tuple-element.26.refs_1_), channel_id=1, source_target_pairs={{0,4},{1,5},{2,6},{3,7},{4,0},{5,1},{6,2},{7,3},{8,12},{9,13},{10,... | collective-permute-start | bytes 393224 | tf_op jit(solution)/shard_map/ppermute | solution.py:244
  52.0 5.0 %collective-permute-start.18 = (bf16[64,1024]{1,0:T(8,128)(2,1)S(1)}, bf16[64,1024]{1,0:T(8,128)(2,1)S(1)}, u32[]{:S(2)}, u32[]{:S(2)}) collective-permute-start(bf16[64,1024]{1,0:T(8,128)(2,1)S(1)} %shard_map.56.piece_ref.refs_0_), channel_id=1, source_target_pairs={{0,2},{1,3},{2,0},{3,1},{4,6},{5,7},{6,4},{7,5},{8,10},{9,11},{10,... | collective-permute-start | bytes 393224 | tf_op jit(solution)/shard_map/ppermute | solution.py:244

commit v14 on v13

--- a/solution.py
+++ b/solution.py
@@ -12,13 +12,6 @@
 
 def upper_depth(leaf, top):
     return top - 1 - sum(((leaf + 1) % 2**power == 0).astype(jnp.int32) for power in range(1, top + 1))
-
-
-def cast_kernel(right_ref, cast_ref, staged, semaphore):
-    values = pltpu.make_async_copy(right_ref.at[1], staged, semaphore)
-    values.start()
-    values.wait()
-    cast_ref[...] = staged[...].astype(BF16)
 
 
 def load_kernel(count, after_ref, *refs):
@@ -61,7 +54,7 @@
     if level == top:
         pieces = [refs[1:2 * rows:2], refs[:2 * rows:2]]
         if plan == "traded":
-            r0, l0, l1, r1 = refs[:4]
+            r0, r1, l0, l1 = refs[:4]
             pieces = [[l0, l1], [r0, r1]]
     elif plan == "rooted":
         r1, r0, l1, l0 = refs[:4]
@@ -282,7 +275,7 @@
     def paired(lefts, rights):
         return [piece for pair in zip(lefts[::-1], rights[::-1]) for piece in pair]
 
-    reduced = call(cast_kernel, [], [right_side], [half], [near((count, width), F32), pltpu.SemaphoreType.DMA(())])
+    reduced = right_side[1].astype(BF16)
     gathered = rows_of(reduced, holders(0))
     inverses = [load(reduced, [inverse_diag]), *swapped]
     plans = ["rooted", "crossed", "traded"] if crossing else ["plain"] * top
@@ -300,7 +293,7 @@
             elif plan == "crossed":
                 pieces = [late, rights[1], rights[0], lefts[1], lefts[0], relayed, rounded]
             elif plan == "traded":
-                pieces = [rights[0], lefts[0], lefts[1], rights[1], mine, relayed, late]
+                pieces = [rights[0], rights[1], lefts[0], lefts[1], mine, relayed, late]
             else:
                 pieces = [*pieces, *older]
             arrays = [block_rows, right, lower, *pieces]

time: 59 us -> 58.6 us (level)
  Pallas kernels: 14.4 us -> 13.4 us
  local copies, waits for them, and re-layouts: 0.01 us -> 0.97 us
    convert_element_type x0 -> x1, local copies, waits for them, and re-layouts: none -> 0.96 us  [local(): reduced = right_side[1].astype(BF16)]
    pallas_call x13 -> x12, Pallas kernels: 14.4 us -> 13.4 us  [call(): pl.pallas_call(kernel, in_specs=[WHOLE] * len(near) + [FAR] * len(far), o...]
  transfers between devices with their start and end apart: 19 -> 19, of which waited for: 9 -> 9; matrix products, arithmetic and copies ran while one was open for 0% -> 2% of each run, Pallas kernels for 15% -> 13%
where the time goes in v14:
time: 58.6 us; the launch traced here: 58.3 us
  starting transfers between devices  22.8 us (39%)
  waiting for transfers between devices  20.9 us (36%)
  Pallas kernels  13.4 us (23%)
  local copies, waits for them, and re-layouts  0.97 us (2%)
    ppermute x14, starting transfers between devices, permute(): return lax.ppermute(value, ('leaf', 'rows', 'rhs'), pairs)  18.5 us
    ppermute x14, waiting for transfers between devices, permute(): return lax.ppermute(value, ('leaf', 'rows', 'rhs'), pairs)  16 us
    pallas_call x12, Pallas kernels, call(): pl.pallas_call(kernel, in_specs=[WHOLE] * len(near) + [FAR] * len(far), o...  13.4 us
    ppermute x4, waiting for transfers between devices, send(): return lax.ppermute(value, places, pairs)  4.93 us
    ppermute x4, starting transfers between devices, send(): return lax.ppermute(value, places, pairs)  3.92 us
  transfers between devices with their start and end apart: 19, of which 9 were waited for; matrix products, arithmetic and copies ran while one was open for 2% of the time, Pallas kernels for 13%

profile of v14, /device:TPU:0, one launch (start us, length us, event | category | flops | bytes accessed | tf_op | source)
XLA Modules:
  0.0 58.3 jit_solution(8280633536890575232)
XLA Ops:
  0.0 0.5 collective-permute-start.1
  0.5 1.0 %fusion.after_ref.refs_0_ = bf16[64,1024]{1,0:T(8,128)(2,1)S(1)} fusion(f32[2,64,1024]{2,1,0:T(8,128)} %refs_0_.3), kind=kLoop, calls=%fused_computation.1 | loop fusion | bytes 262144 | tf_op jit(solution)/shard_map/convert_element_type | solution.py:278
  1.4 0.1 collective-permute-start
  1.5 2.2 %shard_map.46.refs_2_.refs_0_ = bf16[2,2048,512]{2,1,0:T(8,128)(2,1)S(1)} custom-call(bf16[64,1024]{1,0:T(8,128)(2,1)S(1)} %fusion.after_ref.refs_0_, bf16[2,2048,512]{2,1,0:T(8,128)(2,1)} %refs_0_.2), custom_call_target="tpu_custom_call" | custom-call | bytes 4325376 | tf_op jit(solution)/shard_map/pallas_call | solution.py:203
  3.7 3.7 %collective-permute-done.refs_1_ = bf16[64,1024]{1,0:T(8,128)(2,1)S(1)} collective-permute-done((bf16[64,1024]{1,0:T(8,128)(2,1)S(1)}, bf16[64,1024]{1,0:T(8,128)(2,1)S(1)}, u32[]{:S(2)}, u32[]{:S(2)}) %collective-permute-start) | collective-permute-done | bytes 131104 | tf_op jit(solution)/shard_map/ppermute | solution.py:237
  7.4 0.0 collective-permute-done.1.refs_3_.refs_1_
  7.5 0.9 %shard_map.47 = (bf16[64,1024]{1,0:T(8,128)(2,1)S(1)}, f32[64,1024]{1,0:T(8,128)S(1)}) custom-call(bf16[64,1024]{1,0:T(8,128)(2,1)S(1)} %fusion.after_ref.refs_0_, bf16[64,1024]{1,0:T(8,128)(2,1)S(1)} %collective-permute-done.refs_1_, bf16[2,2048,512]{2,1,0:T(8,128)(2,1)S(1)} %shard_map.46.refs_2_.refs_0_, ...), custom_call_target="tpu_custom_call" | custom-call | flops 268435456 | bytes 8650752 | tf_op jit(solution)/shard_map/pallas_call | solution.py:203
  8.3 0.4 collective-permute-start.5
  8.8 0.1 collective-permute-start.4
  8.9 0.4 collective-permute-start.3
  9.3 0.1 collective-permute-start.2
  9.4 3.6 %shard_map.48 = (f32[2,64,1024]{2,1,0:T(8,128)S(1)}, bf16[2,16,128,1024]{3,2,1,0:T(8,128)(2,1)S(1)}) custom-call(bf16[64,1024]{1,0:T(8,128)(2,1)S(1)} %get-tuple-element.17.after_ref.refs_4_.refs_5_, f32[2,64,1024]{2,1,0:T(8,128)} %refs_0_.3, bf16[2,16,128,1024]{3,2,1,0:T(8,128)(2,1)} %refs_1_.1), custom_call_target="tpu_custom_call" | custom-call | bytes 9043968 | tf_op jit(solution)/shard_map/pallas_call | solution.py:203
  13.0 0.0 collective-permute-done.5.refs_3_
  13.0 0.0 collective-permute-done.4.refs_2_
  13.1 0.0 collective-permute-done.3.refs_1_
  13.1 0.0 collective-permute-done.2.refs_0_
  13.1 1.0 %shard_map.49 = (bf16[64,1024]{1,0:T(8,128)(2,1)S(1)}, bf16[64,1024]{1,0:T(8,128)(2,1)S(1)}) custom-call(s32[2,16]{1,0:T(2,128)S(1)} %copy-done, f32[2,64,1024]{2,1,0:T(8,128)S(1)} %get-tuple-element.18.right_ref, bf16[2,16,128,1024]{3,2,1,0:T(8,128)(2,1)S(1)} %get-tuple-element.19.lower_ref, bf16[64,1024]{1,0:T(8,128)(2,1)S(1)} %collective-permute-done.2.refs_0_, ...), custom_call_target="tpu_custom_call" | custom-call | flops 268435456 | bytes 9568384 | tf_op jit(solution)/shard_map/pallas_call | solution.py:203
  14.1 0.4 collective-permute-start.9
  14.5 0.1 collective-permute-start.7
  14.7 8.1 %collective-permute-start.6 = (bf16[64,1024]{1,0:T(8,128)(2,1)S(1)}, bf16[64,1024]{1,0:T(8,128)(2,1)S(1)}, u32[]{:S(2)}, u32[]{:S(2)}) collective-permute-start(bf16[64,1024]{1,0:T(8,128)(2,1)S(1)} %get-tuple-element.20.own_ref), channel_id=1, source_target_pairs={{0,4},{1,5},{2,6},{3,7},{4,0},{5,1},{6,2},{7,3},{8,9},{9,8},{10,11... | collective-permute-start | bytes 393224 | tf_op jit(solution)/shard_map/ppermute | solution.py:237
  22.8 0.9 %shard_map.51 = (bf16[64,1024]{1,0:T(8,128)(2,1)S(1)}, f32[64,1024]{1,0:T(8,128)S(1)}) custom-call(bf16[64,1024]{1,0:T(8,128)(2,1)S(1)} %get-tuple-element.21.refs_0_, bf16[64,1024]{1,0:T(8,128)(2,1)S(1)} %collective-permute-done.9.refs_1_, bf16[2,2048,512]{2,1,0:T(8,128)(2,1)S(1)} %shard_map.46.refs_2_.refs_0_, ...), custom_call_target="tpu_custom_call" | custom-call | flops 268435456 | bytes 9043968 | tf_op jit(solution)/shard_map/pallas_call | solution.py:203
  23.7 1.3 %collective-permute-start.13 = (bf16[64,1024]{1,0:T(8,128)(2,1)S(1)}, bf16[64,1024]{1,0:T(8,128)(2,1)S(1)}, u32[]{:S(2)}, u32[]{:S(2)}) collective-permute-start(bf16[64,1024]{1,0:T(8,128)(2,1)S(1)} %get-tuple-element.23.refs_6_.refs_5_), channel_id=1, source_target_pairs={{4,0},{6,2},{20,16},{22,18},{5,1},{7,3},{21,17},{23,19}} | collective-permute-start | bytes 393224 | tf_op jit(solution)/shard_map/ppermute | solution.py:223
  25.0 1.3 %collective-permute-start.12 = (bf16[64,1024]{1,0:T(8,128)(2,1)S(1)}, bf16[64,1024]{1,0:T(8,128)(2,1)S(1)}, u32[]{:S(2)}, u32[]{:S(2)}) collective-permute-start(bf16[64,1024]{1,0:T(8,128)(2,1)S(1)} %get-tuple-element.23.refs_6_.refs_5_), channel_id=1, source_target_pairs={{4,2},{6,0},{20,18},{22,16},{5,3},{7,1},{21,19},{23,17}} | collective-permute-start | bytes 393224 | tf_op jit(solution)/shard_map/ppermute | solution.py:223
  26.3 0.7 %collective-permute-start.11 = (bf16[64,1024]{1,0:T(8,128)(2,1)S(1)}, bf16[64,1024]{1,0:T(8,128)(2,1)S(1)}, u32[]{:S(2)}, u32[]{:S(2)}) collective-permute-start(bf16[64,1024]{1,0:T(8,128)(2,1)S(1)} %get-tuple-element.23.refs_6_.refs_5_), channel_id=1, source_target_pairs={{4,8},{6,10},{20,24},{22,26},{5,9},{7,11},{21,25},{23,27}} | collective-permute-start | bytes 393224 | tf_op jit(solution)/shard_map/ppermute | solution.py:223
  27.0 0.7 %collective-permute-start.10 = (bf16[64,1024]{1,0:T(8,128)(2,1)S(1)}, bf16[64,1024]{1,0:T(8,128)(2,1)S(1)}, u32[]{:S(2)}, u32[]{:S(2)}) collective-permute-start(bf16[64,1024]{1,0:T(8,128)(2,1)S(1)} %get-tuple-element.23.refs_6_.refs_5_), channel_id=1, source_target_pairs={{4,10},{6,8},{20,26},{22,24},{5,11},{7,9},{21,27},{23,25}} | collective-permute-start | bytes 393224 | tf_op jit(solution)/shard_map/ppermute | solution.py:223
  27.7 0.0 collective-permute-done.6.first_ref
  27.7 1.2 %collective-permute-start.8 = (bf16[64,1024]{1,0:T(8,128)(2,1)S(1)}, bf16[64,1024]{1,0:T(8,128)(2,1)S(1)}, u32[]{:S(2)}, u32[]{:S(2)}) collective-permute-start(bf16[64,1024]{1,0:T(8,128)(2,1)S(1)} %shard_map.50.refs_5_), channel_id=1, source_target_pairs={{0,2},{1,3},{2,0},{3,1},{4,6},{5,7},{6,4},{7,5},{8,10},{9,11},{10,... | collective-permute-start | bytes 393224 | tf_op jit(solution)/shard_map/ppermute | solution.py:237
  28.9 3.1 %collective-permute-done.13.refs_4_ = bf16[64,1024]{1,0:T(8,128)(2,1)S(1)} collective-permute-done((bf16[64,1024]{1,0:T(8,128)(2,1)S(1)}, bf16[64,1024]{1,0:T(8,128)(2,1)S(1)}, u32[]{:S(2)}, u32[]{:S(2)}) %collective-permute-start.13) | collective-permute-done | bytes 131104 | tf_op jit(solution)/shard_map/ppermute | solution.py:223
  32.0 1.8 %collective-permute-done.12.refs_3_ = bf16[64,1024]{1,0:T(8,128)(2,1)S(1)} collective-permute-done((bf16[64,1024]{1,0:T(8,128)(2,1)S(1)}, bf16[64,1024]{1,0:T(8,128)(2,1)S(1)}, u32[]{:S(2)}, u32[]{:S(2)}) %collective-permute-start.12) | collective-permute-done | bytes 131104 | tf_op jit(solution)/shard_map/ppermute | solution.py:223
  33.8 0.0 collective-permute-done.11.refs_2_
  33.9 0.0 collective-permute-done.10.refs_1_
  33.9 1.0 %collective-permute-done.8.refs_0_.refs_6_ = bf16[64,1024]{1,0:T(8,128)(2,1)S(1)} collective-permute-done((bf16[64,1024]{1,0:T(8,128)(2,1)S(1)}, bf16[64,1024]{1,0:T(8,128)(2,1)S(1)}, u32[]{:S(2)}, u32[]{:S(2)}) %collective-permute-start.8) | collective-permute-done | bytes 131104 | tf_op jit(solution)/shard_map/ppermute | solution.py:237
  34.8 1.0 %shard_map.52 = (bf16[64,1024]{1,0:T(8,128)(2,1)S(1)}, bf16[64,4096]{1,0:T(8,128)(2,1)S(1)}) custom-call(s32[2,16]{1,0:T(2,128)S(1)} %copy-done, f32[2,64,1024]{2,1,0:T(8,128)S(1)} %get-tuple-element.18.right_ref, bf16[2,16,128,1024]{3,2,1,0:T(8,128)(2,1)S(1)} %get-tuple-element.19.lower_ref, bf16[64,1024]{1,0:T(8,128)(2,1)S(1)} %collective-permute-done.8.refs_0_.refs_6_, ...), custom_call_target="tpu_custom_call" | custom-call | flops 268435456 | bytes 9830528 | tf_op jit(solution)/shard_map/pallas_call | solution.py:203
  35.8 1.6 %collective-permute-start.14 = (bf16[64,1024]{1,0:T(8,128)(2,1)S(1)}, bf16[64,1024]{1,0:T(8,128)(2,1)S(1)}, u32[]{:S(2)}, u32[]{:S(2)}) collective-permute-start(bf16[64,1024]{1,0:T(8,128)(2,1)S(1)} %get-tuple-element.24.piece_ref.refs_0_), channel_id=1, source_target_pairs={{0,2},{1,3},{2,0},{3,1},{4,12},{5,13},{6,14},{7,15},{8,10},{9,11},... | collective-permute-start | bytes 393224 | tf_op jit(solution)/shard_map/ppermute | solution.py:237
  37.4 0.5 shard_map.53.refs_6_
  37.8 3.0 %collective-permute-done.14.refs_1_ = bf16[64,1024]{1,0:T(8,128)(2,1)S(1)} collective-permute-done((bf16[64,1024]{1,0:T(8,128)(2,1)S(1)}, bf16[64,1024]{1,0:T(8,128)(2,1)S(1)}, u32[]{:S(2)}, u32[]{:S(2)}) %collective-permute-start.14) | collective-permute-done | bytes 131104 | tf_op jit(solution)/shard_map/ppermute | solution.py:237
  40.8 0.6 %shard_map.54 = (bf16[64,1024]{1,0:T(8,128)(2,1)S(1)}, f32[64,1024]{1,0:T(8,128)S(1)}) custom-call(bf16[64,1024]{1,0:T(8,128)(2,1)S(1)} %get-tuple-element.24.piece_ref.refs_0_, bf16[64,1024]{1,0:T(8,128)(2,1)S(1)} %collective-permute-done.14.refs_1_, bf16[2,2048,512]{2,1,0:T(8,128)(2,1)S(1)} %shard_map.46.refs_2_.refs_0_, ...), custom_call_target="tpu_custom_call" | custom-call | flops 268435456 | bytes 9306112 | tf_op jit(solution)/shard_map/pallas_call | solution.py:203
  41.5 1.6 %collective-permute-start.17 = (bf16[64,1024]{1,0:T(8,128)(2,1)S(1)}, bf16[64,1024]{1,0:T(8,128)(2,1)S(1)}, u32[]{:S(2)}, u32[]{:S(2)}) collective-permute-start(bf16[64,1024]{1,0:T(8,128)(2,1)S(1)} %get-tuple-element.26.refs_2_), channel_id=1, source_target_pairs={{0,2},{1,3},{2,0},{3,1},{4,6},{5,7},{6,4},{7,5},{8,10},{9,11},{10,... | collective-permute-start | bytes 393224 | tf_op jit(solution)/shard_map/ppermute | solution.py:237
  43.1 2.9 %collective-permute-start.16 = (bf16[64,1024]{1,0:T(8,128)(2,1)S(1)}, bf16[64,1024]{1,0:T(8,128)(2,1)S(1)}, u32[]{:S(2)}, u32[]{:S(2)}) collective-permute-start(bf16[64,1024]{1,0:T(8,128)(2,1)S(1)} %get-tuple-element.26.refs_2_), channel_id=1, source_target_pairs={{0,6},{1,7},{2,4},{3,5},{4,2},{5,3},{6,0},{7,1},{8,14},{9,15},{10,... | collective-permute-start | bytes 393224 | tf_op jit(solution)/shard_map/ppermute | solution.py:237
  46.0 0.0 collective-permute-start.15
  46.0 2.0 %collective-permute-done.17.refs_3_ = bf16[64,1024]{1,0:T(8,128)(2,1)S(1)} collective-permute-done((bf16[64,1024]{1,0:T(8,128)(2,1)S(1)}, bf16[64,1024]{1,0:T(8,128)(2,1)S(1)}, u32[]{:S(2)}, u32[]{:S(2)}) %collective-permute-start.17) | collective-permute-done | bytes 131104 | tf_op jit(solution)/shard_map/ppermute | solution.py:237
  48.1 1.2 %collective-permute-done.16.refs_1_ = bf16[64,1024]{1,0:T(8,128)(2,1)S(1)} collective-permute-done((bf16[64,1024]{1,0:T(8,128)(2,1)S(1)}, bf16[64,1024]{1,0:T(8,128)(2,1)S(1)}, u32[]{:S(2)}, u32[]{:S(2)}) %collective-permute-start.16) | collective-permute-done | bytes 131104 | tf_op jit(solution)/shard_map/ppermute | solution.py:237
  49.3 1.7 %collective-permute-done.15.refs_0_ = bf16[64,1024]{1,0:T(8,128)(2,1)S(1)} collective-permute-done((bf16[64,1024]{1,0:T(8,128)(2,1)S(1)}, bf16[64,1024]{1,0:T(8,128)(2,1)S(1)}, u32[]{:S(2)}, u32[]{:S(2)}) %collective-permute-start.15) | collective-permute-done | bytes 131104 | tf_op jit(solution)/shard_map/ppermute | solution.py:237
  51.0 1.0 %shard_map.55.piece_ref.refs_0_ = bf16[64,1024]{1,0:T(8,128)(2,1)S(1)} custom-call(s32[2,16]{1,0:T(2,128)S(1)} %copy-done, f32[2,64,1024]{2,1,0:T(8,128)S(1)} %get-tuple-element.18.right_ref, bf16[2,16,128,1024]{3,2,1,0:T(8,128)(2,1)S(1)} %get-tuple-element.19.lower_ref, bf16[64,1024]{1,0:T(8,128)(2,1)S(1)} %collective-permute-done.15.refs_0_, ...), custom_call_target="tpu_custom_call" | custom-call | flops 268435456 | bytes 10223744 | tf_op jit(solution)/shard_map/pallas_call | solution.py:203
  52.0 1.2 %collective-permute-start.18 = (bf16[64,1024]{1,0:T(8,128)(2,1)S(1)}, bf16[64,1024]{1,0:T(8,128)(2,1)S(1)}, u32[]{:S(2)}, u32[]{:S(2)}) collective-permute-start(bf16[64,1024]{1,0:T(8,128)(2,1)S(1)} %shard_map.55.piece_ref.refs_0_), channel_id=1, source_target_pairs={{0,2},{1,3},{2,0},{3,1},{4,6},{5,7},{6,4},{7,5},{8,10},{9,11},{10,... | collective-permute-start | bytes 393224 | tf_op jit(solution)/shard_map/ppermute | solution.py:237
  53.2 0.5 shard_map.56.refs_5_
  53.7 3.3 %collective-permute-done.18.refs_1_ = bf16[64,1024]{1,0:T(8,128)(2,1)S(1)} collective-permute-done((bf16[64,1024]{1,0:T(8,128)(2,1)S(1)}, bf16[64,1024]{1,0:T(8,128)(2,1)S(1)}, u32[]{:S(2)}, u32[]{:S(2)}) %collective-permute-start.18) | collective-permute-done | bytes 131104 | tf_op jit(solution)/shard_map/ppermute | solution.py:237
  57.1 1.3 %shard_map.57 = f32[2,64,1024]{2,1,0:T(8,128)} custom-call(bf16[64,1024]{1,0:T(8,128)(2,1)S(1)} %shard_map.55.piece_ref.refs_0_, bf16[64,1024]{1,0:T(8,128)(2,1)S(1)} %collective-permute-done.18.refs_1_, bf16[2,2048,512]{2,1,0:T(8,128)(2,1)S(1)} %shard_map.46.refs_2_.refs_0_, bf16[2,2048,512]{2,1,0:T(8,128)(2,1)S(1)} %collective-permute-done.1.refs_3_.refs_1_, ...), custom_call_target="tpu_custom_call" | custom-call | flops 268435456 | bytes 9175040 | tf_op jit(solution)/shard_map/pallas_call | solution.py:203
  (5 shorter events, 0.0 us)
Async XLA Ops:
  0.0 7.4 %collective-permute-start.1 = (bf16[2,2048,512]{2,1,0:T(8,128)(2,1)}, bf16[2,2048,512]{2,1,0:T(8,128)(2,1)S(1)}, u32[]{:S(2)}, u32[]{:S(2)}) collective-permute-start(bf16[2,2048,512]{2,1,0:T(8,128)(2,1)} %refs_0_.2), channel_id=1, source_target_pairs={{0,1},{1,0},{2,3},{3,2},{4,5},{5,4},{6,7},{7,6},{8,9},{9,8},{10,11... | collective-permute-start | bytes 12582920 | tf_op jit(solution)/shard_map/ppermute | solution.py:256
  1.4 6.0 %collective-permute-start = (bf16[64,1024]{1,0:T(8,128)(2,1)S(1)}, bf16[64,1024]{1,0:T(8,128)(2,1)S(1)}, u32[]{:S(2)}, u32[]{:S(2)}) collective-permute-start(bf16[64,1024]{1,0:T(8,128)(2,1)S(1)} %fusion.after_ref.refs_0_), channel_id=1, source_target_pairs={{0,1},{1,0},{2,3},{3,2},{4,5},{5,4},{6,7},{7,6},{8,9},{9,8},{10,11... | collective-permute-start | bytes 393224 | tf_op jit(solution)/shard_map/ppermute | solution.py:237
  8.3 4.7 %copy-start = (s32[2,16]{1,0:T(2,128)S(1)}, s32[2,16]{1,0:T(2,128)}, u32[]{:S(2)}) copy-start(s32[2,16]{1,0:T(2,128)} %block_rows_ref.5) | copy-start | bytes 388
  8.3 4.7 %collective-permute-start.5 = (bf16[64,1024]{1,0:T(8,128)(2,1)S(1)}, bf16[64,1024]{1,0:T(8,128)(2,1)S(1)}, u32[]{:S(2)}, u32[]{:S(2)}) collective-permute-start(bf16[64,1024]{1,0:T(8,128)(2,1)S(1)} %get-tuple-element.17.after_ref.refs_4_.refs_5_), channel_id=1, source_target_pairs={{0,1},{1,0},{2,3},{3,2},{4,8},{5,9},{6,10},{7,11},{8,12},{9,13},{1... | collective-permute-start | bytes 393224 | tf_op jit(solution)/shard_map/ppermute | solution.py:237
  8.8 4.3 %collective-permute-start.4 = (bf16[64,1024]{1,0:T(8,128)(2,1)S(1)}, bf16[64,1024]{1,0:T(8,128)(2,1)S(1)}, u32[]{:S(2)}, u32[]{:S(2)}) collective-permute-start(bf16[64,1024]{1,0:T(8,128)(2,1)S(1)} %get-tuple-element.17.after_ref.refs_4_.refs_5_), channel_id=1, source_target_pairs={{0,1},{1,0},{2,3},{3,2},{4,14},{5,15},{6,12},{7,13},{8,9},{9,8},{1... | collective-permute-start | bytes 393224 | tf_op jit(solution)/shard_map/ppermute | solution.py:237
  8.9 4.1 %collective-permute-start.3 = (bf16[64,1024]{1,0:T(8,128)(2,1)S(1)}, bf16[64,1024]{1,0:T(8,128)(2,1)S(1)}, u32[]{:S(2)}, u32[]{:S(2)}) collective-permute-start(bf16[64,1024]{1,0:T(8,128)(2,1)S(1)} %get-tuple-element.17.after_ref.refs_4_.refs_5_), channel_id=1, source_target_pairs={{0,1},{1,0},{2,3},{3,2},{4,5},{5,4},{6,7},{7,6},{8,9},{9,8},{10,11... | collective-permute-start | bytes 393224 | tf_op jit(solution)/shard_map/ppermute | solution.py:237
  9.3 3.8 %collective-permute-start.2 = (bf16[64,1024]{1,0:T(8,128)(2,1)S(1)}, bf16[64,1024]{1,0:T(8,128)(2,1)S(1)}, u32[]{:S(2)}, u32[]{:S(2)}) collective-permute-start(bf16[64,1024]{1,0:T(8,128)(2,1)S(1)} %get-tuple-element.17.after_ref.refs_4_.refs_5_), channel_id=1, source_target_pairs={{0,1},{1,0},{2,3},{3,2},{4,5},{5,4},{6,7},{7,6},{8,9},{9,8},{10,11... | collective-permute-start | bytes 393224 | tf_op jit(solution)/shard_map/ppermute | solution.py:237
  14.1 8.7 %collective-permute-start.9 = (bf16[64,1024]{1,0:T(8,128)(2,1)S(1)}, bf16[64,1024]{1,0:T(8,128)(2,1)S(1)}, u32[]{:S(2)}, u32[]{:S(2)}) collective-permute-start(bf16[64,1024]{1,0:T(8,128)(2,1)S(1)} %get-tuple-element.21.refs_0_), channel_id=1, source_target_pairs={{0,1},{1,0},{2,3},{3,2},{4,6},{5,7},{6,4},{7,5},{8,9},{9,8},{10,11... | collective-permute-start | bytes 393224 | tf_op jit(solution)/shard_map/ppermute | solution.py:237
  14.5 12.5 %collective-permute-start.7 = (bf16[64,1024]{1,0:T(8,128)(2,1)S(1)}, bf16[64,1024]{1,0:T(8,128)(2,1)S(1)}, u32[]{:S(2)}, u32[]{:S(2)}) collective-permute-start(bf16[64,1024]{1,0:T(8,128)(2,1)S(1)} %get-tuple-element.20.own_ref), channel_id=1, source_target_pairs={{0,1},{1,0},{2,3},{3,2},{4,8},{5,9},{6,10},{7,11},{8,4},{9,5},{10,... | collective-permute-start | bytes 393224 | tf_op jit(solution)/shard_map/ppermute | solution.py:237
  14.7 13.0 %collective-permute-start.6 = (bf16[64,1024]{1,0:T(8,128)(2,1)S(1)}, bf16[64,1024]{1,0:T(8,128)(2,1)S(1)}, u32[]{:S(2)}, u32[]{:S(2)}) collective-permute-start(bf16[64,1024]{1,0:T(8,128)(2,1)S(1)} %get-tuple-element.20.own_ref), channel_id=1, source_target_pairs={{0,4},{1,5},{2,6},{3,7},{4,0},{5,1},{6,2},{7,3},{8,9},{9,8},{10,11... | collective-permute-start | bytes 393224 | tf_op jit(solution)/shard_map/ppermute | solution.py:237
  23.7 8.3 %collective-permute-start.13 = (bf16[64,1024]{1,0:T(8,128)(2,1)S(1)}, bf16[64,1024]{1,0:T(8,128)(2,1)S(1)}, u32[]{:S(2)}, u32[]{:S(2)}) collective-permute-start(bf16[64,1024]{1,0:T(8,128)(2,1)S(1)} %get-tuple-element.23.refs_6_.refs_5_), channel_id=1, source_target_pairs={{4,0},{6,2},{20,16},{22,18},{5,1},{7,3},{21,17},{23,19}} | collective-permute-start | bytes 393224 | tf_op jit(solution)/shard_map/ppermute | solution.py:223
  25.0 8.8 %collective-permute-start.12 = (bf16[64,1024]{1,0:T(8,128)(2,1)S(1)}, bf16[64,1024]{1,0:T(8,128)(2,1)S(1)}, u32[]{:S(2)}, u32[]{:S(2)}) collective-permute-start(bf16[64,1024]{1,0:T(8,128)(2,1)S(1)} %get-tuple-element.23.refs_6_.refs_5_), channel_id=1, source_target_pairs={{4,2},{6,0},{20,18},{22,16},{5,3},{7,1},{21,19},{23,17}} | collective-permute-start | bytes 393224 | tf_op jit(solution)/shard_map/ppermute | solution.py:223
  26.3 7.5 %collective-permute-start.11 = (bf16[64,1024]{1,0:T(8,128)(2,1)S(1)}, bf16[64,1024]{1,0:T(8,128)(2,1)S(1)}, u32[]{:S(2)}, u32[]{:S(2)}) collective-permute-start(bf16[64,1024]{1,0:T(8,128)(2,1)S(1)} %get-tuple-element.23.refs_6_.refs_5_), channel_id=1, source_target_pairs={{4,8},{6,10},{20,24},{22,26},{5,9},{7,11},{21,25},{23,27}} | collective-permute-start | bytes 393224 | tf_op jit(solution)/shard_map/ppermute | solution.py:223
  27.0 6.9 %collective-permute-start.10 = (bf16[64,1024]{1,0:T(8,128)(2,1)S(1)}, bf16[64,1024]{1,0:T(8,128)(2,1)S(1)}, u32[]{:S(2)}, u32[]{:S(2)}) collective-permute-start(bf16[64,1024]{1,0:T(8,128)(2,1)S(1)} %get-tuple-element.23.refs_6_.refs_5_), channel_id=1, source_target_pairs={{4,10},{6,8},{20,26},{22,24},{5,11},{7,9},{21,27},{23,25}} | collective-permute-start | bytes 393224 | tf_op jit(solution)/shard_map/ppermute | solution.py:223
  27.7 7.1 %collective-permute-start.8 = (bf16[64,1024]{1,0:T(8,128)(2,1)S(1)}, bf16[64,1024]{1,0:T(8,128)(2,1)S(1)}, u32[]{:S(2)}, u32[]{:S(2)}) collective-permute-start(bf16[64,1024]{1,0:T(8,128)(2,1)S(1)} %shard_map.50.refs_5_), channel_id=1, source_target_pairs={{0,2},{1,3},{2,0},{3,1},{4,6},{5,7},{6,4},{7,5},{8,10},{9,11},{10,... | collective-permute-start | bytes 393224 | tf_op jit(solution)/shard_map/ppermute | solution.py:237
  35.8 5.0 %collective-permute-start.14 = (bf16[64,1024]{1,0:T(8,128)(2,1)S(1)}, bf16[64,1024]{1,0:T(8,128)(2,1)S(1)}, u32[]{:S(2)}, u32[]{:S(2)}) collective-permute-start(bf16[64,1024]{1,0:T(8,128)(2,1)S(1)} %get-tuple-element.24.piece_ref.refs_0_), channel_id=1, source_target_pairs={{0,2},{1,3},{2,0},{3,1},{4,12},{5,13},{6,14},{7,15},{8,10},{9,11},... | collective-permute-start | bytes 393224 | tf_op jit(solution)/shard_map/ppermute | solution.py:237
  41.5 6.6 %collective-permute-start.17 = (bf16[64,1024]{1,0:T(8,128)(2,1)S(1)}, bf16[64,1024]{1,0:T(8,128)(2,1)S(1)}, u32[]{:S(2)}, u32[]{:S(2)}) collective-permute-start(bf16[64,1024]{1,0:T(8,128)(2,1)S(1)} %get-tuple-element.26.refs_2_), channel_id=1, source_target_pairs={{0,2},{1,3},{2,0},{3,1},{4,6},{5,7},{6,4},{7,5},{8,10},{9,11},{10,... | collective-permute-start | bytes 393224 | tf_op jit(solution)/shard_map/ppermute | solution.py:237
  43.1 6.2 %collective-permute-start.16 = (bf16[64,1024]{1,0:T(8,128)(2,1)S(1)}, bf16[64,1024]{1,0:T(8,128)(2,1)S(1)}, u32[]{:S(2)}, u32[]{:S(2)}) collective-permute-start(bf16[64,1024]{1,0:T(8,128)(2,1)S(1)} %get-tuple-element.26.refs_2_), channel_id=1, source_target_pairs={{0,6},{1,7},{2,4},{3,5},{4,2},{5,3},{6,0},{7,1},{8,14},{9,15},{10,... | collective-permute-start | bytes 393224 | tf_op jit(solution)/shard_map/ppermute | solution.py:237
  46.0 5.0 %collective-permute-start.15 = (bf16[64,1024]{1,0:T(8,128)(2,1)S(1)}, bf16[64,1024]{1,0:T(8,128)(2,1)S(1)}, u32[]{:S(2)}, u32[]{:S(2)}) collective-permute-start(bf16[64,1024]{1,0:T(8,128)(2,1)S(1)} %get-tuple-element.26.refs_2_), channel_id=1, source_target_pairs={{0,4},{1,5},{2,6},{3,7},{4,0},{5,1},{6,2},{7,3},{8,12},{9,13},{10,... | collective-permute-start | bytes 393224 | tf_op jit(solution)/shard_map/ppermute | solution.py:237
  52.0 5.0 %collective-permute-start.18 = (bf16[64,1024]{1,0:T(8,128)(2,1)S(1)}, bf16[64,1024]{1,0:T(8,128)(2,1)S(1)}, u32[]{:S(2)}, u32[]{:S(2)}) collective-permute-start(bf16[64,1024]{1,0:T(8,128)(2,1)S(1)} %shard_map.55.piece_ref.refs_0_), channel_id=1, source_target_pairs={{0,2},{1,3},{2,0},{3,1},{4,6},{5,7},{6,4},{7,5},{8,10},{9,11},{10,... | collective-permute-start | bytes 393224 | tf_op jit(solution)/shard_map/ppermute | solution.py:237

commit v15 on v14

--- a/solution.py
+++ b/solution.py
@@ -119,29 +119,30 @@
                     piece_ref[...], weights, preferred_element_type=F32)
 
 
-def apply_inverse(slot, cores, piece_refs, inverse_refs, part_ref, joined, store, turns=None):
+def apply_inverse(slot, cores, piece_refs, inverse_refs, part_ref, joined, store):
     rows = len(piece_refs)
     width = piece_refs[0].shape[1]
     quarter = inverse_refs[0].shape[-1]
-    own = lax.axis_index("rows")
-    if part_ref is None and turns in (None, [0]):
+
+    def share(turn):
+        core = lax.rem(lax.axis_index("rhs") - turn + cores, cores)
+        return pl.ds(pl.multiple_of(core * quarter, quarter), quarter)
+
+    if part_ref is None:
         place_pieces(piece_refs, joined, 0)
-    for turn in range(cores) if turns is None else turns:
-        inverse_ref = inverse_refs[turn]
-        core = lax.rem(lax.axis_index("rhs") - turn + cores, cores)
-        columns = pl.ds(pl.multiple_of(core * quarter, quarter), quarter)
-        if part_ref is None:
-            store(columns, jnp.dot(joined[...], inverse_ref[slot], preferred_element_type=F32))
-            continue
-        for which in range(rows):
-            @pl.when(own == which)
-            def _():
+        for turn, inverse_ref in enumerate(inverse_refs):
+            store(turn, share(turn), jnp.dot(joined[...], inverse_ref[slot], preferred_element_type=F32))
+        return
+    for which in range(rows):
+        @pl.when(lax.axis_index("rows") == which)
+        def _():
+            for turn, inverse_ref in enumerate(inverse_refs):
                 total = part_ref[:, turn * quarter:(turn + 1) * quarter]
                 for shift in range(1, rows):
                     source = (which - shift) % rows
                     weights = inverse_ref[slot, source * width:(source + 1) * width, :]
                     total = total + jnp.dot(piece_refs[shift][...], weights, preferred_element_type=F32)
-                store(columns, total)
+                store(turn, share(turn), total)
 
 
 def solve_kernel(top, depth, rows, cores, plan, split, *refs):
@@ -153,7 +154,7 @@
     leaf = lax.axis_index("leaf")
     active = upper_depth(leaf, top) == depth
 
-    def store(columns, total):
+    def store(turn, columns, total):
         rounded_ref[:, columns] = total.astype(BF16)
         before = before_ref[:, columns] if depth > 0 else jnp.zeros_like(total)
         solved_ref[:, columns] = jnp.where(active, total, before)
@@ -171,23 +172,21 @@
     inverse_refs = refs[rows:rows + cores]
     before_ref, *part, out_ref, joined, staged, semaphores = refs[rows + cores:]
     part_ref = part[0] if split else None
-    copies = [pltpu.make_async_copy(before_ref, out_ref.at[1], semaphores.at[0])]
-    copies[0].start()
-
     quarter = inverse_refs[0].shape[-1]
-
-    def store(columns, total):
+    earlier = pltpu.make_async_copy(before_ref, out_ref.at[1], semaphores.at[0])
+    earlier.start()
+
+    def written(turn, columns):
+        return pltpu.make_async_copy(staged.at[:, columns], out_ref.at[0, :, columns], semaphores.at[turn + 1])
+
+    def store(turn, columns, total):
         staged[:, columns] = total
-
+        written(turn, columns).start()
+
+    apply_inverse(0, cores, piece_refs, inverse_refs, part_ref, joined, store)
     for turn in range(cores):
-        core = lax.rem(lax.axis_index("rhs") - turn + cores, cores)
-        columns = pl.ds(pl.multiple_of(core * quarter, quarter), quarter)
-        apply_inverse(0, cores, piece_refs, inverse_refs, part_ref, joined, store, [turn])
-        copies.append(pltpu.make_async_copy(
-            staged.at[:, columns], out_ref.at[0, :, columns], semaphores.at[turn + 1]))
-        copies[-1].start()
-    for copy in copies:
-        copy.wait()
+        written(turn, pl.ds(0, quarter)).wait()
+    earlier.wait()
 
 
 WHOLE = pl.BlockSpec(memory_space=pltpu.VMEM)
@@ -277,7 +276,8 @@
 
     reduced = right_side[1].astype(BF16)
     gathered = rows_of(reduced, holders(0))
-    inverses = [load(reduced, [inverse_diag]), *swapped]
+    inverse_own, right, lower = load(reduced, [inverse_diag, right_side, lower_blocks])
+    inverses = [inverse_own, *swapped]
     plans = ["rooted", "crossed", "traded"] if crossing else ["plain"] * top
     plans = ["plain", *plans]
     older = []
@@ -344,8 +344,6 @@
             lefts, rights = rows_of(rounded), [ring(rounded, over, shift) for shift in range(rows)]
         else:
             lefts, rights = rows_of(rounded), spread(rounded, over)
-        if depth == 0:
-            right, lower = load(rounded, [right_side, lower_blocks])
 
 
 def solution(mesh):

time: 58.6 us -> 58.2 us (level)
  starting transfers between devices: 22.8 us -> 25.4 us
  waiting for transfers between devices: 20.9 us -> 19.4 us
  Pallas kernels: 13.4 us -> 12.2 us
    ppermute x14, starting transfers between devices: 18.5 us -> 21 us  [permute(): return lax.ppermute(value, ('leaf', 'rows', 'rhs'), pairs)]
    ppermute x14, waiting for transfers between devices: 16 us -> 14.4 us  [permute(): return lax.ppermute(value, ('leaf', 'rows', 'rhs'), pairs)]
    pallas_call x12 -> x11, Pallas kernels: 13.4 us -> 12.2 us  [call(): pl.pallas_call(kernel, in_specs=[WHOLE] * len(near) + [FAR] * len(far), o...]
  transfers between devices with their start and end apart: 19 -> 19, of which waited for: 9 -> 13; matrix products, arithmetic and copies ran while one was open for 2% -> 2% of each run, Pallas kernels for 13% -> 12%
where the time goes in v15:
time: 58.2 us; the launch traced here: 58 us
  starting transfers between devices  25.4 us (44%)
  waiting for transfers between devices  19.4 us (33%)
  Pallas kernels  12.2 us (21%)
  local copies, waits for them, and re-layouts  0.97 us (2%)
    ppermute x14, starting transfers between devices, permute(): return lax.ppermute(value, ('leaf', 'rows', 'rhs'), pairs)  21 us
    ppermute x14, waiting for transfers between devices, permute(): return lax.ppermute(value, ('leaf', 'rows', 'rhs'), pairs)  14.4 us
    pallas_call x11, Pallas kernels, call(): pl.pallas_call(kernel, in_specs=[WHOLE] * len(near) + [FAR] * len(far), o...  12.2 us
    ppermute x4, waiting for transfers between devices, send(): return lax.ppermute(value, places, pairs)  4.93 us
    ppermute x4, starting transfers between devices, send(): return lax.ppermute(value, places, pairs)  3.92 us
  transfers between devices with their start and end apart: 19, of which 13 were waited for; matrix products, arithmetic and copies ran while one was open for 2% of the time, Pallas kernels for 12%

profile of v15, /device:TPU:0, one launch (start us, length us, event | category | flops | bytes accessed | tf_op | source)
XLA Modules:
  0.0 58.0 jit_solution(10597484912898522304)
XLA Ops:
  0.0 0.5 collective-permute-start.1
  0.5 1.0 %fusion.after_ref.refs_0_ = bf16[64,1024]{1,0:T(8,128)(2,1)S(1)} fusion(f32[2,64,1024]{2,1,0:T(8,128)} %refs_1_.1), kind=kLoop, calls=%fused_computation.1 | loop fusion | bytes 262144 | tf_op jit(solution)/shard_map/convert_element_type | solution.py:277
  1.4 0.1 collective-permute-start
  1.5 4.8 %shard_map.46 = (bf16[2,2048,512]{2,1,0:T(8,128)(2,1)S(1)}, f32[2,64,1024]{2,1,0:T(8,128)S(1)}, bf16[2,16,128,1024]{3,2,1,0:T(8,128)(2,1)S(1)}) custom-call(bf16[64,1024]{1,0:T(8,128)(2,1)S(1)} %fusion.after_ref.refs_0_, bf16[2,2048,512]{2,1,0:T(8,128)(2,1)} %refs_0_.1, f32[2,64,1024]{2,1,0:T(8,128)} %refs_1_.1, bf16[2,16,128,1024]{3,2,1,0:T(8,128)(2,1)} %refs_2_.1), custom_call_target="tpu_custom_call" | custom-call | bytes 13238272 | tf_op jit(solution)/shard_map/pallas_call | solution.py:202
  6.4 1.0 %collective-permute-done.refs_1_ = bf16[64,1024]{1,0:T(8,128)(2,1)S(1)} collective-permute-done((bf16[64,1024]{1,0:T(8,128)(2,1)S(1)}, bf16[64,1024]{1,0:T(8,128)(2,1)S(1)}, u32[]{:S(2)}, u32[]{:S(2)}) %collective-permute-start) | collective-permute-done | bytes 131104 | tf_op jit(solution)/shard_map/ppermute | solution.py:236
  7.4 0.0 collective-permute-done.1.refs_3_.refs_1_
  7.5 0.8 %shard_map.47 = (bf16[64,1024]{1,0:T(8,128)(2,1)S(1)}, f32[64,1024]{1,0:T(8,128)S(1)}) custom-call(bf16[64,1024]{1,0:T(8,128)(2,1)S(1)} %fusion.after_ref.refs_0_, bf16[64,1024]{1,0:T(8,128)(2,1)S(1)} %collective-permute-done.refs_1_, bf16[2,2048,512]{2,1,0:T(8,128)(2,1)S(1)} %get-tuple-element.20.refs_2_.refs_0_, ...), custom_call_target="tpu_custom_call" | custom-call | flops 268435456 | bytes 8650752 | tf_op jit(solution)/shard_map/pallas_call | solution.py:202
  8.3 0.4 collective-permute-start.5
  8.7 0.1 collective-permute-start.4
  8.9 0.4 collective-permute-start.3
  9.3 0.1 collective-permute-start.2
  9.4 0.3 collective-permute-done.5.refs_3_
  9.7 0.4 collective-permute-done.4.refs_2_
  10.1 0.2 collective-permute-done.3.refs_1_
  10.3 0.3 collective-permute-done.2.refs_0_
  10.6 1.0 %shard_map.48 = (bf16[64,1024]{1,0:T(8,128)(2,1)S(1)}, bf16[64,1024]{1,0:T(8,128)(2,1)S(1)}) custom-call(s32[2,16]{1,0:T(2,128)S(1)} %copy-done, f32[2,64,1024]{2,1,0:T(8,128)S(1)} %get-tuple-element.18.right_ref, bf16[2,16,128,1024]{3,2,1,0:T(8,128)(2,1)S(1)} %get-tuple-element.19.lower_ref, bf16[64,1024]{1,0:T(8,128)(2,1)S(1)} %collective-permute-done.2.refs_0_, ...), custom_call_target="tpu_custom_call" | custom-call | flops 268435456 | bytes 9568384 | tf_op jit(solution)/shard_map/pallas_call | solution.py:202
  11.6 0.3 collective-permute-start.9
  11.8 0.3 collective-permute-start.7
  12.2 10.6 %collective-permute-start.6 = (bf16[64,1024]{1,0:T(8,128)(2,1)S(1)}, bf16[64,1024]{1,0:T(8,128)(2,1)S(1)}, u32[]{:S(2)}, u32[]{:S(2)}) collective-permute-start(bf16[64,1024]{1,0:T(8,128)(2,1)S(1)} %get-tuple-element.22.own_ref), channel_id=1, source_target_pairs={{0,4},{1,5},{2,6},{3,7},{4,0},{5,1},{6,2},{7,3},{8,9},{9,8},{10,11... | collective-permute-start | bytes 393224 | tf_op jit(solution)/shard_map/ppermute | solution.py:236
  22.8 0.0 collective-permute-done.9.refs_1_
  22.8 0.9 %shard_map.50 = (bf16[64,1024]{1,0:T(8,128)(2,1)S(1)}, f32[64,1024]{1,0:T(8,128)S(1)}) custom-call(bf16[64,1024]{1,0:T(8,128)(2,1)S(1)} %get-tuple-element.23.refs_0_, bf16[64,1024]{1,0:T(8,128)(2,1)S(1)} %collective-permute-done.9.refs_1_, bf16[2,2048,512]{2,1,0:T(8,128)(2,1)S(1)} %get-tuple-element.20.refs_2_.refs_0_, ...), custom_call_target="tpu_custom_call" | custom-call | flops 268435456 | bytes 9043968 | tf_op jit(solution)/shard_map/pallas_call | solution.py:202
  23.6 1.3 %collective-permute-start.13 = (bf16[64,1024]{1,0:T(8,128)(2,1)S(1)}, bf16[64,1024]{1,0:T(8,128)(2,1)S(1)}, u32[]{:S(2)}, u32[]{:S(2)}) collective-permute-start(bf16[64,1024]{1,0:T(8,128)(2,1)S(1)} %get-tuple-element.25.refs_6_.refs_5_), channel_id=1, source_target_pairs={{4,0},{6,2},{20,16},{22,18},{5,1},{7,3},{21,17},{23,19}} | collective-permute-start | bytes 393224 | tf_op jit(solution)/shard_map/ppermute | solution.py:222
  24.9 1.3 %collective-permute-start.12 = (bf16[64,1024]{1,0:T(8,128)(2,1)S(1)}, bf16[64,1024]{1,0:T(8,128)(2,1)S(1)}, u32[]{:S(2)}, u32[]{:S(2)}) collective-permute-start(bf16[64,1024]{1,0:T(8,128)(2,1)S(1)} %get-tuple-element.25.refs_6_.refs_5_), channel_id=1, source_target_pairs={{4,2},{6,0},{20,18},{22,16},{5,3},{7,1},{21,19},{23,17}} | collective-permute-start | bytes 393224 | tf_op jit(solution)/shard_map/ppermute | solution.py:222
  26.2 0.7 %collective-permute-start.11 = (bf16[64,1024]{1,0:T(8,128)(2,1)S(1)}, bf16[64,1024]{1,0:T(8,128)(2,1)S(1)}, u32[]{:S(2)}, u32[]{:S(2)}) collective-permute-start(bf16[64,1024]{1,0:T(8,128)(2,1)S(1)} %get-tuple-element.25.refs_6_.refs_5_), channel_id=1, source_target_pairs={{4,8},{6,10},{20,24},{22,26},{5,9},{7,11},{21,25},{23,27}} | collective-permute-start | bytes 393224 | tf_op jit(solution)/shard_map/ppermute | solution.py:222
  26.9 0.0 collective-permute-done.7.second_ref
  26.9 0.7 %collective-permute-start.10 = (bf16[64,1024]{1,0:T(8,128)(2,1)S(1)}, bf16[64,1024]{1,0:T(8,128)(2,1)S(1)}, u32[]{:S(2)}, u32[]{:S(2)}) collective-permute-start(bf16[64,1024]{1,0:T(8,128)(2,1)S(1)} %get-tuple-element.25.refs_6_.refs_5_), channel_id=1, source_target_pairs={{4,10},{6,8},{20,26},{22,24},{5,11},{7,9},{21,27},{23,25}} | collective-permute-start | bytes 393224 | tf_op jit(solution)/shard_map/ppermute | solution.py:222
  27.6 0.0 collective-permute-done.6.first_ref
  27.7 1.2 %collective-permute-start.8 = (bf16[64,1024]{1,0:T(8,128)(2,1)S(1)}, bf16[64,1024]{1,0:T(8,128)(2,1)S(1)}, u32[]{:S(2)}, u32[]{:S(2)}) collective-permute-start(bf16[64,1024]{1,0:T(8,128)(2,1)S(1)} %shard_map.49.refs_5_), channel_id=1, source_target_pairs={{0,2},{1,3},{2,0},{3,1},{4,6},{5,7},{6,4},{7,5},{8,10},{9,11},{10,... | collective-permute-start | bytes 393224 | tf_op jit(solution)/shard_map/ppermute | solution.py:236
  28.9 3.1 %collective-permute-done.13.refs_4_ = bf16[64,1024]{1,0:T(8,128)(2,1)S(1)} collective-permute-done((bf16[64,1024]{1,0:T(8,128)(2,1)S(1)}, bf16[64,1024]{1,0:T(8,128)(2,1)S(1)}, u32[]{:S(2)}, u32[]{:S(2)}) %collective-permute-start.13) | collective-permute-done | bytes 131104 | tf_op jit(solution)/shard_map/ppermute | solution.py:222
  32.0 1.8 %collective-permute-done.12.refs_3_ = bf16[64,1024]{1,0:T(8,128)(2,1)S(1)} collective-permute-done((bf16[64,1024]{1,0:T(8,128)(2,1)S(1)}, bf16[64,1024]{1,0:T(8,128)(2,1)S(1)}, u32[]{:S(2)}, u32[]{:S(2)}) %collective-permute-start.12) | collective-permute-done | bytes 131104 | tf_op jit(solution)/shard_map/ppermute | solution.py:222
  33.8 0.0 collective-permute-done.11.refs_2_
  33.8 0.9 %collective-permute-done.8.refs_0_.refs_6_ = bf16[64,1024]{1,0:T(8,128)(2,1)S(1)} collective-permute-done((bf16[64,1024]{1,0:T(8,128)(2,1)S(1)}, bf16[64,1024]{1,0:T(8,128)(2,1)S(1)}, u32[]{:S(2)}, u32[]{:S(2)}) %collective-permute-start.8) | collective-permute-done | bytes 131104 | tf_op jit(solution)/shard_map/ppermute | solution.py:236
  34.7 1.0 %shard_map.51 = (bf16[64,1024]{1,0:T(8,128)(2,1)S(1)}, bf16[64,4096]{1,0:T(8,128)(2,1)S(1)}) custom-call(s32[2,16]{1,0:T(2,128)S(1)} %copy-done, f32[2,64,1024]{2,1,0:T(8,128)S(1)} %get-tuple-element.18.right_ref, bf16[2,16,128,1024]{3,2,1,0:T(8,128)(2,1)S(1)} %get-tuple-element.19.lower_ref, bf16[64,1024]{1,0:T(8,128)(2,1)S(1)} %collective-permute-done.8.refs_0_.refs_6_, ...), custom_call_target="tpu_custom_call" | custom-call | flops 268435456 | bytes 9830528 | tf_op jit(solution)/shard_map/pallas_call | solution.py:202
  35.7 1.6 %collective-permute-start.14 = (bf16[64,1024]{1,0:T(8,128)(2,1)S(1)}, bf16[64,1024]{1,0:T(8,128)(2,1)S(1)}, u32[]{:S(2)}, u32[]{:S(2)}) collective-permute-start(bf16[64,1024]{1,0:T(8,128)(2,1)S(1)} %get-tuple-element.26.piece_ref.refs_0_), channel_id=1, source_target_pairs={{0,2},{1,3},{2,0},{3,1},{4,12},{5,13},{6,14},{7,15},{8,10},{9,11},... | collective-permute-start | bytes 393224 | tf_op jit(solution)/shard_map/ppermute | solution.py:236
  37.3 0.5 shard_map.52.refs_6_
  37.8 3.0 %collective-permute-done.14.refs_1_ = bf16[64,1024]{1,0:T(8,128)(2,1)S(1)} collective-permute-done((bf16[64,1024]{1,0:T(8,128)(2,1)S(1)}, bf16[64,1024]{1,0:T(8,128)(2,1)S(1)}, u32[]{:S(2)}, u32[]{:S(2)}) %collective-permute-start.14) | collective-permute-done | bytes 131104 | tf_op jit(solution)/shard_map/ppermute | solution.py:236
  40.7 0.5 shard_map.53
  41.2 1.7 %collective-permute-start.17 = (bf16[64,1024]{1,0:T(8,128)(2,1)S(1)}, bf16[64,1024]{1,0:T(8,128)(2,1)S(1)}, u32[]{:S(2)}, u32[]{:S(2)}) collective-permute-start(bf16[64,1024]{1,0:T(8,128)(2,1)S(1)} %get-tuple-element.28.refs_2_), channel_id=1, source_target_pairs={{0,2},{1,3},{2,0},{3,1},{4,6},{5,7},{6,4},{7,5},{8,10},{9,11},{10,... | collective-permute-start | bytes 393224 | tf_op jit(solution)/shard_map/ppermute | solution.py:236
  42.9 2.9 %collective-permute-start.16 = (bf16[64,1024]{1,0:T(8,128)(2,1)S(1)}, bf16[64,1024]{1,0:T(8,128)(2,1)S(1)}, u32[]{:S(2)}, u32[]{:S(2)}) collective-permute-start(bf16[64,1024]{1,0:T(8,128)(2,1)S(1)} %get-tuple-element.28.refs_2_), channel_id=1, source_target_pairs={{0,6},{1,7},{2,4},{3,5},{4,2},{5,3},{6,0},{7,1},{8,14},{9,15},{10,... | collective-permute-start | bytes 393224 | tf_op jit(solution)/shard_map/ppermute | solution.py:236
  45.8 0.0 collective-permute-start.15
  45.8 2.1 %collective-permute-done.17.refs_3_ = bf16[64,1024]{1,0:T(8,128)(2,1)S(1)} collective-permute-done((bf16[64,1024]{1,0:T(8,128)(2,1)S(1)}, bf16[64,1024]{1,0:T(8,128)(2,1)S(1)}, u32[]{:S(2)}, u32[]{:S(2)}) %collective-permute-start.17) | collective-permute-done | bytes 131104 | tf_op jit(solution)/shard_map/ppermute | solution.py:236
  47.9 1.2 %collective-permute-done.16.refs_1_ = bf16[64,1024]{1,0:T(8,128)(2,1)S(1)} collective-permute-done((bf16[64,1024]{1,0:T(8,128)(2,1)S(1)}, bf16[64,1024]{1,0:T(8,128)(2,1)S(1)}, u32[]{:S(2)}, u32[]{:S(2)}) %collective-permute-start.16) | collective-permute-done | bytes 131104 | tf_op jit(solution)/shard_map/ppermute | solution.py:236
  49.1 1.7 %collective-permute-done.15.refs_0_ = bf16[64,1024]{1,0:T(8,128)(2,1)S(1)} collective-permute-done((bf16[64,1024]{1,0:T(8,128)(2,1)S(1)}, bf16[64,1024]{1,0:T(8,128)(2,1)S(1)}, u32[]{:S(2)}, u32[]{:S(2)}) %collective-permute-start.15) | collective-permute-done | bytes 131104 | tf_op jit(solution)/shard_map/ppermute | solution.py:236
  50.8 1.0 %shard_map.54.piece_ref.refs_0_ = bf16[64,1024]{1,0:T(8,128)(2,1)S(1)} custom-call(s32[2,16]{1,0:T(2,128)S(1)} %copy-done, f32[2,64,1024]{2,1,0:T(8,128)S(1)} %get-tuple-element.18.right_ref, bf16[2,16,128,1024]{3,2,1,0:T(8,128)(2,1)S(1)} %get-tuple-element.19.lower_ref, bf16[64,1024]{1,0:T(8,128)(2,1)S(1)} %collective-permute-done.15.refs_0_, ...), custom_call_target="tpu_custom_call" | custom-call | flops 268435456 | bytes 10223744 | tf_op jit(solution)/shard_map/pallas_call | solution.py:202
  51.8 1.2 %collective-permute-start.18 = (bf16[64,1024]{1,0:T(8,128)(2,1)S(1)}, bf16[64,1024]{1,0:T(8,128)(2,1)S(1)}, u32[]{:S(2)}, u32[]{:S(2)}) collective-permute-start(bf16[64,1024]{1,0:T(8,128)(2,1)S(1)} %shard_map.54.piece_ref.refs_0_), channel_id=1, source_target_pairs={{0,2},{1,3},{2,0},{3,1},{4,6},{5,7},{6,4},{7,5},{8,10},{9,11},{10,... | collective-permute-start | bytes 393224 | tf_op jit(solution)/shard_map/ppermute | solution.py:236
  53.0 0.5 shard_map.55.refs_5_
  53.5 3.3 %collective-permute-done.18.refs_1_ = bf16[64,1024]{1,0:T(8,128)(2,1)S(1)} collective-permute-done((bf16[64,1024]{1,0:T(8,128)(2,1)S(1)}, bf16[64,1024]{1,0:T(8,128)(2,1)S(1)}, u32[]{:S(2)}, u32[]{:S(2)}) %collective-permute-start.18) | collective-permute-done | bytes 131104 | tf_op jit(solution)/shard_map/ppermute | solution.py:236
  56.9 1.2 %shard_map.56 = f32[2,64,1024]{2,1,0:T(8,128)} custom-call(bf16[64,1024]{1,0:T(8,128)(2,1)S(1)} %shard_map.54.piece_ref.refs_0_, bf16[64,1024]{1,0:T(8,128)(2,1)S(1)} %collective-permute-done.18.refs_1_, bf16[2,2048,512]{2,1,0:T(8,128)(2,1)S(1)} %get-tuple-element.20.refs_2_.refs_0_, bf16[2,2048,512]{2,1,0:T(8,128)(2,1)S(1)} %collective-permute-done.1.refs_3_.refs_1_, ...), custom_call_target="tpu_custom_call" | custom-call | flops 268435456 | bytes 9175040 | tf_op jit(solution)/shard_map/pallas_call | solution.py:202
  (4 shorter events, 0.0 us)
Async XLA Ops:
  0.0 7.4 %collective-permute-start.1 = (bf16[2,2048,512]{2,1,0:T(8,128)(2,1)}, bf16[2,2048,512]{2,1,0:T(8,128)(2,1)S(1)}, u32[]{:S(2)}, u32[]{:S(2)}) collective-permute-start(bf16[2,2048,512]{2,1,0:T(8,128)(2,1)} %refs_0_.1), channel_id=1, source_target_pairs={{0,1},{1,0},{2,3},{3,2},{4,5},{5,4},{6,7},{7,6},{8,9},{9,8},{10,11... | collective-permute-start | bytes 12582920 | tf_op jit(solution)/shard_map/ppermute | solution.py:255
  1.4 6.0 %collective-permute-start = (bf16[64,1024]{1,0:T(8,128)(2,1)S(1)}, bf16[64,1024]{1,0:T(8,128)(2,1)S(1)}, u32[]{:S(2)}, u32[]{:S(2)}) collective-permute-start(bf16[64,1024]{1,0:T(8,128)(2,1)S(1)} %fusion.after_ref.refs_0_), channel_id=1, source_target_pairs={{0,1},{1,0},{2,3},{3,2},{4,5},{5,4},{6,7},{7,6},{8,9},{9,8},{10,11... | collective-permute-start | bytes 393224 | tf_op jit(solution)/shard_map/ppermute | solution.py:236
  7.5 3.2 %copy-start = (s32[2,16]{1,0:T(2,128)S(1)}, s32[2,16]{1,0:T(2,128)}, u32[]{:S(2)}) copy-start(s32[2,16]{1,0:T(2,128)} %block_rows_ref.5) | copy-start | bytes 388
  8.3 1.4 %collective-permute-start.5 = (bf16[64,1024]{1,0:T(8,128)(2,1)S(1)}, bf16[64,1024]{1,0:T(8,128)(2,1)S(1)}, u32[]{:S(2)}, u32[]{:S(2)}) collective-permute-start(bf16[64,1024]{1,0:T(8,128)(2,1)S(1)} %get-tuple-element.21.refs_4_.refs_5_), channel_id=1, source_target_pairs={{0,1},{1,0},{2,3},{3,2},{4,8},{5,9},{6,10},{7,11},{8,12},{9,13},{1... | collective-permute-start | bytes 393224 | tf_op jit(solution)/shard_map/ppermute | solution.py:236
  8.7 1.3 %collective-permute-start.4 = (bf16[64,1024]{1,0:T(8,128)(2,1)S(1)}, bf16[64,1024]{1,0:T(8,128)(2,1)S(1)}, u32[]{:S(2)}, u32[]{:S(2)}) collective-permute-start(bf16[64,1024]{1,0:T(8,128)(2,1)S(1)} %get-tuple-element.21.refs_4_.refs_5_), channel_id=1, source_target_pairs={{0,1},{1,0},{2,3},{3,2},{4,14},{5,15},{6,12},{7,13},{8,9},{9,8},{1... | collective-permute-start | bytes 393224 | tf_op jit(solution)/shard_map/ppermute | solution.py:236
  8.9 1.4 %collective-permute-start.3 = (bf16[64,1024]{1,0:T(8,128)(2,1)S(1)}, bf16[64,1024]{1,0:T(8,128)(2,1)S(1)}, u32[]{:S(2)}, u32[]{:S(2)}) collective-permute-start(bf16[64,1024]{1,0:T(8,128)(2,1)S(1)} %get-tuple-element.21.refs_4_.refs_5_), channel_id=1, source_target_pairs={{0,1},{1,0},{2,3},{3,2},{4,5},{5,4},{6,7},{7,6},{8,9},{9,8},{10,11... | collective-permute-start | bytes 393224 | tf_op jit(solution)/shard_map/ppermute | solution.py:236
  9.3 1.3 %collective-permute-start.2 = (bf16[64,1024]{1,0:T(8,128)(2,1)S(1)}, bf16[64,1024]{1,0:T(8,128)(2,1)S(1)}, u32[]{:S(2)}, u32[]{:S(2)}) collective-permute-start(bf16[64,1024]{1,0:T(8,128)(2,1)S(1)} %get-tuple-element.21.refs_4_.refs_5_), channel_id=1, source_target_pairs={{0,1},{1,0},{2,3},{3,2},{4,5},{5,4},{6,7},{7,6},{8,9},{9,8},{10,11... | collective-permute-start | bytes 393224 | tf_op jit(solution)/shard_map/ppermute | solution.py:236
  11.6 11.2 %collective-permute-start.9 = (bf16[64,1024]{1,0:T(8,128)(2,1)S(1)}, bf16[64,1024]{1,0:T(8,128)(2,1)S(1)}, u32[]{:S(2)}, u32[]{:S(2)}) collective-permute-start(bf16[64,1024]{1,0:T(8,128)(2,1)S(1)} %get-tuple-element.23.refs_0_), channel_id=1, source_target_pairs={{0,1},{1,0},{2,3},{3,2},{4,6},{5,7},{6,4},{7,5},{8,9},{9,8},{10,11... | collective-permute-start | bytes 393224 | tf_op jit(solution)/shard_map/ppermute | solution.py:236
  11.8 15.1 %collective-permute-start.7 = (bf16[64,1024]{1,0:T(8,128)(2,1)S(1)}, bf16[64,1024]{1,0:T(8,128)(2,1)S(1)}, u32[]{:S(2)}, u32[]{:S(2)}) collective-permute-start(bf16[64,1024]{1,0:T(8,128)(2,1)S(1)} %get-tuple-element.22.own_ref), channel_id=1, source_target_pairs={{0,1},{1,0},{2,3},{3,2},{4,8},{5,9},{6,10},{7,11},{8,4},{9,5},{10,... | collective-permute-start | bytes 393224 | tf_op jit(solution)/shard_map/ppermute | solution.py:236
  12.2 15.4 %collective-permute-start.6 = (bf16[64,1024]{1,0:T(8,128)(2,1)S(1)}, bf16[64,1024]{1,0:T(8,128)(2,1)S(1)}, u32[]{:S(2)}, u32[]{:S(2)}) collective-permute-start(bf16[64,1024]{1,0:T(8,128)(2,1)S(1)} %get-tuple-element.22.own_ref), channel_id=1, source_target_pairs={{0,4},{1,5},{2,6},{3,7},{4,0},{5,1},{6,2},{7,3},{8,9},{9,8},{10,11... | collective-permute-start | bytes 393224 | tf_op jit(solution)/shard_map/ppermute | solution.py:236
  23.6 8.3 %collective-permute-start.13 = (bf16[64,1024]{1,0:T(8,128)(2,1)S(1)}, bf16[64,1024]{1,0:T(8,128)(2,1)S(1)}, u32[]{:S(2)}, u32[]{:S(2)}) collective-permute-start(bf16[64,1024]{1,0:T(8,128)(2,1)S(1)} %get-tuple-element.25.refs_6_.refs_5_), channel_id=1, source_target_pairs={{4,0},{6,2},{20,16},{22,18},{5,1},{7,3},{21,17},{23,19}} | collective-permute-start | bytes 393224 | tf_op jit(solution)/shard_map/ppermute | solution.py:222
  24.9 8.8 %collective-permute-start.12 = (bf16[64,1024]{1,0:T(8,128)(2,1)S(1)}, bf16[64,1024]{1,0:T(8,128)(2,1)S(1)}, u32[]{:S(2)}, u32[]{:S(2)}) collective-permute-start(bf16[64,1024]{1,0:T(8,128)(2,1)S(1)} %get-tuple-element.25.refs_6_.refs_5_), channel_id=1, source_target_pairs={{4,2},{6,0},{20,18},{22,16},{5,3},{7,1},{21,19},{23,17}} | collective-permute-start | bytes 393224 | tf_op jit(solution)/shard_map/ppermute | solution.py:222
  26.2 7.5 %collective-permute-start.11 = (bf16[64,1024]{1,0:T(8,128)(2,1)S(1)}, bf16[64,1024]{1,0:T(8,128)(2,1)S(1)}, u32[]{:S(2)}, u32[]{:S(2)}) collective-permute-start(bf16[64,1024]{1,0:T(8,128)(2,1)S(1)} %get-tuple-element.25.refs_6_.refs_5_), channel_id=1, source_target_pairs={{4,8},{6,10},{20,24},{22,26},{5,9},{7,11},{21,25},{23,27}} | collective-permute-start | bytes 393224 | tf_op jit(solution)/shard_map/ppermute | solution.py:222
  26.9 6.9 %collective-permute-start.10 = (bf16[64,1024]{1,0:T(8,128)(2,1)S(1)}, bf16[64,1024]{1,0:T(8,128)(2,1)S(1)}, u32[]{:S(2)}, u32[]{:S(2)}) collective-permute-start(bf16[64,1024]{1,0:T(8,128)(2,1)S(1)} %get-tuple-element.25.refs_6_.refs_5_), channel_id=1, source_target_pairs={{4,10},{6,8},{20,26},{22,24},{5,11},{7,9},{21,27},{23,25}} | collective-permute-start | bytes 393224 | tf_op jit(solution)/shard_map/ppermute | solution.py:222
  27.7 7.1 %collective-permute-start.8 = (bf16[64,1024]{1,0:T(8,128)(2,1)S(1)}, bf16[64,1024]{1,0:T(8,128)(2,1)S(1)}, u32[]{:S(2)}, u32[]{:S(2)}) collective-permute-start(bf16[64,1024]{1,0:T(8,128)(2,1)S(1)} %shard_map.49.refs_5_), channel_id=1, source_target_pairs={{0,2},{1,3},{2,0},{3,1},{4,6},{5,7},{6,4},{7,5},{8,10},{9,11},{10,... | collective-permute-start | bytes 393224 | tf_op jit(solution)/shard_map/ppermute | solution.py:236
  35.7 5.0 %collective-permute-start.14 = (bf16[64,1024]{1,0:T(8,128)(2,1)S(1)}, bf16[64,1024]{1,0:T(8,128)(2,1)S(1)}, u32[]{:S(2)}, u32[]{:S(2)}) collective-permute-start(bf16[64,1024]{1,0:T(8,128)(2,1)S(1)} %get-tuple-element.26.piece_ref.refs_0_), channel_id=1, source_target_pairs={{0,2},{1,3},{2,0},{3,1},{4,12},{5,13},{6,14},{7,15},{8,10},{9,11},... | collective-permute-start | bytes 393224 | tf_op jit(solution)/shard_map/ppermute | solution.py:236
  41.2 6.7 %collective-permute-start.17 = (bf16[64,1024]{1,0:T(8,128)(2,1)S(1)}, bf16[64,1024]{1,0:T(8,128)(2,1)S(1)}, u32[]{:S(2)}, u32[]{:S(2)}) collective-permute-start(bf16[64,1024]{1,0:T(8,128)(2,1)S(1)} %get-tuple-element.28.refs_2_), channel_id=1, source_target_pairs={{0,2},{1,3},{2,0},{3,1},{4,6},{5,7},{6,4},{7,5},{8,10},{9,11},{10,... | collective-permute-start | bytes 393224 | tf_op jit(solution)/shard_map/ppermute | solution.py:236
  42.9 6.2 %collective-permute-start.16 = (bf16[64,1024]{1,0:T(8,128)(2,1)S(1)}, bf16[64,1024]{1,0:T(8,128)(2,1)S(1)}, u32[]{:S(2)}, u32[]{:S(2)}) collective-permute-start(bf16[64,1024]{1,0:T(8,128)(2,1)S(1)} %get-tuple-element.28.refs_2_), channel_id=1, source_target_pairs={{0,6},{1,7},{2,4},{3,5},{4,2},{5,3},{6,0},{7,1},{8,14},{9,15},{10,... | collective-permute-start | bytes 393224 | tf_op jit(solution)/shard_map/ppermute | solution.py:236
  45.8 5.0 %collective-permute-start.15 = (bf16[64,1024]{1,0:T(8,128)(2,1)S(1)}, bf16[64,1024]{1,0:T(8,128)(2,1)S(1)}, u32[]{:S(2)}, u32[]{:S(2)}) collective-permute-start(bf16[64,1024]{1,0:T(8,128)(2,1)S(1)} %get-tuple-element.28.refs_2_), channel_id=1, source_target_pairs={{0,4},{1,5},{2,6},{3,7},{4,0},{5,1},{6,2},{7,3},{8,12},{9,13},{10,... | collective-permute-start | bytes 393224 | tf_op jit(solution)/shard_map/ppermute | solution.py:236
  51.8 5.0 %collective-permute-start.18 = (bf16[64,1024]{1,0:T(8,128)(2,1)S(1)}, bf16[64,1024]{1,0:T(8,128)(2,1)S(1)}, u32[]{:S(2)}, u32[]{:S(2)}) collective-permute-start(bf16[64,1024]{1,0:T(8,128)(2,1)S(1)} %shard_map.54.piece_ref.refs_0_), channel_id=1, source_target_pairs={{0,2},{1,3},{2,0},{3,1},{4,6},{5,7},{6,4},{7,5},{8,10},{9,11},{10,... | collective-permute-start | bytes 393224 | tf_op jit(solution)/shard_map/ppermute | solution.py:236

commit v16 on v15

--- a/solution.py
+++ b/solution.py
@@ -91,27 +91,37 @@
         place_pieces([extra[0], late_ref], joined, 0)
     blocks, block_width = lower_ref.shape[1:3]
     highest = joined.shape[1] // block_width - 1
-    numbers = block_rows_ref[...]
-    for index in range(blocks):
-        number = jnp.clip(numbers[slot, index], 0, highest)
-        column = pl.multiple_of(number * block_width, block_width)
-        picked[:, index * block_width:(index + 1) * block_width] = joined[:, pl.ds(column, block_width)]
-    weights = lower_ref[slot].reshape(blocks * block_width, width)
-    offset = jnp.dot(picked[...], weights, preferred_element_type=F32)
-    reduced_ref[...] = (right_ref[slot] - offset).astype(BF16)
-    if plan == "crossed":
-        @pl.when(leaf % 2 == 1)
-        def _():
-            reduced_ref[...] = extra[1][...]
-
-
-def begin_kernel(slot, rows, cores, piece_ref, *refs):
+
+    def product():
+        numbers = block_rows_ref[...]
+        for index in range(blocks):
+            number = jnp.clip(numbers[slot, index], 0, highest)
+            column = pl.multiple_of(number * block_width, block_width)
+            picked[:, index * block_width:(index + 1) * block_width] = joined[:, pl.ds(column, block_width)]
+        weights = lower_ref[slot].reshape(blocks * block_width, width)
+        offset = jnp.dot(picked[...], weights, preferred_element_type=F32)
+        reduced_ref[...] = (right_ref[slot] - offset).astype(BF16)
+
+    if level == top:
+        product()
+        return
+    active = upper_depth(leaf, top) == level
+    pl.when(active)(product)
+
+    @pl.when(jnp.logical_not(active))
+    def _():
+        reduced_ref[...] = extra[1][...] if plan == "crossed" else jnp.zeros_like(reduced_ref)
+
+
+def begin_kernel(top, depth, rows, cores, piece_ref, *refs):
     inverse_refs, part_ref = refs[:cores], refs[cores]
     width = piece_ref.shape[1]
     quarter = inverse_refs[0].shape[-1]
+    slot = 0 if depth == top else 1
     own = lax.axis_index("rows")
+    active = (upper_depth(lax.axis_index("leaf"), top) == depth) | (depth == top)
     for which in range(rows):
-        @pl.when(own == which)
+        @pl.when((own == which) & active)
         def _():
             for turn, inverse_ref in enumerate(inverse_refs):
                 weights = inverse_ref[slot, which * width:(which + 1) * width, :]
@@ -156,10 +166,17 @@
 
     def store(turn, columns, total):
         rounded_ref[:, columns] = total.astype(BF16)
-        before = before_ref[:, columns] if depth > 0 else jnp.zeros_like(total)
-        solved_ref[:, columns] = jnp.where(active, total, before)
-
-    apply_inverse(1, cores, piece_refs, inverse_refs, part_ref, joined, store)
+        solved_ref[:, columns] = total
+
+    @pl.when(active)
+    def _():
+        apply_inverse(1, cores, piece_refs, inverse_refs, part_ref, joined, store)
+
+    @pl.when(jnp.logical_not(active))
+    def _():
+        rounded_ref[...] = jnp.zeros_like(rounded_ref)
+        solved_ref[...] = before_ref[...] if depth > 0 else jnp.zeros_like(solved_ref)
+
     if plan == "crossed":
         for wanted, ref in ((leaf % 4 == 1, held_ref), (leaf % 4 == 3, piece_refs[1])):
             @pl.when(wanted)
@@ -310,7 +327,7 @@
         split = crossing and depth > 1
         part = []
         if split:
-            kernel = functools.partial(begin_kernel, 0 if depth == top else 1, rows, cores)
+            kernel = functools.partial(begin_kernel, top, depth, rows, cores)
             part = [call(kernel, [reduced, *inverses], [], [half_f32], (), work // rows)]
         if depth == top:
             staged = [near((count, width), F32), semaphores(cores + 1)]

time: 58.2 us -> 57.4 us (0.986); the launches traced: 58 us -> 56.6 us
  Pallas kernels: 12.2 us -> 9.59 us
  waiting for transfers between devices: 19.4 us -> 20.3 us
    pallas_call x11, Pallas kernels: 12.2 us -> 9.59 us  [call(): pl.pallas_call(kernel, in_specs=[WHOLE] * len(near) + [FAR] * len(far), o...]
    ppermute x4, waiting for transfers between devices: 4.93 us -> 5.62 us  [send(): return lax.ppermute(value, places, pairs)]
  transfers between devices with their start and end apart: 19 -> 19, of which waited for: 13 -> 14; matrix products, arithmetic and copies ran while one was open for 2% -> 2% of each run, Pallas kernels for 12% -> 10%
where the time goes in v16:
time: 57.4 us; the launch traced here: 56.6 us
  starting transfers between devices  25.6 us (45%)
  waiting for transfers between devices  20.3 us (35%)
  Pallas kernels  9.59 us (17%)
  local copies, waits for them, and re-layouts  0.97 us (2%)
    ppermute x14, starting transfers between devices, permute(): return lax.ppermute(value, ('leaf', 'rows', 'rhs'), pairs)  21.2 us
    ppermute x14, waiting for transfers between devices, permute(): return lax.ppermute(value, ('leaf', 'rows', 'rhs'), pairs)  14.7 us
    pallas_call x11, Pallas kernels, call(): pl.pallas_call(kernel, in_specs=[WHOLE] * len(near) + [FAR] * len(far), o...  9.59 us
    ppermute x4, waiting for transfers between devices, send(): return lax.ppermute(value, places, pairs)  5.62 us
    ppermute x4, starting transfers between devices, send(): return lax.ppermute(value, places, pairs)  3.92 us
  transfers between devices with their start and end apart: 19, of which 14 were waited for; matrix products, arithmetic and copies ran while one was open for 2% of the time, Pallas kernels for 10%

profile of v16, /device:TPU:0, one launch (start us, length us, event | category | flops | bytes accessed | tf_op | source)
XLA Modules:
  0.0 56.6 jit_solution(14390523703933892099)
XLA Ops:
  0.0 0.5 collective-permute-start.1
  0.5 1.0 %fusion.after_ref.refs_0_ = bf16[64,1024]{1,0:T(8,128)(2,1)S(1)} fusion(f32[2,64,1024]{2,1,0:T(8,128)} %refs_1_.1), kind=kLoop, calls=%fused_computation.1 | loop fusion | bytes 262144 | tf_op jit(solution)/shard_map/convert_element_type | solution.py:294
  1.4 0.1 collective-permute-start
  1.5 4.8 %shard_map.46 = (bf16[2,2048,512]{2,1,0:T(8,128)(2,1)S(1)}, f32[2,64,1024]{2,1,0:T(8,128)S(1)}, bf16[2,16,128,1024]{3,2,1,0:T(8,128)(2,1)S(1)}) custom-call(bf16[64,1024]{1,0:T(8,128)(2,1)S(1)} %fusion.after_ref.refs_0_, bf16[2,2048,512]{2,1,0:T(8,128)(2,1)} %refs_0_.1, f32[2,64,1024]{2,1,0:T(8,128)} %refs_1_.1, bf16[2,16,128,1024]{3,2,1,0:T(8,128)(2,1)} %refs_2_.1), custom_call_target="tpu_custom_call" | custom-call | bytes 13238272 | tf_op jit(solution)/shard_map/pallas_call | solution.py:219
  6.4 1.0 %collective-permute-done.refs_1_ = bf16[64,1024]{1,0:T(8,128)(2,1)S(1)} collective-permute-done((bf16[64,1024]{1,0:T(8,128)(2,1)S(1)}, bf16[64,1024]{1,0:T(8,128)(2,1)S(1)}, u32[]{:S(2)}, u32[]{:S(2)}) %collective-permute-start) | collective-permute-done | bytes 131104 | tf_op jit(solution)/shard_map/ppermute | solution.py:253
  7.4 0.0 collective-permute-done.1.refs_3_.refs_1_
  7.5 0.4 collective-permute-start.5
  7.9 0.1 collective-permute-start.4
  8.1 0.4 collective-permute-start.3
  8.4 0.1 collective-permute-start.2
  8.6 0.3 collective-permute-done.5.refs_3_
  8.9 0.4 collective-permute-done.4.refs_2_
  9.3 0.2 collective-permute-done.3.refs_1_
  9.5 0.3 collective-permute-done.2.refs_0_
  9.8 0.0 copy-done
  9.8 0.1 shard_map.48
  9.9 0.3 collective-permute-start.9
  10.1 0.3 collective-permute-start.7
  10.4 11.7 %collective-permute-start.6 = (bf16[64,1024]{1,0:T(8,128)(2,1)S(1)}, bf16[64,1024]{1,0:T(8,128)(2,1)S(1)}, u32[]{:S(2)}, u32[]{:S(2)}) collective-permute-start(bf16[64,1024]{1,0:T(8,128)(2,1)S(1)} %get-tuple-element.22.own_ref), channel_id=1, source_target_pairs={{0,4},{1,5},{2,6},{3,7},{4,0},{5,1},{6,2},{7,3},{8,9},{9,8},{10,11... | collective-permute-start | bytes 393224 | tf_op jit(solution)/shard_map/ppermute | solution.py:253
  22.2 0.0 collective-permute-done.9.refs_1_
  22.2 1.3 %collective-permute-start.13 = (bf16[64,1024]{1,0:T(8,128)(2,1)S(1)}, bf16[64,1024]{1,0:T(8,128)(2,1)S(1)}, u32[]{:S(2)}, u32[]{:S(2)}) collective-permute-start(bf16[64,1024]{1,0:T(8,128)(2,1)S(1)} %get-tuple-element.25.refs_6_.refs_5_), channel_id=1, source_target_pairs={{4,0},{6,2},{20,16},{22,18},{5,1},{7,3},{21,17},{23,19}} | collective-permute-start | bytes 393224 | tf_op jit(solution)/shard_map/ppermute | solution.py:239
  23.5 1.3 %collective-permute-start.12 = (bf16[64,1024]{1,0:T(8,128)(2,1)S(1)}, bf16[64,1024]{1,0:T(8,128)(2,1)S(1)}, u32[]{:S(2)}, u32[]{:S(2)}) collective-permute-start(bf16[64,1024]{1,0:T(8,128)(2,1)S(1)} %get-tuple-element.25.refs_6_.refs_5_), channel_id=1, source_target_pairs={{4,2},{6,0},{20,18},{22,16},{5,3},{7,1},{21,19},{23,17}} | collective-permute-start | bytes 393224 | tf_op jit(solution)/shard_map/ppermute | solution.py:239
  24.8 0.7 %collective-permute-start.11 = (bf16[64,1024]{1,0:T(8,128)(2,1)S(1)}, bf16[64,1024]{1,0:T(8,128)(2,1)S(1)}, u32[]{:S(2)}, u32[]{:S(2)}) collective-permute-start(bf16[64,1024]{1,0:T(8,128)(2,1)S(1)} %get-tuple-element.25.refs_6_.refs_5_), channel_id=1, source_target_pairs={{4,8},{6,10},{20,24},{22,26},{5,9},{7,11},{21,25},{23,27}} | collective-permute-start | bytes 393224 | tf_op jit(solution)/shard_map/ppermute | solution.py:239
  25.5 0.0 collective-permute-done.7.second_ref
  25.5 0.7 %collective-permute-start.10 = (bf16[64,1024]{1,0:T(8,128)(2,1)S(1)}, bf16[64,1024]{1,0:T(8,128)(2,1)S(1)}, u32[]{:S(2)}, u32[]{:S(2)}) collective-permute-start(bf16[64,1024]{1,0:T(8,128)(2,1)S(1)} %get-tuple-element.25.refs_6_.refs_5_), channel_id=1, source_target_pairs={{4,10},{6,8},{20,26},{22,24},{5,11},{7,9},{21,27},{23,25}} | collective-permute-start | bytes 393224 | tf_op jit(solution)/shard_map/ppermute | solution.py:239
  26.2 1.2 %collective-permute-done.6.first_ref = bf16[64,1024]{1,0:T(8,128)(2,1)S(1)} collective-permute-done((bf16[64,1024]{1,0:T(8,128)(2,1)S(1)}, bf16[64,1024]{1,0:T(8,128)(2,1)S(1)}, u32[]{:S(2)}, u32[]{:S(2)}) %collective-permute-start.6) | collective-permute-done | bytes 131104 | tf_op jit(solution)/shard_map/ppermute | solution.py:253
  27.4 1.3 %collective-permute-start.8 = (bf16[64,1024]{1,0:T(8,128)(2,1)S(1)}, bf16[64,1024]{1,0:T(8,128)(2,1)S(1)}, u32[]{:S(2)}, u32[]{:S(2)}) collective-permute-start(bf16[64,1024]{1,0:T(8,128)(2,1)S(1)} %shard_map.49.refs_5_), channel_id=1, source_target_pairs={{0,2},{1,3},{2,0},{3,1},{4,6},{5,7},{6,4},{7,5},{8,10},{9,11},{10,... | collective-permute-start | bytes 393224 | tf_op jit(solution)/shard_map/ppermute | solution.py:253
  28.7 3.8 %collective-permute-done.13.refs_4_ = bf16[64,1024]{1,0:T(8,128)(2,1)S(1)} collective-permute-done((bf16[64,1024]{1,0:T(8,128)(2,1)S(1)}, bf16[64,1024]{1,0:T(8,128)(2,1)S(1)}, u32[]{:S(2)}, u32[]{:S(2)}) %collective-permute-start.13) | collective-permute-done | bytes 131104 | tf_op jit(solution)/shard_map/ppermute | solution.py:239
  32.4 1.9 %collective-permute-done.12.refs_3_ = bf16[64,1024]{1,0:T(8,128)(2,1)S(1)} collective-permute-done((bf16[64,1024]{1,0:T(8,128)(2,1)S(1)}, bf16[64,1024]{1,0:T(8,128)(2,1)S(1)}, u32[]{:S(2)}, u32[]{:S(2)}) %collective-permute-start.12) | collective-permute-done | bytes 131104 | tf_op jit(solution)/shard_map/ppermute | solution.py:239
  34.3 0.0 collective-permute-done.11.refs_2_
  34.3 0.0 collective-permute-done.10.refs_1_
  34.3 0.3 collective-permute-done.8.refs_0_.refs_6_
  34.6 1.0 %shard_map.51 = (bf16[64,1024]{1,0:T(8,128)(2,1)S(1)}, bf16[64,4096]{1,0:T(8,128)(2,1)S(1)}) custom-call(s32[2,16]{1,0:T(2,128)S(1)} %copy-done, f32[2,64,1024]{2,1,0:T(8,128)S(1)} %get-tuple-element.18.right_ref, bf16[2,16,128,1024]{3,2,1,0:T(8,128)(2,1)S(1)} %get-tuple-element.19.lower_ref, bf16[64,1024]{1,0:T(8,128)(2,1)S(1)} %collective-permute-done.8.refs_0_.refs_6_, ...), custom_call_target="tpu_custom_call" | custom-call | flops 268435456 | bytes 9830528 | tf_op jit(solution)/shard_map/pallas_call | solution.py:219
  35.6 1.3 %collective-permute-start.14 = (bf16[64,1024]{1,0:T(8,128)(2,1)S(1)}, bf16[64,1024]{1,0:T(8,128)(2,1)S(1)}, u32[]{:S(2)}, u32[]{:S(2)}) collective-permute-start(bf16[64,1024]{1,0:T(8,128)(2,1)S(1)} %get-tuple-element.26.piece_ref.refs_0_), channel_id=1, source_target_pairs={{0,2},{1,3},{2,0},{3,1},{4,12},{5,13},{6,14},{7,15},{8,10},{9,11},... | collective-permute-start | bytes 393224 | tf_op jit(solution)/shard_map/ppermute | solution.py:253
  36.9 0.5 shard_map.52.refs_6_
  37.3 3.7 %collective-permute-done.14.refs_1_ = bf16[64,1024]{1,0:T(8,128)(2,1)S(1)} collective-permute-done((bf16[64,1024]{1,0:T(8,128)(2,1)S(1)}, bf16[64,1024]{1,0:T(8,128)(2,1)S(1)}, u32[]{:S(2)}, u32[]{:S(2)}) %collective-permute-start.14) | collective-permute-done | bytes 131104 | tf_op jit(solution)/shard_map/ppermute | solution.py:253
  41.0 0.5 shard_map.53
  41.5 1.6 %collective-permute-start.17 = (bf16[64,1024]{1,0:T(8,128)(2,1)S(1)}, bf16[64,1024]{1,0:T(8,128)(2,1)S(1)}, u32[]{:S(2)}, u32[]{:S(2)}) collective-permute-start(bf16[64,1024]{1,0:T(8,128)(2,1)S(1)} %get-tuple-element.28.refs_2_), channel_id=1, source_target_pairs={{0,2},{1,3},{2,0},{3,1},{4,6},{5,7},{6,4},{7,5},{8,10},{9,11},{10,... | collective-permute-start | bytes 393224 | tf_op jit(solution)/shard_map/ppermute | solution.py:253
  43.1 1.3 %collective-permute-start.16 = (bf16[64,1024]{1,0:T(8,128)(2,1)S(1)}, bf16[64,1024]{1,0:T(8,128)(2,1)S(1)}, u32[]{:S(2)}, u32[]{:S(2)}) collective-permute-start(bf16[64,1024]{1,0:T(8,128)(2,1)S(1)} %get-tuple-element.28.refs_2_), channel_id=1, source_target_pairs={{0,6},{1,7},{2,4},{3,5},{4,2},{5,3},{6,0},{7,1},{8,14},{9,15},{10,... | collective-permute-start | bytes 393224 | tf_op jit(solution)/shard_map/ppermute | solution.py:253
  44.4 0.7 %collective-permute-start.15 = (bf16[64,1024]{1,0:T(8,128)(2,1)S(1)}, bf16[64,1024]{1,0:T(8,128)(2,1)S(1)}, u32[]{:S(2)}, u32[]{:S(2)}) collective-permute-start(bf16[64,1024]{1,0:T(8,128)(2,1)S(1)} %get-tuple-element.28.refs_2_), channel_id=1, source_target_pairs={{0,4},{1,5},{2,6},{3,7},{4,0},{5,1},{6,2},{7,3},{8,12},{9,13},{10,... | collective-permute-start | bytes 393224 | tf_op jit(solution)/shard_map/ppermute | solution.py:253
  45.1 1.5 %collective-permute-done.17.refs_3_ = bf16[64,1024]{1,0:T(8,128)(2,1)S(1)} collective-permute-done((bf16[64,1024]{1,0:T(8,128)(2,1)S(1)}, bf16[64,1024]{1,0:T(8,128)(2,1)S(1)}, u32[]{:S(2)}, u32[]{:S(2)}) %collective-permute-start.17) | collective-permute-done | bytes 131104 | tf_op jit(solution)/shard_map/ppermute | solution.py:253
  46.5 2.5 %collective-permute-done.16.refs_1_ = bf16[64,1024]{1,0:T(8,128)(2,1)S(1)} collective-permute-done((bf16[64,1024]{1,0:T(8,128)(2,1)S(1)}, bf16[64,1024]{1,0:T(8,128)(2,1)S(1)}, u32[]{:S(2)}, u32[]{:S(2)}) %collective-permute-start.16) | collective-permute-done | bytes 131104 | tf_op jit(solution)/shard_map/ppermute | solution.py:253
  49.0 0.4 collective-permute-done.15.refs_0_
  49.4 1.0 %shard_map.54.piece_ref.refs_0_ = bf16[64,1024]{1,0:T(8,128)(2,1)S(1)} custom-call(s32[2,16]{1,0:T(2,128)S(1)} %copy-done, f32[2,64,1024]{2,1,0:T(8,128)S(1)} %get-tuple-element.18.right_ref, bf16[2,16,128,1024]{3,2,1,0:T(8,128)(2,1)S(1)} %get-tuple-element.19.lower_ref, bf16[64,1024]{1,0:T(8,128)(2,1)S(1)} %collective-permute-done.15.refs_0_, ...), custom_call_target="tpu_custom_call" | custom-call | flops 268435456 | bytes 10223744 | tf_op jit(solution)/shard_map/pallas_call | solution.py:219
  50.4 1.6 %collective-permute-start.18 = (bf16[64,1024]{1,0:T(8,128)(2,1)S(1)}, bf16[64,1024]{1,0:T(8,128)(2,1)S(1)}, u32[]{:S(2)}, u32[]{:S(2)}) collective-permute-start(bf16[64,1024]{1,0:T(8,128)(2,1)S(1)} %shard_map.54.piece_ref.refs_0_), channel_id=1, source_target_pairs={{0,2},{1,3},{2,0},{3,1},{4,6},{5,7},{6,4},{7,5},{8,10},{9,11},{10,... | collective-permute-start | bytes 393224 | tf_op jit(solution)/shard_map/ppermute | solution.py:253
  52.0 0.5 shard_map.55.refs_5_
  52.5 3.0 %collective-permute-done.18.refs_1_ = bf16[64,1024]{1,0:T(8,128)(2,1)S(1)} collective-permute-done((bf16[64,1024]{1,0:T(8,128)(2,1)S(1)}, bf16[64,1024]{1,0:T(8,128)(2,1)S(1)}, u32[]{:S(2)}, u32[]{:S(2)}) %collective-permute-start.18) | collective-permute-done | bytes 131104 | tf_op jit(solution)/shard_map/ppermute | solution.py:253
  55.5 1.2 %shard_map.56 = f32[2,64,1024]{2,1,0:T(8,128)} custom-call(bf16[64,1024]{1,0:T(8,128)(2,1)S(1)} %shard_map.54.piece_ref.refs_0_, bf16[64,1024]{1,0:T(8,128)(2,1)S(1)} %collective-permute-done.18.refs_1_, bf16[2,2048,512]{2,1,0:T(8,128)(2,1)S(1)} %get-tuple-element.20.refs_2_.refs_0_, bf16[2,2048,512]{2,1,0:T(8,128)(2,1)S(1)} %collective-permute-done.1.refs_3_.refs_1_, ...), custom_call_target="tpu_custom_call" | custom-call | flops 268435456 | bytes 9175040 | tf_op jit(solution)/shard_map/pallas_call | solution.py:219
  (4 shorter events, 0.1 us)
Async XLA Ops:
  0.0 7.4 %collective-permute-start.1 = (bf16[2,2048,512]{2,1,0:T(8,128)(2,1)}, bf16[2,2048,512]{2,1,0:T(8,128)(2,1)S(1)}, u32[]{:S(2)}, u32[]{:S(2)}) collective-permute-start(bf16[2,2048,512]{2,1,0:T(8,128)(2,1)} %refs_0_.1), channel_id=1, source_target_pairs={{0,1},{1,0},{2,3},{3,2},{4,5},{5,4},{6,7},{7,6},{8,9},{9,8},{10,11... | collective-permute-start | bytes 12582920 | tf_op jit(solution)/shard_map/ppermute | solution.py:272
  1.4 6.0 %collective-permute-start = (bf16[64,1024]{1,0:T(8,128)(2,1)S(1)}, bf16[64,1024]{1,0:T(8,128)(2,1)S(1)}, u32[]{:S(2)}, u32[]{:S(2)}) collective-permute-start(bf16[64,1024]{1,0:T(8,128)(2,1)S(1)} %fusion.after_ref.refs_0_), channel_id=1, source_target_pairs={{0,1},{1,0},{2,3},{3,2},{4,5},{5,4},{6,7},{7,6},{8,9},{9,8},{10,11... | collective-permute-start | bytes 393224 | tf_op jit(solution)/shard_map/ppermute | solution.py:253
  7.5 2.3 %copy-start = (s32[2,16]{1,0:T(2,128)S(1)}, s32[2,16]{1,0:T(2,128)}, u32[]{:S(2)}) copy-start(s32[2,16]{1,0:T(2,128)} %block_rows_ref.5) | copy-start | bytes 388
  7.5 1.4 %collective-permute-start.5 = (bf16[64,1024]{1,0:T(8,128)(2,1)S(1)}, bf16[64,1024]{1,0:T(8,128)(2,1)S(1)}, u32[]{:S(2)}, u32[]{:S(2)}) collective-permute-start(bf16[64,1024]{1,0:T(8,128)(2,1)S(1)} %get-tuple-element.21.refs_4_.refs_5_), channel_id=1, source_target_pairs={{0,1},{1,0},{2,3},{3,2},{4,8},{5,9},{6,10},{7,11},{8,12},{9,13},{1... | collective-permute-start | bytes 393224 | tf_op jit(solution)/shard_map/ppermute | solution.py:253
  7.9 1.3 %collective-permute-start.4 = (bf16[64,1024]{1,0:T(8,128)(2,1)S(1)}, bf16[64,1024]{1,0:T(8,128)(2,1)S(1)}, u32[]{:S(2)}, u32[]{:S(2)}) collective-permute-start(bf16[64,1024]{1,0:T(8,128)(2,1)S(1)} %get-tuple-element.21.refs_4_.refs_5_), channel_id=1, source_target_pairs={{0,1},{1,0},{2,3},{3,2},{4,14},{5,15},{6,12},{7,13},{8,9},{9,8},{1... | collective-permute-start | bytes 393224 | tf_op jit(solution)/shard_map/ppermute | solution.py:253
  8.1 1.4 %collective-permute-start.3 = (bf16[64,1024]{1,0:T(8,128)(2,1)S(1)}, bf16[64,1024]{1,0:T(8,128)(2,1)S(1)}, u32[]{:S(2)}, u32[]{:S(2)}) collective-permute-start(bf16[64,1024]{1,0:T(8,128)(2,1)S(1)} %get-tuple-element.21.refs_4_.refs_5_), channel_id=1, source_target_pairs={{0,1},{1,0},{2,3},{3,2},{4,5},{5,4},{6,7},{7,6},{8,9},{9,8},{10,11... | collective-permute-start | bytes 393224 | tf_op jit(solution)/shard_map/ppermute | solution.py:253
  8.4 1.3 %collective-permute-start.2 = (bf16[64,1024]{1,0:T(8,128)(2,1)S(1)}, bf16[64,1024]{1,0:T(8,128)(2,1)S(1)}, u32[]{:S(2)}, u32[]{:S(2)}) collective-permute-start(bf16[64,1024]{1,0:T(8,128)(2,1)S(1)} %get-tuple-element.21.refs_4_.refs_5_), channel_id=1, source_target_pairs={{0,1},{1,0},{2,3},{3,2},{4,5},{5,4},{6,7},{7,6},{8,9},{9,8},{10,11... | collective-permute-start | bytes 393224 | tf_op jit(solution)/shard_map/ppermute | solution.py:253
  9.9 12.3 %collective-permute-start.9 = (bf16[64,1024]{1,0:T(8,128)(2,1)S(1)}, bf16[64,1024]{1,0:T(8,128)(2,1)S(1)}, u32[]{:S(2)}, u32[]{:S(2)}) collective-permute-start(bf16[64,1024]{1,0:T(8,128)(2,1)S(1)} %get-tuple-element.23.refs_0_), channel_id=1, source_target_pairs={{0,1},{1,0},{2,3},{3,2},{4,6},{5,7},{6,4},{7,5},{8,9},{9,8},{10,11... | collective-permute-start | bytes 393224 | tf_op jit(solution)/shard_map/ppermute | solution.py:253
  10.1 15.4 %collective-permute-start.7 = (bf16[64,1024]{1,0:T(8,128)(2,1)S(1)}, bf16[64,1024]{1,0:T(8,128)(2,1)S(1)}, u32[]{:S(2)}, u32[]{:S(2)}) collective-permute-start(bf16[64,1024]{1,0:T(8,128)(2,1)S(1)} %get-tuple-element.22.own_ref), channel_id=1, source_target_pairs={{0,1},{1,0},{2,3},{3,2},{4,8},{5,9},{6,10},{7,11},{8,4},{9,5},{10,... | collective-permute-start | bytes 393224 | tf_op jit(solution)/shard_map/ppermute | solution.py:253
  10.4 16.9 %collective-permute-start.6 = (bf16[64,1024]{1,0:T(8,128)(2,1)S(1)}, bf16[64,1024]{1,0:T(8,128)(2,1)S(1)}, u32[]{:S(2)}, u32[]{:S(2)}) collective-permute-start(bf16[64,1024]{1,0:T(8,128)(2,1)S(1)} %get-tuple-element.22.own_ref), channel_id=1, source_target_pairs={{0,4},{1,5},{2,6},{3,7},{4,0},{5,1},{6,2},{7,3},{8,9},{9,8},{10,11... | collective-permute-start | bytes 393224 | tf_op jit(solution)/shard_map/ppermute | solution.py:253
  22.2 10.2 %collective-permute-start.13 = (bf16[64,1024]{1,0:T(8,128)(2,1)S(1)}, bf16[64,1024]{1,0:T(8,128)(2,1)S(1)}, u32[]{:S(2)}, u32[]{:S(2)}) collective-permute-start(bf16[64,1024]{1,0:T(8,128)(2,1)S(1)} %get-tuple-element.25.refs_6_.refs_5_), channel_id=1, source_target_pairs={{4,0},{6,2},{20,16},{22,18},{5,1},{7,3},{21,17},{23,19}} | collective-permute-start | bytes 393224 | tf_op jit(solution)/shard_map/ppermute | solution.py:239
  23.5 10.8 %collective-permute-start.12 = (bf16[64,1024]{1,0:T(8,128)(2,1)S(1)}, bf16[64,1024]{1,0:T(8,128)(2,1)S(1)}, u32[]{:S(2)}, u32[]{:S(2)}) collective-permute-start(bf16[64,1024]{1,0:T(8,128)(2,1)S(1)} %get-tuple-element.25.refs_6_.refs_5_), channel_id=1, source_target_pairs={{4,2},{6,0},{20,18},{22,16},{5,3},{7,1},{21,19},{23,17}} | collective-permute-start | bytes 393224 | tf_op jit(solution)/shard_map/ppermute | solution.py:239
  24.8 9.5 %collective-permute-start.11 = (bf16[64,1024]{1,0:T(8,128)(2,1)S(1)}, bf16[64,1024]{1,0:T(8,128)(2,1)S(1)}, u32[]{:S(2)}, u32[]{:S(2)}) collective-permute-start(bf16[64,1024]{1,0:T(8,128)(2,1)S(1)} %get-tuple-element.25.refs_6_.refs_5_), channel_id=1, source_target_pairs={{4,8},{6,10},{20,24},{22,26},{5,9},{7,11},{21,25},{23,27}} | collective-permute-start | bytes 393224 | tf_op jit(solution)/shard_map/ppermute | solution.py:239
  25.5 8.8 %collective-permute-start.10 = (bf16[64,1024]{1,0:T(8,128)(2,1)S(1)}, bf16[64,1024]{1,0:T(8,128)(2,1)S(1)}, u32[]{:S(2)}, u32[]{:S(2)}) collective-permute-start(bf16[64,1024]{1,0:T(8,128)(2,1)S(1)} %get-tuple-element.25.refs_6_.refs_5_), channel_id=1, source_target_pairs={{4,10},{6,8},{20,26},{22,24},{5,11},{7,9},{21,27},{23,25}} | collective-permute-start | bytes 393224 | tf_op jit(solution)/shard_map/ppermute | solution.py:239
  27.4 7.2 %collective-permute-start.8 = (bf16[64,1024]{1,0:T(8,128)(2,1)S(1)}, bf16[64,1024]{1,0:T(8,128)(2,1)S(1)}, u32[]{:S(2)}, u32[]{:S(2)}) collective-permute-start(bf16[64,1024]{1,0:T(8,128)(2,1)S(1)} %shard_map.49.refs_5_), channel_id=1, source_target_pairs={{0,2},{1,3},{2,0},{3,1},{4,6},{5,7},{6,4},{7,5},{8,10},{9,11},{10,... | collective-permute-start | bytes 393224 | tf_op jit(solution)/shard_map/ppermute | solution.py:253
  35.6 5.4 %collective-permute-start.14 = (bf16[64,1024]{1,0:T(8,128)(2,1)S(1)}, bf16[64,1024]{1,0:T(8,128)(2,1)S(1)}, u32[]{:S(2)}, u32[]{:S(2)}) collective-permute-start(bf16[64,1024]{1,0:T(8,128)(2,1)S(1)} %get-tuple-element.26.piece_ref.refs_0_), channel_id=1, source_target_pairs={{0,2},{1,3},{2,0},{3,1},{4,12},{5,13},{6,14},{7,15},{8,10},{9,11},... | collective-permute-start | bytes 393224 | tf_op jit(solution)/shard_map/ppermute | solution.py:253
  41.5 5.0 %collective-permute-start.17 = (bf16[64,1024]{1,0:T(8,128)(2,1)S(1)}, bf16[64,1024]{1,0:T(8,128)(2,1)S(1)}, u32[]{:S(2)}, u32[]{:S(2)}) collective-permute-start(bf16[64,1024]{1,0:T(8,128)(2,1)S(1)} %get-tuple-element.28.refs_2_), channel_id=1, source_target_pairs={{0,2},{1,3},{2,0},{3,1},{4,6},{5,7},{6,4},{7,5},{8,10},{9,11},{10,... | collective-permute-start | bytes 393224 | tf_op jit(solution)/shard_map/ppermute | solution.py:253
  43.1 6.0 %collective-permute-start.16 = (bf16[64,1024]{1,0:T(8,128)(2,1)S(1)}, bf16[64,1024]{1,0:T(8,128)(2,1)S(1)}, u32[]{:S(2)}, u32[]{:S(2)}) collective-permute-start(bf16[64,1024]{1,0:T(8,128)(2,1)S(1)} %get-tuple-element.28.refs_2_), channel_id=1, source_target_pairs={{0,6},{1,7},{2,4},{3,5},{4,2},{5,3},{6,0},{7,1},{8,14},{9,15},{10,... | collective-permute-start | bytes 393224 | tf_op jit(solution)/shard_map/ppermute | solution.py:253
  44.4 5.0 %collective-permute-start.15 = (bf16[64,1024]{1,0:T(8,128)(2,1)S(1)}, bf16[64,1024]{1,0:T(8,128)(2,1)S(1)}, u32[]{:S(2)}, u32[]{:S(2)}) collective-permute-start(bf16[64,1024]{1,0:T(8,128)(2,1)S(1)} %get-tuple-element.28.refs_2_), channel_id=1, source_target_pairs={{0,4},{1,5},{2,6},{3,7},{4,0},{5,1},{6,2},{7,3},{8,12},{9,13},{10,... | collective-permute-start | bytes 393224 | tf_op jit(solution)/shard_map/ppermute | solution.py:253
  50.4 5.0 %collective-permute-start.18 = (bf16[64,1024]{1,0:T(8,128)(2,1)S(1)}, bf16[64,1024]{1,0:T(8,128)(2,1)S(1)}, u32[]{:S(2)}, u32[]{:S(2)}) collective-permute-start(bf16[64,1024]{1,0:T(8,128)(2,1)S(1)} %shard_map.54.piece_ref.refs_0_), channel_id=1, source_target_pairs={{0,2},{1,3},{2,0},{3,1},{4,6},{5,7},{6,4},{7,5},{8,10},{9,11},{10,... | collective-permute-start | bytes 393224 | tf_op jit(solution)/shard_map/ppermute | solution.py:253

commit v17 on v16

--- a/solution.py
+++ b/solution.py
@@ -54,7 +54,7 @@
     if level == top:
         pieces = [refs[1:2 * rows:2], refs[:2 * rows:2]]
         if plan == "traded":
-            r0, r1, l0, l1 = refs[:4]
+            r1, l0, l1, r0 = refs[:4]
             pieces = [[l0, l1], [r0, r1]]
     elif plan == "rooted":
         r1, r0, l1, l0 = refs[:4]
@@ -310,7 +310,7 @@
             elif plan == "crossed":
                 pieces = [late, rights[1], rights[0], lefts[1], lefts[0], relayed, rounded]
             elif plan == "traded":
-                pieces = [rights[0], rights[1], lefts[0], lefts[1], mine, relayed, late]
+                pieces = [rights[1], lefts[0], lefts[1], rights[0], mine, relayed, late]
             else:
                 pieces = [*pieces, *older]
             arrays = [block_rows, right, lower, *pieces]

time: 57.4 us -> 57.2 us (level)
  no operation moved by 1% of the time
where the time goes in v17:
time: 57.2 us; the launch traced here: 56.9 us
  starting transfers between devices  25.3 us (44%)
  waiting for transfers between devices  20.8 us (36%)
  Pallas kernels  9.59 us (17%)
  local copies, waits for them, and re-layouts  0.97 us (2%)
    ppermute x14, starting transfers between devices, permute(): return lax.ppermute(value, ('leaf', 'rows', 'rhs'), pairs)  21 us
    ppermute x14, waiting for transfers between devices, permute(): return lax.ppermute(value, ('leaf', 'rows', 'rhs'), pairs)  15.2 us
    pallas_call x11, Pallas kernels, call(): pl.pallas_call(kernel, in_specs=[WHOLE] * len(near) + [FAR] * len(far), o...  9.59 us
    ppermute x4, waiting for transfers between devices, send(): return lax.ppermute(value, places, pairs)  5.62 us
    ppermute x4, starting transfers between devices, send(): return lax.ppermute(value, places, pairs)  3.92 us
  transfers between devices with their start and end apart: 19, of which 14 were waited for; matrix products, arithmetic and copies ran while one was open for 2% of the time, Pallas kernels for 10%

profile of v17, /device:TPU:0, one launch (start us, length us, event | category | flops | bytes accessed | tf_op | source)
XLA Modules:
  0.0 56.9 jit_solution(235646722880259510)
XLA Ops:
  0.0 0.5 collective-permute-start.1
  0.5 1.0 %fusion.after_ref.refs_0_ = bf16[64,1024]{1,0:T(8,128)(2,1)S(1)} fusion(f32[2,64,1024]{2,1,0:T(8,128)} %refs_1_.1), kind=kLoop, calls=%fused_computation.1 | loop fusion | bytes 262144 | tf_op jit(solution)/shard_map/convert_element_type | solution.py:294
  1.4 0.1 collective-permute-start
  1.5 4.8 %shard_map.46 = (bf16[2,2048,512]{2,1,0:T(8,128)(2,1)S(1)}, f32[2,64,1024]{2,1,0:T(8,128)S(1)}, bf16[2,16,128,1024]{3,2,1,0:T(8,128)(2,1)S(1)}) custom-call(bf16[64,1024]{1,0:T(8,128)(2,1)S(1)} %fusion.after_ref.refs_0_, bf16[2,2048,512]{2,1,0:T(8,128)(2,1)} %refs_0_.1, f32[2,64,1024]{2,1,0:T(8,128)} %refs_1_.1, bf16[2,16,128,1024]{3,2,1,0:T(8,128)(2,1)} %refs_2_.1), custom_call_target="tpu_custom_call" | custom-call | bytes 13238272 | tf_op jit(solution)/shard_map/pallas_call | solution.py:219
  6.4 1.0 %collective-permute-done.refs_1_ = bf16[64,1024]{1,0:T(8,128)(2,1)S(1)} collective-permute-done((bf16[64,1024]{1,0:T(8,128)(2,1)S(1)}, bf16[64,1024]{1,0:T(8,128)(2,1)S(1)}, u32[]{:S(2)}, u32[]{:S(2)}) %collective-permute-start) | collective-permute-done | bytes 131104 | tf_op jit(solution)/shard_map/ppermute | solution.py:253
  7.4 0.0 collective-permute-done.1.refs_3_.refs_1_
  7.5 0.4 collective-permute-start.5
  7.9 0.1 collective-permute-start.4
  8.1 0.4 collective-permute-start.3
  8.4 0.1 collective-permute-start.2
  8.6 0.3 collective-permute-done.5.refs_3_
  8.9 0.4 collective-permute-done.4.refs_2_
  9.3 0.2 collective-permute-done.3.refs_1_
  9.5 0.3 collective-permute-done.2.refs_0_
  9.8 0.0 copy-done
  9.8 0.1 shard_map.48
  9.9 0.3 collective-permute-start.9
  10.1 0.3 collective-permute-start.7
  10.4 11.7 %collective-permute-start.6 = (bf16[64,1024]{1,0:T(8,128)(2,1)S(1)}, bf16[64,1024]{1,0:T(8,128)(2,1)S(1)}, u32[]{:S(2)}, u32[]{:S(2)}) collective-permute-start(bf16[64,1024]{1,0:T(8,128)(2,1)S(1)} %get-tuple-element.22.own_ref), channel_id=1, source_target_pairs={{0,4},{1,5},{2,6},{3,7},{4,0},{5,1},{6,2},{7,3},{8,9},{9,8},{10,11... | collective-permute-start | bytes 393224 | tf_op jit(solution)/shard_map/ppermute | solution.py:253
  22.2 0.0 collective-permute-done.9.refs_1_
  22.2 1.3 %collective-permute-start.13 = (bf16[64,1024]{1,0:T(8,128)(2,1)S(1)}, bf16[64,1024]{1,0:T(8,128)(2,1)S(1)}, u32[]{:S(2)}, u32[]{:S(2)}) collective-permute-start(bf16[64,1024]{1,0:T(8,128)(2,1)S(1)} %get-tuple-element.25.refs_6_.refs_5_), channel_id=1, source_target_pairs={{4,0},{6,2},{20,16},{22,18},{5,1},{7,3},{21,17},{23,19}} | collective-permute-start | bytes 393224 | tf_op jit(solution)/shard_map/ppermute | solution.py:239
  23.5 1.3 %collective-permute-start.12 = (bf16[64,1024]{1,0:T(8,128)(2,1)S(1)}, bf16[64,1024]{1,0:T(8,128)(2,1)S(1)}, u32[]{:S(2)}, u32[]{:S(2)}) collective-permute-start(bf16[64,1024]{1,0:T(8,128)(2,1)S(1)} %get-tuple-element.25.refs_6_.refs_5_), channel_id=1, source_target_pairs={{4,2},{6,0},{20,18},{22,16},{5,3},{7,1},{21,19},{23,17}} | collective-permute-start | bytes 393224 | tf_op jit(solution)/shard_map/ppermute | solution.py:239
  24.8 0.7 %collective-permute-start.11 = (bf16[64,1024]{1,0:T(8,128)(2,1)S(1)}, bf16[64,1024]{1,0:T(8,128)(2,1)S(1)}, u32[]{:S(2)}, u32[]{:S(2)}) collective-permute-start(bf16[64,1024]{1,0:T(8,128)(2,1)S(1)} %get-tuple-element.25.refs_6_.refs_5_), channel_id=1, source_target_pairs={{4,8},{6,10},{20,24},{22,26},{5,9},{7,11},{21,25},{23,27}} | collective-permute-start | bytes 393224 | tf_op jit(solution)/shard_map/ppermute | solution.py:239
  25.5 0.0 collective-permute-done.7.second_ref
  25.5 0.7 %collective-permute-start.10 = (bf16[64,1024]{1,0:T(8,128)(2,1)S(1)}, bf16[64,1024]{1,0:T(8,128)(2,1)S(1)}, u32[]{:S(2)}, u32[]{:S(2)}) collective-permute-start(bf16[64,1024]{1,0:T(8,128)(2,1)S(1)} %get-tuple-element.25.refs_6_.refs_5_), channel_id=1, source_target_pairs={{4,10},{6,8},{20,26},{22,24},{5,11},{7,9},{21,27},{23,25}} | collective-permute-start | bytes 393224 | tf_op jit(solution)/shard_map/ppermute | solution.py:239
  26.2 1.2 %collective-permute-done.6.first_ref = bf16[64,1024]{1,0:T(8,128)(2,1)S(1)} collective-permute-done((bf16[64,1024]{1,0:T(8,128)(2,1)S(1)}, bf16[64,1024]{1,0:T(8,128)(2,1)S(1)}, u32[]{:S(2)}, u32[]{:S(2)}) %collective-permute-start.6) | collective-permute-done | bytes 131104 | tf_op jit(solution)/shard_map/ppermute | solution.py:253
  27.4 1.3 %collective-permute-start.8 = (bf16[64,1024]{1,0:T(8,128)(2,1)S(1)}, bf16[64,1024]{1,0:T(8,128)(2,1)S(1)}, u32[]{:S(2)}, u32[]{:S(2)}) collective-permute-start(bf16[64,1024]{1,0:T(8,128)(2,1)S(1)} %shard_map.49.refs_5_), channel_id=1, source_target_pairs={{0,2},{1,3},{2,0},{3,1},{4,6},{5,7},{6,4},{7,5},{8,10},{9,11},{10,... | collective-permute-start | bytes 393224 | tf_op jit(solution)/shard_map/ppermute | solution.py:253
  28.7 3.5 %collective-permute-done.13.refs_4_ = bf16[64,1024]{1,0:T(8,128)(2,1)S(1)} collective-permute-done((bf16[64,1024]{1,0:T(8,128)(2,1)S(1)}, bf16[64,1024]{1,0:T(8,128)(2,1)S(1)}, u32[]{:S(2)}, u32[]{:S(2)}) %collective-permute-start.13) | collective-permute-done | bytes 131104 | tf_op jit(solution)/shard_map/ppermute | solution.py:239
  32.1 2.2 %collective-permute-done.12.refs_3_ = bf16[64,1024]{1,0:T(8,128)(2,1)S(1)} collective-permute-done((bf16[64,1024]{1,0:T(8,128)(2,1)S(1)}, bf16[64,1024]{1,0:T(8,128)(2,1)S(1)}, u32[]{:S(2)}, u32[]{:S(2)}) %collective-permute-start.12) | collective-permute-done | bytes 131104 | tf_op jit(solution)/shard_map/ppermute | solution.py:239
  34.3 0.0 collective-permute-done.11.refs_2_
  34.3 0.0 collective-permute-done.10.refs_1_
  34.3 0.3 collective-permute-done.8.refs_0_.refs_6_
  34.6 1.0 %shard_map.51 = (bf16[64,1024]{1,0:T(8,128)(2,1)S(1)}, bf16[64,4096]{1,0:T(8,128)(2,1)S(1)}) custom-call(s32[2,16]{1,0:T(2,128)S(1)} %copy-done, f32[2,64,1024]{2,1,0:T(8,128)S(1)} %get-tuple-element.18.right_ref, bf16[2,16,128,1024]{3,2,1,0:T(8,128)(2,1)S(1)} %get-tuple-element.19.lower_ref, bf16[64,1024]{1,0:T(8,128)(2,1)S(1)} %collective-permute-done.8.refs_0_.refs_6_, ...), custom_call_target="tpu_custom_call" | custom-call | flops 268435456 | bytes 9830528 | tf_op jit(solution)/shard_map/pallas_call | solution.py:219
  35.6 1.3 %collective-permute-start.14 = (bf16[64,1024]{1,0:T(8,128)(2,1)S(1)}, bf16[64,1024]{1,0:T(8,128)(2,1)S(1)}, u32[]{:S(2)}, u32[]{:S(2)}) collective-permute-start(bf16[64,1024]{1,0:T(8,128)(2,1)S(1)} %get-tuple-element.26.piece_ref.refs_0_), channel_id=1, source_target_pairs={{0,2},{1,3},{2,0},{3,1},{4,12},{5,13},{6,14},{7,15},{8,10},{9,11},... | collective-permute-start | bytes 393224 | tf_op jit(solution)/shard_map/ppermute | solution.py:253
  36.9 0.5 shard_map.52.refs_6_
  37.4 3.2 %collective-permute-done.14.refs_1_ = bf16[64,1024]{1,0:T(8,128)(2,1)S(1)} collective-permute-done((bf16[64,1024]{1,0:T(8,128)(2,1)S(1)}, bf16[64,1024]{1,0:T(8,128)(2,1)S(1)}, u32[]{:S(2)}, u32[]{:S(2)}) %collective-permute-start.14) | collective-permute-done | bytes 131104 | tf_op jit(solution)/shard_map/ppermute | solution.py:253
  40.6 0.5 shard_map.53
  41.1 1.8 %collective-permute-start.17 = (bf16[64,1024]{1,0:T(8,128)(2,1)S(1)}, bf16[64,1024]{1,0:T(8,128)(2,1)S(1)}, u32[]{:S(2)}, u32[]{:S(2)}) collective-permute-start(bf16[64,1024]{1,0:T(8,128)(2,1)S(1)} %get-tuple-element.28.refs_1_), channel_id=1, source_target_pairs={{0,4},{1,5},{2,6},{3,7},{4,0},{5,1},{6,2},{7,3},{8,12},{9,13},{10,... | collective-permute-start | bytes 393224 | tf_op jit(solution)/shard_map/ppermute | solution.py:253
  42.9 0.8 %collective-permute-start.16 = (bf16[64,1024]{1,0:T(8,128)(2,1)S(1)}, bf16[64,1024]{1,0:T(8,128)(2,1)S(1)}, u32[]{:S(2)}, u32[]{:S(2)}) collective-permute-start(bf16[64,1024]{1,0:T(8,128)(2,1)S(1)} %get-tuple-element.28.refs_1_), channel_id=1, source_target_pairs={{0,2},{1,3},{2,0},{3,1},{4,6},{5,7},{6,4},{7,5},{8,10},{9,11},{10,... | collective-permute-start | bytes 393224 | tf_op jit(solution)/shard_map/ppermute | solution.py:253
  43.7 1.0 %collective-permute-start.15 = (bf16[64,1024]{1,0:T(8,128)(2,1)S(1)}, bf16[64,1024]{1,0:T(8,128)(2,1)S(1)}, u32[]{:S(2)}, u32[]{:S(2)}) collective-permute-start(bf16[64,1024]{1,0:T(8,128)(2,1)S(1)} %get-tuple-element.28.refs_1_), channel_id=1, source_target_pairs={{0,6},{1,7},{2,4},{3,5},{4,2},{5,3},{6,0},{7,1},{8,14},{9,15},{10,... | collective-permute-start | bytes 393224 | tf_op jit(solution)/shard_map/ppermute | solution.py:253
  44.7 1.5 %collective-permute-done.17.refs_3_ = bf16[64,1024]{1,0:T(8,128)(2,1)S(1)} collective-permute-done((bf16[64,1024]{1,0:T(8,128)(2,1)S(1)}, bf16[64,1024]{1,0:T(8,128)(2,1)S(1)}, u32[]{:S(2)}, u32[]{:S(2)}) %collective-permute-start.17) | collective-permute-done | bytes 131104 | tf_op jit(solution)/shard_map/ppermute | solution.py:253
  46.1 1.7 %collective-permute-done.16.refs_2_ = bf16[64,1024]{1,0:T(8,128)(2,1)S(1)} collective-permute-done((bf16[64,1024]{1,0:T(8,128)(2,1)S(1)}, bf16[64,1024]{1,0:T(8,128)(2,1)S(1)}, u32[]{:S(2)}, u32[]{:S(2)}) %collective-permute-start.16) | collective-permute-done | bytes 131104 | tf_op jit(solution)/shard_map/ppermute | solution.py:253
  47.9 1.8 %collective-permute-done.15.refs_0_ = bf16[64,1024]{1,0:T(8,128)(2,1)S(1)} collective-permute-done((bf16[64,1024]{1,0:T(8,128)(2,1)S(1)}, bf16[64,1024]{1,0:T(8,128)(2,1)S(1)}, u32[]{:S(2)}, u32[]{:S(2)}) %collective-permute-start.15) | collective-permute-done | bytes 131104 | tf_op jit(solution)/shard_map/ppermute | solution.py:253
  49.7 1.0 %shard_map.54.piece_ref.refs_0_ = bf16[64,1024]{1,0:T(8,128)(2,1)S(1)} custom-call(s32[2,16]{1,0:T(2,128)S(1)} %copy-done, f32[2,64,1024]{2,1,0:T(8,128)S(1)} %get-tuple-element.18.right_ref, bf16[2,16,128,1024]{3,2,1,0:T(8,128)(2,1)S(1)} %get-tuple-element.19.lower_ref, bf16[64,1024]{1,0:T(8,128)(2,1)S(1)} %collective-permute-done.15.refs_0_, ...), custom_call_target="tpu_custom_call" | custom-call | flops 268435456 | bytes 10223744 | tf_op jit(solution)/shard_map/pallas_call | solution.py:219
  50.7 1.3 %collective-permute-start.18 = (bf16[64,1024]{1,0:T(8,128)(2,1)S(1)}, bf16[64,1024]{1,0:T(8,128)(2,1)S(1)}, u32[]{:S(2)}, u32[]{:S(2)}) collective-permute-start(bf16[64,1024]{1,0:T(8,128)(2,1)S(1)} %shard_map.54.piece_ref.refs_0_), channel_id=1, source_target_pairs={{0,2},{1,3},{2,0},{3,1},{4,6},{5,7},{6,4},{7,5},{8,10},{9,11},{10,... | collective-permute-start | bytes 393224 | tf_op jit(solution)/shard_map/ppermute | solution.py:253
  52.0 0.5 shard_map.55.refs_5_
  52.5 3.2 %collective-permute-done.18.refs_1_ = bf16[64,1024]{1,0:T(8,128)(2,1)S(1)} collective-permute-done((bf16[64,1024]{1,0:T(8,128)(2,1)S(1)}, bf16[64,1024]{1,0:T(8,128)(2,1)S(1)}, u32[]{:S(2)}, u32[]{:S(2)}) %collective-permute-start.18) | collective-permute-done | bytes 131104 | tf_op jit(solution)/shard_map/ppermute | solution.py:253
  55.7 1.2 %shard_map.56 = f32[2,64,1024]{2,1,0:T(8,128)} custom-call(bf16[64,1024]{1,0:T(8,128)(2,1)S(1)} %shard_map.54.piece_ref.refs_0_, bf16[64,1024]{1,0:T(8,128)(2,1)S(1)} %collective-permute-done.18.refs_1_, bf16[2,2048,512]{2,1,0:T(8,128)(2,1)S(1)} %get-tuple-element.20.refs_2_.refs_0_, bf16[2,2048,512]{2,1,0:T(8,128)(2,1)S(1)} %collective-permute-done.1.refs_3_.refs_1_, ...), custom_call_target="tpu_custom_call" | custom-call | flops 268435456 | bytes 9175040 | tf_op jit(solution)/shard_map/pallas_call | solution.py:219
  (4 shorter events, 0.1 us)
Async XLA Ops:
  0.0 7.4 %collective-permute-start.1 = (bf16[2,2048,512]{2,1,0:T(8,128)(2,1)}, bf16[2,2048,512]{2,1,0:T(8,128)(2,1)S(1)}, u32[]{:S(2)}, u32[]{:S(2)}) collective-permute-start(bf16[2,2048,512]{2,1,0:T(8,128)(2,1)} %refs_0_.1), channel_id=1, source_target_pairs={{0,1},{1,0},{2,3},{3,2},{4,5},{5,4},{6,7},{7,6},{8,9},{9,8},{10,11... | collective-permute-start | bytes 12582920 | tf_op jit(solution)/shard_map/ppermute | solution.py:272
  1.4 6.0 %collective-permute-start = (bf16[64,1024]{1,0:T(8,128)(2,1)S(1)}, bf16[64,1024]{1,0:T(8,128)(2,1)S(1)}, u32[]{:S(2)}, u32[]{:S(2)}) collective-permute-start(bf16[64,1024]{1,0:T(8,128)(2,1)S(1)} %fusion.after_ref.refs_0_), channel_id=1, source_target_pairs={{0,1},{1,0},{2,3},{3,2},{4,5},{5,4},{6,7},{7,6},{8,9},{9,8},{10,11... | collective-permute-start | bytes 393224 | tf_op jit(solution)/shard_map/ppermute | solution.py:253
  7.5 2.3 %copy-start = (s32[2,16]{1,0:T(2,128)S(1)}, s32[2,16]{1,0:T(2,128)}, u32[]{:S(2)}) copy-start(s32[2,16]{1,0:T(2,128)} %block_rows_ref.5) | copy-start | bytes 388
  7.5 1.4 %collective-permute-start.5 = (bf16[64,1024]{1,0:T(8,128)(2,1)S(1)}, bf16[64,1024]{1,0:T(8,128)(2,1)S(1)}, u32[]{:S(2)}, u32[]{:S(2)}) collective-permute-start(bf16[64,1024]{1,0:T(8,128)(2,1)S(1)} %get-tuple-element.21.refs_4_.refs_5_), channel_id=1, source_target_pairs={{0,1},{1,0},{2,3},{3,2},{4,8},{5,9},{6,10},{7,11},{8,12},{9,13},{1... | collective-permute-start | bytes 393224 | tf_op jit(solution)/shard_map/ppermute | solution.py:253
  7.9 1.3 %collective-permute-start.4 = (bf16[64,1024]{1,0:T(8,128)(2,1)S(1)}, bf16[64,1024]{1,0:T(8,128)(2,1)S(1)}, u32[]{:S(2)}, u32[]{:S(2)}) collective-permute-start(bf16[64,1024]{1,0:T(8,128)(2,1)S(1)} %get-tuple-element.21.refs_4_.refs_5_), channel_id=1, source_target_pairs={{0,1},{1,0},{2,3},{3,2},{4,14},{5,15},{6,12},{7,13},{8,9},{9,8},{1... | collective-permute-start | bytes 393224 | tf_op jit(solution)/shard_map/ppermute | solution.py:253
  8.1 1.4 %collective-permute-start.3 = (bf16[64,1024]{1,0:T(8,128)(2,1)S(1)}, bf16[64,1024]{1,0:T(8,128)(2,1)S(1)}, u32[]{:S(2)}, u32[]{:S(2)}) collective-permute-start(bf16[64,1024]{1,0:T(8,128)(2,1)S(1)} %get-tuple-element.21.refs_4_.refs_5_), channel_id=1, source_target_pairs={{0,1},{1,0},{2,3},{3,2},{4,5},{5,4},{6,7},{7,6},{8,9},{9,8},{10,11... | collective-permute-start | bytes 393224 | tf_op jit(solution)/shard_map/ppermute | solution.py:253
  8.4 1.3 %collective-permute-start.2 = (bf16[64,1024]{1,0:T(8,128)(2,1)S(1)}, bf16[64,1024]{1,0:T(8,128)(2,1)S(1)}, u32[]{:S(2)}, u32[]{:S(2)}) collective-permute-start(bf16[64,1024]{1,0:T(8,128)(2,1)S(1)} %get-tuple-element.21.refs_4_.refs_5_), channel_id=1, source_target_pairs={{0,1},{1,0},{2,3},{3,2},{4,5},{5,4},{6,7},{7,6},{8,9},{9,8},{10,11... | collective-permute-start | bytes 393224 | tf_op jit(solution)/shard_map/ppermute | solution.py:253
  9.9 12.3 %collective-permute-start.9 = (bf16[64,1024]{1,0:T(8,128)(2,1)S(1)}, bf16[64,1024]{1,0:T(8,128)(2,1)S(1)}, u32[]{:S(2)}, u32[]{:S(2)}) collective-permute-start(bf16[64,1024]{1,0:T(8,128)(2,1)S(1)} %get-tuple-element.23.refs_0_), channel_id=1, source_target_pairs={{0,1},{1,0},{2,3},{3,2},{4,6},{5,7},{6,4},{7,5},{8,9},{9,8},{10,11... | collective-permute-start | bytes 393224 | tf_op jit(solution)/shard_map/ppermute | solution.py:253
  10.1 15.4 %collective-permute-start.7 = (bf16[64,1024]{1,0:T(8,128)(2,1)S(1)}, bf16[64,1024]{1,0:T(8,128)(2,1)S(1)}, u32[]{:S(2)}, u32[]{:S(2)}) collective-permute-start(bf16[64,1024]{1,0:T(8,128)(2,1)S(1)} %get-tuple-element.22.own_ref), channel_id=1, source_target_pairs={{0,1},{1,0},{2,3},{3,2},{4,8},{5,9},{6,10},{7,11},{8,4},{9,5},{10,... | collective-permute-start | bytes 393224 | tf_op jit(solution)/shard_map/ppermute | solution.py:253
  10.4 16.9 %collective-permute-start.6 = (bf16[64,1024]{1,0:T(8,128)(2,1)S(1)}, bf16[64,1024]{1,0:T(8,128)(2,1)S(1)}, u32[]{:S(2)}, u32[]{:S(2)}) collective-permute-start(bf16[64,1024]{1,0:T(8,128)(2,1)S(1)} %get-tuple-element.22.own_ref), channel_id=1, source_target_pairs={{0,4},{1,5},{2,6},{3,7},{4,0},{5,1},{6,2},{7,3},{8,9},{9,8},{10,11... | collective-permute-start | bytes 393224 | tf_op jit(solution)/shard_map/ppermute | solution.py:253
  22.2 9.9 %collective-permute-start.13 = (bf16[64,1024]{1,0:T(8,128)(2,1)S(1)}, bf16[64,1024]{1,0:T(8,128)(2,1)S(1)}, u32[]{:S(2)}, u32[]{:S(2)}) collective-permute-start(bf16[64,1024]{1,0:T(8,128)(2,1)S(1)} %get-tuple-element.25.refs_6_.refs_5_), channel_id=1, source_target_pairs={{4,0},{6,2},{20,16},{22,18},{5,1},{7,3},{21,17},{23,19}} | collective-permute-start | bytes 393224 | tf_op jit(solution)/shard_map/ppermute | solution.py:239
  23.5 10.8 %collective-permute-start.12 = (bf16[64,1024]{1,0:T(8,128)(2,1)S(1)}, bf16[64,1024]{1,0:T(8,128)(2,1)S(1)}, u32[]{:S(2)}, u32[]{:S(2)}) collective-permute-start(bf16[64,1024]{1,0:T(8,128)(2,1)S(1)} %get-tuple-element.25.refs_6_.refs_5_), channel_id=1, source_target_pairs={{4,2},{6,0},{20,18},{22,16},{5,3},{7,1},{21,19},{23,17}} | collective-permute-start | bytes 393224 | tf_op jit(solution)/shard_map/ppermute | solution.py:239
  24.8 9.5 %collective-permute-start.11 = (bf16[64,1024]{1,0:T(8,128)(2,1)S(1)}, bf16[64,1024]{1,0:T(8,128)(2,1)S(1)}, u32[]{:S(2)}, u32[]{:S(2)}) collective-permute-start(bf16[64,1024]{1,0:T(8,128)(2,1)S(1)} %get-tuple-element.25.refs_6_.refs_5_), channel_id=1, source_target_pairs={{4,8},{6,10},{20,24},{22,26},{5,9},{7,11},{21,25},{23,27}} | collective-permute-start | bytes 393224 | tf_op jit(solution)/shard_map/ppermute | solution.py:239
  25.5 8.8 %collective-permute-start.10 = (bf16[64,1024]{1,0:T(8,128)(2,1)S(1)}, bf16[64,1024]{1,0:T(8,128)(2,1)S(1)}, u32[]{:S(2)}, u32[]{:S(2)}) collective-permute-start(bf16[64,1024]{1,0:T(8,128)(2,1)S(1)} %get-tuple-element.25.refs_6_.refs_5_), channel_id=1, source_target_pairs={{4,10},{6,8},{20,26},{22,24},{5,11},{7,9},{21,27},{23,25}} | collective-permute-start | bytes 393224 | tf_op jit(solution)/shard_map/ppermute | solution.py:239
  27.4 7.2 %collective-permute-start.8 = (bf16[64,1024]{1,0:T(8,128)(2,1)S(1)}, bf16[64,1024]{1,0:T(8,128)(2,1)S(1)}, u32[]{:S(2)}, u32[]{:S(2)}) collective-permute-start(bf16[64,1024]{1,0:T(8,128)(2,1)S(1)} %shard_map.49.refs_5_), channel_id=1, source_target_pairs={{0,2},{1,3},{2,0},{3,1},{4,6},{5,7},{6,4},{7,5},{8,10},{9,11},{10,... | collective-permute-start | bytes 393224 | tf_op jit(solution)/shard_map/ppermute | solution.py:253
  35.6 5.0 %collective-permute-start.14 = (bf16[64,1024]{1,0:T(8,128)(2,1)S(1)}, bf16[64,1024]{1,0:T(8,128)(2,1)S(1)}, u32[]{:S(2)}, u32[]{:S(2)}) collective-permute-start(bf16[64,1024]{1,0:T(8,128)(2,1)S(1)} %get-tuple-element.26.piece_ref.refs_0_), channel_id=1, source_target_pairs={{0,2},{1,3},{2,0},{3,1},{4,12},{5,13},{6,14},{7,15},{8,10},{9,11},... | collective-permute-start | bytes 393224 | tf_op jit(solution)/shard_map/ppermute | solution.py:253
  41.1 5.0 %collective-permute-start.17 = (bf16[64,1024]{1,0:T(8,128)(2,1)S(1)}, bf16[64,1024]{1,0:T(8,128)(2,1)S(1)}, u32[]{:S(2)}, u32[]{:S(2)}) collective-permute-start(bf16[64,1024]{1,0:T(8,128)(2,1)S(1)} %get-tuple-element.28.refs_1_), channel_id=1, source_target_pairs={{0,4},{1,5},{2,6},{3,7},{4,0},{5,1},{6,2},{7,3},{8,12},{9,13},{10,... | collective-permute-start | bytes 393224 | tf_op jit(solution)/shard_map/ppermute | solution.py:253
  42.9 5.0 %collective-permute-start.16 = (bf16[64,1024]{1,0:T(8,128)(2,1)S(1)}, bf16[64,1024]{1,0:T(8,128)(2,1)S(1)}, u32[]{:S(2)}, u32[]{:S(2)}) collective-permute-start(bf16[64,1024]{1,0:T(8,128)(2,1)S(1)} %get-tuple-element.28.refs_1_), channel_id=1, source_target_pairs={{0,2},{1,3},{2,0},{3,1},{4,6},{5,7},{6,4},{7,5},{8,10},{9,11},{10,... | collective-permute-start | bytes 393224 | tf_op jit(solution)/shard_map/ppermute | solution.py:253
  43.7 6.0 %collective-permute-start.15 = (bf16[64,1024]{1,0:T(8,128)(2,1)S(1)}, bf16[64,1024]{1,0:T(8,128)(2,1)S(1)}, u32[]{:S(2)}, u32[]{:S(2)}) collective-permute-start(bf16[64,1024]{1,0:T(8,128)(2,1)S(1)} %get-tuple-element.28.refs_1_), channel_id=1, source_target_pairs={{0,6},{1,7},{2,4},{3,5},{4,2},{5,3},{6,0},{7,1},{8,14},{9,15},{10,... | collective-permute-start | bytes 393224 | tf_op jit(solution)/shard_map/ppermute | solution.py:253
  50.7 5.0 %collective-permute-start.18 = (bf16[64,1024]{1,0:T(8,128)(2,1)S(1)}, bf16[64,1024]{1,0:T(8,128)(2,1)S(1)}, u32[]{:S(2)}, u32[]{:S(2)}) collective-permute-start(bf16[64,1024]{1,0:T(8,128)(2,1)S(1)} %shard_map.54.piece_ref.refs_0_), channel_id=1, source_target_pairs={{0,2},{1,3},{2,0},{3,1},{4,6},{5,7},{6,4},{7,5},{8,10},{9,11},{10,... | collective-permute-start | bytes 393224 | tf_op jit(solution)/shard_map/ppermute | solution.py:253
